TPU v7x, 32 devices: a whole 2x2x4 slice. The times are simulated.
32 devices in a mesh: rep: 8 (over z, y), shard: 4 (over x, core).
Axes of the slice: x: 2, y: 2, z: 4, core: 2. Of those that a mesh axis runs over, the one named last changes fastest.
Arguments:
- tokens: bfloat16 [2048, 4096], P('rep'), may hold values from -6 to 6
- in_weight: bfloat16 [3, 4096, 2048], P(None, None, 'shard'), may hold values from -0.09375 to 0.09375
- kernel: float32 [7, 3, 2048], P(None, None, 'shard'), may hold values from -2.5 to 2.5
- out_grad: bfloat16 [2048, 2048], P('rep', 'shard'), may hold values from -6 to 6
Outputs:
- token_grad: bfloat16 [2048, 4096], P('rep', 'shard')
- weight_grad: float32 [12288, 2048], P('rep', 'shard')
- kernel_grad: float32 [7, 3, 2048], P(None, None, 'shard')
All inputs are finite; a program needn't handle non-finite values.
Results may differ from a plain program's by a relative error of at most 0.0064.
Values sent between devices are 32-bit elements; how exact they have to be, the bound alone decides.
No kernel may reach another device: no remote copies, remote signals or barrier semaphores. Data moves between devices by JAX's collectives and lax.ppermute only.
A program may use at most 128 MiB of HBM per device.

v0:
```python
import math

import jax
import jax.numpy as jnp
from jax import lax
from jax.sharding import PartitionSpec as P

SEQ = 128


def causal_mix(values, kernel):
    width = kernel.shape[0]
    length = values.shape[1]
    padded = jnp.pad(values, ((0, 0), (width - 1, 0), (0, 0), (0, 0)))
    total = jnp.zeros_like(values)
    for offset in range(width):
        total = total + kernel[offset] * padded[:, width - 1 - offset : width - 1 - offset + length]
    return total


def causal_mix_back(grads, kernel):
    width = kernel.shape[0]
    length = grads.shape[1]
    padded = jnp.pad(grads, ((0, 0), (0, width - 1), (0, 0), (0, 0)))
    total = jnp.zeros_like(grads)
    for offset in range(width):
        total = total + kernel[offset] * padded[:, offset : offset + length]
    return total


def kernel_terms(values, grads, width):
    length = values.shape[1]
    padded = jnp.pad(values, ((0, 0), (width - 1, 0), (0, 0), (0, 0)))
    terms = []
    for offset in range(width):
        shifted = padded[:, width - 1 - offset : width - 1 - offset + length]
        terms.append(jnp.sum(shifted * grads, axis=(0, 1)))
    return jnp.stack(terms, axis=0)


def local(tokens, in_weight, kernel, out_grad):
    rows = tokens.shape[0]
    features = tokens.shape[1]
    chans = in_weight.shape[2]
    total_rows = rows * lax.axis_size("rep")
    mixed = jnp.einsum("td,sdc->tsc", tokens, in_weight, preferred_element_type=jnp.float32)
    stored = lax.optimization_barrier(mixed.astype(jnp.bfloat16))
    values = stored.astype(jnp.float32).reshape(rows // SEQ, SEQ, 3, chans)
    conv = causal_mix(values, kernel)
    query = conv[:, :, 0]
    keyed = conv[:, :, 1]
    valued = conv[:, :, 2]
    upstream = out_grad.astype(jnp.float32).reshape(rows // SEQ, SEQ, chans)
    conv_grad = jnp.stack(
        [upstream * keyed * valued, upstream * query * valued, upstream * query * keyed], axis=2
    )
    mixed_grad = causal_mix_back(conv_grad, kernel).reshape(rows, 3, chans).astype(jnp.bfloat16)
    scale = 1.0 / math.sqrt(total_rows)
    kernel_local = kernel_terms(values, conv_grad, kernel.shape[0]) * scale
    partial_grad = jnp.einsum(
        "tsc,sdc->td", mixed_grad, in_weight, preferred_element_type=jnp.float32
    )
    token_grad = lax.psum_scatter(partial_grad, "shard", scatter_dimension=1, tiled=True).astype(
        jnp.bfloat16
    )
    local_grad = (
        jnp.einsum("td,tsc->sdc", tokens, mixed_grad, preferred_element_type=jnp.float32) * scale
    )
    weight_grad = lax.psum_scatter(
        local_grad.reshape(3 * features, chans), "rep", scatter_dimension=0, tiled=True
    )
    kernel_grad = lax.psum(kernel_local, "rep")
    return (token_grad, weight_grad, kernel_grad)


def solution(mesh):
    placed = (P("rep", None), P(None, None, "shard"), P(None, None, "shard"), P("rep", "shard"))
    return jax.shard_map(
        local,
        mesh=mesh,
        in_specs=placed,
        out_specs=(P("rep", "shard"), P("rep", "shard"), P(None, None, "shard")),
        check_vma=False,
    )
```

profile of v0, /device:TPU:0, one launch (start us, length us, event | category | flops | bytes accessed | tf_op | source)
XLA Modules:
  0.0 498.5 jit_solution(17459930732396556700)
XLA Ops:
  7.2 0.0 copy-start
  7.2 0.0 reduce-scatter.3.cloned.1.call-start
  7.2 1.2 fusion.10
  8.4 0.5 copy-done
  8.9 6.5 %fusion.6 = bf16[256,3,512]{2,0,1:T(8,128)(2,1)S(1)} fusion(bf16[3,4096,512]{2,1,0:T(8,128)(2,1)} %param.5, bf16[256,4096]{1,0:T(8,128)(2,1)S(1)} %copy-done), kind=kOutput, calls=%fused_computation.24 | convolution fusion | flops 3221618688 | bytes 15466496 | tf_op jit(solution)/shard_map/td,sdc->tsc/dot_general | solution.py:46
  15.4 0.2 bitcast_convert_fusion
  15.7 0.6 copy-done.4
  16.3 1.3 multiply_add_fusion
  17.6 0.2 fusion.9
  17.8 1.4 multiply_reduce_fusion
  19.2 1.3 add_convert_fusion
  20.5 0.0 copy-start.3
  20.5 0.9 copy-done.3
  21.4 14.1 %convolution_bitcast_fusion = f32[256,4096]{1,0:T(8,128)} fusion(bf16[256,3,512]{2,0,1:T(8,128)(2,1)S(1)} %bitcast.58, bf16[3,4096,512]{2,1,0:T(8,128)(2,1)} %param.5), kind=kOutput, calls=%fused_computation.1 | convolution fusion | flops 3221225472 | bytes 17563648 | tf_op jit(solution)/shard_map/tsc,sdc->td/dot_general | solution.py:60
  35.4 0.0 reduce-scatter.3.cloned.1.call-update
  35.5 0.0 reduce-scatter.5.cloned.1.call-start
  35.5 12.8 %multiply_bitcast_fusion = f32[3,4096,512]{1,2,0:T(8,128)} fusion(bf16[256,3,512]{2,0,1:T(8,128)(2,1)} %bitcast.59, bf16[256,4096]{1,0:T(8,128)(2,1)S(1)} %copy-done), kind=kOutput, calls=%fused_computation | convolution fusion | flops 3227516928 | bytes 28049408 | tf_op jit(solution)/shard_map/td,tsc->sdc/dot_general | solution.py:67
  48.3 24.8 %copy.11 = f32[3,4096,512]{2,1,0:T(8,128)} copy(f32[3,4096,512]{1,2,0:T(8,128)} %multiply_bitcast_fusion) | data formatting | bytes 50331648 | tf_op jit(solution)/shard_map/mul | solution.py:67
  73.2 0.0 reduce-scatter.5.cloned.1.call-update
  73.2 1.7 fusion.3
  75.0 40.5 %psum.7 = f32[7,3,512]{2,1,0:T(4,128)S(1)} all-reduce(f32[7,3,512]{2,1,0:T(4,128)S(1)} %broadcast_multiply_fusion), channel_id=1, replica_groups=mesh['rep'=8,'shard'=4] {'rep'}, use_global_device_ids=true, to_apply=%region_9.10 | all-reduce | flops 10752 | bytes 86016 | tf_op jit(solution)/shard_map/psum | solution.py:72
  115.5 0.6 copy.12
  116.2 2.1 convert_element_type.25
  118.3 373.4 %reduce-scatter.5.cloned.1.call-done = f32[1536,512]{1,0:T(8,128)} async-done(((f32[12288,512]{1,0:T(8,128)}), f32[1536,512]{1,0:T(8,128)}) %reduce-scatter.5.cloned.1.call-update) | async-done | bytes 3145744 | tf_op jit(solution)/shard_map/reduce_scatter | solution.py:69
  (20 shorter events, 0.1 us)
Async XLA Ops:
  7.2 1.8 copy-start
  7.2 109.0 %reduce-scatter.3.cloned.1.call-start = ((), (), s32[]{:S(2)}) async-start(), calls=%async_computation.2 | async-start | bytes 5242880 | tf_op jit(solution)/shard_map/reduce_scatter | solution.py:63
  15.4 0.9 copy-start.4
  16.3 1.3 copy-start.5
  17.8 1.4 copy-start.2
  20.5 0.9 copy-start.3
  35.5 456.2 %reduce-scatter.5.cloned.1.call-start = ((), (), s32[]{:S(2)}) async-start(), calls=%async_computation.3 | async-start | bytes 28311552 | tf_op jit(solution)/shard_map/reduce_scatter | solution.py:69
  73.2 418.5 %copy-start.1 = (bf16[256,4096]{1,0:T(8,128)(2,1)S(1)}, bf16[256,4096]{1,0:T(8,128)(2,1)}, u32[]{:S(2)}) copy-start(bf16[256,4096]{1,0:T(8,128)(2,1)} %param.4) | copy-start | bytes 6291460
Sparse Core Ops, SparseCore 0:
  35.6 47.2 reduce-scatter.2
  87.8 403.7 reduce-scatter.4
where the time goes:
time: 499 us
  waiting for transfers between devices  373 us (75%)
  blocking collectives  40.5 us (8%)
  matrix products  33.4 us (7%)
  local copies, waits for them, and re-layouts  28.8 us (6%)
  between operations  14.2 us (3%)
  other arithmetic  8.14 us (2%)
    reduce_scatter x1, waiting for transfers between devices, local(): lax.psum_scatter(local_grad.reshape(3 * features, chans), 'rep', scatter_...  373 us
    psum x1, blocking collectives, local(): kernel_grad = lax.psum(kernel_local, 'rep')  40.5 us
    mul x1, local copies, waits for them, and re-layouts, local(): jnp.einsum('td,tsc->sdc', tokens, mixed_grad, preferred_element_type=jnp....  24.8 us
    dot_general x1, matrix products, local(): jnp.einsum('tsc,sdc->td', mixed_grad, in_weight, preferred_element_type=j...  14.1 us
    dot_general x1, matrix products, local(): jnp.einsum('td,tsc->sdc', tokens, mixed_grad, preferred_element_type=jnp....  12.8 us
  transfers between devices with their start and end apart: 2, of which 1 were waited for; matrix products, arithmetic and copies ran while one was open for 8% of the time, Pallas kernels for 0%

commit v1 on v0

--- a/solution.py
+++ b/solution.py
@@ -1,8 +1,11 @@
+import functools
 import math
 
 import jax
 import jax.numpy as jnp
 from jax import lax
+from jax.experimental import pallas as pl
+from jax.experimental.pallas import tpu as pltpu
 from jax.sharding import PartitionSpec as P
 
 SEQ = 128
@@ -38,11 +41,9 @@
     return jnp.stack(terms, axis=0)
 
 
-def local(tokens, in_weight, kernel, out_grad):
+def gated_grads(tokens, in_weight, kernel, out_grad):
     rows = tokens.shape[0]
-    features = tokens.shape[1]
     chans = in_weight.shape[2]
-    total_rows = rows * lax.axis_size("rep")
     mixed = jnp.einsum("td,sdc->tsc", tokens, in_weight, preferred_element_type=jnp.float32)
     stored = lax.optimization_barrier(mixed.astype(jnp.bfloat16))
     values = stored.astype(jnp.float32).reshape(rows // SEQ, SEQ, 3, chans)
@@ -54,9 +55,16 @@
     conv_grad = jnp.stack(
         [upstream * keyed * valued, upstream * query * valued, upstream * query * keyed], axis=2
     )
-    mixed_grad = causal_mix_back(conv_grad, kernel).reshape(rows, 3, chans).astype(jnp.bfloat16)
-    scale = 1.0 / math.sqrt(total_rows)
-    kernel_local = kernel_terms(values, conv_grad, kernel.shape[0]) * scale
+    mixed_grad = causal_mix_back(conv_grad, kernel).reshape(rows, 3, chans)
+    return mixed_grad, kernel_terms(values, conv_grad, kernel.shape[0])
+
+
+def plain(tokens, in_weight, kernel, out_grad):
+    features = tokens.shape[1]
+    chans = in_weight.shape[2]
+    scale = 1.0 / math.sqrt(tokens.shape[0] * lax.axis_size("rep"))
+    wide_grad, taps = gated_grads(tokens, in_weight, kernel, out_grad)
+    mixed_grad = wide_grad.astype(jnp.bfloat16)
     partial_grad = jnp.einsum(
         "tsc,sdc->td", mixed_grad, in_weight, preferred_element_type=jnp.float32
     )
@@ -69,14 +77,236 @@
     weight_grad = lax.psum_scatter(
         local_grad.reshape(3 * features, chans), "rep", scatter_dimension=0, tiled=True
     )
-    kernel_grad = lax.psum(kernel_local, "rep")
+    kernel_grad = lax.psum(taps * scale, "rep")
     return (token_grad, weight_grad, kernel_grad)
+
+
+LEVELS = 4
+BLOCK = 512
+
+
+def along(array, levels, shift):
+    perm = [(2 * z + y, 2 * (z + shift) + y) for z in levels for y in range(2)]
+    return lax.ppermute(array, "rep", perm) if perm else None
+
+
+def spread(array, needed):
+    ups, downs = [], []
+    for going, out in ((1, ups), (-1, downs)):
+        now = array
+        for step in range(LEVELS - 1):
+            if going == 1:
+                levels = [z for z in range(step, LEVELS - 1) if z + 1 <= max(needed)]
+            else:
+                levels = [z for z in range(1, LEVELS - step) if z - 1 >= min(needed)]
+            now = along(now, levels, going) if levels else None
+            if now is None:
+                break
+            out.append(now)
+    return ups, downs
+
+
+def source(level, slot):
+    if slot == 1:
+        return ("up", 1) if level >= 2 else ("down", 1)
+    if slot == 2:
+        return ("up", 2) if level >= 2 else ("down", 2)
+    return (("down", 3), ("up", 1), ("down", 1), ("up", 3))[level]
+
+
+def gather_tokens_body(rows, place, own, p1, p2, s1, s3, out, held):
+    level, quarter = place[0], place[2]
+    part = rows // 4
+    inner = jnp.logical_or(level == 1, level == 2)
+    for j in range(6):
+        cols = slice(BLOCK * j, BLOCK * (j + 1))
+        block = lax.rem(6 * level + j, 8)
+        column = pl.ds(pl.multiple_of(block * BLOCK, BLOCK), BLOCK)
+        held[0:rows, :] = own[:, column].astype(jnp.float32)
+        for k in range(4):
+            where = pl.multiple_of(jnp.bitwise_xor(quarter, k) * part, part)
+            held[pl.ds(rows + where, part), :] = p1[k][:, cols]
+            held[pl.ds(2 * rows + where, part), :] = p2[k][:, cols]
+
+            @pl.when(inner)
+            def _():
+                held[pl.ds(3 * rows + where, part), :] = s1[k][:, cols]
+
+            @pl.when(jnp.logical_not(inner))
+            def _():
+                held[pl.ds(3 * rows + where, part), :] = s3[k][:, cols]
+
+        out[j] = held[...].T.astype(jnp.bfloat16)
+
+
+def gather_tokens(place, own, slots):
+    rows = own.shape[0]
+
+    def body(place, own, *refs):
+        groups = [refs[4 * i : 4 * i + 4] for i in range(4)]
+        gather_tokens_body(rows, place, own, *groups, refs[16], refs[17])
+
+    return pl.pallas_call(
+        body,
+        out_shape=jax.ShapeDtypeStruct((6, BLOCK, 4 * rows), jnp.bfloat16),
+        in_specs=[pl.BlockSpec(memory_space=pltpu.SMEM)]
+        + [pl.BlockSpec(memory_space=pltpu.VMEM)] * 17,
+        out_specs=pl.BlockSpec(memory_space=pltpu.VMEM),
+        scratch_shapes=[pltpu.VMEM((4 * rows, BLOCK), jnp.float32)],
+        compiler_params=pltpu.CompilerParams(vmem_limit_bytes=48 * 2**20),
+        name="arrange_tokens",
+    )(place, own, *[piece for slot in slots for piece in slot])
+
+
+def weight_part(place, tok, own, moved, names):
+    rows = own.shape[1]
+    width = own.shape[2]
+
+    def body(place, tok, own, *refs):
+        send, keep, held = refs[-3], refs[-2], refs[-1]
+        table = dict(zip(names, refs[:-3]))
+        level, column = place[0], place[1]
+        for z in range(LEVELS):
+
+            @pl.when(level == z)
+            def _():
+                low = (6 * z) // 8
+                for side, stream in enumerate((low, min(low + 1, (6 * z + 5) // 8))):
+                    held[side, 0:rows, :] = own[stream].astype(jnp.bfloat16)
+                    for slot in (1, 2, 3):
+                        way, far = source(z, slot)
+                        held[side, slot * rows : (slot + 1) * rows, :] = table[(stream, way, far)][
+                            ...
+                        ].astype(jnp.bfloat16)
+
+        low = lax.div(6 * level, 8)
+        for i in range(3):
+            for out, col in ((send, 1 - column), (keep, column)):
+                j = 3 * col + i
+                side = lax.div(6 * level + j, 8) - low
+                out[BLOCK * i : BLOCK * (i + 1), :] = jnp.dot(
+                    tok[j], held[side], preferred_element_type=jnp.float32
+                )
+
+    half = jax.ShapeDtypeStruct((3 * BLOCK, width), jnp.float32)
+    return pl.pallas_call(
+        body,
+        out_shape=(half, half),
+        in_specs=[pl.BlockSpec(memory_space=pltpu.SMEM)]
+        + [pl.BlockSpec(memory_space=pltpu.VMEM)] * (2 + len(names)),
+        out_specs=(pl.BlockSpec(memory_space=pltpu.VMEM),) * 2,
+        scratch_shapes=[pltpu.VMEM((2, 4 * rows, width), jnp.bfloat16)],
+        compiler_params=pltpu.CompilerParams(vmem_limit_bytes=48 * 2**20),
+        name="weight_part",
+    )(place, tok, own, *[moved[name] for name in names])
+
+
+CHUNKS = 2
+
+
+def lined(tokens, in_weight, kernel, out_grad):
+    rows, features = tokens.shape
+    chans = in_weight.shape[2]
+    rep = lax.axis_index("rep")
+    quarter = lax.axis_index("shard")
+    level, column = rep // 2, rep % 2
+    place = jnp.stack([level, column, quarter]).astype(jnp.int32)
+    scale = 1.0 / math.sqrt(rows * lax.axis_size("rep"))
+    part = rows // 4
+    wide = features // 4
+    upper = level >= 2
+
+    piece = lax.dynamic_slice(tokens, (quarter * part, 0), (part, features)).astype(jnp.float32)
+    ups, downs = {}, {}
+    for k in range(4):
+        needed = [z for z in range(LEVELS) if any((3 * z + i) % 4 == k for i in range(3))]
+        ups[k], downs[k] = spread(piece[:, wide * k : wide * (k + 1)], needed)
+
+    def chosen(use_up, far_up, far_down):
+        whole = []
+        for k in range(4):
+            up = ups[k][far_up - 1] if len(ups[k]) >= far_up else None
+            down = downs[k][far_down - 1] if len(downs[k]) >= far_down else None
+            if up is None:
+                up = down
+            if down is None:
+                down = up
+            whole.append(jnp.where(use_up, up, down))
+        doubled = jnp.concatenate(whole + whole[:2], axis=1)
+        return lax.dynamic_slice(doubled, (0, wide * ((3 * level) % 4)), (part, 3 * wide))
+
+    def share(array, levels):
+        def pairs(flip):
+            return [
+                (4 * (2 * z + y) + q, 4 * (2 * z + y) + (q ^ flip))
+                for z in levels
+                for y in range(2)
+                for q in range(4)
+            ]
+
+        across = lax.ppermute(array, ("rep", "shard"), pairs(2))
+        beside = lax.ppermute(array, ("rep", "shard"), pairs(1))
+        both = lax.ppermute(across, ("rep", "shard"), pairs(1))
+        return (array, beside, across, both)
+
+    slots = [
+        share(chosen(upper, 1, 1), range(LEVELS)),
+        share(chosen(upper, 2, 2), range(LEVELS)),
+        share(chosen(level == 1, 1, 1), (1, 2)),
+        share(chosen(level == 3, 3, 3), (0, 3)),
+    ]
+
+    wide_grad, taps = gated_grads(tokens, in_weight, kernel, out_grad)
+    wide_grad = jnp.transpose(wide_grad, (1, 0, 2))
+
+    tok = gather_tokens(place, tokens, slots)
+    got = []
+    cw = chans // CHUNKS
+    for h in range(CHUNKS):
+        moved = {}
+        mine = wide_grad[:, :, cw * h : cw * (h + 1)]
+        for stream in range(3):
+            needed = [
+                z for z in range(LEVELS) if (6 * z) // 8 <= stream <= (6 * z + 5) // 8
+            ]
+            up, down = spread(mine[stream], needed)
+            for i, array in enumerate(up):
+                moved[(stream, "up", i + 1)] = array
+            for i, array in enumerate(down):
+                moved[(stream, "down", i + 1)] = array
+        used = set()
+        for z in range(LEVELS):
+            for stream in {(6 * z) // 8, (6 * z + 5) // 8}:
+                for slot in (1, 2, 3):
+                    used.add((stream,) + source(z, slot))
+        names = sorted(used)
+        send, keep = weight_part(place, tok, mine, moved, names)
+        other = lax.ppermute(send, "rep", [(r, r ^ 1) for r in range(2 * LEVELS)])
+        got.append((keep + other) * scale)
+    weight_grad = jnp.concatenate(got, axis=1)
+
+    mixed_grad = wide_grad.astype(jnp.bfloat16)
+    partial = jnp.einsum("stc,sdc->td", mixed_grad, in_weight, preferred_element_type=jnp.float32)
+    partial = partial.reshape(rows, 2, 2, wide)
+    core, side = quarter % 2, quarter // 2
+    pick = lambda array, index, axis: lax.dynamic_index_in_dim(array, index, axis, keepdims=False)
+    first = pick(partial, core, 2) + lax.ppermute(
+        pick(partial, 1 - core, 2), "shard", [(q, q ^ 1) for q in range(4)]
+    )
+    token_grad = pick(first, side, 1) + lax.ppermute(
+        pick(first, 1 - side, 1), "shard", [(q, q ^ 2) for q in range(4)]
+    )
+
+    for bit in (1, 2, 4):
+        taps = taps + lax.ppermute(taps, "rep", [(r, r ^ bit) for r in range(2 * LEVELS)])
+    return (token_grad.astype(jnp.bfloat16), weight_grad, taps * scale)
 
 
 def solution(mesh):
     placed = (P("rep", None), P(None, None, "shard"), P(None, None, "shard"), P("rep", "shard"))
+    line = mesh.shape["rep"] == 2 * LEVELS and mesh.shape["shard"] == 4
     return jax.shard_map(
-        local,
+        lined if line else plain,
         mesh=mesh,
         in_specs=placed,
         out_specs=(P("rep", "shard"), P("rep", "shard"), P(None, None, "shard")),

time: 499 us -> 342 us (0.69)
  waiting for transfers between devices: 373 us -> 130 us
  starting transfers between devices: 0.08 us -> 113 us
  blocking collectives: 40.5 us -> 0 us
  Pallas kernels: 0 us -> 22.5 us
  matrix products: 33.4 us -> 21.3 us
  between operations: 14.2 us -> 2.18 us
  other arithmetic: 8.14 us -> 18.6 us
    reduce_scatter x2 -> x0, waiting for transfers between devices: 373 us -> none  [the longest x1 373 us: local(): lax.psum_scatter(local_grad.reshape(3 * features, chans), 'rep', scatter_...]
    ppermute x0 -> x65, waiting for transfers between devices: none -> 130 us  [the longest x46 53.1 us: along(): return lax.ppermute(array, 'rep', perm) if perm else None]
    ppermute x0 -> x65, starting transfers between devices: none -> 113 us  [the longest x46 86.3 us: along(): return lax.ppermute(array, 'rep', perm) if perm else None]
    psum x1 -> x0, blocking collectives: 40.5 us -> none  [local(): kernel_grad = lax.psum(kernel_local, 'rep')]
    mul x1 -> x0, local copies, waits for them, and re-layouts: 24.8 us -> none  [local(): jnp.einsum('td,tsc->sdc', tokens, mixed_grad, preferred_element_type=jnp....]
    pallas_call x0 -> x3, Pallas kernels: none -> 22.5 us  [the longest x2 11.8 us: weight_part(): pl.pallas_call(body, out_shape=(half, half), in_specs=[pl.BlockSpec(memor...]
    dot_general x3 -> x2, matrix products: 33.4 us -> 21.3 us  [the longest x1 14.8 us: lined(): jnp.einsum('stc,sdc->td', mixed_grad, in_weight, preferred_element_type=j...]
    dynamic_slice x0 -> x5, local copies, waits for them, and re-layouts: none -> 10.9 us  [the longest x1 9.79 us: lined(): lax.dynamic_index_in_dim(array, index, axis, keepdims=False)]
  transfers between devices with their start and end apart: 2 -> 65, of which waited for: 1 -> 18; matrix products, arithmetic and copies ran while one was open for 8% -> 18% of each run, Pallas kernels for 0% -> 7%
where the time goes in v1:
time: 342 us; the launch traced here: 340 us
  waiting for transfers between devices  130 us (38%)
  starting transfers between devices  113 us (33%)
  local copies, waits for them, and re-layouts  32.3 us (9%)
  Pallas kernels  22.5 us (7%)
  matrix products  21.3 us (6%)
  other arithmetic  18.6 us (5%)
    ppermute x46, starting transfers between devices, along(): return lax.ppermute(array, 'rep', perm) if perm else None  86.3 us
    ppermute x46, waiting for transfers between devices, along(): return lax.ppermute(array, 'rep', perm) if perm else None  53.1 us
    ppermute x3, waiting for transfers between devices, lined(): lax.ppermute(taps, 'rep', [(r, r ^ bit) for r in range(2 * LEVELS)])  50.3 us
    ppermute x4, waiting for transfers between devices, share(): across = lax.ppermute(array, ('rep', 'shard'), pairs(2))  26.5 us
    dot_general x1, matrix products, lined(): jnp.einsum('stc,sdc->td', mixed_grad, in_weight, preferred_element_type=j...  14.8 us
    pallas_call x2, Pallas kernels, weight_part(): pl.pallas_call(body, out_shape=(half, half), in_specs=[pl.BlockSpec(memor...  11.8 us
    pallas_call x1, Pallas kernels, gather_tokens(): pl.pallas_call(body, out_shape=jax.ShapeDtypeStruct((6, BLOCK, 4 * rows),...  10.7 us
    unnamed x117, local copies, waits for them, and re-layouts  9.8 us
  transfers between devices with their start and end apart: 65, of which 18 were waited for; matrix products, arithmetic and copies ran while one was open for 18% of the time, Pallas kernels for 7%

profile of v1, /device:TPU:0, one launch (start us, length us, event | category | flops | bytes accessed | tf_op | source)
XLA Modules:
  0.0 340.0 jit_solution(691661543227495352)
XLA Ops:
  2.9 4.9 %collective-permute-start.2 = (f32[64,1024]{1,0:T(8,128)}, f32[64,1024]{1,0:T(8,128)S(1)}, u32[]{:S(2)}, u32[]{:S(2)}) collective-permute-start(f32[64,1024]{1,0:T(8,128)} %get-tuple-element.39), channel_id=1, source_target_pairs={{0,8},{4,12},{8,16},{12,20},{1,9},{5,13},{9,17},{13,21},{2,10},{6,... | collective-permute-start | bytes 786440 | tf_op jit(solution)/shard_map/ppermute | solution.py:90
  9.2 4.6 %collective-permute-start.4 = (f32[64,1024]{1,0:T(8,128)}, f32[64,1024]{1,0:T(8,128)S(1)}, u32[]{:S(2)}, u32[]{:S(2)}) collective-permute-start(f32[64,1024]{1,0:T(8,128)} %get-tuple-element.38), channel_id=1, source_target_pairs={{0,8},{4,12},{8,16},{12,20},{16,24},{20,28},{1,9},{5,13},{9,17},{1... | collective-permute-start | bytes 786440 | tf_op jit(solution)/shard_map/ppermute | solution.py:90
  15.0 4.6 %collective-permute-start.6 = (f32[64,1024]{1,0:T(8,128)}, f32[64,1024]{1,0:T(8,128)S(1)}, u32[]{:S(2)}, u32[]{:S(2)}) collective-permute-start(f32[64,1024]{1,0:T(8,128)} %get-tuple-element.37), channel_id=1, source_target_pairs={{0,8},{4,12},{8,16},{12,20},{16,24},{20,28},{1,9},{5,13},{9,17},{1... | collective-permute-start | bytes 786440 | tf_op jit(solution)/shard_map/ppermute | solution.py:90
  19.7 6.5 %fusion.6 = bf16[256,3,512]{2,0,1:T(8,128)(2,1)S(1)} fusion(bf16[3,4096,512]{2,1,0:T(8,128)(2,1)} %param.5, bf16[256,4096]{1,0:T(8,128)(2,1)S(1)} %copy-done.36), kind=kOutput, calls=%fused_computation.28 | convolution fusion | flops 3221618688 | bytes 15466496 | tf_op jit(solution)/shard_map/td,sdc->tsc/dot_general | solution.py:47
  31.4 14.8 %convolution_bitcast_fusion = f32[256,4096]{1,0:T(8,128)} fusion(bf16[3,4096,512]{2,1,0:T(8,128)(2,1)} %param.5, f32[3,256,512]{2,1,0:T(8,128)S(1)} %bitcast.77), kind=kOutput, calls=%fused_computation | convolution fusion | flops 3221618688 | bytes 18350080 | tf_op jit(solution)/shard_map/stc,sdc->td/dot_general | solution.py:289
  46.2 6.6 %reshape.38 = f32[256,2,2,1024]{3,2,1,0:T(2,128)} reshape(f32[256,4096]{1,0:T(8,128)} %convolution_bitcast_fusion) | data formatting | bytes 8388608 | tf_op jit(solution)/shard_map/reshape | solution.py:290
  52.8 9.8 %constant_dynamic-slice_fusion.5 = (f32[256,2,1,1024]{3,2,1,0:T(1,128)}, f32[256,2,1,1024]{3,2,1,0:T(1,128)}) fusion(f32[256,2,2,1024]{3,2,1,0:T(2,128)} %reshape.38, s32[]{:T(128)S(6)} %select_n.120, s32[]{:T(128)S(6)} %select_n.121), kind=kLoop, calls=%fused_computation.96 | loop fusion | bytes 8388616 | tf_op jit(solution)/shard_map/jit(dynamic_index_in_dim)/dynamic_slice | solution.py:292
  68.7 4.6 %collective-permute-start.8 = (f32[64,1024]{1,0:T(8,128)S(1)}, f32[64,1024]{1,0:T(8,128)S(1)}, u32[]{:S(2)}, u32[]{:S(2)}) collective-permute-start(f32[64,1024]{1,0:T(8,128)S(1)} %copy-done.49), channel_id=1, source_target_pairs={{0,8},{4,12},{8,16},{12,20},{16,24},{20,28},{1,9},{5,13},{9,17},{1... | collective-permute-start | bytes 786440 | tf_op jit(solution)/shard_map/ppermute | solution.py:90
  81.6 13.2 %collective-permute-done.14 = f32[64,1024]{1,0:T(8,128)S(1)} collective-permute-done((f32[64,1024]{1,0:T(8,128)S(1)}, f32[64,1024]{1,0:T(8,128)S(1)}, u32[]{:S(2)}, u32[]{:S(2)}) %collective-permute-start.14) | collective-permute-done | bytes 262176 | tf_op jit(solution)/shard_map/ppermute | solution.py:90
  103.1 10.1 %collective-permute-start.42 = (f32[256,256]{1,0:T(8,128)S(1)}, f32[256,256]{1,0:T(8,128)S(1)}, u32[]{:S(2)}, u32[]{:S(2)}) collective-permute-start(f32[256,256]{1,0:T(8,128)S(1)} %copy-done.47), channel_id=1, source_target_pairs={{0,8},{4,12},{8,16},{12,20},{1,9},{5,13},{9,17},{13,21},{2,10},{6,... | collective-permute-start | bytes 786440 | tf_op jit(solution)/shard_map/ppermute | solution.py:90
  113.3 5.2 %collective-permute-start.39 = (f32[256,256]{1,0:T(8,128)}, f32[256,256]{1,0:T(8,128)S(1)}, u32[]{:S(2)}, u32[]{:S(2)}) collective-permute-start(f32[256,256]{1,0:T(8,128)} %get-tuple-element.33), channel_id=1, source_target_pairs={{0,8},{4,12},{1,9},{5,13},{2,10},{6,14},{3,11},{7,15}} | collective-permute-start | bytes 786440 | tf_op jit(solution)/shard_map/ppermute | solution.py:90
  120.6 9.1 %collective-permute-done.45.refs_9_ = f32[256,256]{1,0:T(8,128)S(1)} collective-permute-done((f32[256,256]{1,0:T(8,128)S(1)}, f32[256,256]{1,0:T(8,128)S(1)}, u32[]{:S(2)}, u32[]{:S(2)}) %collective-permute-start.45) | collective-permute-done | bytes 262176 | tf_op jit(solution)/shard_map/ppermute | solution.py:90
  130.4 5.0 %collective-permute-start.55 = (f32[256,256]{1,0:T(8,128)S(1)}, f32[256,256]{1,0:T(8,128)S(1)}, u32[]{:S(2)}, u32[]{:S(2)}) collective-permute-start(f32[256,256]{1,0:T(8,128)S(1)} %copy-done.45), channel_id=1, source_target_pairs={{0,8},{4,12},{8,16},{12,20},{1,9},{5,13},{9,17},{13,21},{2,10},{6,... | collective-permute-start | bytes 786440 | tf_op jit(solution)/shard_map/ppermute | solution.py:90
  137.5 5.2 %collective-permute-start.58 = (f32[256,256]{1,0:T(8,128)S(1)}, f32[256,256]{1,0:T(8,128)S(1)}, u32[]{:S(2)}, u32[]{:S(2)}) collective-permute-start(f32[256,256]{1,0:T(8,128)S(1)} %get-tuple-element.29), channel_id=1, source_target_pairs={{0,8},{4,12},{8,16},{12,20},{16,24},{20,28},{1,9},{5,13},{9,17},{1... | collective-permute-start | bytes 786440 | tf_op jit(solution)/shard_map/ppermute | solution.py:90
  151.8 5.2 %collective-permute-done.27 = f32[64,1024]{1,0:T(8,128)S(1)} collective-permute-done((f32[64,1024]{1,0:T(8,128)S(1)}, f32[64,1024]{1,0:T(8,128)S(1)}, u32[]{:S(2)}, u32[]{:S(2)}) %collective-permute-start.27) | collective-permute-done | bytes 262176 | tf_op jit(solution)/shard_map/ppermute | solution.py:90
  187.5 11.7 %collective-permute-done.22.refs_6_ = f32[64,3072]{1,0:T(8,128)} collective-permute-done((f32[64,3072]{1,0:T(8,128)S(1)}, f32[64,3072]{1,0:T(8,128)}, u32[]{:S(2)}, u32[]{:S(2)}) %collective-permute-start.22) | collective-permute-done | bytes 786464 | tf_op jit(solution)/shard_map/ppermute | solution.py:247
  200.8 11.8 %collective-permute-done.34.refs_14_ = f32[64,3072]{1,0:T(8,128)} collective-permute-done((f32[64,3072]{1,0:T(8,128)}, f32[64,3072]{1,0:T(8,128)}, u32[]{:S(2)}, u32[]{:S(2)}) %collective-permute-start.34) | collective-permute-done | bytes 786464 | tf_op jit(solution)/shard_map/ppermute | solution.py:247
  216.9 7.2 %collective-permute-start.52 = (f32[256,256]{1,0:T(8,128)}, f32[256,256]{1,0:T(8,128)S(1)}, u32[]{:S(2)}, u32[]{:S(2)}) collective-permute-start(f32[256,256]{1,0:T(8,128)} %get-tuple-element.31), channel_id=1, source_target_pairs={{0,8},{4,12},{1,9},{5,13},{2,10},{6,14},{3,11},{7,15}} | collective-permute-start | bytes 786440 | tf_op jit(solution)/shard_map/ppermute | solution.py:90
  230.2 10.7 %arrange_tokens.1.tok = bf16[6,512,1024]{2,1,0:T(8,128)(2,1)} custom-call(s32[3]{0:T(128)S(1)} %pad_add_fusion.place, bf16[256,4096]{1,0:T(8,128)(2,1)} %own.1, f32[64,3072]{1,0:T(8,128)S(1)} %constant_dynamic-slice_fusion.3.refs_0_, f32[64,3072]{1,0:T(8,128)S(1)} %collective-permute-done.10.refs_1_, f32[64,3072]{1,0:T(8,128)S(1)} %collective-permute-done.11.refs_2_, ...), custom_call_target="tpu_custom_call" | custom-call | tf_op jit(solution)/shard_map/arrange_tokens/pallas_call | solution.py:149
  241.0 5.9 %weight_part.2 = (f32[1536,256]{1,0:T(8,128)S(1)}, f32[1536,256]{1,0:T(8,128)}) custom-call(s32[3]{0:T(128)S(1)} %pad_add_fusion.place, bf16[6,512,1024]{2,1,0:T(8,128)(2,1)} %arrange_tokens.1.tok, f32[3,256,256]{2,1,0:T(8,128)S(1)} %get-tuple-element.34.own, f32[256,256]{1,0:T(8,128)S(1)} %collective-permute-done.36.refs_0_, f32[256,256]{1,0:T(8,128)S(1)} %copy-done.19, ...), custom_call_target="tpu_custom_call" | custom-call | tf_op jit(solution)/shard_map/weight_part/pallas_call | solution.py:192
  253.9 11.1 %collective-permute-done.51.refs_2_ = f32[256,256]{1,0:T(8,128)S(1)} collective-permute-done((f32[256,256]{1,0:T(8,128)S(1)}, f32[256,256]{1,0:T(8,128)S(1)}, u32[]{:S(2)}, u32[]{:S(2)}) %collective-permute-start.51) | collective-permute-done | bytes 262176 | tf_op jit(solution)/shard_map/ppermute | solution.py:90
  265.0 5.9 %weight_part.3 = (f32[1536,256]{1,0:T(8,128)S(1)}, f32[1536,256]{1,0:T(8,128)}) custom-call(s32[3]{0:T(128)S(1)} %pad_add_fusion.place, bf16[6,512,1024]{2,1,0:T(8,128)(2,1)} %arrange_tokens.1.tok, f32[3,256,256]{2,1,0:T(8,128)S(1)} %get-tuple-element.35.own, f32[256,256]{1,0:T(8,128)S(1)} %copy-done.5, f32[256,256]{1,0:T(8,128)S(1)} %collective-permute-done.50.refs_1_, ...), custom_call_target="tpu_custom_call" | custom-call | tf_op jit(solution)/shard_map/weight_part/pallas_call | solution.py:192
  272.9 45.4 %collective-permute-done.62 = f32[7,3,512]{2,1,0:T(4,128)S(1)} collective-permute-done((f32[7,3,512]{2,1,0:T(4,128)S(1)}, f32[7,3,512]{2,1,0:T(4,128)S(1)}, u32[]{:S(2)}, u32[]{:S(2)}) %collective-permute-start.62) | collective-permute-done | bytes 43040 | tf_op jit(solution)/shard_map/ppermute | solution.py:301
  324.3 4.2 %collective-permute-start.64 = (f32[7,3,512]{2,1,0:T(4,128)S(1)}, f32[7,3,512]{2,1,0:T(4,128)S(1)}, u32[]{:S(2)}, u32[]{:S(2)}) collective-permute-start(f32[7,3,512]{2,1,0:T(4,128)S(1)} %add.127), channel_id=1, source_target_pairs={{0,16},{4,20},{8,24},{12,28},{16,0},{20,4},{24,8},{28,12},{1,17},{... | collective-permute-start | bytes 129032 | tf_op jit(solution)/shard_map/ppermute | solution.py:301
  (275 shorter events, 114.6 us)
Async XLA Ops:
  2.9 64.5 %collective-permute-start.2 = (f32[64,1024]{1,0:T(8,128)}, f32[64,1024]{1,0:T(8,128)S(1)}, u32[]{:S(2)}, u32[]{:S(2)}) collective-permute-start(f32[64,1024]{1,0:T(8,128)} %get-tuple-element.39), channel_id=1, source_target_pairs={{0,8},{4,12},{8,16},{12,20},{1,9},{5,13},{9,17},{13,21},{2,10},{6,... | collective-permute-start | bytes 786440 | tf_op jit(solution)/shard_map/ppermute | solution.py:90
  7.9 60.8 %collective-permute-start.3 = (f32[64,1024]{1,0:T(8,128)}, f32[64,1024]{1,0:T(8,128)S(1)}, u32[]{:S(2)}, u32[]{:S(2)}) collective-permute-start(f32[64,1024]{1,0:T(8,128)} %get-tuple-element.39), channel_id=1, source_target_pairs={{8,0},{12,4},{16,8},{20,12},{24,16},{28,20},{9,1},{13,5},{17,9},{2... | collective-permute-start | bytes 786440 | tf_op jit(solution)/shard_map/ppermute | solution.py:90
  9.2 64.1 %collective-permute-start.4 = (f32[64,1024]{1,0:T(8,128)}, f32[64,1024]{1,0:T(8,128)S(1)}, u32[]{:S(2)}, u32[]{:S(2)}) collective-permute-start(f32[64,1024]{1,0:T(8,128)} %get-tuple-element.38), channel_id=1, source_target_pairs={{0,8},{4,12},{8,16},{12,20},{16,24},{20,28},{1,9},{5,13},{9,17},{1... | collective-permute-start | bytes 786440 | tf_op jit(solution)/shard_map/ppermute | solution.py:90
  13.7 60.3 %collective-permute-start.5 = (f32[64,1024]{1,0:T(8,128)}, f32[64,1024]{1,0:T(8,128)S(1)}, u32[]{:S(2)}, u32[]{:S(2)}) collective-permute-start(f32[64,1024]{1,0:T(8,128)} %get-tuple-element.38), channel_id=1, source_target_pairs={{8,0},{12,4},{16,8},{20,12},{24,16},{28,20},{9,1},{13,5},{17,9},{2... | collective-permute-start | bytes 786440 | tf_op jit(solution)/shard_map/ppermute | solution.py:90
  15.0 60.3 %collective-permute-start.6 = (f32[64,1024]{1,0:T(8,128)}, f32[64,1024]{1,0:T(8,128)S(1)}, u32[]{:S(2)}, u32[]{:S(2)}) collective-permute-start(f32[64,1024]{1,0:T(8,128)} %get-tuple-element.37), channel_id=1, source_target_pairs={{0,8},{4,12},{8,16},{12,20},{16,24},{20,28},{1,9},{5,13},{9,17},{1... | collective-permute-start | bytes 786440 | tf_op jit(solution)/shard_map/ppermute | solution.py:90
  74.0 28.4 %collective-permute-start.36 = (f32[256,256]{1,0:T(8,128)}, f32[256,256]{1,0:T(8,128)S(1)}, u32[]{:S(2)}, u32[]{:S(2)}) collective-permute-start(f32[256,256]{1,0:T(8,128)} %get-tuple-element.33), channel_id=1, source_target_pairs={{8,0},{12,4},{16,8},{20,12},{24,16},{28,20},{9,1},{13,5},{17,9},{2... | collective-permute-start | bytes 786440 | tf_op jit(solution)/shard_map/ppermute | solution.py:90
  96.8 21.7 %collective-permute-start.19 = (f32[64,1024]{1,0:T(8,128)S(1)}, f32[64,1024]{1,0:T(8,128)S(1)}, u32[]{:S(2)}, u32[]{:S(2)}) collective-permute-start(f32[64,1024]{1,0:T(8,128)S(1)} %collective-permute-done.8), channel_id=1, source_target_pairs={{8,16},{12,20},{16,24},{20,28},{9,17},{13,21},{17,25},{21,29},{10,... | collective-permute-start | bytes 786440 | tf_op jit(solution)/shard_map/ppermute | solution.py:90
  102.4 27.9 %collective-permute-start.40 = (f32[256,256]{1,0:T(8,128)S(1)}, f32[256,256]{1,0:T(8,128)S(1)}, u32[]{:S(2)}, u32[]{:S(2)}) collective-permute-start(f32[256,256]{1,0:T(8,128)S(1)} %copy-done.47), channel_id=1, source_target_pairs={{16,8},{20,12},{24,16},{28,20},{17,9},{21,13},{25,17},{29,21},{18,... | collective-permute-start | bytes 786440 | tf_op jit(solution)/shard_map/ppermute | solution.py:90
  103.1 32.3 %collective-permute-start.42 = (f32[256,256]{1,0:T(8,128)S(1)}, f32[256,256]{1,0:T(8,128)S(1)}, u32[]{:S(2)}, u32[]{:S(2)}) collective-permute-start(f32[256,256]{1,0:T(8,128)S(1)} %copy-done.47), channel_id=1, source_target_pairs={{0,8},{4,12},{8,16},{12,20},{1,9},{5,13},{9,17},{13,21},{2,10},{6,... | collective-permute-start | bytes 786440 | tf_op jit(solution)/shard_map/ppermute | solution.py:90
  113.3 23.4 %collective-permute-start.39 = (f32[256,256]{1,0:T(8,128)}, f32[256,256]{1,0:T(8,128)S(1)}, u32[]{:S(2)}, u32[]{:S(2)}) collective-permute-start(f32[256,256]{1,0:T(8,128)} %get-tuple-element.33), channel_id=1, source_target_pairs={{0,8},{4,12},{1,9},{5,13},{2,10},{6,14},{3,11},{7,15}} | collective-permute-start | bytes 786440 | tf_op jit(solution)/shard_map/ppermute | solution.py:90
  119.8 22.8 %collective-permute-start.44 = (f32[256,256]{1,0:T(8,128)S(1)}, f32[256,256]{1,0:T(8,128)S(1)}, u32[]{:S(2)}, u32[]{:S(2)}) collective-permute-start(f32[256,256]{1,0:T(8,128)S(1)} %copy-done.46), channel_id=1, source_target_pairs={{24,16},{28,20},{25,17},{29,21},{26,18},{30,22},{27,19},{31,23}} | collective-permute-start | bytes 786440 | tf_op jit(solution)/shard_map/ppermute | solution.py:90
  174.7 51.4 %collective-permute-start = (f32[256,2,1024]{2,0,1:T(8,128)}, f32[256,2,1024]{2,0,1:T(8,128)}, u32[]{:S(2)}, u32[]{:S(2)}) collective-permute-start(f32[256,2,1024]{2,0,1:T(8,128)} %bitcast.75), channel_id=1, source_target_pairs={{0,1},{1,0},{2,3},{3,2},{4,5},{5,4},{6,7},{7,6},{8,9},{9,8},{10,11... | collective-permute-start | bytes 6291464 | tf_op jit(solution)/shard_map/ppermute | solution.py:293
  180.1 32.5 %collective-permute-start.34 = (f32[64,3072]{1,0:T(8,128)}, f32[64,3072]{1,0:T(8,128)}, u32[]{:S(2)}, u32[]{:S(2)}) collective-permute-start(f32[64,3072]{1,0:T(8,128)} %constant_dynamic-slice_fusion.refs_12_), channel_id=1, source_target_pairs={{0,2},{1,3},{2,0},{3,1},{4,6},{5,7},{6,4},{7,5},{24,26},{25,27},{2... | collective-permute-start | bytes 2359304 | tf_op jit(solution)/shard_map/ppermute | solution.py:247
  183.5 29.1 %collective-permute-start.33 = (f32[64,3072]{1,0:T(8,128)}, f32[64,3072]{1,0:T(8,128)}, u32[]{:S(2)}, u32[]{:S(2)}) collective-permute-start(f32[64,3072]{1,0:T(8,128)} %constant_dynamic-slice_fusion.refs_12_), channel_id=1, source_target_pairs={{0,1},{1,0},{2,3},{3,2},{4,5},{5,4},{6,7},{7,6},{24,25},{25,24},{2... | collective-permute-start | bytes 2359304 | tf_op jit(solution)/shard_map/ppermute | solution.py:248
  199.3 24.8 %collective-permute-start.26 = (f32[64,3072]{1,0:T(8,128)}, f32[64,3072]{1,0:T(8,128)}, u32[]{:S(2)}, u32[]{:S(2)}) collective-permute-start(f32[64,3072]{1,0:T(8,128)} %collective-permute-done.25.refs_10_), channel_id=1, source_target_pairs={{8,9},{9,8},{10,11},{11,10},{12,13},{13,12},{14,15},{15,14},{16,17... | collective-permute-start | bytes 2359304 | tf_op jit(solution)/shard_map/ppermute | solution.py:249
  216.9 30.0 %collective-permute-start.52 = (f32[256,256]{1,0:T(8,128)}, f32[256,256]{1,0:T(8,128)S(1)}, u32[]{:S(2)}, u32[]{:S(2)}) collective-permute-start(f32[256,256]{1,0:T(8,128)} %get-tuple-element.31), channel_id=1, source_target_pairs={{0,8},{4,12},{1,9},{5,13},{2,10},{6,14},{3,11},{7,15}} | collective-permute-start | bytes 786440 | tf_op jit(solution)/shard_map/ppermute | solution.py:90
  224.1 25.5 %collective-permute-start.57 = (f32[256,256]{1,0:T(8,128)S(1)}, f32[256,256]{1,0:T(8,128)S(1)}, u32[]{:S(2)}, u32[]{:S(2)}) collective-permute-start(f32[256,256]{1,0:T(8,128)S(1)} %copy-done.43), channel_id=1, source_target_pairs={{24,16},{28,20},{25,17},{29,21},{26,18},{30,22},{27,19},{31,23}} | collective-permute-start | bytes 786440 | tf_op jit(solution)/shard_map/ppermute | solution.py:90
  224.8 25.5 %collective-permute-start.50 = (f32[256,256]{1,0:T(8,128)S(1)}, f32[256,256]{1,0:T(8,128)S(1)}, u32[]{:S(2)}, u32[]{:S(2)}) collective-permute-start(f32[256,256]{1,0:T(8,128)S(1)} %copy-done.5), channel_id=1, source_target_pairs={{8,0},{12,4},{16,8},{20,12},{9,1},{13,5},{17,9},{21,13},{10,2},{14... | collective-permute-start | bytes 786440 | tf_op jit(solution)/shard_map/ppermute | solution.py:90
  226.1 25.5 %collective-permute-start.59 = (f32[256,256]{1,0:T(8,128)S(1)}, f32[256,256]{1,0:T(8,128)S(1)}, u32[]{:S(2)}, u32[]{:S(2)}) collective-permute-start(f32[256,256]{1,0:T(8,128)S(1)} %copy-done.7), channel_id=1, source_target_pairs={{8,16},{12,20},{16,24},{20,28},{9,17},{13,21},{17,25},{21,29},{10,... | collective-permute-start | bytes 786440 | tf_op jit(solution)/shard_map/ppermute | solution.py:90
  226.8 25.5 %collective-permute-start.54 = (f32[256,256]{1,0:T(8,128)S(1)}, f32[256,256]{1,0:T(8,128)S(1)}, u32[]{:S(2)}, u32[]{:S(2)}) collective-permute-start(f32[256,256]{1,0:T(8,128)S(1)} %copy-done.1), channel_id=1, source_target_pairs={{16,8},{20,12},{17,9},{21,13},{18,10},{22,14},{19,11},{23,15}} | collective-permute-start | bytes 786440 | tf_op jit(solution)/shard_map/ppermute | solution.py:90
  246.9 87.5 %collective-permute-start.48 = (f32[1536,256]{1,0:T(8,128)S(1)}, f32[1536,256]{1,0:T(8,128)}, u32[]{:S(2)}, u32[]{:S(2)}) collective-permute-start(f32[1536,256]{1,0:T(8,128)S(1)} %get-tuple-element.8), channel_id=1, source_target_pairs={{0,4},{4,0},{8,12},{12,8},{16,20},{20,16},{24,28},{28,24},{1,5},{5... | collective-permute-start | bytes 4718600 | tf_op jit(solution)/shard_map/ppermute | solution.py:284
  252.3 79.6 %collective-permute-start.1 = (f32[256,1024]{1,0:T(8,128)}, f32[256,1024]{1,0:T(8,128)}, u32[]{:S(2)}, u32[]{:S(2)}) collective-permute-start(f32[256,1024]{1,0:T(8,128)} %dynamic-slice_bitcast_fusion), channel_id=1, source_target_pairs={{0,2},{1,3},{2,0},{3,1},{4,6},{5,7},{6,4},{7,5},{8,10},{9,11},{10,... | collective-permute-start | bytes 3145736 | tf_op jit(solution)/shard_map/ppermute | solution.py:296
  270.8 65.3 %collective-permute-start.61 = (f32[1536,256]{1,0:T(8,128)S(1)}, f32[1536,256]{1,0:T(8,128)}, u32[]{:S(2)}, u32[]{:S(2)}) collective-permute-start(f32[1536,256]{1,0:T(8,128)S(1)} %get-tuple-element.10), channel_id=1, source_target_pairs={{0,4},{4,0},{8,12},{12,8},{16,20},{20,16},{24,28},{28,24},{1,5},{5... | collective-permute-start | bytes 4718600 | tf_op jit(solution)/shard_map/ppermute | solution.py:284
  271.4 47.0 %collective-permute-start.62 = (f32[7,3,512]{2,1,0:T(4,128)S(1)}, f32[7,3,512]{2,1,0:T(4,128)S(1)}, u32[]{:S(2)}, u32[]{:S(2)}) collective-permute-start(f32[7,3,512]{2,1,0:T(4,128)S(1)} %constant_dynamic-update-slice_fusion.3), channel_id=1, source_target_pairs={{0,4},{4,0},{8,12},{12,8},{16,20},{20,16},{24,28},{28,24},{1,5},{5... | collective-permute-start | bytes 129032 | tf_op jit(solution)/shard_map/ppermute | solution.py:301
  (92 other events, 1228.6 us)

commit v2 on v0

--- a/solution.py
+++ b/solution.py
@@ -1,8 +1,11 @@
+import functools
 import math
 
 import jax
 import jax.numpy as jnp
 from jax import lax
+from jax.experimental import pallas as pl
+from jax.experimental.pallas import tpu as pltpu
 from jax.sharding import PartitionSpec as P
 
 SEQ = 128
@@ -38,11 +41,9 @@
     return jnp.stack(terms, axis=0)
 
 
-def local(tokens, in_weight, kernel, out_grad):
+def gated_grads(tokens, in_weight, kernel, out_grad):
     rows = tokens.shape[0]
-    features = tokens.shape[1]
     chans = in_weight.shape[2]
-    total_rows = rows * lax.axis_size("rep")
     mixed = jnp.einsum("td,sdc->tsc", tokens, in_weight, preferred_element_type=jnp.float32)
     stored = lax.optimization_barrier(mixed.astype(jnp.bfloat16))
     values = stored.astype(jnp.float32).reshape(rows // SEQ, SEQ, 3, chans)
@@ -54,9 +55,16 @@
     conv_grad = jnp.stack(
         [upstream * keyed * valued, upstream * query * valued, upstream * query * keyed], axis=2
     )
-    mixed_grad = causal_mix_back(conv_grad, kernel).reshape(rows, 3, chans).astype(jnp.bfloat16)
-    scale = 1.0 / math.sqrt(total_rows)
-    kernel_local = kernel_terms(values, conv_grad, kernel.shape[0]) * scale
+    mixed_grad = causal_mix_back(conv_grad, kernel).reshape(rows, 3, chans)
+    return mixed_grad, kernel_terms(values, conv_grad, kernel.shape[0])
+
+
+def plain(tokens, in_weight, kernel, out_grad):
+    features = tokens.shape[1]
+    chans = in_weight.shape[2]
+    scale = 1.0 / math.sqrt(tokens.shape[0] * lax.axis_size("rep"))
+    wide_grad, taps = gated_grads(tokens, in_weight, kernel, out_grad)
+    mixed_grad = wide_grad.astype(jnp.bfloat16)
     partial_grad = jnp.einsum(
         "tsc,sdc->td", mixed_grad, in_weight, preferred_element_type=jnp.float32
     )
@@ -69,14 +77,239 @@
     weight_grad = lax.psum_scatter(
         local_grad.reshape(3 * features, chans), "rep", scatter_dimension=0, tiled=True
     )
-    kernel_grad = lax.psum(kernel_local, "rep")
+    kernel_grad = lax.psum(taps * scale, "rep")
     return (token_grad, weight_grad, kernel_grad)
+
+
+LEVELS = 4
+BLOCK = 512
+BLOCKS = 8
+OWN = 6
+VMEM = pl.BlockSpec(memory_space=pltpu.VMEM)
+SMEM = pl.BlockSpec(memory_space=pltpu.SMEM)
+PARAMS = pltpu.CompilerParams(vmem_limit_bytes=48 * 2**20)
+
+
+def lines(array, hops):
+    perm = [(2 * a + y, 2 * b + y) for a, b in hops for y in range(2)]
+    return lax.ppermute(array, "rep", perm)
+
+
+PAIRS = ((0, 1), (1, 0), (2, 3), (3, 2))
+INWARD = ((0, 1), (3, 2))
+MIDDLE = ((1, 2), (2, 1))
+OUTWARD = ((1, 0), (2, 3))
+
+
+def turn_tokens(place, tokens):
+    rows = tokens.shape[0]
+    slab = BLOCK // 4
+
+    def body(place, tokens, whole, piece):
+        start = pl.multiple_of(place[2] * slab, slab)
+        for b in range(BLOCKS):
+            whole[b] = tokens[:, BLOCK * b : BLOCK * (b + 1)].T
+            piece[b] = tokens[:, pl.ds(pl.multiple_of(BLOCK * b + start, slab), slab)].astype(
+                jnp.float32
+            ).T
+
+    return pl.pallas_call(
+        body,
+        out_shape=(
+            jax.ShapeDtypeStruct((BLOCKS, BLOCK, rows), jnp.bfloat16),
+            jax.ShapeDtypeStruct((BLOCKS, slab, rows), jnp.float32),
+        ),
+        in_specs=[SMEM, VMEM],
+        out_specs=(VMEM, VMEM),
+        compiler_params=PARAMS,
+        name="turn_tokens",
+    )(place, tokens)
+
+
+def arrange_tokens(place, whole, slots):
+    rows = whole.shape[2]
+    slab = BLOCK // 4
+
+    def body(place, whole, *refs):
+        out = refs[-1]
+        for j in range(OWN):
+            out[j, :, 0:rows] = whole[lax.rem(OWN * place[0] + j, BLOCKS)]
+            for slot in range(3):
+                for k in range(4):
+                    where = pl.multiple_of(jnp.bitwise_xor(place[2], k) * slab, slab)
+                    out[j, pl.ds(where, slab), (slot + 1) * rows : (slot + 2) * rows] = refs[
+                        4 * slot + k
+                    ][j].astype(jnp.bfloat16)
+
+    return pl.pallas_call(
+        body,
+        out_shape=jax.ShapeDtypeStruct((OWN, BLOCK, 4 * rows), jnp.bfloat16),
+        in_specs=[SMEM] + [VMEM] * 13,
+        out_specs=VMEM,
+        compiler_params=PARAMS,
+        name="arrange_tokens",
+    )(place, whole, *[piece for slot in slots for piece in slot])
+
+
+def weight_part(place, tok, own, first, inner, middle, relayed, outer):
+    rows, width = own.shape[1:]
+
+    def body(place, tok, own, first, inner, middle, relayed, outer, send, keep, held):
+        level, column = place[0], place[1]
+
+        def fill(side, *parts):
+            for slot, part in enumerate(parts):
+                held[side, slot * rows : (slot + 1) * rows, :] = part.astype(jnp.bfloat16)
+
+        @pl.when(level == 0)
+        def _():
+            fill(0, own[0], first[...], outer[0], outer[1])
+
+        @pl.when(level == 1)
+        def _():
+            fill(0, own[0], inner[0], middle[0], relayed[0])
+            fill(1, own[1], inner[1], middle[1], relayed[1])
+
+        @pl.when(level == 2)
+        def _():
+            fill(0, own[1], inner[0], middle[0], relayed[1])
+            fill(1, own[2], inner[1], middle[1], relayed[0])
+
+        @pl.when(level == 3)
+        def _():
+            fill(0, own[2], first[...], outer[0], outer[1])
+
+        low = lax.div(OWN * level, BLOCKS)
+        for out, col in ((send, 1 - column), (keep, column)):
+            for i in range(OWN // 2):
+                j = (OWN // 2) * col + i
+                side = lax.div(OWN * level + j, BLOCKS) - low
+                out[BLOCK * i : BLOCK * (i + 1), :] = jnp.dot(
+                    tok[j], held[side], preferred_element_type=jnp.float32
+                )
+
+    half = jax.ShapeDtypeStruct((OWN // 2 * BLOCK, width), jnp.float32)
+    return pl.pallas_call(
+        body,
+        out_shape=(half, half),
+        in_specs=[SMEM] + [VMEM] * 7,
+        out_specs=(VMEM, VMEM),
+        scratch_shapes=[pltpu.VMEM((2, 4 * rows, width), jnp.bfloat16)],
+        compiler_params=PARAMS,
+        name="weight_part",
+    )(place, tok, own, first, inner, middle, relayed, outer)
+
+
+def token_part(order, grads, weight):
+    rows, chans = grads.shape[1:]
+    wide = weight.shape[1] // 4
+    count = order.shape[0]
+
+    def body(order, grads, weight, out):
+        now = lax.dot_general(
+            grads[...], weight[...], (((1,), (1,)), ((), ())), preferred_element_type=jnp.float32
+        )
+
+        @pl.when(pl.program_id(1) == 0)
+        def _():
+            out[...] = now
+
+        @pl.when(pl.program_id(1) > 0)
+        def _():
+            out[...] += now
+
+    return pl.pallas_call(
+        body,
+        out_shape=jax.ShapeDtypeStruct((count, rows, wide), jnp.float32),
+        grid_spec=pltpu.PrefetchScalarGridSpec(
+            num_scalar_prefetch=1,
+            grid=(count, 3),
+            in_specs=[
+                pl.BlockSpec((None, rows, chans), lambda i, s, order: (s, 0, 0)),
+                pl.BlockSpec((None, wide, chans), lambda i, s, order: (s, order[i], 0)),
+            ],
+            out_specs=pl.BlockSpec((None, rows, wide), lambda i, s, order: (i, 0, 0)),
+        ),
+        compiler_params=PARAMS,
+        name="token_part",
+    )(order, grads, weight)
+
+
+CHUNKS = 2
+
+
+def lined(tokens, in_weight, kernel, out_grad):
+    rows, features = tokens.shape
+    chans = in_weight.shape[2]
+    rep = lax.axis_index("rep")
+    quarter = lax.axis_index("shard")
+    level, column = rep // 2, rep % 2
+    place = jnp.stack([level, column, quarter]).astype(jnp.int32)
+    scale = 1.0 / math.sqrt(rows * lax.axis_size("rep"))
+    inside = jnp.logical_or(level == 1, level == 2)
+    low = level <= 1
+
+    whole, piece = turn_tokens(place, tokens)
+    near = lines(piece, PAIRS)
+    mid = lines(piece, MIDDLE)
+    far = lines(near, MIDDLE)
+
+    def ended(array):
+        return jnp.where(low, array[:OWN], array[BLOCKS - OWN :])
+
+    def level_blocks(array):
+        z1 = jnp.concatenate([array[6:], array[:4]], axis=0)
+        z2 = jnp.concatenate([array[4:], array[:2]], axis=0)
+        return jnp.where(level == 1, z1, z2)
+
+    def share(array):
+        across = lax.ppermute(array, "shard", [(q, q ^ 2) for q in range(4)])
+        beside = lax.ppermute(array, "shard", [(q, q ^ 1) for q in range(4)])
+        both = lax.ppermute(across, "shard", [(q, q ^ 1) for q in range(4)])
+        return (array, beside, across, both)
+
+    slots = [share(jnp.where(inside, level_blocks(near), ended(near)))]
+    for got in (mid, far):
+        outer = lines(ended(got), OUTWARD)
+        slots.append(share(jnp.where(inside, level_blocks(got), outer)))
+
+    wide_grad, taps = gated_grads(tokens, in_weight, kernel, out_grad)
+    wide_grad = jnp.transpose(wide_grad, (1, 0, 2))
+
+    tok = arrange_tokens(place, whole, slots)
+    parts = []
+    cw = chans // CHUNKS
+    for h in range(CHUNKS):
+        mine = wide_grad[:, :, cw * h : cw * (h + 1)]
+        even = jnp.logical_or(level == 0, level == 2)
+        first = lines(jnp.where(even, mine[2], mine[0]), PAIRS)
+        inner = lines(jnp.where(low, mine[0:2], mine[1:3]), INWARD)
+        middle = lines(jnp.where(low, mine[1:3], mine[0:2]), MIDDLE)
+        relayed = lines(jnp.stack([first, jnp.where(low, inner[1], inner[0])]), MIDDLE)
+        outer = lines(jnp.stack([jnp.where(low, middle[0], middle[1]), relayed[0]]), OUTWARD)
+        send, keep = weight_part(place, tok, mine, first, inner, middle, relayed, outer)
+        other = lax.ppermute(send, "rep", [(r, r ^ 1) for r in range(2 * LEVELS)])
+        parts.append((keep + other) * scale)
+    weight_grad = jnp.concatenate(parts, axis=1)
+
+    mixed_grad = wide_grad.astype(jnp.bfloat16)
+    order = [jnp.bitwise_xor(quarter, k).astype(jnp.int32) for k in (3, 1, 2, 0)]
+    send = token_part(jnp.stack(order[:2]), mixed_grad, in_weight)
+    keep = token_part(jnp.stack(order[2:]), mixed_grad, in_weight)
+    other = lax.ppermute(send, "shard", [(q, q ^ 1) for q in range(4)])
+    last = lax.ppermute(keep[0] + other[0], "shard", [(q, q ^ 2) for q in range(4)])
+    token_grad = (keep[1] + other[1] + last).astype(jnp.bfloat16)
+
+    for bit in (1, 2, 4):
+        taps = taps + lax.ppermute(taps, "rep", [(r, r ^ bit) for r in range(2 * LEVELS)])
+    return (token_grad, weight_grad, taps * scale)
 
 
 def solution(mesh):
     placed = (P("rep", None), P(None, None, "shard"), P(None, None, "shard"), P("rep", "shard"))
+    line = mesh.shape["rep"] == 2 * LEVELS and mesh.shape["shard"] == 4
     return jax.shard_map(
-        local,
+        lined if line else plain,
         mesh=mesh,
         in_specs=placed,
         out_specs=(P("rep", "shard"), P("rep", "shard"), P(None, None, "shard")),

time: 499 us -> 266 us (0.53)
  waiting for transfers between devices: 373 us -> 149 us
  blocking collectives: 40.5 us -> 0 us
  starting transfers between devices: 0.08 us -> 37.1 us
  Pallas kernels: 0 us -> 35.7 us
  matrix products: 33.4 us -> 6.5 us
  local copies, waits for them, and re-layouts: 28.8 us -> 14.2 us
  between operations: 14.2 us -> 1.33 us
  other arithmetic: 8.14 us -> 20.8 us
    reduce_scatter x2 -> x0, waiting for transfers between devices: 373 us -> none  [the longest x1 373 us: local(): lax.psum_scatter(local_grad.reshape(3 * features, chans), 'rep', scatter_...]
    ppermute x0 -> x31, waiting for transfers between devices: none -> 149 us  [the longest x3 65.7 us: lined(): lax.ppermute(taps, 'rep', [(r, r ^ bit) for r in range(2 * LEVELS)])]
    psum x1 -> x0, blocking collectives: 40.5 us -> none  [local(): kernel_grad = lax.psum(kernel_local, 'rep')]
    ppermute x0 -> x31, starting transfers between devices: none -> 37.1 us  [the longest x15 25.2 us: lines(): return lax.ppermute(array, 'rep', perm)]
    pallas_call x0 -> x6, Pallas kernels: none -> 35.7 us  [the longest x2 14.5 us: token_part(): pl.pallas_call(body, out_shape=jax.ShapeDtypeStruct((count, rows, wide),...]
    dot_general x3 -> x1, matrix products: 33.4 us -> 6.5 us  [gated_grads(): jnp.einsum('td,sdc->tsc', tokens, in_weight, preferred_element_type=jnp.f...]
    mul x1 -> x0, local copies, waits for them, and re-layouts: 24.8 us -> none  [local(): jnp.einsum('td,tsc->sdc', tokens, mixed_grad, preferred_element_type=jnp....]
    select_n x0 -> x11, other arithmetic: none -> 6.82 us  [the longest x1 1.58 us: lined(): slots = [share(jnp.where(inside, level_blocks(near), ended(near)))]]
  transfers between devices with their start and end apart: 2 -> 31, of which waited for: 1 -> 13; matrix products, arithmetic and copies ran while one was open for 8% -> 12% of each run, Pallas kernels for 0% -> 13%
where the time goes in v2:
time: 266 us; the launch traced here: 265 us
  waiting for transfers between devices  149 us (56%)
  starting transfers between devices  37.1 us (14%)
  Pallas kernels  35.7 us (13%)
  other arithmetic  20.8 us (8%)
  local copies, waits for them, and re-layouts  14.2 us (5%)
  matrix products  6.5 us (2%)
    ppermute x3, waiting for transfers between devices, lined(): lax.ppermute(taps, 'rep', [(r, r ^ bit) for r in range(2 * LEVELS)])  65.7 us
    ppermute x15, waiting for transfers between devices, lines(): return lax.ppermute(array, 'rep', perm)  59.1 us
    ppermute x15, starting transfers between devices, lines(): return lax.ppermute(array, 'rep', perm)  25.2 us
    ppermute x3, waiting for transfers between devices, share(): across = lax.ppermute(array, 'shard', [(q, q ^ 2) for q in range(4)])  24.5 us
    pallas_call x2, Pallas kernels, token_part(): pl.pallas_call(body, out_shape=jax.ShapeDtypeStruct((count, rows, wide),...  14.5 us
    pallas_call x2, Pallas kernels, weight_part(): pl.pallas_call(body, out_shape=(half, half), in_specs=[SMEM] + [VMEM] * 7...  11.8 us
    unnamed x77, local copies, waits for them, and re-layouts  7.73 us
    pallas_call x1, Pallas kernels, arrange_tokens(): pl.pallas_call(body, out_shape=jax.ShapeDtypeStruct((OWN, BLOCK, 4 * rows...  7.05 us
  transfers between devices with their start and end apart: 31, of which 13 were waited for; matrix products, arithmetic and copies ran while one was open for 12% of the time, Pallas kernels for 13%

profile of v2, /device:TPU:0, one launch (start us, length us, event | category | flops | bytes accessed | tf_op | source)
XLA Modules:
  0.0 264.8 jit_solution(11560982979198242125)
XLA Ops:
  2.3 2.3 turn_tokens.1
  6.0 3.0 %collective-permute-start.2 = (f32[8,128,256]{2,1,0:T(8,128)}, f32[8,128,256]{2,1,0:T(8,128)}, u32[]{:S(2)}, u32[]{:S(2)}) collective-permute-start(f32[8,128,256]{2,1,0:T(8,128)} %get-tuple-element.10), channel_id=1, source_target_pairs={{0,8},{4,12},{8,0},{12,4},{16,24},{20,28},{24,16},{28,20},{1,9},{5... | collective-permute-start | bytes 3145736 | tf_op jit(solution)/shard_map/ppermute | solution.py:95
  10.8 6.5 %fusion.5 = bf16[256,3,512]{2,0,1:T(8,128)(2,1)S(1)} fusion(bf16[3,4096,512]{2,1,0:T(8,128)(2,1)} %weight.3, bf16[256,4096]{1,0:T(8,128)(2,1)S(1)} %copy-done.6), kind=kOutput, calls=%fused_computation.24 | convolution fusion | flops 3221618688 | bytes 15466496 | tf_op jit(solution)/shard_map/td,sdc->tsc/dot_general | solution.py:47
  23.4 5.3 %collective-permute-start.17 = (f32[2,256,256]{2,1,0:T(8,128)}, f32[2,256,256]{2,1,0:T(8,128)S(1)}, u32[]{:S(2)}, u32[]{:S(2)}) collective-permute-start(f32[2,256,256]{2,1,0:T(8,128)} %get-tuple-element.32), channel_id=1, source_target_pairs={{0,8},{4,12},{24,16},{28,20},{1,9},{5,13},{25,17},{29,21},{2,10},{... | collective-permute-start | bytes 1572872 | tf_op jit(solution)/shard_map/ppermute | solution.py:95
  29.5 3.9 %collective-permute-start.23 = (f32[2,256,256]{2,1,0:T(8,128)}, f32[2,256,256]{2,1,0:T(8,128)S(1)}, u32[]{:S(2)}, u32[]{:S(2)}) collective-permute-start(f32[2,256,256]{2,1,0:T(8,128)} %get-tuple-element.31), channel_id=1, source_target_pairs={{0,8},{4,12},{24,16},{28,20},{1,9},{5,13},{25,17},{29,21},{2,10},{... | collective-permute-start | bytes 1572872 | tf_op jit(solution)/shard_map/ppermute | solution.py:95
  35.4 7.9 %token_part.3 = f32[2,256,1024]{2,1,0:T(8,128)} custom-call(s32[2]{0:T(128)S(1)} %pad_add_fusion.1.order, bf16[3,256,512]{2,1,0:T(8,128)(2,1)S(1)} %bitcast_convert_fusion.grads, bf16[3,4096,512]{2,1,0:T(8,128)(2,1)} %weight.3), custom_call_target="tpu_custom_call" | custom-call | tf_op jit(solution)/shard_map/token_part/pallas_call | solution.py:221
  44.9 4.9 %collective-permute-done.16.first = f32[256,256]{1,0:T(8,128)S(1)} collective-permute-done((f32[256,256]{1,0:T(8,128)}, f32[256,256]{1,0:T(8,128)S(1)}, u32[]{:S(2)}, u32[]{:S(2)}) %collective-permute-start.16) | collective-permute-done | bytes 262176 | tf_op jit(solution)/shard_map/ppermute | solution.py:95
  49.8 2.4 collective-permute-start.22
  52.2 8.8 %collective-permute-done.23.inner = f32[2,256,256]{2,1,0:T(8,128)S(1)} collective-permute-done((f32[2,256,256]{2,1,0:T(8,128)}, f32[2,256,256]{2,1,0:T(8,128)S(1)}, u32[]{:S(2)}, u32[]{:S(2)}) %collective-permute-start.23) | collective-permute-done | bytes 524320 | tf_op jit(solution)/shard_map/ppermute | solution.py:95
  61.8 3.6 %collective-permute-done.22.first = f32[256,256]{1,0:T(8,128)S(1)} collective-permute-done((f32[256,256]{1,0:T(8,128)S(1)}, f32[256,256]{1,0:T(8,128)S(1)}, u32[]{:S(2)}, u32[]{:S(2)}) %collective-permute-start.22) | collective-permute-done | bytes 262176 | tf_op jit(solution)/shard_map/ppermute | solution.py:95
  77.4 15.5 %collective-permute-done.7 = f32[6,128,256]{2,1,0:T(8,128)S(1)} collective-permute-done((f32[6,128,256]{2,1,0:T(8,128)S(1)}, f32[6,128,256]{2,1,0:T(8,128)S(1)}, u32[]{:S(2)}, u32[]{:S(2)}) %collective-permute-start.7) | collective-permute-done | bytes 786464 | tf_op jit(solution)/shard_map/ppermute | solution.py:95
  96.0 19.4 %collective-permute-done.12 = f32[6,128,256]{2,1,0:T(8,128)S(1)} collective-permute-done((f32[6,128,256]{2,1,0:T(8,128)S(1)}, f32[6,128,256]{2,1,0:T(8,128)S(1)}, u32[]{:S(2)}, u32[]{:S(2)}) %collective-permute-start.12) | collective-permute-done | bytes 786464 | tf_op jit(solution)/shard_map/ppermute | solution.py:95
  121.7 6.6 %token_part.2 = f32[2,256,1024]{2,1,0:T(8,128)S(1)} custom-call(s32[2]{0:T(128)S(1)} %pad_add_fusion.order, bf16[3,256,512]{2,1,0:T(8,128)(2,1)S(1)} %bitcast_convert_fusion.grads, bf16[3,4096,512]{2,1,0:T(8,128)(2,1)} %weight.3), custom_call_target="tpu_custom_call" | custom-call | tf_op jit(solution)/shard_map/token_part/pallas_call | solution.py:221
  128.4 8.5 %collective-permute-done.9.refs_6_ = f32[6,128,256]{2,1,0:T(8,128)} collective-permute-done((f32[6,128,256]{2,1,0:T(8,128)S(1)}, f32[6,128,256]{2,1,0:T(8,128)}, u32[]{:S(2)}, u32[]{:S(2)}) %collective-permute-start.9) | collective-permute-done | bytes 786464 | tf_op jit(solution)/shard_map/ppermute | solution.py:266
  137.5 16.0 %collective-permute-done.14.refs_10_ = f32[6,128,256]{2,1,0:T(8,128)} collective-permute-done((f32[6,128,256]{2,1,0:T(8,128)}, f32[6,128,256]{2,1,0:T(8,128)}, u32[]{:S(2)}, u32[]{:S(2)}) %collective-permute-start.14) | collective-permute-done | bytes 786464 | tf_op jit(solution)/shard_map/ppermute | solution.py:266
  161.3 7.1 %arrange_tokens.1.tok = bf16[6,512,1024]{2,1,0:T(8,128)(2,1)} custom-call(s32[3]{0:T(128)S(1)} %pad_add_fusion.2.place, bf16[8,512,256]{2,1,0:T(8,128)(2,1)} %copy-done, f32[6,128,256]{2,1,0:T(8,128)S(1)} %fusion.12.refs_0_, f32[6,128,256]{2,1,0:T(8,128)} %collective-permute-done.3.refs_1_, f32[6,128,256]{2,1,0:T(8,128)S(1)} %copy-done.16, ...), custom_call_target="tpu_custom_call" | custom-call | tf_op jit(solution)/shard_map/arrange_tokens/pallas_call | solution.py:144
  168.4 2.7 %collective-permute-done.20.outer = f32[2,256,256]{2,1,0:T(8,128)S(1)} collective-permute-done((f32[2,256,256]{2,1,0:T(8,128)}, f32[2,256,256]{2,1,0:T(8,128)S(1)}, u32[]{:S(2)}, u32[]{:S(2)}) %collective-permute-start.20) | collective-permute-done | bytes 524320 | tf_op jit(solution)/shard_map/ppermute | solution.py:95
  171.1 6.0 %weight_part.2 = (f32[1536,256]{1,0:T(8,128)S(1)}, f32[1536,256]{1,0:T(8,128)}) custom-call(s32[3]{0:T(128)S(1)} %pad_add_fusion.2.place, bf16[6,512,1024]{2,1,0:T(8,128)(2,1)} %arrange_tokens.1.tok, f32[3,256,256]{2,1,0:T(8,128)S(1)} %get-tuple-element.36.own, f32[256,256]{1,0:T(8,128)S(1)} %copy-done.12, f32[2,256,256]{2,1,0:T(8,128)S(1)} %collective-permute-done.17.inner, ...), custom_call_target="tpu_custom_call" | custom-call | tf_op jit(solution)/shard_map/weight_part/pallas_call | solution.py:192
  178.6 3.3 %collective-permute-done.26.outer = f32[2,256,256]{2,1,0:T(8,128)S(1)} collective-permute-done((f32[2,256,256]{2,1,0:T(8,128)S(1)}, f32[2,256,256]{2,1,0:T(8,128)S(1)}, u32[]{:S(2)}, u32[]{:S(2)}) %collective-permute-start.26) | collective-permute-done | bytes 524320 | tf_op jit(solution)/shard_map/ppermute | solution.py:95
  181.9 5.8 %weight_part.3 = (f32[1536,256]{1,0:T(8,128)S(1)}, f32[1536,256]{1,0:T(8,128)}) custom-call(s32[3]{0:T(128)S(1)} %pad_add_fusion.2.place, bf16[6,512,1024]{2,1,0:T(8,128)(2,1)} %arrange_tokens.1.tok, f32[3,256,256]{2,1,0:T(8,128)S(1)} %get-tuple-element.37.own, f32[256,256]{1,0:T(8,128)S(1)} %copy-done.14, f32[2,256,256]{2,1,0:T(8,128)S(1)} %collective-permute-done.23.inner, ...), custom_call_target="tpu_custom_call" | custom-call | tf_op jit(solution)/shard_map/weight_part/pallas_call | solution.py:192
  189.9 57.9 %collective-permute-done.28 = f32[7,3,512]{2,1,0:T(4,128)S(1)} collective-permute-done((f32[7,3,512]{2,1,0:T(4,128)S(1)}, f32[7,3,512]{2,1,0:T(4,128)S(1)}, u32[]{:S(2)}, u32[]{:S(2)}) %collective-permute-start.28) | collective-permute-done | bytes 43040 | tf_op jit(solution)/shard_map/ppermute | solution.py:304
  248.4 3.6 %collective-permute-done.29 = f32[7,3,512]{2,1,0:T(4,128)S(1)} collective-permute-done((f32[7,3,512]{2,1,0:T(4,128)S(1)}, f32[7,3,512]{2,1,0:T(4,128)S(1)}, u32[]{:S(2)}, u32[]{:S(2)}) %collective-permute-start.29) | collective-permute-done | bytes 43040 | tf_op jit(solution)/shard_map/ppermute | solution.py:304
  253.7 4.1 %collective-permute-done.30 = f32[7,3,512]{2,1,0:T(4,128)S(1)} collective-permute-done((f32[7,3,512]{2,1,0:T(4,128)S(1)}, f32[7,3,512]{2,1,0:T(4,128)S(1)}, u32[]{:S(2)}, u32[]{:S(2)}) %collective-permute-start.30) | collective-permute-done | bytes 43040 | tf_op jit(solution)/shard_map/ppermute | solution.py:304
  258.5 2.7 %fusion.11 = bf16[256,1024]{1,0:T(8,128)(2,1)} fusion(f32[256,1024]{1,0:T(8,128)} %collective-permute-done.1, f32[2,256,1024]{2,1,0:T(8,128)} %collective-permute-done, f32[2,256,1024]{2,1,0:T(8,128)S(1)} %token_part.2), kind=kLoop, calls=%fused_computation.30 | loop fusion | flops 786432 | bytes 3670016 | tf_op jit(solution)/shard_map/convert_element_type | solution.py:301
  (168 shorter events, 55.6 us)
Async XLA Ops:
  6.0 59.4 %collective-permute-start.2 = (f32[8,128,256]{2,1,0:T(8,128)}, f32[8,128,256]{2,1,0:T(8,128)}, u32[]{:S(2)}, u32[]{:S(2)}) collective-permute-start(f32[8,128,256]{2,1,0:T(8,128)} %get-tuple-element.10), channel_id=1, source_target_pairs={{0,8},{4,12},{8,0},{12,4},{16,24},{20,28},{24,16},{28,20},{1,9},{5... | collective-permute-start | bytes 3145736 | tf_op jit(solution)/shard_map/ppermute | solution.py:95
  9.1 57.8 %collective-permute-start.6 = (f32[8,128,256]{2,1,0:T(8,128)}, f32[8,128,256]{2,1,0:T(8,128)}, u32[]{:S(2)}, u32[]{:S(2)}) collective-permute-start(f32[8,128,256]{2,1,0:T(8,128)} %get-tuple-element.10), channel_id=1, source_target_pairs={{8,16},{12,20},{16,8},{20,12},{9,17},{13,21},{17,9},{21,13},{10,18... | collective-permute-start | bytes 3145736 | tf_op jit(solution)/shard_map/ppermute | solution.py:95
  23.4 20.8 %collective-permute-start.17 = (f32[2,256,256]{2,1,0:T(8,128)}, f32[2,256,256]{2,1,0:T(8,128)S(1)}, u32[]{:S(2)}, u32[]{:S(2)}) collective-permute-start(f32[2,256,256]{2,1,0:T(8,128)} %get-tuple-element.32), channel_id=1, source_target_pairs={{0,8},{4,12},{24,16},{28,20},{1,9},{5,13},{25,17},{29,21},{2,10},{... | collective-permute-start | bytes 1572872 | tf_op jit(solution)/shard_map/ppermute | solution.py:95
  29.5 20.3 %collective-permute-start.16 = (f32[256,256]{1,0:T(8,128)}, f32[256,256]{1,0:T(8,128)S(1)}, u32[]{:S(2)}, u32[]{:S(2)}) collective-permute-start(f32[256,256]{1,0:T(8,128)} %get-tuple-element.34), channel_id=1, source_target_pairs={{0,8},{4,12},{8,0},{12,4},{16,24},{20,28},{24,16},{28,20},{1,9},{5... | collective-permute-start | bytes 786440 | tf_op jit(solution)/shard_map/ppermute | solution.py:95
  29.5 31.5 %collective-permute-start.23 = (f32[2,256,256]{2,1,0:T(8,128)}, f32[2,256,256]{2,1,0:T(8,128)S(1)}, u32[]{:S(2)}, u32[]{:S(2)}) collective-permute-start(f32[2,256,256]{2,1,0:T(8,128)} %get-tuple-element.31), channel_id=1, source_target_pairs={{0,8},{4,12},{24,16},{28,20},{1,9},{5,13},{25,17},{29,21},{2,10},{... | collective-permute-start | bytes 1572872 | tf_op jit(solution)/shard_map/ppermute | solution.py:95
  44.2 50.3 %collective-permute-start.18 = (f32[2,256,256]{2,1,0:T(8,128)S(1)}, f32[2,256,256]{2,1,0:T(8,128)S(1)}, u32[]{:S(2)}, u32[]{:S(2)}) collective-permute-start(f32[2,256,256]{2,1,0:T(8,128)S(1)} %copy-done.30), channel_id=1, source_target_pairs={{8,16},{12,20},{16,8},{20,12},{9,17},{13,21},{17,9},{21,13},{10,18... | collective-permute-start | bytes 1572872 | tf_op jit(solution)/shard_map/ppermute | solution.py:95
  61.0 34.2 %collective-permute-start.24 = (f32[2,256,256]{2,1,0:T(8,128)S(1)}, f32[2,256,256]{2,1,0:T(8,128)S(1)}, u32[]{:S(2)}, u32[]{:S(2)}) collective-permute-start(f32[2,256,256]{2,1,0:T(8,128)S(1)} %copy-done.29), channel_id=1, source_target_pairs={{8,16},{12,20},{16,8},{20,12},{9,17},{13,21},{17,9},{21,13},{10,18... | collective-permute-start | bytes 1572872 | tf_op jit(solution)/shard_map/ppermute | solution.py:95
  65.4 71.5 %collective-permute-start = (f32[2,256,1024]{2,1,0:T(8,128)}, f32[2,256,1024]{2,1,0:T(8,128)}, u32[]{:S(2)}, u32[]{:S(2)}) collective-permute-start(f32[2,256,1024]{2,1,0:T(8,128)} %token_part.3), channel_id=1, source_target_pairs={{0,1},{1,0},{2,3},{3,2},{4,5},{5,4},{6,7},{7,6},{8,9},{9,8},{10,11... | collective-permute-start | bytes 6291464 | tf_op jit(solution)/shard_map/ppermute | solution.py:299
  68.4 24.4 %collective-permute-start.7 = (f32[6,128,256]{2,1,0:T(8,128)S(1)}, f32[6,128,256]{2,1,0:T(8,128)S(1)}, u32[]{:S(2)}, u32[]{:S(2)}) collective-permute-start(f32[6,128,256]{2,1,0:T(8,128)S(1)} %slice_select_fusion.1), channel_id=1, source_target_pairs={{8,0},{12,4},{16,24},{20,28},{9,1},{13,5},{17,25},{21,29},{10,2},{... | collective-permute-start | bytes 2359304 | tf_op jit(solution)/shard_map/ppermute | solution.py:95
  73.4 42.0 %collective-permute-start.12 = (f32[6,128,256]{2,1,0:T(8,128)S(1)}, f32[6,128,256]{2,1,0:T(8,128)S(1)}, u32[]{:S(2)}, u32[]{:S(2)}) collective-permute-start(f32[6,128,256]{2,1,0:T(8,128)S(1)} %slice_select_fusion), channel_id=1, source_target_pairs={{8,0},{12,4},{16,24},{20,28},{9,1},{13,5},{17,25},{21,29},{10,2},{... | collective-permute-start | bytes 2359304 | tf_op jit(solution)/shard_map/ppermute | solution.py:95
  92.8 25.4 %collective-permute-start.4 = (f32[6,128,256]{2,1,0:T(8,128)S(1)}, f32[6,128,256]{2,1,0:T(8,128)S(1)}, u32[]{:S(2)}, u32[]{:S(2)}) collective-permute-start(f32[6,128,256]{2,1,0:T(8,128)S(1)} %fusion.12.refs_0_), channel_id=1, source_target_pairs={{0,2},{1,3},{2,0},{3,1},{4,6},{5,7},{6,4},{7,5},{8,10},{9,11},{10,... | collective-permute-start | bytes 2359304 | tf_op jit(solution)/shard_map/ppermute | solution.py:266
  94.5 22.0 %collective-permute-start.19 = (f32[2,256,256]{2,1,0:T(8,128)S(1)}, f32[2,256,256]{2,1,0:T(8,128)S(1)}, u32[]{:S(2)}, u32[]{:S(2)}) collective-permute-start(f32[2,256,256]{2,1,0:T(8,128)S(1)} %pad_maximum_fusion.2), channel_id=1, source_target_pairs={{8,16},{12,20},{16,8},{20,12},{9,17},{13,21},{17,9},{21,13},{10,18... | collective-permute-start | bytes 1572872 | tf_op jit(solution)/shard_map/ppermute | solution.py:95
  95.2 22.8 %collective-permute-start.25 = (f32[2,256,256]{2,1,0:T(8,128)S(1)}, f32[2,256,256]{2,1,0:T(8,128)S(1)}, u32[]{:S(2)}, u32[]{:S(2)}) collective-permute-start(f32[2,256,256]{2,1,0:T(8,128)S(1)} %pad_maximum_fusion.4), channel_id=1, source_target_pairs={{8,16},{12,20},{16,8},{20,12},{9,17},{13,21},{17,9},{21,13},{10,18... | collective-permute-start | bytes 1572872 | tf_op jit(solution)/shard_map/ppermute | solution.py:95
  116.5 20.4 %collective-permute-start.9 = (f32[6,128,256]{2,1,0:T(8,128)S(1)}, f32[6,128,256]{2,1,0:T(8,128)}, u32[]{:S(2)}, u32[]{:S(2)}) collective-permute-start(f32[6,128,256]{2,1,0:T(8,128)S(1)} %fusion.13.refs_4_), channel_id=1, source_target_pairs={{0,2},{1,3},{2,0},{3,1},{4,6},{5,7},{6,4},{7,5},{8,10},{9,11},{10,... | collective-permute-start | bytes 2359304 | tf_op jit(solution)/shard_map/ppermute | solution.py:266
  118.0 36.3 %collective-permute-start.8 = (f32[6,128,256]{2,1,0:T(8,128)S(1)}, f32[6,128,256]{2,1,0:T(8,128)}, u32[]{:S(2)}, u32[]{:S(2)}) collective-permute-start(f32[6,128,256]{2,1,0:T(8,128)S(1)} %fusion.13.refs_4_), channel_id=1, source_target_pairs={{0,1},{1,0},{2,3},{3,2},{4,5},{5,4},{6,7},{7,6},{8,9},{9,8},{10,11... | collective-permute-start | bytes 2359304 | tf_op jit(solution)/shard_map/ppermute | solution.py:267
  118.8 34.6 %collective-permute-start.14 = (f32[6,128,256]{2,1,0:T(8,128)}, f32[6,128,256]{2,1,0:T(8,128)}, u32[]{:S(2)}, u32[]{:S(2)}) collective-permute-start(f32[6,128,256]{2,1,0:T(8,128)} %fusion.14.refs_8_), channel_id=1, source_target_pairs={{0,2},{1,3},{2,0},{3,1},{4,6},{5,7},{6,4},{7,5},{8,10},{9,11},{10,... | collective-permute-start | bytes 2359304 | tf_op jit(solution)/shard_map/ppermute | solution.py:266
  121.4 34.5 %collective-permute-start.5 = (f32[6,128,256]{2,1,0:T(8,128)S(1)}, f32[6,128,256]{2,1,0:T(8,128)S(1)}, u32[]{:S(2)}, u32[]{:S(2)}) collective-permute-start(f32[6,128,256]{2,1,0:T(8,128)S(1)} %copy-done.16), channel_id=1, source_target_pairs={{0,1},{1,0},{2,3},{3,2},{4,5},{5,4},{6,7},{7,6},{8,9},{9,8},{10,11... | collective-permute-start | bytes 2359304 | tf_op jit(solution)/shard_map/ppermute | solution.py:268
  136.9 21.6 %collective-permute-start.10 = (f32[6,128,256]{2,1,0:T(8,128)}, f32[6,128,256]{2,1,0:T(8,128)S(1)}, u32[]{:S(2)}, u32[]{:S(2)}) collective-permute-start(f32[6,128,256]{2,1,0:T(8,128)} %collective-permute-done.9.refs_6_), channel_id=1, source_target_pairs={{0,1},{1,0},{2,3},{3,2},{4,5},{5,4},{6,7},{7,6},{8,9},{9,8},{10,11... | collective-permute-start | bytes 2359304 | tf_op jit(solution)/shard_map/ppermute | solution.py:268
  137.0 23.2 %collective-permute-start.13 = (f32[6,128,256]{2,1,0:T(8,128)}, f32[6,128,256]{2,1,0:T(8,128)S(1)}, u32[]{:S(2)}, u32[]{:S(2)}) collective-permute-start(f32[6,128,256]{2,1,0:T(8,128)} %fusion.14.refs_8_), channel_id=1, source_target_pairs={{0,1},{1,0},{2,3},{3,2},{4,5},{5,4},{6,7},{7,6},{8,9},{9,8},{10,11... | collective-permute-start | bytes 2359304 | tf_op jit(solution)/shard_map/ppermute | solution.py:267
  155.9 26.1 %collective-permute-start.26 = (f32[2,256,256]{2,1,0:T(8,128)S(1)}, f32[2,256,256]{2,1,0:T(8,128)S(1)}, u32[]{:S(2)}, u32[]{:S(2)}) collective-permute-start(f32[2,256,256]{2,1,0:T(8,128)S(1)} %pad_maximum_fusion.5), channel_id=1, source_target_pairs={{8,0},{12,4},{16,24},{20,28},{9,1},{13,5},{17,25},{21,29},{10,2},{... | collective-permute-start | bytes 1572872 | tf_op jit(solution)/shard_map/ppermute | solution.py:95
  158.6 99.9 %collective-permute-start.1 = (f32[256,1024]{1,0:T(8,128)S(1)}, f32[256,1024]{1,0:T(8,128)}, u32[]{:S(2)}, u32[]{:S(2)}) collective-permute-start(f32[256,1024]{1,0:T(8,128)S(1)} %fusion.8), channel_id=1, source_target_pairs={{0,2},{1,3},{2,0},{3,1},{4,6},{5,7},{6,4},{7,5},{8,10},{9,11},{10,... | collective-permute-start | bytes 3145736 | tf_op jit(solution)/shard_map/ppermute | solution.py:300
  177.1 84.0 %collective-permute-start.21 = (f32[1536,256]{1,0:T(8,128)S(1)}, f32[1536,256]{1,0:T(8,128)S(1)}, u32[]{:S(2)}, u32[]{:S(2)}) collective-permute-start(f32[1536,256]{1,0:T(8,128)S(1)} %get-tuple-element.12), channel_id=1, source_target_pairs={{0,4},{4,0},{8,12},{12,8},{16,20},{20,16},{24,28},{28,24},{1,5},{5... | collective-permute-start | bytes 4718600 | tf_op jit(solution)/shard_map/ppermute | solution.py:291
  187.8 73.6 %collective-permute-start.27 = (f32[1536,256]{1,0:T(8,128)S(1)}, f32[1536,256]{1,0:T(8,128)S(1)}, u32[]{:S(2)}, u32[]{:S(2)}) collective-permute-start(f32[1536,256]{1,0:T(8,128)S(1)} %get-tuple-element.14), channel_id=1, source_target_pairs={{0,4},{4,0},{8,12},{12,8},{16,20},{20,16},{24,28},{28,24},{1,5},{5... | collective-permute-start | bytes 4718600 | tf_op jit(solution)/shard_map/ppermute | solution.py:291
  189.3 58.5 %collective-permute-start.28 = (f32[7,3,512]{2,1,0:T(4,128)S(1)}, f32[7,3,512]{2,1,0:T(4,128)S(1)}, u32[]{:S(2)}, u32[]{:S(2)}) collective-permute-start(f32[7,3,512]{2,1,0:T(4,128)S(1)} %constant_dynamic-update-slice_fusion), channel_id=1, source_target_pairs={{0,4},{4,0},{8,12},{12,8},{16,20},{20,16},{24,28},{28,24},{1,5},{5... | collective-permute-start | bytes 129032 | tf_op jit(solution)/shard_map/ppermute | solution.py:304
  (42 other events, 349.8 us)

commit v3 on v2

--- a/solution.py
+++ b/solution.py
@@ -93,6 +93,10 @@
 def lines(array, hops):
     perm = [(2 * a + y, 2 * b + y) for a, b in hops for y in range(2)]
     return lax.ppermute(array, "rep", perm)
+
+
+def after(array, *earlier):
+    return lax.optimization_barrier((array,) + earlier)[0]
 
 
 PAIRS = ((0, 1), (1, 0), (2, 3), (3, 2))
@@ -249,10 +253,12 @@
     inside = jnp.logical_or(level == 1, level == 2)
     low = level <= 1
 
+    wide_grad, taps = gated_grads(tokens, in_weight, kernel, out_grad)
+    wide_grad = jnp.transpose(wide_grad, (1, 0, 2))
+
     whole, piece = turn_tokens(place, tokens)
     near = lines(piece, PAIRS)
     mid = lines(piece, MIDDLE)
-    far = lines(near, MIDDLE)
 
     def ended(array):
         return jnp.where(low, array[:OWN], array[BLOCKS - OWN :])
@@ -268,40 +274,55 @@
         both = lax.ppermute(across, "shard", [(q, q ^ 1) for q in range(4)])
         return (array, beside, across, both)
 
+    cw = chans // CHUNKS
+    chunks = [wide_grad[:, :, cw * h : cw * (h + 1)] for h in range(CHUNKS)]
+    even = jnp.logical_or(level == 0, level == 2)
+    inners = [lines(jnp.where(low, mine[0:2], mine[1:3]), INWARD) for mine in chunks]
+    firsts = [lines(jnp.where(even, mine[2], mine[0]), PAIRS) for mine in chunks]
+
+    def tap_step(taps, bit):
+        return taps + lax.ppermute(taps, "rep", [(r, r ^ bit) for r in range(2 * LEVELS)])
+
+    taps = tap_step(taps, 1)
+
+    far = lines(near, MIDDLE)
     slots = [share(jnp.where(inside, level_blocks(near), ended(near)))]
-    for got in (mid, far):
-        outer = lines(ended(got), OUTWARD)
-        slots.append(share(jnp.where(inside, level_blocks(got), outer)))
-
-    wide_grad, taps = gated_grads(tokens, in_weight, kernel, out_grad)
-    wide_grad = jnp.transpose(wide_grad, (1, 0, 2))
+    outer2 = lines(after(ended(mid), near), OUTWARD)
+
+    middles = [
+        lines(after(jnp.where(low, mine[1:3], mine[0:2]), near, mid), MIDDLE) for mine in chunks
+    ]
+    slots.append(share(jnp.where(inside, level_blocks(mid), outer2)))
+    outer3 = lines(ended(far), OUTWARD)
+    taps = tap_step(after(taps, far), 2)
+    slots.append(share(after(jnp.where(inside, level_blocks(far), outer3), slots[1][3], taps)))
+
+    mixed_grad = after(wide_grad, far, taps).astype(jnp.bfloat16)
+    order = [jnp.bitwise_xor(quarter, k).astype(jnp.int32) for k in (3, 1, 2, 0)]
+    send = token_part(jnp.stack(order[:2]), mixed_grad, in_weight)
+    keep = token_part(jnp.stack(order[2:]), mixed_grad, in_weight)
+    other = lax.ppermute(send, "shard", [(q, q ^ 1) for q in range(4)])
+    last = lax.ppermute(
+        after(keep[0] + other[0], slots[2][2]), "shard", [(q, q ^ 2) for q in range(4)]
+    )
+    token_grad = (keep[1] + other[1] + last).astype(jnp.bfloat16)
 
     tok = arrange_tokens(place, whole, slots)
     parts = []
-    cw = chans // CHUNKS
-    for h in range(CHUNKS):
-        mine = wide_grad[:, :, cw * h : cw * (h + 1)]
-        even = jnp.logical_or(level == 0, level == 2)
-        first = lines(jnp.where(even, mine[2], mine[0]), PAIRS)
-        inner = lines(jnp.where(low, mine[0:2], mine[1:3]), INWARD)
-        middle = lines(jnp.where(low, mine[1:3], mine[0:2]), MIDDLE)
-        relayed = lines(jnp.stack([first, jnp.where(low, inner[1], inner[0])]), MIDDLE)
-        outer = lines(jnp.stack([jnp.where(low, middle[0], middle[1]), relayed[0]]), OUTWARD)
+    for h, mine in enumerate(chunks):
+        first, inner, middle = firsts[h], inners[h], middles[h]
+        relay = jnp.stack([first, jnp.where(low, inner[1], inner[0])])
+        relayed = lines(after(relay, far), MIDDLE)
+        outgoing = jnp.stack([jnp.where(low, middle[0], middle[1]), relayed[0]])
+        if h == 0:
+            taps = tap_step(taps, 4)
+        else:
+            outgoing = after(outgoing, taps)
+        outer = lines(outgoing, OUTWARD)
         send, keep = weight_part(place, tok, mine, first, inner, middle, relayed, outer)
         other = lax.ppermute(send, "rep", [(r, r ^ 1) for r in range(2 * LEVELS)])
         parts.append((keep + other) * scale)
     weight_grad = jnp.concatenate(parts, axis=1)
-
-    mixed_grad = wide_grad.astype(jnp.bfloat16)
-    order = [jnp.bitwise_xor(quarter, k).astype(jnp.int32) for k in (3, 1, 2, 0)]
-    send = token_part(jnp.stack(order[:2]), mixed_grad, in_weight)
-    keep = token_part(jnp.stack(order[2:]), mixed_grad, in_weight)
-    other = lax.ppermute(send, "shard", [(q, q ^ 1) for q in range(4)])
-    last = lax.ppermute(keep[0] + other[0], "shard", [(q, q ^ 2) for q in range(4)])
-    token_grad = (keep[1] + other[1] + last).astype(jnp.bfloat16)
-
-    for bit in (1, 2, 4):
-        taps = taps + lax.ppermute(taps, "rep", [(r, r ^ bit) for r in range(2 * LEVELS)])
     return (token_grad, weight_grad, taps * scale)
 
 

time: 266 us -> 238 us (0.89)
  waiting for transfers between devices: 149 us -> 116 us
  other arithmetic: 20.8 us -> 29.1 us
  local copies, waits for them, and re-layouts: 14.2 us -> 10 us
    ppermute x15, waiting for transfers between devices: 59.1 us -> 11.8 us  [lines(): return lax.ppermute(array, 'rep', perm)]
    ppermute x2, waiting for transfers between devices: 0.01 us -> 39.3 us  [lined(): other = lax.ppermute(send, 'rep', [(r, r ^ 1) for r in range(2 * LEVELS)])]
    ppermute x4, waiting for transfers between devices: 65.7 us -> 41.2 us  [the longest x3 24.2 us: tap_step(): lax.ppermute(taps, 'rep', [(r, r ^ bit) for r in range(2 * LEVELS)])]
    add x1, other arithmetic: 1.28 us -> 7.03 us  [causal_mix_back(): total = total + kernel[offset] * padded[:, offset:offset + length]]
    unnamed x77 -> x83, local copies, waits for them, and re-layouts: 7.73 us -> 4.01 us
    ppermute x4, starting transfers between devices: 4.34 us -> 7.31 us  [the longest x3 5.75 us: tap_step(): lax.ppermute(taps, 'rep', [(r, r ^ bit) for r in range(2 * LEVELS)])]
  transfers between devices with their start and end apart: 31 -> 31, of which waited for: 13 -> 8; matrix products, arithmetic and copies ran while one was open for 12% -> 17% of each run, Pallas kernels for 13% -> 14%
where the time goes in v3:
time: 238 us; the launch traced here: 237 us
  waiting for transfers between devices  116 us (49%)
  starting transfers between devices  38.7 us (16%)
  Pallas kernels  34.3 us (14%)
  other arithmetic  29.1 us (12%)
  local copies, waits for them, and re-layouts  10 us (4%)
  matrix products  6.49 us (3%)
    ppermute x2, waiting for transfers between devices, lined(): other = lax.ppermute(send, 'rep', [(r, r ^ 1) for r in range(2 * LEVELS)])  39.3 us
    ppermute x3, waiting for transfers between devices, tap_step(): lax.ppermute(taps, 'rep', [(r, r ^ bit) for r in range(2 * LEVELS)])  24.2 us
    ppermute x3, waiting for transfers between devices, share(): across = lax.ppermute(array, 'shard', [(q, q ^ 2) for q in range(4)])  24.1 us
    ppermute x15, starting transfers between devices, lines(): return lax.ppermute(array, 'rep', perm)  23.5 us
    ppermute x1, waiting for transfers between devices, lined(): lax.ppermute(after(keep[0] + other[0], slots[2][2]), 'shard', [(q, q ^ 2)...  16.9 us
    pallas_call x2, Pallas kernels, token_part(): pl.pallas_call(body, out_shape=jax.ShapeDtypeStruct((count, rows, wide),...  14.5 us
    ppermute x15, waiting for transfers between devices, lines(): return lax.ppermute(array, 'rep', perm)  11.8 us
    pallas_call x2, Pallas kernels, weight_part(): pl.pallas_call(body, out_shape=(half, half), in_specs=[SMEM] + [VMEM] * 7...  11.8 us
  transfers between devices with their start and end apart: 31, of which 8 were waited for; matrix products, arithmetic and copies ran while one was open for 17% of the time, Pallas kernels for 14%

profile of v3, /device:TPU:0, one launch (start us, length us, event | category | flops | bytes accessed | tf_op | source)
XLA Modules:
  0.0 236.6 jit_solution(3653774802794705877)
XLA Ops:
  3.7 3.1 %collective-permute-start = (f32[8,128,256]{2,1,0:T(8,128)S(1)}, f32[8,128,256]{2,1,0:T(8,128)}, u32[]{:S(2)}, u32[]{:S(2)}) collective-permute-start(f32[8,128,256]{2,1,0:T(8,128)S(1)} %get-tuple-element.19), channel_id=1, source_target_pairs={{0,8},{4,12},{8,0},{12,4},{16,24},{20,28},{24,16},{28,20},{1,9},{5... | collective-permute-start | bytes 3145736 | tf_op jit(solution)/shard_map/ppermute | solution.py:95
  8.4 6.5 %fusion.5 = bf16[256,3,512]{2,0,1:T(8,128)(2,1)S(1)} fusion(bf16[3,4096,512]{2,1,0:T(8,128)(2,1)} %weight.3, bf16[256,4096]{1,0:T(8,128)(2,1)S(1)} %copy-done.10), kind=kOutput, calls=%fused_computation.24 | convolution fusion | flops 3221618688 | bytes 15466496 | tf_op jit(solution)/shard_map/td,sdc->tsc/dot_general | solution.py:47
  17.4 2.1 multiply_reduce_fusion
  21.5 7.0 %multiply_add_fusion = f32[2,128,3,512]{3,1,0,2:T(8,128)S(1)} fusion(f32[2,128,3,512]{3,1,0,2:T(8,128)} %get-tuple-element.59, f32[3,512]{1,0:T(4,128)S(1)} %get-tuple-element.79, f32[3,512]{1,0:T(4,128)S(1)} %get-tuple-element.80, f32[3,512]{1,0:T(4,128)S(1)} %get-tuple-element.81, f32[3,512]{1,0:T(4,128)S(1)} %get-tuple-element.82, ...), kind=kLoop, calls=%fused_computation.14 | loop fusion | flops 5111808 | bytes 3188736 | tf_op jit(solution)/shard_map/add | solution.py:30
  29.5 3.4 %collective-permute-start.24 = (f32[256,256]{1,0:T(8,128)}, f32[256,256]{1,0:T(8,128)S(1)}, u32[]{:S(2)}, u32[]{:S(2)}) collective-permute-start(f32[256,256]{1,0:T(8,128)} %get-tuple-element.56), channel_id=1, source_target_pairs={{0,8},{4,12},{8,0},{12,4},{16,24},{20,28},{24,16},{28,20},{1,9},{5... | collective-permute-start | bytes 786440 | tf_op jit(solution)/shard_map/ppermute | solution.py:95
  32.9 2.3 slice_select_fusion.1
  38.0 4.6 %collective-permute-start.25 = (f32[2,256,256]{2,1,0:T(8,128)}, f32[2,256,256]{2,1,0:T(8,128)S(1)}, u32[]{:S(2)}, u32[]{:S(2)}) collective-permute-start(f32[2,256,256]{2,1,0:T(8,128)} %get-tuple-element.52), channel_id=1, source_target_pairs={{0,8},{4,12},{24,16},{28,20},{1,9},{5,13},{25,17},{29,21},{2,10},{... | collective-permute-start | bytes 1572872 | tf_op jit(solution)/shard_map/ppermute | solution.py:95
  46.1 11.8 %collective-permute-done.7 = f32[6,128,256]{2,1,0:T(8,128)S(1)} collective-permute-done((f32[6,128,256]{2,1,0:T(8,128)}, f32[6,128,256]{2,1,0:T(8,128)S(1)}, u32[]{:S(2)}, u32[]{:S(2)}) %collective-permute-start.7) | collective-permute-done | bytes 786464 | tf_op jit(solution)/shard_map/ppermute | solution.py:95
  67.0 8.5 %collective-permute-done.8.refs_6_ = f32[6,128,256]{2,1,0:T(8,128)S(1)} collective-permute-done((f32[6,128,256]{2,1,0:T(8,128)S(1)}, f32[6,128,256]{2,1,0:T(8,128)S(1)}, u32[]{:S(2)}, u32[]{:S(2)}) %collective-permute-start.8) | collective-permute-done | bytes 786464 | tf_op jit(solution)/shard_map/ppermute | solution.py:272
  75.5 1.9 fusion.12.refs_0_
  79.1 11.2 %collective-permute-done.3 = f32[7,3,512]{2,1,0:T(4,128)S(1)} collective-permute-done((f32[7,3,512]{2,1,0:T(4,128)S(1)}, f32[7,3,512]{2,1,0:T(4,128)S(1)}, u32[]{:S(2)}, u32[]{:S(2)}) %collective-permute-start.3) | collective-permute-done | bytes 43040 | tf_op jit(solution)/shard_map/ppermute | solution.py:284
  91.2 7.9 %token_part.3 = f32[2,256,1024]{2,1,0:T(8,128)} custom-call(s32[2]{0:T(128)S(1)} %pad_add_fusion.2.order, bf16[3,256,512]{2,1,0:T(8,128)(2,1)S(1)} %convert_element_type.20.grads, bf16[3,4096,512]{2,1,0:T(8,128)(2,1)} %weight.3), custom_call_target="tpu_custom_call" | custom-call | tf_op jit(solution)/shard_map/token_part/pallas_call | solution.py:225
  99.9 4.2 %collective-permute-start.28 = (f32[7,3,512]{2,1,0:T(4,128)S(1)}, f32[7,3,512]{2,1,0:T(4,128)S(1)}, u32[]{:S(2)}, u32[]{:S(2)}) collective-permute-start(f32[7,3,512]{2,1,0:T(4,128)S(1)} %add.89), channel_id=1, source_target_pairs={{0,16},{4,20},{8,24},{12,28},{16,0},{20,4},{24,8},{28,12},{1,17},{... | collective-permute-start | bytes 129032 | tf_op jit(solution)/shard_map/ppermute | solution.py:284
  105.7 13.0 %collective-permute-done.28 = f32[7,3,512]{2,1,0:T(4,128)S(1)} collective-permute-done((f32[7,3,512]{2,1,0:T(4,128)S(1)}, f32[7,3,512]{2,1,0:T(4,128)S(1)}, u32[]{:S(2)}, u32[]{:S(2)}) %collective-permute-start.28) | collective-permute-done | bytes 43040 | tf_op jit(solution)/shard_map/ppermute | solution.py:284
  122.6 15.6 %collective-permute-done.10.refs_10_ = f32[6,128,256]{2,1,0:T(8,128)} collective-permute-done((f32[6,128,256]{2,1,0:T(8,128)}, f32[6,128,256]{2,1,0:T(8,128)}, u32[]{:S(2)}, u32[]{:S(2)}) %collective-permute-start.10) | collective-permute-done | bytes 786464 | tf_op jit(solution)/shard_map/ppermute | solution.py:272
  142.8 6.6 %token_part.2 = f32[2,256,1024]{2,1,0:T(8,128)S(1)} custom-call(s32[2]{0:T(128)S(1)} %pad_add_fusion.order, bf16[3,256,512]{2,1,0:T(8,128)(2,1)S(1)} %convert_element_type.20.grads, bf16[3,4096,512]{2,1,0:T(8,128)(2,1)} %weight.3), custom_call_target="tpu_custom_call" | custom-call | tf_op jit(solution)/shard_map/token_part/pallas_call | solution.py:225
  151.0 6.7 %arrange_tokens.1.tok = bf16[6,512,1024]{2,1,0:T(8,128)(2,1)} custom-call(s32[3]{0:T(128)S(1)} %pad_add_fusion.1.place, bf16[8,512,256]{2,1,0:T(8,128)(2,1)} %copy-done.1, f32[6,128,256]{2,1,0:T(8,128)S(1)} %fusion.12.refs_0_, f32[6,128,256]{2,1,0:T(8,128)S(1)} %copy-done.22, f32[6,128,256]{2,1,0:T(8,128)S(1)} %copy-done.20, f32[6,128,256]{2,1,0:T(8,128)S(1)} %copy-done.24, ...), custom_call_target="tpu_custom_call" | custom-call | tf_op jit(solution)/shard_map/arrange_tokens/pallas_call | solution.py:148
  157.7 6.0 %weight_part.3 = (f32[1536,256]{1,0:T(8,128)S(1)}, f32[1536,256]{1,0:T(8,128)}) custom-call(s32[3]{0:T(128)S(1)} %pad_add_fusion.1.place, bf16[6,512,1024]{2,1,0:T(8,128)(2,1)} %arrange_tokens.1.tok, f32[3,256,256]{2,1,0:T(8,128)S(1)} %copy-done, f32[256,256]{1,0:T(8,128)S(1)} %copy-done.16, f32[2,256,256]{2,1,0:T(8,128)S(1)} %copy-done.3, ...), custom_call_target="tpu_custom_call" | custom-call | tf_op jit(solution)/shard_map/weight_part/pallas_call | solution.py:196
  168.6 5.8 %weight_part.2 = (f32[1536,256]{1,0:T(8,128)S(1)}, f32[1536,256]{1,0:T(8,128)}) custom-call(s32[3]{0:T(128)S(1)} %pad_add_fusion.1.place, bf16[6,512,1024]{2,1,0:T(8,128)(2,1)} %arrange_tokens.1.tok, f32[3,256,256]{2,1,0:T(8,128)S(1)} %get-tuple-element.57.own, f32[256,256]{1,0:T(8,128)S(1)} %collective-permute-done.18.first, f32[2,256,256]{2,1,0:T(8,128)S(1)} %copy-done.5, ...), custom_call_target="tpu_custom_call" | custom-call | tf_op jit(solution)/shard_map/weight_part/pallas_call | solution.py:196
  175.4 16.9 %collective-permute-done.11 = f32[256,1024]{1,0:T(8,128)S(1)} collective-permute-done((f32[256,1024]{1,0:T(8,128)S(1)}, f32[256,1024]{1,0:T(8,128)S(1)}, u32[]{:S(2)}, u32[]{:S(2)}) %collective-permute-start.11) | collective-permute-done | bytes 1048608 | tf_op jit(solution)/shard_map/ppermute | solution.py:305
  192.3 2.3 fusion.11
  194.6 6.4 %collective-permute-done.30 = f32[1536,256]{1,0:T(8,128)S(1)} collective-permute-done((f32[1536,256]{1,0:T(8,128)S(1)}, f32[1536,256]{1,0:T(8,128)S(1)}, u32[]{:S(2)}, u32[]{:S(2)}) %collective-permute-start.30) | collective-permute-done | bytes 1572896 | tf_op jit(solution)/shard_map/ppermute | solution.py:323
  201.4 33.0 %collective-permute-done.23 = f32[1536,256]{1,0:T(8,128)S(1)} collective-permute-done((f32[1536,256]{1,0:T(8,128)S(1)}, f32[1536,256]{1,0:T(8,128)S(1)}, u32[]{:S(2)}, u32[]{:S(2)}) %collective-permute-start.23) | collective-permute-done | bytes 1572896 | tf_op jit(solution)/shard_map/ppermute | solution.py:323
  234.5 2.1 pad_maximum_fusion
  (173 shorter events, 46.2 us)
Async XLA Ops:
  3.7 31.6 %collective-permute-start = (f32[8,128,256]{2,1,0:T(8,128)S(1)}, f32[8,128,256]{2,1,0:T(8,128)}, u32[]{:S(2)}, u32[]{:S(2)}) collective-permute-start(f32[8,128,256]{2,1,0:T(8,128)S(1)} %get-tuple-element.19), channel_id=1, source_target_pairs={{0,8},{4,12},{8,0},{12,4},{16,24},{20,28},{24,16},{28,20},{1,9},{5... | collective-permute-start | bytes 3145736 | tf_op jit(solution)/shard_map/ppermute | solution.py:95
  6.8 26.2 %collective-permute-start.6 = (f32[8,128,256]{2,1,0:T(8,128)S(1)}, f32[8,128,256]{2,1,0:T(8,128)}, u32[]{:S(2)}, u32[]{:S(2)}) collective-permute-start(f32[8,128,256]{2,1,0:T(8,128)S(1)} %get-tuple-element.19), channel_id=1, source_target_pairs={{8,16},{12,20},{16,8},{20,12},{9,17},{13,21},{17,9},{21,13},{10,18... | collective-permute-start | bytes 3145736 | tf_op jit(solution)/shard_map/ppermute | solution.py:95
  19.9 22.9 %collective-permute-start.2 = (f32[7,3,512]{2,1,0:T(4,128)S(1)}, f32[7,3,512]{2,1,0:T(4,128)S(1)}, u32[]{:S(2)}, u32[]{:S(2)}) collective-permute-start(f32[7,3,512]{2,1,0:T(4,128)S(1)} %constant_dynamic-update-slice_fusion), channel_id=1, source_target_pairs={{0,4},{4,0},{8,12},{12,8},{16,20},{20,16},{24,28},{28,24},{1,5},{5... | collective-permute-start | bytes 129032 | tf_op jit(solution)/shard_map/ppermute | solution.py:284
  29.5 36.1 %collective-permute-start.24 = (f32[256,256]{1,0:T(8,128)}, f32[256,256]{1,0:T(8,128)S(1)}, u32[]{:S(2)}, u32[]{:S(2)}) collective-permute-start(f32[256,256]{1,0:T(8,128)} %get-tuple-element.56), channel_id=1, source_target_pairs={{0,8},{4,12},{8,0},{12,4},{16,24},{20,28},{24,16},{28,20},{1,9},{5... | collective-permute-start | bytes 786440 | tf_op jit(solution)/shard_map/ppermute | solution.py:95
  35.3 22.6 %collective-permute-start.7 = (f32[6,128,256]{2,1,0:T(8,128)}, f32[6,128,256]{2,1,0:T(8,128)S(1)}, u32[]{:S(2)}, u32[]{:S(2)}) collective-permute-start(f32[6,128,256]{2,1,0:T(8,128)} %slice_select_fusion.1), channel_id=1, source_target_pairs={{8,0},{12,4},{16,24},{20,28},{9,1},{13,5},{17,25},{21,29},{10,2},{... | collective-permute-start | bytes 2359304 | tf_op jit(solution)/shard_map/ppermute | solution.py:95
  38.0 22.7 %collective-permute-start.25 = (f32[2,256,256]{2,1,0:T(8,128)}, f32[2,256,256]{2,1,0:T(8,128)S(1)}, u32[]{:S(2)}, u32[]{:S(2)}) collective-permute-start(f32[2,256,256]{2,1,0:T(8,128)} %get-tuple-element.52), channel_id=1, source_target_pairs={{0,8},{4,12},{24,16},{28,20},{1,9},{5,13},{25,17},{29,21},{2,10},{... | collective-permute-start | bytes 1572872 | tf_op jit(solution)/shard_map/ppermute | solution.py:95
  42.7 34.8 %collective-permute-start.18 = (f32[256,256]{1,0:T(8,128)}, f32[256,256]{1,0:T(8,128)S(1)}, u32[]{:S(2)}, u32[]{:S(2)}) collective-permute-start(f32[256,256]{1,0:T(8,128)} %get-tuple-element.55), channel_id=1, source_target_pairs={{0,8},{4,12},{8,0},{12,4},{16,24},{20,28},{24,16},{28,20},{1,9},{5... | collective-permute-start | bytes 786440 | tf_op jit(solution)/shard_map/ppermute | solution.py:95
  42.8 22.0 %collective-permute-start.1 = (f32[8,128,256]{2,1,0:T(8,128)}, f32[8,128,256]{2,1,0:T(8,128)S(1)}, u32[]{:S(2)}, u32[]{:S(2)}) collective-permute-start(f32[8,128,256]{2,1,0:T(8,128)} %collective-permute-done), channel_id=1, source_target_pairs={{8,16},{12,20},{16,8},{20,12},{9,17},{13,21},{17,9},{21,13},{10,18... | collective-permute-start | bytes 3145736 | tf_op jit(solution)/shard_map/ppermute | solution.py:95
  57.9 21.1 %collective-permute-start.19 = (f32[2,256,256]{2,1,0:T(8,128)S(1)}, f32[2,256,256]{2,1,0:T(8,128)S(1)}, u32[]{:S(2)}, u32[]{:S(2)}) collective-permute-start(f32[2,256,256]{2,1,0:T(8,128)S(1)} %copy-done.33), channel_id=1, source_target_pairs={{0,8},{4,12},{24,16},{28,20},{1,9},{5,13},{25,17},{29,21},{2,10},{... | collective-permute-start | bytes 1572872 | tf_op jit(solution)/shard_map/ppermute | solution.py:95
  64.9 34.3 %collective-permute-start.26 = (f32[2,256,256]{2,1,0:T(8,128)S(1)}, f32[2,256,256]{2,1,0:T(8,128)S(1)}, u32[]{:S(2)}, u32[]{:S(2)}) collective-permute-start(f32[2,256,256]{2,1,0:T(8,128)S(1)} %copy-done.32), channel_id=1, source_target_pairs={{8,16},{12,20},{16,8},{20,12},{9,17},{13,21},{17,9},{21,13},{10,18... | collective-permute-start | bytes 1572872 | tf_op jit(solution)/shard_map/ppermute | solution.py:95
  65.7 33.5 %collective-permute-start.5 = (f32[6,128,256]{2,1,0:T(8,128)S(1)}, f32[6,128,256]{2,1,0:T(8,128)S(1)}, u32[]{:S(2)}, u32[]{:S(2)}) collective-permute-start(f32[6,128,256]{2,1,0:T(8,128)S(1)} %slice_select_fusion.2), channel_id=1, source_target_pairs={{8,0},{12,4},{16,24},{20,28},{9,1},{13,5},{17,25},{21,29},{10,2},{... | collective-permute-start | bytes 2359304 | tf_op jit(solution)/shard_map/ppermute | solution.py:95
  75.5 24.4 %collective-permute-start.9 = (f32[6,128,256]{2,1,0:T(8,128)S(1)}, f32[6,128,256]{2,1,0:T(8,128)S(1)}, u32[]{:S(2)}, u32[]{:S(2)}) collective-permute-start(f32[6,128,256]{2,1,0:T(8,128)S(1)} %collective-permute-done.8.refs_6_), channel_id=1, source_target_pairs={{0,1},{1,0},{2,3},{3,2},{4,5},{5,4},{6,7},{7,6},{8,9},{9,8},{10,11... | collective-permute-start | bytes 2359304 | tf_op jit(solution)/shard_map/ppermute | solution.py:274
  77.4 27.8 %collective-permute-start.13 = (f32[6,128,256]{2,1,0:T(8,128)S(1)}, f32[6,128,256]{2,1,0:T(8,128)S(1)}, u32[]{:S(2)}, u32[]{:S(2)}) collective-permute-start(f32[6,128,256]{2,1,0:T(8,128)S(1)} %fusion.12.refs_0_), channel_id=1, source_target_pairs={{0,2},{1,3},{2,0},{3,1},{4,6},{5,7},{6,4},{7,5},{8,10},{9,11},{10,... | collective-permute-start | bytes 2359304 | tf_op jit(solution)/shard_map/ppermute | solution.py:272
  99.1 66.4 %collective-permute-start.4 = (f32[2,256,1024]{2,1,0:T(8,128)}, f32[2,256,1024]{2,1,0:T(8,128)}, u32[]{:S(2)}, u32[]{:S(2)}) collective-permute-start(f32[2,256,1024]{2,1,0:T(8,128)} %token_part.3), channel_id=1, source_target_pairs={{0,1},{1,0},{2,3},{3,2},{4,5},{5,4},{6,7},{7,6},{8,9},{9,8},{10,11... | collective-permute-start | bytes 6291464 | tf_op jit(solution)/shard_map/ppermute | solution.py:304
  99.2 21.1 %collective-permute-start.27 = (f32[2,256,256]{2,1,0:T(8,128)S(1)}, f32[2,256,256]{2,1,0:T(8,128)S(1)}, u32[]{:S(2)}, u32[]{:S(2)}) collective-permute-start(f32[2,256,256]{2,1,0:T(8,128)S(1)} %pad_maximum_fusion.4), channel_id=1, source_target_pairs={{8,16},{12,20},{16,8},{20,12},{9,17},{13,21},{17,9},{21,13},{10,18... | collective-permute-start | bytes 1572872 | tf_op jit(solution)/shard_map/ppermute | solution.py:95
  99.9 18.8 %collective-permute-start.28 = (f32[7,3,512]{2,1,0:T(4,128)S(1)}, f32[7,3,512]{2,1,0:T(4,128)S(1)}, u32[]{:S(2)}, u32[]{:S(2)}) collective-permute-start(f32[7,3,512]{2,1,0:T(4,128)S(1)} %add.89), channel_id=1, source_target_pairs={{0,16},{4,20},{8,24},{12,28},{16,0},{20,4},{24,8},{28,12},{1,17},{... | collective-permute-start | bytes 129032 | tf_op jit(solution)/shard_map/ppermute | solution.py:284
  118.7 19.5 %collective-permute-start.10 = (f32[6,128,256]{2,1,0:T(8,128)}, f32[6,128,256]{2,1,0:T(8,128)}, u32[]{:S(2)}, u32[]{:S(2)}) collective-permute-start(f32[6,128,256]{2,1,0:T(8,128)} %fusion.13.refs_8_), channel_id=1, source_target_pairs={{0,2},{1,3},{2,0},{3,1},{4,6},{5,7},{6,4},{7,5},{8,10},{9,11},{10,... | collective-permute-start | bytes 2359304 | tf_op jit(solution)/shard_map/ppermute | solution.py:272
  120.3 18.7 %collective-permute-start.21 = (f32[2,256,256]{2,1,0:T(8,128)S(1)}, f32[2,256,256]{2,1,0:T(8,128)S(1)}, u32[]{:S(2)}, u32[]{:S(2)}) collective-permute-start(f32[2,256,256]{2,1,0:T(8,128)S(1)} %pad_maximum_fusion.2), channel_id=1, source_target_pairs={{8,16},{12,20},{16,8},{20,12},{9,17},{13,21},{17,9},{21,13},{10,18... | collective-permute-start | bytes 1572872 | tf_op jit(solution)/shard_map/ppermute | solution.py:95
  121.2 28.3 %collective-permute-start.15 = (f32[6,128,256]{2,1,0:T(8,128)S(1)}, f32[6,128,256]{2,1,0:T(8,128)}, u32[]{:S(2)}, u32[]{:S(2)}) collective-permute-start(f32[6,128,256]{2,1,0:T(8,128)S(1)} %fusion.14.refs_4_), channel_id=1, source_target_pairs={{0,1},{1,0},{2,3},{3,2},{4,5},{5,4},{6,7},{7,6},{8,9},{9,8},{10,11... | collective-permute-start | bytes 2359304 | tf_op jit(solution)/shard_map/ppermute | solution.py:273
  122.3 28.6 %collective-permute-start.16 = (f32[6,128,256]{2,1,0:T(8,128)}, f32[6,128,256]{2,1,0:T(8,128)}, u32[]{:S(2)}, u32[]{:S(2)}) collective-permute-start(f32[6,128,256]{2,1,0:T(8,128)} %fusion.13.refs_8_), channel_id=1, source_target_pairs={{0,1},{1,0},{2,3},{3,2},{4,5},{5,4},{6,7},{7,6},{8,9},{9,8},{10,11... | collective-permute-start | bytes 2359304 | tf_op jit(solution)/shard_map/ppermute | solution.py:273
  149.4 19.1 %collective-permute-start.22 = (f32[2,256,256]{2,1,0:T(8,128)S(1)}, f32[2,256,256]{2,1,0:T(8,128)S(1)}, u32[]{:S(2)}, u32[]{:S(2)}) collective-permute-start(f32[2,256,256]{2,1,0:T(8,128)S(1)} %pad_maximum_fusion.3), channel_id=1, source_target_pairs={{8,0},{12,4},{16,24},{20,28},{9,1},{13,5},{17,25},{21,29},{10,2},{... | collective-permute-start | bytes 1572872 | tf_op jit(solution)/shard_map/ppermute | solution.py:95
  163.7 37.2 %collective-permute-start.30 = (f32[1536,256]{1,0:T(8,128)S(1)}, f32[1536,256]{1,0:T(8,128)S(1)}, u32[]{:S(2)}, u32[]{:S(2)}) collective-permute-start(f32[1536,256]{1,0:T(8,128)S(1)} %get-tuple-element.34), channel_id=1, source_target_pairs={{0,4},{4,0},{8,12},{12,8},{16,20},{20,16},{24,28},{28,24},{1,5},{5... | collective-permute-start | bytes 4718600 | tf_op jit(solution)/shard_map/ppermute | solution.py:323
  167.0 25.4 %collective-permute-start.11 = (f32[256,1024]{1,0:T(8,128)S(1)}, f32[256,1024]{1,0:T(8,128)S(1)}, u32[]{:S(2)}, u32[]{:S(2)}) collective-permute-start(f32[256,1024]{1,0:T(8,128)S(1)} %fusion.8), channel_id=1, source_target_pairs={{0,2},{1,3},{2,0},{3,1},{4,6},{5,7},{6,4},{7,5},{8,10},{9,11},{10,... | collective-permute-start | bytes 3145736 | tf_op jit(solution)/shard_map/ppermute | solution.py:305
  174.4 60.0 %collective-permute-start.23 = (f32[1536,256]{1,0:T(8,128)S(1)}, f32[1536,256]{1,0:T(8,128)S(1)}, u32[]{:S(2)}, u32[]{:S(2)}) collective-permute-start(f32[1536,256]{1,0:T(8,128)S(1)} %get-tuple-element.29), channel_id=1, source_target_pairs={{0,4},{4,0},{8,12},{12,8},{16,20},{20,16},{24,28},{28,24},{1,5},{5... | collective-permute-start | bytes 4718600 | tf_op jit(solution)/shard_map/ppermute | solution.py:323
  (44 other events, 465.1 us)

commit v4 on v3

--- a/solution.py
+++ b/solution.py
@@ -130,6 +130,111 @@
     )(place, tokens)
 
 
+def gate(place, tokens, in_weight, kernel, out_grad, chunk, width):
+    rows, features = tokens.shape
+    taps = kernel.shape[0]
+    steps = 4
+    deep = features // steps
+    pad = 8
+
+    def body(place, tokens, weight, kernel, out_grad, own, grad, first, inner, middle, total, held, pads, back):
+        step = pl.program_id(0)
+        for s in range(3):
+            now = jnp.dot(tokens[...], weight[s], preferred_element_type=jnp.float32)
+
+            @pl.when(step == 0)
+            def _():
+                total[s] = now
+
+            @pl.when(step > 0)
+            def _():
+                total[s] += now
+
+        @pl.when(step == steps - 1)
+        def _():
+            blank = jnp.zeros((pad, width), jnp.float32)
+            sums = [[None] * taps for _ in range(3)]
+            for q in range(rows // SEQ):
+                here = slice(q * SEQ, (q + 1) * SEQ)
+                conv = []
+                for s in range(3):
+                    values = total[s, here, :].astype(jnp.bfloat16).astype(jnp.float32)
+                    pads[s, 0:pad, :] = blank
+                    pads[s, pad : pad + SEQ, :] = values
+                    mix = kernel[0, s : s + 1, :] * values
+                    for j in range(1, taps):
+                        mix += kernel[j, s : s + 1, :] * pads[s, pad - j : pad - j + SEQ, :]
+                    conv.append(mix)
+                up = out_grad[here, :].astype(jnp.float32)
+                query, keyed, valued = conv
+                grads = (up * keyed * valued, up * query * valued, up * query * keyed)
+                for s in range(3):
+                    g = grads[s]
+                    back[s, 0:SEQ, :] = g
+                    back[s, SEQ : SEQ + pad, :] = blank
+                    mixed = kernel[0, s : s + 1, :] * g
+                    for j in range(taps):
+                        if j:
+                            mixed += kernel[j, s : s + 1, :] * back[s, j : j + SEQ, :]
+                        term = jnp.sum(
+                            pads[s, pad - j : pad - j + SEQ, :] * g, axis=0, keepdims=True
+                        )
+                        sums[s][j] = term if q == 0 else sums[s][j] + term
+                    held[s, here, :] = mixed
+            for s in range(3):
+                own[s] = held[s].astype(jnp.bfloat16)
+                for j in range(taps):
+                    grad[j, s : s + 1, :] = sums[s][j]
+            level = place[0]
+            first[...] = held[2 - 2 * lax.rem(level, 2)]
+            low = jnp.where(level <= 1, 0, 1)
+            for i in range(2):
+                inner[i] = held[low + i]
+                middle[i] = held[1 - low + i]
+
+    one = jax.ShapeDtypeStruct((rows, width), jnp.float32)
+    two = jax.ShapeDtypeStruct((2, rows, width), jnp.float32)
+    full = lambda shape: pl.BlockSpec(shape, lambda k: (0,) * len(shape))
+    return pl.pallas_call(
+        body,
+        out_shape=(
+            jax.ShapeDtypeStruct((3, rows, width), jnp.bfloat16),
+            jax.ShapeDtypeStruct((taps, 3, width), jnp.float32),
+            one,
+            two,
+            two,
+        ),
+        grid=(steps,),
+        in_specs=[
+            SMEM,
+            pl.BlockSpec((rows, deep), lambda k: (0, k)),
+            pl.BlockSpec((3, deep, width), lambda k: (0, k, chunk)),
+            pl.BlockSpec((taps, 3, width), lambda k: (0, 0, chunk)),
+            pl.BlockSpec((rows, width), lambda k: (0, chunk)),
+        ],
+        out_specs=(
+            full((3, rows, width)),
+            full((taps, 3, width)),
+            full((rows, width)),
+            full((2, rows, width)),
+            full((2, rows, width)),
+        ),
+        scratch_shapes=[
+            pltpu.VMEM((3, rows, width), jnp.float32),
+            pltpu.VMEM((3, rows, width), jnp.float32),
+            pltpu.VMEM((3, pad + SEQ, width), jnp.float32),
+            pltpu.VMEM((3, SEQ + pad, width), jnp.float32),
+        ],
+        compiler_params=PARAMS,
+        cost_estimate=pl.CostEstimate(
+            flops=2 * rows * features * 3 * width,
+            bytes_accessed=2 * features * 3 * width,
+            transcendentals=0,
+        ),
+        name="gate",
+    )(place, tokens, in_weight, kernel, out_grad)
+
+
 def arrange_tokens(place, whole, slots):
     rows = whole.shape[2]
     slab = BLOCK // 4
@@ -205,14 +310,22 @@
 
 
 def token_part(order, grads, weight):
-    rows, chans = grads.shape[1:]
+    rows, width = grads[0].shape[1:]
     wide = weight.shape[1] // 4
+    chans = weight.shape[2]
     count = order.shape[0]
 
-    def body(order, grads, weight, out):
-        now = lax.dot_general(
-            grads[...], weight[...], (((1,), (1,)), ((), ())), preferred_element_type=jnp.float32
-        )
+    def body(order, *refs):
+        weight, out = refs[-2:]
+        now = None
+        for h, part in enumerate(refs[:-2]):
+            term = lax.dot_general(
+                part[...],
+                weight[:, width * h : width * (h + 1)],
+                (((1,), (1,)), ((), ())),
+                preferred_element_type=jnp.float32,
+            )
+            now = term if now is None else now + term
 
         @pl.when(pl.program_id(1) == 0)
         def _():
@@ -228,15 +341,18 @@
         grid_spec=pltpu.PrefetchScalarGridSpec(
             num_scalar_prefetch=1,
             grid=(count, 3),
-            in_specs=[
-                pl.BlockSpec((None, rows, chans), lambda i, s, order: (s, 0, 0)),
-                pl.BlockSpec((None, wide, chans), lambda i, s, order: (s, order[i], 0)),
-            ],
+            in_specs=[pl.BlockSpec((None, rows, width), lambda i, s, order: (s, 0, 0))] * len(grads)
+            + [pl.BlockSpec((None, wide, chans), lambda i, s, order: (s, order[i], 0))],
             out_specs=pl.BlockSpec((None, rows, wide), lambda i, s, order: (i, 0, 0)),
         ),
         compiler_params=PARAMS,
+        cost_estimate=pl.CostEstimate(
+            flops=2 * count * rows * wide * 3 * chans,
+            bytes_accessed=2 * count * wide * 3 * chans,
+            transcendentals=0,
+        ),
         name="token_part",
-    )(order, grads, weight)
+    )(order, *grads, weight)
 
 
 CHUNKS = 2
@@ -253,9 +369,6 @@
     inside = jnp.logical_or(level == 1, level == 2)
     low = level <= 1
 
-    wide_grad, taps = gated_grads(tokens, in_weight, kernel, out_grad)
-    wide_grad = jnp.transpose(wide_grad, (1, 0, 2))
-
     whole, piece = turn_tokens(place, tokens)
     near = lines(piece, PAIRS)
     mid = lines(piece, MIDDLE)
@@ -274,33 +387,42 @@
         both = lax.ppermute(across, "shard", [(q, q ^ 1) for q in range(4)])
         return (array, beside, across, both)
 
+    def tap_step(taps, bit, *earlier):
+        other = lax.ppermute(taps, "rep", [(r, r ^ bit) for r in range(2 * LEVELS)])
+        return taps + after(other, *earlier)
+
     cw = chans // CHUNKS
-    chunks = [wide_grad[:, :, cw * h : cw * (h + 1)] for h in range(CHUNKS)]
-    even = jnp.logical_or(level == 0, level == 2)
-    inners = [lines(jnp.where(low, mine[0:2], mine[1:3]), INWARD) for mine in chunks]
-    firsts = [lines(jnp.where(even, mine[2], mine[0]), PAIRS) for mine in chunks]
-
-    def tap_step(taps, bit):
-        return taps + lax.ppermute(taps, "rep", [(r, r ^ bit) for r in range(2 * LEVELS)])
-
-    taps = tap_step(taps, 1)
+    owns, firsts, inners, middles, taps = [], [], [], [], []
+    for h in range(CHUNKS):
+        own, tap, first, inner, middle = gate(place, tokens, in_weight, kernel, out_grad, h, cw)
+        owns.append(own)
+        taps.append(tap)
+        inners.append(lines(inner, INWARD))
+        firsts.append(lines(first, PAIRS))
+        middles.append(middle)
+    taps = jnp.concatenate(taps, axis=2)
 
     far = lines(near, MIDDLE)
+    middles = [lines(after(middle, near), MIDDLE) for middle in middles]
     slots = [share(jnp.where(inside, level_blocks(near), ended(near)))]
     outer2 = lines(after(ended(mid), near), OUTWARD)
 
-    middles = [
-        lines(after(jnp.where(low, mine[1:3], mine[0:2]), near, mid), MIDDLE) for mine in chunks
-    ]
-    slots.append(share(jnp.where(inside, level_blocks(mid), outer2)))
+    taps = tap_step(taps, 1, far)
     outer3 = lines(ended(far), OUTWARD)
-    taps = tap_step(after(taps, far), 2)
-    slots.append(share(after(jnp.where(inside, level_blocks(far), outer3), slots[1][3], taps)))
-
-    mixed_grad = after(wide_grad, far, taps).astype(jnp.bfloat16)
+    slots.append(share(jnp.where(inside, level_blocks(mid), after(outer2, far))))
+
+    def relay(h, *earlier):
+        first, inner = after(firsts[h], *earlier), after(inners[h], *earlier)
+        return lines(jnp.stack([first, jnp.where(low, inner[1], inner[0])]), MIDDLE)
+
+    relays = [relay(0, middles[0]), relay(1, middles[1])]
+    taps = tap_step(taps, 2, middles[0])
+    slots.append(share(jnp.where(inside, level_blocks(far), after(outer3, middles[0]))))
+
+    grads = [after(own, far) for own in owns]
     order = [jnp.bitwise_xor(quarter, k).astype(jnp.int32) for k in (3, 1, 2, 0)]
-    send = token_part(jnp.stack(order[:2]), mixed_grad, in_weight)
-    keep = token_part(jnp.stack(order[2:]), mixed_grad, in_weight)
+    send = token_part(jnp.stack(order[:2]), grads, in_weight)
+    keep = token_part(jnp.stack(order[2:]), [after(g, middles[1]) for g in grads], in_weight)
     other = lax.ppermute(send, "shard", [(q, q ^ 1) for q in range(4)])
     last = lax.ppermute(
         after(keep[0] + other[0], slots[2][2]), "shard", [(q, q ^ 2) for q in range(4)]
@@ -309,17 +431,17 @@
 
     tok = arrange_tokens(place, whole, slots)
     parts = []
-    for h, mine in enumerate(chunks):
-        first, inner, middle = firsts[h], inners[h], middles[h]
-        relay = jnp.stack([first, jnp.where(low, inner[1], inner[0])])
-        relayed = lines(after(relay, far), MIDDLE)
+    for h in range(CHUNKS):
+        middle, relayed = middles[h], relays[h]
         outgoing = jnp.stack([jnp.where(low, middle[0], middle[1]), relayed[0]])
         if h == 0:
             taps = tap_step(taps, 4)
         else:
             outgoing = after(outgoing, taps)
         outer = lines(outgoing, OUTWARD)
-        send, keep = weight_part(place, tok, mine, first, inner, middle, relayed, outer)
+        send, keep = weight_part(
+            place, tok, owns[h], firsts[h], inners[h], middle, relayed, outer
+        )
         other = lax.ppermute(send, "rep", [(r, r ^ 1) for r in range(2 * LEVELS)])
         parts.append((keep + other) * scale)
     weight_grad = jnp.concatenate(parts, axis=1)

time: 238 us -> 243 us (1.021)
  Pallas kernels: 34.3 us -> 54.2 us
  other arithmetic: 29.1 us -> 14.1 us
  matrix products: 6.49 us -> 0 us
  starting transfers between devices: 38.7 us -> 44.4 us
    ppermute x3, waiting for transfers between devices: 24.2 us -> 2.48 us  [tap_step(): other = lax.ppermute(taps, 'rep', [(r, r ^ bit) for r in range(2 * LEVELS)])]
    pallas_call x0 -> x2, Pallas kernels: none -> 20.7 us  [gate(): pl.pallas_call(body, out_shape=(jax.ShapeDtypeStruct((3, rows, width), jn...]
    ppermute x15, waiting for transfers between devices: 11.8 us -> 31.5 us  [lines(): return lax.ppermute(array, 'rep', perm)]
    add x4 -> x2, other arithmetic: 8.35 us -> 0.04 us  [tap_step(): return taps + after(other, *earlier)]
    ppermute x15, starting transfers between devices: 23.5 us -> 30.2 us  [lines(): return lax.ppermute(array, 'rep', perm)]
    dot_general x1 -> x0, matrix products: 6.49 us -> none  [gated_grads(): jnp.einsum('td,sdc->tsc', tokens, in_weight, preferred_element_type=jnp.f...]
    select_n x6 -> x4, other arithmetic: 4.89 us -> 1.31 us  [the longest x1 1.06 us: lined(): jnp.where(inside, level_blocks(far), after(outer3, middles[0]))]
    pallas_call x2, Pallas kernels: 11.8 us -> 9.33 us  [weight_part(): pl.pallas_call(body, out_shape=(half, half), in_specs=[SMEM] + [VMEM] * 7...]
  transfers between devices with their start and end apart: 31 -> 31, of which waited for: 8 -> 11; matrix products, arithmetic and copies ran while one was open for 17% -> 8% of each run, Pallas kernels for 14% -> 21%
where the time goes in v4:
time: 243 us; the launch traced here: 242 us
  waiting for transfers between devices  115 us (47%)
  Pallas kernels  54.2 us (22%)
  starting transfers between devices  44.4 us (18%)
  other arithmetic  14.1 us (6%)
  local copies, waits for them, and re-layouts  12.3 us (5%)
    ppermute x2, waiting for transfers between devices, lined(): other = lax.ppermute(send, 'rep', [(r, r ^ 1) for r in range(2 * LEVELS)])  38.6 us
    ppermute x15, waiting for transfers between devices, lines(): return lax.ppermute(array, 'rep', perm)  31.5 us
    ppermute x15, starting transfers between devices, lines(): return lax.ppermute(array, 'rep', perm)  30.2 us
    ppermute x3, waiting for transfers between devices, share(): across = lax.ppermute(array, 'shard', [(q, q ^ 2) for q in range(4)])  24.7 us
    pallas_call x2, Pallas kernels, gate(): pl.pallas_call(body, out_shape=(jax.ShapeDtypeStruct((3, rows, width), jn...  20.7 us
    ppermute x1, waiting for transfers between devices, lined(): lax.ppermute(after(keep[0] + other[0], slots[2][2]), 'shard', [(q, q ^ 2)...  18.1 us
    pallas_call x2, Pallas kernels, token_part(): pl.pallas_call(body, out_shape=jax.ShapeDtypeStruct((count, rows, wide),...  14.5 us
    pallas_call x2, Pallas kernels, weight_part(): pl.pallas_call(body, out_shape=(half, half), in_specs=[SMEM] + [VMEM] * 7...  9.33 us
  transfers between devices with their start and end apart: 31, of which 11 were waited for; matrix products, arithmetic and copies ran while one was open for 8% of the time, Pallas kernels for 21%

profile of v4, /device:TPU:0, one launch (start us, length us, event | category | flops | bytes accessed | tf_op | source)
XLA Modules:
  0.0 241.7 jit_solution(15864561440280393954)
XLA Ops:
  2.3 2.3 turn_tokens.1
  6.0 3.0 %collective-permute-start = (f32[8,128,256]{2,1,0:T(8,128)}, f32[8,128,256]{2,1,0:T(8,128)}, u32[]{:S(2)}, u32[]{:S(2)}) collective-permute-start(f32[8,128,256]{2,1,0:T(8,128)} %get-tuple-element.37), channel_id=1, source_target_pairs={{0,8},{4,12},{8,0},{12,4},{16,24},{20,28},{24,16},{28,20},{1,9},{5... | collective-permute-start | bytes 3145736 | tf_op jit(solution)/shard_map/ppermute | solution.py:95
  10.8 10.4 %gate.2 = (bf16[3,256,256]{2,1,0:T(8,128)(2,1)S(1)}, f32[7,3,256]{2,1,0:T(4,128)S(1)}, f32[256,256]{1,0:T(8,128)}, f32[2,256,256]{2,1,0:T(8,128)S(1)}, f32[2,256,256]{2,1,0:T(8,128)}) custom-call(s32[3]{0:T(128)S(1)} %pad_add_fusion.1.place, bf16[256,4096]{1,0:T(8,128)(2,1)S(1)} %copy-done, bf16[3,4096,512]{2,1,0:T(8,128)(2,1)} %refs_2_.3, ...), custom_call_target="tpu_custom_call" | custom-call | flops 1610612736 | bytes 6291456 | tf_op jit(solution)/shard_map/gate/pallas_call | solution.py:198
  21.2 5.3 %collective-permute-start.19 = (f32[2,256,256]{2,1,0:T(8,128)S(1)}, f32[2,256,256]{2,1,0:T(8,128)S(1)}, u32[]{:S(2)}, u32[]{:S(2)}) collective-permute-start(f32[2,256,256]{2,1,0:T(8,128)S(1)} %get-tuple-element.53), channel_id=1, source_target_pairs={{0,8},{4,12},{24,16},{28,20},{1,9},{5,13},{25,17},{29,21},{2,10},{... | collective-permute-start | bytes 1572872 | tf_op jit(solution)/shard_map/ppermute | solution.py:95
  26.6 10.3 %gate.3 = (bf16[3,256,256]{2,1,0:T(8,128)(2,1)S(1)}, f32[7,3,256]{2,1,0:T(4,128)S(1)}, f32[256,256]{1,0:T(8,128)S(1)}, f32[2,256,256]{2,1,0:T(8,128)}, f32[2,256,256]{2,1,0:T(8,128)S(1)}) custom-call(s32[3]{0:T(128)S(1)} %pad_add_fusion.1.place, bf16[256,4096]{1,0:T(8,128)(2,1)S(1)} %copy-done, bf16[3,4096,512]{2,1,0:T(8,128)(2,1)} %refs_2_.3, ...), custom_call_target="tpu_custom_call" | custom-call | flops 1610612736 | bytes 6291456 | tf_op jit(solution)/shard_map/gate/pallas_call | solution.py:198
  37.6 3.9 %collective-permute-start.24 = (f32[2,256,256]{2,1,0:T(8,128)}, f32[2,256,256]{2,1,0:T(8,128)S(1)}, u32[]{:S(2)}, u32[]{:S(2)}) collective-permute-start(f32[2,256,256]{2,1,0:T(8,128)} %get-tuple-element.59), channel_id=1, source_target_pairs={{0,8},{4,12},{24,16},{28,20},{1,9},{5,13},{25,17},{29,21},{2,10},{... | collective-permute-start | bytes 1572872 | tf_op jit(solution)/shard_map/ppermute | solution.py:95
  50.6 7.4 %collective-permute-start.23 = (f32[256,256]{1,0:T(8,128)S(1)}, f32[256,256]{1,0:T(8,128)S(1)}, u32[]{:S(2)}, u32[]{:S(2)}) collective-permute-start(f32[256,256]{1,0:T(8,128)S(1)} %copy-done.18), channel_id=1, source_target_pairs={{0,8},{4,12},{8,0},{12,4},{16,24},{20,28},{24,16},{28,20},{1,9},{5... | collective-permute-start | bytes 786440 | tf_op jit(solution)/shard_map/ppermute | solution.py:95
  67.0 11.8 %collective-permute-done.12 = f32[6,128,256]{2,1,0:T(8,128)S(1)} collective-permute-done((f32[6,128,256]{2,1,0:T(8,128)S(1)}, f32[6,128,256]{2,1,0:T(8,128)S(1)}, u32[]{:S(2)}, u32[]{:S(2)}) %collective-permute-start.12) | collective-permute-done | bytes 786464 | tf_op jit(solution)/shard_map/ppermute | solution.py:95
  79.7 7.9 %token_part.3 = f32[2,256,1024]{2,1,0:T(8,128)} custom-call(s32[2]{0:T(128)S(1)} %pad_add_fusion.2.order, bf16[3,256,256]{2,1,0:T(8,128)(2,1)S(1)} %get-tuple-element.41.refs_0_.own, bf16[3,256,256]{2,1,0:T(8,128)(2,1)S(1)} %get-tuple-element.44.refs_1_.own, bf16[3,4096,512]{2,1,0:T(8,128)(2,1)} %refs_2_.3), custom_call_target="tpu_custom_call" | custom-call | flops 1610612736 | bytes 6291456 | tf_op jit(solution)/shard_map/token_part/pallas_call | solution.py:338
  88.6 17.7 %collective-permute-done.4 = f32[6,128,256]{2,1,0:T(8,128)S(1)} collective-permute-done((f32[6,128,256]{2,1,0:T(8,128)S(1)}, f32[6,128,256]{2,1,0:T(8,128)S(1)}, u32[]{:S(2)}, u32[]{:S(2)}) %collective-permute-start.4) | collective-permute-done | bytes 786464 | tf_op jit(solution)/shard_map/ppermute | solution.py:95
  112.3 3.5 %collective-permute-start.28 = (f32[7,3,512]{2,1,0:T(4,128)S(1)}, f32[7,3,512]{2,1,0:T(4,128)S(1)}, u32[]{:S(2)}, u32[]{:S(2)}) collective-permute-start(f32[7,3,512]{2,1,0:T(4,128)S(1)} %add.43), channel_id=1, source_target_pairs={{0,16},{4,20},{8,24},{12,28},{16,0},{20,4},{24,8},{28,12},{1,17},{... | collective-permute-start | bytes 129032 | tf_op jit(solution)/shard_map/ppermute | solution.py:391
  115.7 2.2 collective-permute-done.28
  120.7 8.7 %collective-permute-done.14.refs_6_ = f32[6,128,256]{2,1,0:T(8,128)} collective-permute-done((f32[6,128,256]{2,1,0:T(8,128)S(1)}, f32[6,128,256]{2,1,0:T(8,128)}, u32[]{:S(2)}, u32[]{:S(2)}) %collective-permute-start.14) | collective-permute-done | bytes 786464 | tf_op jit(solution)/shard_map/ppermute | solution.py:385
  129.4 16.0 %collective-permute-done.6.refs_10_ = f32[6,128,256]{2,1,0:T(8,128)} collective-permute-done((f32[6,128,256]{2,1,0:T(8,128)}, f32[6,128,256]{2,1,0:T(8,128)}, u32[]{:S(2)}, u32[]{:S(2)}) %collective-permute-start.6) | collective-permute-done | bytes 786464 | tf_op jit(solution)/shard_map/ppermute | solution.py:385
  147.6 6.6 %token_part.2 = f32[2,256,1024]{2,1,0:T(8,128)S(1)} custom-call(s32[2]{0:T(128)S(1)} %pad_add_fusion.order, bf16[3,256,256]{2,1,0:T(8,128)(2,1)S(1)} %get-tuple-element.41.refs_0_.own, bf16[3,256,256]{2,1,0:T(8,128)(2,1)S(1)} %get-tuple-element.44.refs_1_.own, bf16[3,4096,512]{2,1,0:T(8,128)(2,1)} %refs_2_.3), custom_call_target="tpu_custom_call" | custom-call | flops 1610612736 | bytes 6291456 | tf_op jit(solution)/shard_map/token_part/pallas_call | solution.py:338
  156.8 7.3 %arrange_tokens.1.tok = bf16[6,512,1024]{2,1,0:T(8,128)(2,1)} custom-call(s32[3]{0:T(128)S(1)} %pad_add_fusion.1.place, bf16[8,512,256]{2,1,0:T(8,128)(2,1)} %copy-done.1, f32[6,128,256]{2,1,0:T(8,128)S(1)} %fusion.4.refs_0_, f32[6,128,256]{2,1,0:T(8,128)S(1)} %copy-done.16, f32[6,128,256]{2,1,0:T(8,128)} %collective-permute-done.9.refs_2_, ...), custom_call_target="tpu_custom_call" | custom-call | tf_op jit(solution)/shard_map/arrange_tokens/pallas_call | solution.py:253
  164.1 4.7 %weight_part.2 = (f32[1536,256]{1,0:T(8,128)S(1)}, f32[1536,256]{1,0:T(8,128)S(1)}) custom-call(s32[3]{0:T(128)S(1)} %pad_add_fusion.1.place, bf16[6,512,1024]{2,1,0:T(8,128)(2,1)} %arrange_tokens.1.tok, bf16[3,256,256]{2,1,0:T(8,128)(2,1)S(1)} %get-tuple-element.41.refs_0_.own, f32[256,256]{1,0:T(8,128)S(1)} %copy-done.12, ...), custom_call_target="tpu_custom_call" | custom-call | tf_op jit(solution)/shard_map/weight_part/pallas_call | solution.py:301
  170.4 2.4 fusion
  174.3 4.7 %weight_part.3 = (f32[1536,256]{1,0:T(8,128)S(1)}, f32[1536,256]{1,0:T(8,128)S(1)}) custom-call(s32[3]{0:T(128)S(1)} %pad_add_fusion.1.place, bf16[6,512,1024]{2,1,0:T(8,128)(2,1)} %arrange_tokens.1.tok, bf16[3,256,256]{2,1,0:T(8,128)(2,1)S(1)} %get-tuple-element.44.refs_1_.own, f32[256,256]{1,0:T(8,128)S(1)} %copy-done.14, ...), custom_call_target="tpu_custom_call" | custom-call | tf_op jit(solution)/shard_map/weight_part/pallas_call | solution.py:301
  180.2 18.1 %collective-permute-done.7 = f32[256,1024]{1,0:T(8,128)S(1)} collective-permute-done((f32[256,1024]{1,0:T(8,128)}, f32[256,1024]{1,0:T(8,128)S(1)}, u32[]{:S(2)}, u32[]{:S(2)}) %collective-permute-start.7) | collective-permute-done | bytes 1048608 | tf_op jit(solution)/shard_map/ppermute | solution.py:427
  198.3 2.3 fusion.3
  200.6 5.5 %collective-permute-done.22 = f32[1536,256]{1,0:T(8,128)S(1)} collective-permute-done((f32[1536,256]{1,0:T(8,128)S(1)}, f32[1536,256]{1,0:T(8,128)S(1)}, u32[]{:S(2)}, u32[]{:S(2)}) %collective-permute-start.22) | collective-permute-done | bytes 1572896 | tf_op jit(solution)/shard_map/ppermute | solution.py:445
  206.3 33.1 %collective-permute-done.30 = f32[1536,256]{1,0:T(8,128)S(1)} collective-permute-done((f32[1536,256]{1,0:T(8,128)S(1)}, f32[1536,256]{1,0:T(8,128)S(1)}, u32[]{:S(2)}, u32[]{:S(2)}) %collective-permute-start.30) | collective-permute-done | bytes 1572896 | tf_op jit(solution)/shard_map/ppermute | solution.py:445
  239.6 2.1 pad_maximum_fusion
  (133 shorter events, 43.2 us)
Async XLA Ops:
  6.0 35.6 %collective-permute-start = (f32[8,128,256]{2,1,0:T(8,128)}, f32[8,128,256]{2,1,0:T(8,128)}, u32[]{:S(2)}, u32[]{:S(2)}) collective-permute-start(f32[8,128,256]{2,1,0:T(8,128)} %get-tuple-element.37), channel_id=1, source_target_pairs={{0,8},{4,12},{8,0},{12,4},{16,24},{20,28},{24,16},{28,20},{1,9},{5... | collective-permute-start | bytes 3145736 | tf_op jit(solution)/shard_map/ppermute | solution.py:95
  9.1 35.7 %collective-permute-start.11 = (f32[8,128,256]{2,1,0:T(8,128)}, f32[8,128,256]{2,1,0:T(8,128)}, u32[]{:S(2)}, u32[]{:S(2)}) collective-permute-start(f32[8,128,256]{2,1,0:T(8,128)} %get-tuple-element.37), channel_id=1, source_target_pairs={{8,16},{12,20},{16,8},{20,12},{9,17},{13,21},{17,9},{21,13},{10,18... | collective-permute-start | bytes 3145736 | tf_op jit(solution)/shard_map/ppermute | solution.py:95
  21.2 27.0 %collective-permute-start.19 = (f32[2,256,256]{2,1,0:T(8,128)S(1)}, f32[2,256,256]{2,1,0:T(8,128)S(1)}, u32[]{:S(2)}, u32[]{:S(2)}) collective-permute-start(f32[2,256,256]{2,1,0:T(8,128)S(1)} %get-tuple-element.53), channel_id=1, source_target_pairs={{0,8},{4,12},{24,16},{28,20},{1,9},{5,13},{25,17},{29,21},{2,10},{... | collective-permute-start | bytes 1572872 | tf_op jit(solution)/shard_map/ppermute | solution.py:95
  26.5 32.5 %collective-permute-start.18 = (f32[256,256]{1,0:T(8,128)}, f32[256,256]{1,0:T(8,128)S(1)}, u32[]{:S(2)}, u32[]{:S(2)}) collective-permute-start(f32[256,256]{1,0:T(8,128)} %get-tuple-element.52), channel_id=1, source_target_pairs={{0,8},{4,12},{8,0},{12,4},{16,24},{20,28},{24,16},{28,20},{1,9},{5... | collective-permute-start | bytes 786440 | tf_op jit(solution)/shard_map/ppermute | solution.py:95
  37.6 23.4 %collective-permute-start.24 = (f32[2,256,256]{2,1,0:T(8,128)}, f32[2,256,256]{2,1,0:T(8,128)S(1)}, u32[]{:S(2)}, u32[]{:S(2)}) collective-permute-start(f32[2,256,256]{2,1,0:T(8,128)} %get-tuple-element.59), channel_id=1, source_target_pairs={{0,8},{4,12},{24,16},{28,20},{1,9},{5,13},{25,17},{29,21},{2,10},{... | collective-permute-start | bytes 1572872 | tf_op jit(solution)/shard_map/ppermute | solution.py:95
  44.7 17.8 %collective-permute-start.2 = (f32[2,256,256]{2,1,0:T(8,128)S(1)}, f32[2,256,256]{2,1,0:T(8,128)S(1)}, u32[]{:S(2)}, u32[]{:S(2)}) collective-permute-start(f32[2,256,256]{2,1,0:T(8,128)S(1)} %get-tuple-element.40), channel_id=1, source_target_pairs={{8,16},{12,20},{16,8},{20,12},{9,17},{13,21},{17,9},{21,13},{10,18... | collective-permute-start | bytes 1572872 | tf_op jit(solution)/shard_map/ppermute | solution.py:95
  59.1 19.7 %collective-permute-start.12 = (f32[6,128,256]{2,1,0:T(8,128)S(1)}, f32[6,128,256]{2,1,0:T(8,128)S(1)}, u32[]{:S(2)}, u32[]{:S(2)}) collective-permute-start(f32[6,128,256]{2,1,0:T(8,128)S(1)} %slice_select_fusion), channel_id=1, source_target_pairs={{8,0},{12,4},{16,24},{20,28},{9,1},{13,5},{17,25},{21,29},{10,2},{... | collective-permute-start | bytes 2359304 | tf_op jit(solution)/shard_map/ppermute | solution.py:95
  61.0 26.6 %collective-permute-start.26 = (f32[7,3,512]{2,1,0:T(4,128)S(1)}, f32[7,3,512]{2,1,0:T(4,128)S(1)}, u32[]{:S(2)}, u32[]{:S(2)}) collective-permute-start(f32[7,3,512]{2,1,0:T(4,128)S(1)} %constant_dynamic-update-slice_fusion), channel_id=1, source_target_pairs={{0,4},{4,0},{8,12},{12,8},{16,20},{20,16},{24,28},{28,24},{1,5},{5... | collective-permute-start | bytes 129032 | tf_op jit(solution)/shard_map/ppermute | solution.py:391
  62.6 43.8 %collective-permute-start.9 = (f32[6,128,256]{2,1,0:T(8,128)S(1)}, f32[6,128,256]{2,1,0:T(8,128)}, u32[]{:S(2)}, u32[]{:S(2)}) collective-permute-start(f32[6,128,256]{2,1,0:T(8,128)S(1)} %fusion.4.refs_0_), channel_id=1, source_target_pairs={{0,2},{1,3},{2,0},{3,1},{4,6},{5,7},{6,4},{7,5},{8,10},{9,11},{10,... | collective-permute-start | bytes 2359304 | tf_op jit(solution)/shard_map/ppermute | solution.py:385
  65.4 42.1 %collective-permute-start.8 = (f32[6,128,256]{2,1,0:T(8,128)S(1)}, f32[6,128,256]{2,1,0:T(8,128)S(1)}, u32[]{:S(2)}, u32[]{:S(2)}) collective-permute-start(f32[6,128,256]{2,1,0:T(8,128)S(1)} %fusion.4.refs_0_), channel_id=1, source_target_pairs={{0,1},{1,0},{2,3},{3,2},{4,5},{5,4},{6,7},{7,6},{8,9},{9,8},{10,11... | collective-permute-start | bytes 2359304 | tf_op jit(solution)/shard_map/ppermute | solution.py:386
  65.6 40.7 %collective-permute-start.4 = (f32[6,128,256]{2,1,0:T(8,128)S(1)}, f32[6,128,256]{2,1,0:T(8,128)S(1)}, u32[]{:S(2)}, u32[]{:S(2)}) collective-permute-start(f32[6,128,256]{2,1,0:T(8,128)S(1)} %slice_select_fusion.2), channel_id=1, source_target_pairs={{8,0},{12,4},{16,24},{20,28},{9,1},{13,5},{17,25},{21,29},{10,2},{... | collective-permute-start | bytes 2359304 | tf_op jit(solution)/shard_map/ppermute | solution.py:95
  78.8 30.1 %collective-permute-start.20 = (f32[2,256,256]{2,1,0:T(8,128)S(1)}, f32[2,256,256]{2,1,0:T(8,128)S(1)}, u32[]{:S(2)}, u32[]{:S(2)}) collective-permute-start(f32[2,256,256]{2,1,0:T(8,128)S(1)} %pad_maximum_fusion.1), channel_id=1, source_target_pairs={{8,16},{12,20},{16,8},{20,12},{9,17},{13,21},{17,9},{21,13},{10,18... | collective-permute-start | bytes 1572872 | tf_op jit(solution)/shard_map/ppermute | solution.py:95
  87.7 24.6 %collective-permute-start.25 = (f32[2,256,256]{2,1,0:T(8,128)S(1)}, f32[2,256,256]{2,1,0:T(8,128)S(1)}, u32[]{:S(2)}, u32[]{:S(2)}) collective-permute-start(f32[2,256,256]{2,1,0:T(8,128)S(1)} %pad_maximum_fusion.3), channel_id=1, source_target_pairs={{8,16},{12,20},{16,8},{20,12},{9,17},{13,21},{17,9},{21,13},{10,18... | collective-permute-start | bytes 1572872 | tf_op jit(solution)/shard_map/ppermute | solution.py:95
  106.3 64.1 %collective-permute-start.3 = (f32[2,256,1024]{2,1,0:T(8,128)}, f32[2,256,1024]{2,1,0:T(8,128)}, u32[]{:S(2)}, u32[]{:S(2)}) collective-permute-start(f32[2,256,1024]{2,1,0:T(8,128)} %token_part.3), channel_id=1, source_target_pairs={{0,1},{1,0},{2,3},{3,2},{4,5},{5,4},{6,7},{7,6},{8,9},{9,8},{10,11... | collective-permute-start | bytes 6291464 | tf_op jit(solution)/shard_map/ppermute | solution.py:426
  108.9 20.5 %collective-permute-start.14 = (f32[6,128,256]{2,1,0:T(8,128)S(1)}, f32[6,128,256]{2,1,0:T(8,128)}, u32[]{:S(2)}, u32[]{:S(2)}) collective-permute-start(f32[6,128,256]{2,1,0:T(8,128)S(1)} %fusion.6.refs_4_), channel_id=1, source_target_pairs={{0,2},{1,3},{2,0},{3,1},{4,6},{5,7},{6,4},{7,5},{8,10},{9,11},{10,... | collective-permute-start | bytes 2359304 | tf_op jit(solution)/shard_map/ppermute | solution.py:385
  110.7 34.7 %collective-permute-start.6 = (f32[6,128,256]{2,1,0:T(8,128)}, f32[6,128,256]{2,1,0:T(8,128)}, u32[]{:S(2)}, u32[]{:S(2)}) collective-permute-start(f32[6,128,256]{2,1,0:T(8,128)} %fusion.5.refs_8_), channel_id=1, source_target_pairs={{0,2},{1,3},{2,0},{3,1},{4,6},{5,7},{6,4},{7,5},{8,10},{9,11},{10,... | collective-permute-start | bytes 2359304 | tf_op jit(solution)/shard_map/ppermute | solution.py:385
  117.9 27.5 %collective-permute-start.13 = (f32[6,128,256]{2,1,0:T(8,128)S(1)}, f32[6,128,256]{2,1,0:T(8,128)}, u32[]{:S(2)}, u32[]{:S(2)}) collective-permute-start(f32[6,128,256]{2,1,0:T(8,128)S(1)} %fusion.6.refs_4_), channel_id=1, source_target_pairs={{0,1},{1,0},{2,3},{3,2},{4,5},{5,4},{6,7},{7,6},{8,9},{9,8},{10,11... | collective-permute-start | bytes 2359304 | tf_op jit(solution)/shard_map/ppermute | solution.py:386
  120.1 35.5 %collective-permute-start.16 = (f32[6,128,256]{2,1,0:T(8,128)}, f32[6,128,256]{2,1,0:T(8,128)S(1)}, u32[]{:S(2)}, u32[]{:S(2)}) collective-permute-start(f32[6,128,256]{2,1,0:T(8,128)} %fusion.5.refs_8_), channel_id=1, source_target_pairs={{0,1},{1,0},{2,3},{3,2},{4,5},{5,4},{6,7},{7,6},{8,9},{9,8},{10,11... | collective-permute-start | bytes 2359304 | tf_op jit(solution)/shard_map/ppermute | solution.py:386
  129.4 24.9 %collective-permute-start.15 = (f32[6,128,256]{2,1,0:T(8,128)}, f32[6,128,256]{2,1,0:T(8,128)S(1)}, u32[]{:S(2)}, u32[]{:S(2)}) collective-permute-start(f32[6,128,256]{2,1,0:T(8,128)} %collective-permute-done.14.refs_6_), channel_id=1, source_target_pairs={{0,1},{1,0},{2,3},{3,2},{4,5},{5,4},{6,7},{7,6},{8,9},{9,8},{10,11... | collective-permute-start | bytes 2359304 | tf_op jit(solution)/shard_map/ppermute | solution.py:387
  145.4 18.7 %collective-permute-start.21 = (f32[2,256,256]{2,1,0:T(8,128)S(1)}, f32[2,256,256]{2,1,0:T(8,128)S(1)}, u32[]{:S(2)}, u32[]{:S(2)}) collective-permute-start(f32[2,256,256]{2,1,0:T(8,128)S(1)} %pad_maximum_fusion.2), channel_id=1, source_target_pairs={{8,0},{12,4},{16,24},{20,28},{9,1},{13,5},{17,25},{21,29},{10,2},{... | collective-permute-start | bytes 1572872 | tf_op jit(solution)/shard_map/ppermute | solution.py:95
  154.3 20.0 %collective-permute-start.29 = (f32[2,256,256]{2,1,0:T(8,128)}, f32[2,256,256]{2,1,0:T(8,128)S(1)}, u32[]{:S(2)}, u32[]{:S(2)}) collective-permute-start(f32[2,256,256]{2,1,0:T(8,128)} %pad_maximum_fusion.4), channel_id=1, source_target_pairs={{8,0},{12,4},{16,24},{20,28},{9,1},{13,5},{17,25},{21,29},{10,2},{... | collective-permute-start | bytes 1572872 | tf_op jit(solution)/shard_map/ppermute | solution.py:95
  168.8 37.3 %collective-permute-start.22 = (f32[1536,256]{1,0:T(8,128)S(1)}, f32[1536,256]{1,0:T(8,128)S(1)}, u32[]{:S(2)}, u32[]{:S(2)}) collective-permute-start(f32[1536,256]{1,0:T(8,128)S(1)} %get-tuple-element.57), channel_id=1, source_target_pairs={{0,4},{4,0},{8,12},{12,8},{16,20},{20,16},{24,28},{28,24},{1,5},{5... | collective-permute-start | bytes 4718600 | tf_op jit(solution)/shard_map/ppermute | solution.py:445
  172.8 25.5 %collective-permute-start.7 = (f32[256,1024]{1,0:T(8,128)}, f32[256,1024]{1,0:T(8,128)S(1)}, u32[]{:S(2)}, u32[]{:S(2)}) collective-permute-start(f32[256,1024]{1,0:T(8,128)} %fusion), channel_id=1, source_target_pairs={{0,2},{1,3},{2,0},{3,1},{4,6},{5,7},{6,4},{7,5},{8,10},{9,11},{10,... | collective-permute-start | bytes 3145736 | tf_op jit(solution)/shard_map/ppermute | solution.py:427
  179.0 60.4 %collective-permute-start.30 = (f32[1536,256]{1,0:T(8,128)S(1)}, f32[1536,256]{1,0:T(8,128)S(1)}, u32[]{:S(2)}, u32[]{:S(2)}) collective-permute-start(f32[1536,256]{1,0:T(8,128)S(1)} %get-tuple-element.68), channel_id=1, source_target_pairs={{0,4},{4,0},{8,12},{12,8},{16,20},{20,16},{24,28},{28,24},{1,5},{5... | collective-permute-start | bytes 4718600 | tf_op jit(solution)/shard_map/ppermute | solution.py:445
  (33 other events, 273.7 us)

commit v5 on v0

--- a/solution.py
+++ b/solution.py
@@ -1,8 +1,11 @@
+import functools
 import math
 
 import jax
 import jax.numpy as jnp
 from jax import lax
+from jax.experimental import pallas as pl
+from jax.experimental.pallas import tpu as pltpu
 from jax.sharding import PartitionSpec as P
 
 SEQ = 128
@@ -38,11 +41,9 @@
     return jnp.stack(terms, axis=0)
 
 
-def local(tokens, in_weight, kernel, out_grad):
+def gated_grads(tokens, in_weight, kernel, out_grad):
     rows = tokens.shape[0]
-    features = tokens.shape[1]
     chans = in_weight.shape[2]
-    total_rows = rows * lax.axis_size("rep")
     mixed = jnp.einsum("td,sdc->tsc", tokens, in_weight, preferred_element_type=jnp.float32)
     stored = lax.optimization_barrier(mixed.astype(jnp.bfloat16))
     values = stored.astype(jnp.float32).reshape(rows // SEQ, SEQ, 3, chans)
@@ -54,9 +55,16 @@
     conv_grad = jnp.stack(
         [upstream * keyed * valued, upstream * query * valued, upstream * query * keyed], axis=2
     )
-    mixed_grad = causal_mix_back(conv_grad, kernel).reshape(rows, 3, chans).astype(jnp.bfloat16)
-    scale = 1.0 / math.sqrt(total_rows)
-    kernel_local = kernel_terms(values, conv_grad, kernel.shape[0]) * scale
+    mixed_grad = causal_mix_back(conv_grad, kernel).reshape(rows, 3, chans)
+    return mixed_grad, kernel_terms(values, conv_grad, kernel.shape[0])
+
+
+def plain(tokens, in_weight, kernel, out_grad):
+    features = tokens.shape[1]
+    chans = in_weight.shape[2]
+    scale = 1.0 / math.sqrt(tokens.shape[0] * lax.axis_size("rep"))
+    wide_grad, taps = gated_grads(tokens, in_weight, kernel, out_grad)
+    mixed_grad = wide_grad.astype(jnp.bfloat16)
     partial_grad = jnp.einsum(
         "tsc,sdc->td", mixed_grad, in_weight, preferred_element_type=jnp.float32
     )
@@ -69,14 +77,469 @@
     weight_grad = lax.psum_scatter(
         local_grad.reshape(3 * features, chans), "rep", scatter_dimension=0, tiled=True
     )
-    kernel_grad = lax.psum(kernel_local, "rep")
+    kernel_grad = lax.psum(taps * scale, "rep")
     return (token_grad, weight_grad, kernel_grad)
+
+
+LEVELS = 4
+BLOCK = 512
+BLOCKS = 8
+OWN = 6
+HALF = 3
+LANES = 128
+VMEM = pl.BlockSpec(memory_space=pltpu.VMEM)
+SMEM = pl.BlockSpec(memory_space=pltpu.SMEM)
+PARAMS = pltpu.CompilerParams(vmem_limit_bytes=48 * 2**20)
+PAIRS = ((0, 1), (1, 0), (2, 3), (3, 2))
+INWARD = ((0, 1), (3, 2))
+MIDDLE = ((1, 2), (2, 1))
+OUTWARD = ((1, 0), (2, 3))
+ENDS = (0, 3)
+INNER = (1, 2)
+
+
+def lines(array, hops):
+    perm = [(2 * a + y, 2 * b + y) for a, b in hops for y in range(2)]
+    return lax.ppermute(array, "rep", perm)
+
+
+def sides(array, levels=range(LEVELS)):
+    return lax.ppermute(array, "rep", [(2 * z + y, 2 * z + 1 - y) for z in levels for y in range(2)])
+
+
+def share(array):
+    across = lax.ppermute(array, "shard", [(q, q ^ 2) for q in range(4)])
+    beside = lax.ppermute(array, "shard", [(q, q ^ 1) for q in range(4)])
+    both = lax.ppermute(across, "shard", [(q, q ^ 1) for q in range(4)])
+    return (array, beside, across, both)
+
+
+def device_block(level, column, i):
+    return lax.rem(OWN * level + HALF * column + i, BLOCKS)
+
+
+def turn_tokens(place, tokens):
+    rows = tokens.shape[0]
+    slab = BLOCK // 4
+
+    def body(place, tokens, piece, theirs):
+        start = pl.multiple_of(place[2] * slab, slab)
+        for b in range(BLOCKS):
+            piece[b] = tokens[:, pl.ds(pl.multiple_of(BLOCK * b + start, slab), slab)].astype(
+                jnp.float32
+            ).T
+        for i in range(HALF):
+            theirs[i] = piece[device_block(place[0], 1 - place[1], i)]
+
+    return pl.pallas_call(
+        body,
+        out_shape=(
+            jax.ShapeDtypeStruct((BLOCKS, slab, rows), jnp.float32),
+            jax.ShapeDtypeStruct((HALF, slab, rows), jnp.float32),
+        ),
+        in_specs=[SMEM, VMEM],
+        out_specs=(VMEM, VMEM),
+        compiler_params=PARAMS,
+        name="turn_tokens",
+    )(place, tokens)
+
+
+def other_blocks(place, inner, ends=None):
+    def body(place, *refs):
+        inner, out = refs[0], refs[-1]
+        for i in range(HALF):
+            if ends is None:
+                out[i] = inner[device_block(place[0], 1 - place[1], i)]
+                continue
+            inside = jnp.logical_or(place[0] == 1, place[0] == 2)
+
+            @pl.when(inside)
+            def _():
+                out[i] = inner[device_block(place[0], 1 - place[1], i)]
+
+            @pl.when(jnp.logical_not(inside))
+            def _():
+                out[i] = refs[1][HALF * (1 - place[1]) + i]
+
+    arrays = (inner,) if ends is None else (inner, ends)
+    return pl.pallas_call(
+        body,
+        out_shape=jax.ShapeDtypeStruct((HALF,) + inner.shape[1:], inner.dtype),
+        in_specs=[SMEM] + [VMEM] * len(arrays),
+        out_specs=VMEM,
+        compiler_params=PARAMS,
+        name="other_blocks",
+    )(place, *arrays)
+
+
+def own_blocks(place, got, inner, ends=None):
+    def body(place, got, *refs):
+        inner, out = refs[0], refs[-1]
+        for i in range(HALF):
+            out[HALF + i] = got[i]
+            if ends is None:
+                out[i] = inner[device_block(place[0], place[1], i)]
+                continue
+            inside = jnp.logical_or(place[0] == 1, place[0] == 2)
+
+            @pl.when(inside)
+            def _():
+                out[i] = inner[device_block(place[0], place[1], i)]
+
+            @pl.when(jnp.logical_not(inside))
+            def _():
+                out[i] = refs[1][HALF * place[1] + i]
+
+    arrays = (inner,) if ends is None else (inner, ends)
+    return pl.pallas_call(
+        body,
+        out_shape=jax.ShapeDtypeStruct((OWN,) + inner.shape[1:], inner.dtype),
+        in_specs=[SMEM] + [VMEM] * (1 + len(arrays)),
+        out_specs=VMEM,
+        compiler_params=PARAMS,
+        name="own_blocks",
+    )(place, got, *arrays)
+
+
+def gate(place, tokens, in_weight, kernel, out_grad):
+    rows, features = tokens.shape
+    chans = in_weight.shape[2]
+    taps = kernel.shape[0]
+    steps = 4
+    width = min(chans, 2 * LANES)
+    deep = features // steps
+    pad = 8
+
+    def body(place, tokens, weight, kernel, out_grad, own, grad, first, inner, middle, total, held, pads, back):
+        step = pl.program_id(1)
+        for s in range(3):
+            now = jnp.dot(tokens[...], weight[s], preferred_element_type=jnp.float32)
+
+            @pl.when(step == 0)
+            def _():
+                total[s] = now
+
+            @pl.when(step > 0)
+            def _():
+                total[s] += now
+
+        @pl.when(step == steps - 1)
+        def _():
+            blank = jnp.zeros((pad, LANES), jnp.float32)
+            for lane in range(0, width, LANES):
+                lanes = slice(lane, lane + LANES)
+                sums = [[None] * taps for _ in range(3)]
+                for q in range(rows // SEQ):
+                    here = slice(q * SEQ, (q + 1) * SEQ)
+                    conv = []
+                    for s in range(3):
+                        values = total[s, here, lanes].astype(jnp.bfloat16).astype(jnp.float32)
+                        pads[s, 0:pad, :] = blank
+                        pads[s, pad : pad + SEQ, :] = values
+                        mix = kernel[0, s : s + 1, lanes] * values
+                        for j in range(1, taps):
+                            mix += kernel[j, s : s + 1, lanes] * pads[s, pad - j : pad - j + SEQ, :]
+                        conv.append(mix)
+                    up = out_grad[here, lanes].astype(jnp.float32)
+                    query, keyed, valued = conv
+                    grads = (up * keyed * valued, up * query * valued, up * query * keyed)
+                    for s in range(3):
+                        back[s, 0:SEQ, :] = grads[s]
+                        back[s, SEQ : SEQ + pad, :] = blank
+                    for s in range(3):
+                        values = pads[s, pad : pad + SEQ, :]
+                        mixed = None
+                        for j in range(taps):
+                            moved = back[s, j : j + SEQ, :]
+                            term = kernel[j, s : s + 1, lanes] * moved
+                            mixed = term if mixed is None else mixed + term
+                            folded = jnp.sum((values * moved).reshape(SEQ // 8, 8, LANES), axis=0)
+                            sums[s][j] = folded if q == 0 else sums[s][j] + folded
+                        held[s, here, lanes] = mixed
+                for s in range(3):
+                    for j in range(taps):
+                        grad[j, s : s + 1, lanes] = jnp.sum(sums[s][j], axis=0, keepdims=True)
+            for s in range(3):
+                own[s] = held[s].astype(jnp.bfloat16)
+            level = place[0]
+            first[...] = held[2 - 2 * lax.rem(level, 2)]
+            low = jnp.where(level <= 1, 0, 1)
+            for i in range(2):
+                inner[i] = held[low + i]
+                middle[i] = held[1 - low + i]
+
+    one = jax.ShapeDtypeStruct((rows, chans), jnp.float32)
+    two = jax.ShapeDtypeStruct((2, rows, chans), jnp.float32)
+    return pl.pallas_call(
+        body,
+        out_shape=(
+            jax.ShapeDtypeStruct((3, rows, chans), jnp.bfloat16),
+            jax.ShapeDtypeStruct((taps, 3, chans), jnp.float32),
+            one,
+            two,
+            two,
+        ),
+        grid=(chans // width, steps),
+        in_specs=[
+            SMEM,
+            pl.BlockSpec((rows, deep), lambda c, k: (0, k)),
+            pl.BlockSpec((3, deep, width), lambda c, k: (0, k, c)),
+            pl.BlockSpec((taps, 3, width), lambda c, k: (0, 0, c)),
+            pl.BlockSpec((rows, width), lambda c, k: (0, c)),
+        ],
+        out_specs=(
+            pl.BlockSpec((3, rows, width), lambda c, k: (0, 0, c)),
+            pl.BlockSpec((taps, 3, width), lambda c, k: (0, 0, c)),
+            pl.BlockSpec((rows, width), lambda c, k: (0, c)),
+            pl.BlockSpec((2, rows, width), lambda c, k: (0, 0, c)),
+            pl.BlockSpec((2, rows, width), lambda c, k: (0, 0, c)),
+        ),
+        scratch_shapes=[
+            pltpu.VMEM((3, rows, width), jnp.float32),
+            pltpu.VMEM((3, rows, width), jnp.float32),
+            pltpu.VMEM((3, pad + SEQ, LANES), jnp.float32),
+            pltpu.VMEM((3, SEQ + pad, LANES), jnp.float32),
+        ],
+        compiler_params=PARAMS,
+        cost_estimate=pl.CostEstimate(
+            flops=2 * rows * features * 3 * chans,
+            bytes_accessed=2 * features * 3 * chans,
+            transcendentals=0,
+        ),
+        name="gate",
+    )(place, tokens, in_weight, kernel, out_grad)
+
+
+def relay_payload(place, first, inner):
+    def body(place, first, inner, out):
+        @pl.when(place[0] <= 1)
+        def _():
+            out[0] = inner[1]
+            out[1] = first[...]
+
+        @pl.when(place[0] > 1)
+        def _():
+            out[0] = first[...]
+            out[1] = inner[0]
+
+    return pl.pallas_call(
+        body,
+        out_shape=jax.ShapeDtypeStruct(inner.shape, inner.dtype),
+        in_specs=[SMEM, VMEM, VMEM],
+        out_specs=VMEM,
+        compiler_params=PARAMS,
+        name="relay_payload",
+    )(place, first, inner)
+
+
+def arrange_tokens(place, own, slots):
+    slab = BLOCK // 4
+    rows = slots[0][0].shape[2]
+    counts = [slot[0].shape[0] // HALF for slot in slots]
+    total = (0 if own is None else 1) + sum(counts)
+
+    def body(place, *refs):
+        out = refs[-1]
+        at = 0
+        if own is not None:
+            for i in range(HALF):
+                block = device_block(place[0], place[1], i)
+                columns = pl.ds(pl.multiple_of(block * BLOCK, BLOCK), BLOCK)
+                out[i, :, 0:rows] = refs[0][:, columns].T
+            refs = refs[1:]
+            at = 1
+        for n, count in enumerate(counts):
+            for c in range(count):
+                for i in range(HALF):
+                    for k in range(4):
+                        where = pl.multiple_of(jnp.bitwise_xor(place[2], k) * slab, slab)
+                        out[i, pl.ds(where, slab), (at + c) * rows : (at + c + 1) * rows] = refs[
+                            4 * n + k
+                        ][HALF * c + i].astype(jnp.bfloat16)
+            at += count
+
+    arrays = ([] if own is None else [own]) + [piece for slot in slots for piece in slot]
+    return pl.pallas_call(
+        body,
+        out_shape=jax.ShapeDtypeStruct((HALF, BLOCK, total * rows), jnp.bfloat16),
+        in_specs=[SMEM] + [VMEM] * len(arrays),
+        out_specs=VMEM,
+        compiler_params=PARAMS,
+        name="arrange_tokens",
+    )(place, *arrays)
+
+
+def weight_part(place, tok, own, slots, scale=None, so_far=None):
+    rows, chans = slots[0][1].shape[1:]
+    count = (0 if own is None else 1) + len(slots)
+    arrays = ([] if own is None else [own]) + [a for slot in slots for a in slot if a is not None]
+    last = scale is not None
+
+    def body(place, tok, *refs):
+        out, held = refs[-2], refs[-1]
+        level, column = place[0], place[1]
+        i = pl.program_id(0)
+        inside = jnp.logical_or(level == 1, level == 2)
+        at = 0
+
+        @pl.when(i == 0)
+        def _():
+            at = 0
+            refs_left = list(refs)
+            if own is not None:
+                ref = refs_left.pop(0)
+                major = jnp.where(inside, level - 1 + column, jnp.where(level == 0, 0, 2))
+                held[0, 0:rows, :] = ref[major]
+                held[1, 0:rows, :] = ref[1]
+                at = 1
+            for ends, _inner in slots:
+                here = slice(at * rows, (at + 1) * rows)
+                if ends is None:
+                    ref = refs_left.pop(0)
+                    major = jnp.where(inside, column, jnp.where(level == 0, 0, 1))
+                    held[0, here, :] = ref[major].astype(jnp.bfloat16)
+                    held[1, here, :] = ref[jnp.where(level == 2, 0, 1)].astype(jnp.bfloat16)
+                else:
+                    end, ref = refs_left.pop(0), refs_left.pop(0)
+
+                    @pl.when(inside)
+                    def _():
+                        held[0, here, :] = ref[column].astype(jnp.bfloat16)
+                        held[1, here, :] = ref[jnp.where(level == 2, 0, 1)].astype(jnp.bfloat16)
+
+                    @pl.when(jnp.logical_not(inside))
+                    def _():
+                        held[0, here, :] = end[...].astype(jnp.bfloat16)
+
+                at += 1
+
+        second = jnp.logical_or(
+            jnp.logical_and(jnp.logical_and(level == 1, column == 0), i == 2),
+            jnp.logical_and(jnp.logical_and(level == 2, column == 1), i == 0),
+        )
+        got = jnp.dot(
+            tok[...], held[second.astype(jnp.int32)], preferred_element_type=jnp.float32
+        )
+        if so_far is not None:
+            got = got + refs[-3][...]
+        out[...] = got * scale if last else got
+
+    whole = lambda a: pl.BlockSpec(a.shape, lambda i: (0,) * a.ndim)
+    more = [] if so_far is None else [so_far]
+    part = pl.BlockSpec((BLOCK, chans), lambda i: (i, 0))
+    return pl.pallas_call(
+        body,
+        out_shape=jax.ShapeDtypeStruct((HALF * BLOCK, chans), jnp.float32),
+        grid=(HALF,),
+        in_specs=[SMEM, pl.BlockSpec((None, BLOCK, count * rows), lambda i: (i, 0, 0))]
+        + [whole(a) for a in arrays]
+        + [part] * len(more),
+        out_specs=part,
+        scratch_shapes=[pltpu.VMEM((2, count * rows, chans), jnp.bfloat16)],
+        compiler_params=PARAMS,
+        cost_estimate=pl.CostEstimate(
+            flops=2 * HALF * BLOCK * count * rows * chans,
+            bytes_accessed=2 * HALF * BLOCK * count * rows + 8 * count * rows * chans,
+            transcendentals=0,
+        ),
+        name="weight_part",
+    )(place, tok, *arrays, *more)
+
+
+def token_part(grads, weight):
+    rows, chans = grads.shape[1:]
+    wide = weight.shape[1] // 4
+
+    def body(grads, weight, out):
+        now = lax.dot_general(
+            grads[...], weight[...], (((1,), (1,)), ((), ())), preferred_element_type=jnp.float32
+        )
+
+        @pl.when(pl.program_id(1) == 0)
+        def _():
+            out[...] = now
+
+        @pl.when(pl.program_id(1) > 0)
+        def _():
+            out[...] += now
+
+    return pl.pallas_call(
+        body,
+        out_shape=jax.ShapeDtypeStruct((rows, 4 * wide), jnp.float32),
+        grid=(4, 3),
+        in_specs=[
+            pl.BlockSpec((None, rows, chans), lambda i, s: (s, 0, 0)),
+            pl.BlockSpec((None, wide, chans), lambda i, s: (s, i, 0)),
+        ],
+        out_specs=pl.BlockSpec((rows, wide), lambda i, s: (0, i)),
+        compiler_params=PARAMS,
+        cost_estimate=pl.CostEstimate(
+            flops=8 * rows * wide * 3 * chans,
+            bytes_accessed=8 * wide * 3 * chans + 16 * rows * wide,
+            transcendentals=0,
+        ),
+        name="token_part",
+    )(grads, weight)
+
+
+def lined(tokens, in_weight, kernel, out_grad):
+    rows, features = tokens.shape
+    rep = lax.axis_index("rep")
+    level, column = rep // 2, rep % 2
+    place = jnp.stack([level, column, lax.axis_index("shard")]).astype(jnp.int32)
+    scale = 1.0 / math.sqrt(rows * lax.axis_size("rep"))
+    later = jnp.where(level <= 1, 0, 1)
+
+    piece, theirs = turn_tokens(place, tokens)
+    near = lines(piece, PAIRS)
+    mid = lines(piece, MIDDLE)
+    slots = [share(sides(theirs))]
+
+    own, taps, first_out, inner_out, middle_out = gate(place, tokens, in_weight, kernel, out_grad)
+    partial = token_part(own, in_weight)
+    token_grad = lax.psum_scatter(partial, "shard", scatter_dimension=1, tiled=True)
+
+    def ended(array):
+        return lax.dynamic_slice_in_dim(array, 2 * later, OWN, 0)
+
+    far = lines(near, MIDDLE)
+    got = sides(other_blocks(place, near))
+    slots.append(share(own_blocks(place, got, near)))
+    for array in (mid, far):
+        outer = lines(ended(array), OUTWARD)
+        got = sides(other_blocks(place, array, outer))
+        slots.append(share(own_blocks(place, got, array, outer)))
+
+    own_y = sides(inner_out)
+    middle = lines(middle_out, MIDDLE)
+    inner = lines(inner_out, INWARD)
+    first = lines(first_out, PAIRS)
+    relayed = lines(relay_payload(place, first, inner), MIDDLE)
+    pick = lambda array: lax.dynamic_index_in_dim(array, later, 0, keepdims=False)
+    middle_end = lines(pick(middle), OUTWARD)
+    relayed_end = lines(pick(relayed), OUTWARD)
+
+    def both(ends, inner):
+        return [(ends, inner), (sides(ends, ENDS), sides(inner, INNER))]
+
+    early = [(None, own_y)] + both(first, inner) + both(middle_end, middle)
+    late = both(relayed_end, relayed)
+
+    for bit in (1, 2, 4):
+        taps = taps + lax.ppermute(taps, "rep", [(r, r ^ bit) for r in range(2 * LEVELS)])
+
+    so_far = weight_part(place, arrange_tokens(place, tokens, slots[:3]), own, early)
+    weight_grad = weight_part(
+        place, arrange_tokens(place, None, slots[3:]), None, late, scale, so_far
+    )
+    return (token_grad.astype(jnp.bfloat16), weight_grad, taps * scale)
 
 
 def solution(mesh):
     placed = (P("rep", None), P(None, None, "shard"), P(None, None, "shard"), P("rep", "shard"))
+    line = mesh.shape["rep"] == 2 * LEVELS and mesh.shape["shard"] == 4
     return jax.shard_map(
-        local,
+        lined if line else plain,
         mesh=mesh,
         in_specs=placed,
         out_specs=(P("rep", "shard"), P("rep", "shard"), P(None, None, "shard")),

time: 499 us -> 279 us (0.56)
  the two profiles are of different devices: /device:TPU:0 before, /device:TPU:18 now
where the time goes in v5:
time: 279 us; the launch traced here: 278 us
  waiting for transfers between devices  149 us (53%)
  Pallas kernels  52.5 us (19%)
  starting transfers between devices  44.5 us (16%)
  local copies, waits for them, and re-layouts  15.3 us (5%)
  between operations  14.6 us (5%)
    ppermute x11, waiting for transfers between devices, sides(): lax.ppermute(array, 'rep', [(2 * z + y, 2 * z + 1 - y) for z in levels fo...  57.1 us
    ppermute x3, waiting for transfers between devices, lined(): lax.ppermute(taps, 'rep', [(r, r ^ bit) for r in range(2 * LEVELS)])  34.7 us
    ppermute x4, waiting for transfers between devices, share(): across = lax.ppermute(array, 'shard', [(q, q ^ 2) for q in range(4)])  29.7 us
    ppermute x11, waiting for transfers between devices, lines(): return lax.ppermute(array, 'rep', perm)  26.4 us
    ppermute x11, starting transfers between devices, lines(): return lax.ppermute(array, 'rep', perm)  20.5 us
    ppermute x11, starting transfers between devices, sides(): lax.ppermute(array, 'rep', [(2 * z + y, 2 * z + 1 - y) for z in levels fo...  18.8 us
    pallas_call x1, Pallas kernels, gate(): pl.pallas_call(body, out_shape=(jax.ShapeDtypeStruct((3, rows, chans), jn...  15.3 us
    unnamed x58, local copies, waits for them, and re-layouts  14.1 us
  transfers between devices with their start and end apart: 38, of which 15 were waited for; matrix products, arithmetic and copies ran while one was open for 1% of the time, Pallas kernels for 9%

profile of v5, /device:TPU:18, one launch (start us, length us, event | category | flops | bytes accessed | tf_op | source)
XLA Modules:
  0.0 278.1 jit_solution(213646309545667845)
XLA Ops:
  10.7 15.3 %gate.1 = (bf16[3,256,512]{2,1,0:T(8,128)(2,1)S(1)}, f32[7,3,512]{2,1,0:T(4,128)S(1)}, f32[256,512]{1,0:T(8,128)S(1)}, f32[2,256,512]{2,1,0:T(8,128)S(1)}, f32[2,256,512]{2,1,0:T(8,128)S(1)}) custom-call(s32[3]{0:T(128)S(1)} %pad_add_fusion.place, bf16[256,4096]{1,0:T(8,128)(2,1)S(1)} %copy-done, bf16[3,4096,512]{2,1,0:T(8,128)(2,1)} %weight.3, ...), custom_call_target="tpu_custom_call" | custom-call | flops 3221225472 | bytes 12582912 | tf_op jit(solution)/shard_map/gate/pallas_call | solution.py:273
  28.0 11.8 %token_part.1 = f32[256,4096]{1,0:T(8,128)S(1)} custom-call(bf16[3,256,512]{2,1,0:T(8,128)(2,1)S(1)} %get-tuple-element.10.grads.refs_0_, bf16[3,4096,512]{2,1,0:T(8,128)(2,1)} %weight.3), custom_call_target="tpu_custom_call" | custom-call | flops 3221225472 | bytes 16777216 | tf_op jit(solution)/shard_map/token_part/pallas_call | solution.py:466
  50.8 9.8 %collective-permute-done.34 = f32[7,3,512]{2,1,0:T(4,128)S(1)} collective-permute-done((f32[7,3,512]{2,1,0:T(4,128)S(1)}, f32[7,3,512]{2,1,0:T(4,128)S(1)}, u32[]{:S(2)}, u32[]{:S(2)}) %collective-permute-start.34) | collective-permute-done | bytes 43040 | tf_op jit(solution)/shard_map/ppermute | solution.py:529
  62.4 20.2 %collective-permute-done.35 = f32[7,3,512]{2,1,0:T(4,128)S(1)} collective-permute-done((f32[7,3,512]{2,1,0:T(4,128)S(1)}, f32[7,3,512]{2,1,0:T(4,128)S(1)}, u32[]{:S(2)}, u32[]{:S(2)}) %collective-permute-start.35) | collective-permute-done | bytes 43040 | tf_op jit(solution)/shard_map/ppermute | solution.py:529
  83.0 4.8 %collective-permute-done.36 = f32[7,3,512]{2,1,0:T(4,128)S(1)} collective-permute-done((f32[7,3,512]{2,1,0:T(4,128)S(1)}, f32[7,3,512]{2,1,0:T(4,128)S(1)}, u32[]{:S(2)}, u32[]{:S(2)}) %collective-permute-start.36) | collective-permute-done | bytes 43040 | tf_op jit(solution)/shard_map/ppermute | solution.py:529
  92.0 3.5 %collective-permute-start.1 = (f32[8,128,256]{2,1,0:T(8,128)}, f32[8,128,256]{2,1,0:T(8,128)S(1)}, u32[]{:S(2)}, u32[]{:S(2)}) collective-permute-start(f32[8,128,256]{2,1,0:T(8,128)} %collective-permute-done.refs_0_), channel_id=1, source_target_pairs={{8,16},{12,20},{16,8},{20,12},{9,17},{13,21},{17,9},{21,13},{10,18... | collective-permute-start | bytes 3145736 | tf_op jit(solution)/shard_map/ppermute | solution.py:103
  95.5 3.3 %collective-permute-done.15.refs_3_ = f32[3,128,256]{2,1,0:T(8,128)S(1)} collective-permute-done((f32[3,128,256]{2,1,0:T(8,128)S(1)}, f32[3,128,256]{2,1,0:T(8,128)S(1)}, u32[]{:S(2)}, u32[]{:S(2)}) %collective-permute-start.15) | collective-permute-done | bytes 393248 | tf_op jit(solution)/shard_map/ppermute | solution.py:111
  102.3 3.5 %collective-permute-start.22 = (f32[6,128,256]{2,1,0:T(8,128)S(1)}, f32[6,128,256]{2,1,0:T(8,128)S(1)}, u32[]{:S(2)}, u32[]{:S(2)}) collective-permute-start(f32[6,128,256]{2,1,0:T(8,128)S(1)} %constant_dynamic-slice_fusion), channel_id=1, source_target_pairs={{8,0},{12,4},{16,24},{20,28},{9,1},{13,5},{17,25},{21,29},{10,2},{... | collective-permute-start | bytes 2359304 | tf_op jit(solution)/shard_map/ppermute | solution.py:103
  105.8 10.3 %collective-permute-done.30.refs_7_ = f32[2,256,512]{2,1,0:T(8,128)} collective-permute-done((f32[2,256,512]{2,1,0:T(8,128)}, f32[2,256,512]{2,1,0:T(8,128)}, u32[]{:S(2)}, u32[]{:S(2)}) %collective-permute-start.30) | collective-permute-done | bytes 1048608 | tf_op jit(solution)/shard_map/ppermute | solution.py:103
  119.2 16.1 %collective-permute-done.1.refs_0_ = f32[8,128,256]{2,1,0:T(8,128)S(1)} collective-permute-done((f32[8,128,256]{2,1,0:T(8,128)}, f32[8,128,256]{2,1,0:T(8,128)S(1)}, u32[]{:S(2)}, u32[]{:S(2)}) %collective-permute-start.1) | collective-permute-done | bytes 1048608 | tf_op jit(solution)/shard_map/ppermute | solution.py:103
  137.5 3.4 %collective-permute-start.29 = (f32[2,256,512]{2,1,0:T(8,128)S(1)}, f32[2,256,512]{2,1,0:T(8,128)S(1)}, u32[]{:S(2)}, u32[]{:S(2)}) collective-permute-start(f32[2,256,512]{2,1,0:T(8,128)S(1)} %collective-permute-done.8.inner.refs_3_), channel_id=1, source_target_pairs={{8,12},{12,8},{16,20},{20,16},{9,13},{13,9},{17,21},{21,17},{10,14... | collective-permute-start | bytes 3145736 | tf_op jit(solution)/shard_map/ppermute | solution.py:107
  143.5 2.3 collective-permute-start.9
  147.2 26.3 %collective-permute-done.17.got = f32[3,128,256]{2,1,0:T(8,128)S(1)} collective-permute-done((f32[3,128,256]{2,1,0:T(8,128)S(1)}, f32[3,128,256]{2,1,0:T(8,128)S(1)}, u32[]{:S(2)}, u32[]{:S(2)}) %collective-permute-start.17) | collective-permute-done | bytes 393248 | tf_op jit(solution)/shard_map/ppermute | solution.py:107
  177.5 6.7 %collective-permute-done.23.got = f32[3,128,256]{2,1,0:T(8,128)S(1)} collective-permute-done((f32[3,128,256]{2,1,0:T(8,128)S(1)}, f32[3,128,256]{2,1,0:T(8,128)S(1)}, u32[]{:S(2)}, u32[]{:S(2)}) %collective-permute-start.23) | collective-permute-done | bytes 393248 | tf_op jit(solution)/shard_map/ppermute | solution.py:107
  187.0 7.1 %collective-permute-done.3.got = f32[3,128,256]{2,1,0:T(8,128)S(1)} collective-permute-done((f32[3,128,256]{2,1,0:T(8,128)S(1)}, f32[3,128,256]{2,1,0:T(8,128)S(1)}, u32[]{:S(2)}, u32[]{:S(2)}) %collective-permute-start.3) | collective-permute-done | bytes 393248 | tf_op jit(solution)/shard_map/ppermute | solution.py:107
  197.3 16.3 %collective-permute-done.25.refs_11_ = f32[6,128,256]{2,1,0:T(8,128)S(1)} collective-permute-done((f32[6,128,256]{2,1,0:T(8,128)S(1)}, f32[6,128,256]{2,1,0:T(8,128)S(1)}, u32[]{:S(2)}, u32[]{:S(2)}) %collective-permute-start.25) | collective-permute-done | bytes 786464 | tf_op jit(solution)/shard_map/ppermute | solution.py:111
  213.7 2.4 collective-permute-start.33
  216.1 3.4 %collective-permute-start.12 = (f32[2,256,512]{2,1,0:T(8,128)S(1)}, f32[2,256,512]{2,1,0:T(8,128)S(1)}, u32[]{:S(2)}, u32[]{:S(2)}) collective-permute-start(f32[2,256,512]{2,1,0:T(8,128)S(1)} %collective-permute-done.9.refs_1_), channel_id=1, source_target_pairs={{8,12},{12,8},{16,20},{20,16},{9,13},{13,9},{17,21},{21,17},{10,14... | collective-permute-start | bytes 3145736 | tf_op jit(solution)/shard_map/ppermute | solution.py:107
  219.6 9.3 %collective-permute-done.5.refs_2_ = f32[6,128,256]{2,1,0:T(8,128)S(1)} collective-permute-done((f32[6,128,256]{2,1,0:T(8,128)S(1)}, f32[6,128,256]{2,1,0:T(8,128)S(1)}, u32[]{:S(2)}, u32[]{:S(2)}) %collective-permute-start.5) | collective-permute-done | bytes 786464 | tf_op jit(solution)/shard_map/ppermute | solution.py:111
  233.1 5.4 %arrange_tokens.3.tok = bf16[3,512,1536]{2,1,0:T(8,128)(2,1)} custom-call(s32[3]{0:T(128)S(1)} %pad_add_fusion.place, bf16[256,4096]{1,0:T(8,128)(2,1)} %refs_0_.1, f32[3,128,256]{2,1,0:T(8,128)S(1)} %copy-done.14, f32[3,128,256]{2,1,0:T(8,128)} %collective-permute-done.14.refs_2_, f32[3,128,256]{2,1,0:T(8,128)S(1)} %copy-done.16, ...), custom_call_target="tpu_custom_call" | custom-call | tf_op jit(solution)/shard_map/arrange_tokens/pallas_call | solution.py:362
  238.5 3.3 %collective-permute-done.33.refs_9_ = f32[2,256,512]{2,1,0:T(8,128)} collective-permute-done((f32[2,256,512]{2,1,0:T(8,128)}, f32[2,256,512]{2,1,0:T(8,128)}, u32[]{:S(2)}, u32[]{:S(2)}) %collective-permute-start.33) | collective-permute-done | bytes 1048608 | tf_op jit(solution)/shard_map/ppermute | solution.py:107
  241.8 7.5 %weight_part.2.refs_4_ = f32[1536,512]{1,0:T(8,128)} custom-call(s32[3]{0:T(128)S(1)} %pad_add_fusion.place, bf16[3,512,1536]{2,1,0:T(8,128)(2,1)} %arrange_tokens.3.tok, bf16[3,256,512]{2,1,0:T(8,128)(2,1)S(1)} %copy-done.4, f32[2,256,512]{2,1,0:T(8,128)} %collective-permute-done.27.refs_1_, f32[256,512]{1,0:T(8,128)S(1)} %copy-done.6, ...), custom_call_target="tpu_custom_call" | custom-call | flops 2415919104 | bytes 11010048 | tf_op jit(solution)/shard_map/weight_part/pallas_call | solution.py:430
  250.0 13.8 %collective-permute-done.12.refs_3_ = f32[2,256,512]{2,1,0:T(8,128)S(1)} collective-permute-done((f32[2,256,512]{2,1,0:T(8,128)S(1)}, f32[2,256,512]{2,1,0:T(8,128)S(1)}, u32[]{:S(2)}, u32[]{:S(2)}) %collective-permute-start.12) | collective-permute-done | bytes 1048608 | tf_op jit(solution)/shard_map/ppermute | solution.py:107
  263.8 5.4 %weight_part.3 = f32[1536,512]{1,0:T(8,128)} custom-call(s32[3]{0:T(128)S(1)} %pad_add_fusion.place, bf16[3,512,512]{2,1,0:T(8,128)(2,1)S(1)} %arrange_tokens.2.tok, f32[256,512]{1,0:T(8,128)S(1)} %collective-permute-done.10.refs_0_, f32[2,256,512]{2,1,0:T(8,128)S(1)} %collective-permute-done.9.refs_1_, f32[256,512]{1,0:T(8,128)} %collective-permute-done.11.refs_2_, ...), custom_call_target="tpu_custom_call" | custom-call | flops 805306368 | bytes 3670016 | tf_op jit(solution)/shard_map/weight_part/pallas_call | solution.py:430
  (134 shorter events, 52.4 us)
Async XLA Ops:
  7.2 262.0 %reduce-scatter.2.cloned.1.call-start = ((), (), s32[]{:S(2)}) async-start(), calls=%async_computation.1 | async-start | bytes 5242880 | tf_op jit(solution)/shard_map/reduce_scatter | solution.py:500
  45.1 46.9 %collective-permute-start = (f32[8,128,256]{2,1,0:T(8,128)S(1)}, f32[8,128,256]{2,1,0:T(8,128)}, u32[]{:S(2)}, u32[]{:S(2)}) collective-permute-start(f32[8,128,256]{2,1,0:T(8,128)S(1)} %get-tuple-element.11), channel_id=1, source_target_pairs={{0,8},{4,12},{8,0},{12,4},{16,24},{20,28},{24,16},{28,20},{1,9},{5... | collective-permute-start | bytes 3145736 | tf_op jit(solution)/shard_map/ppermute | solution.py:103
  46.8 53.6 %collective-permute-start.21 = (f32[8,128,256]{2,1,0:T(8,128)S(1)}, f32[8,128,256]{2,1,0:T(8,128)S(1)}, u32[]{:S(2)}, u32[]{:S(2)}) collective-permute-start(f32[8,128,256]{2,1,0:T(8,128)S(1)} %get-tuple-element.11), channel_id=1, source_target_pairs={{8,16},{12,20},{16,8},{20,12},{9,17},{13,21},{17,9},{21,13},{10,18... | collective-permute-start | bytes 3145736 | tf_op jit(solution)/shard_map/ppermute | solution.py:103
  48.7 42.0 %collective-permute-start.7 = (f32[256,512]{1,0:T(8,128)S(1)}, f32[256,512]{1,0:T(8,128)S(1)}, u32[]{:S(2)}, u32[]{:S(2)}) collective-permute-start(f32[256,512]{1,0:T(8,128)S(1)} %get-tuple-element.12), channel_id=1, source_target_pairs={{0,8},{4,12},{8,0},{12,4},{16,24},{20,28},{24,16},{28,20},{1,9},{5... | collective-permute-start | bytes 1572872 | tf_op jit(solution)/shard_map/ppermute | solution.py:103
  48.7 41.3 %collective-permute-start.13 = (f32[3,128,256]{2,1,0:T(8,128)S(1)}, f32[3,128,256]{2,1,0:T(8,128)S(1)}, u32[]{:S(2)}, u32[]{:S(2)}) collective-permute-start(f32[3,128,256]{2,1,0:T(8,128)S(1)} %get-tuple-element.14), channel_id=1, source_target_pairs={{0,4},{4,0},{8,12},{12,8},{16,20},{20,16},{24,28},{28,24},{1,5},{5... | collective-permute-start | bytes 1179656 | tf_op jit(solution)/shard_map/ppermute | solution.py:107
  87.8 28.3 %collective-permute-start.30 = (f32[2,256,512]{2,1,0:T(8,128)}, f32[2,256,512]{2,1,0:T(8,128)}, u32[]{:S(2)}, u32[]{:S(2)}) collective-permute-start(f32[2,256,512]{2,1,0:T(8,128)} %copy-done.21), channel_id=1, source_target_pairs={{8,16},{12,20},{16,8},{20,12},{9,17},{13,21},{17,9},{21,13},{10,18... | collective-permute-start | bytes 3145736 | tf_op jit(solution)/shard_map/ppermute | solution.py:103
  90.7 27.2 %collective-permute-start.8 = (f32[2,256,512]{2,1,0:T(8,128)}, f32[2,256,512]{2,1,0:T(8,128)S(1)}, u32[]{:S(2)}, u32[]{:S(2)}) collective-permute-start(f32[2,256,512]{2,1,0:T(8,128)} %copy-done.20), channel_id=1, source_target_pairs={{0,8},{4,12},{24,16},{28,20},{1,9},{5,13},{25,17},{29,21},{2,10},{... | collective-permute-start | bytes 3145736 | tf_op jit(solution)/shard_map/ppermute | solution.py:103
  92.0 43.3 %collective-permute-start.1 = (f32[8,128,256]{2,1,0:T(8,128)}, f32[8,128,256]{2,1,0:T(8,128)S(1)}, u32[]{:S(2)}, u32[]{:S(2)}) collective-permute-start(f32[8,128,256]{2,1,0:T(8,128)} %collective-permute-done.refs_0_), channel_id=1, source_target_pairs={{8,16},{12,20},{16,8},{20,12},{9,17},{13,21},{17,9},{21,13},{10,18... | collective-permute-start | bytes 3145736 | tf_op jit(solution)/shard_map/ppermute | solution.py:103
  98.8 38.7 %collective-permute-start.27 = (f32[2,256,512]{2,1,0:T(8,128)}, f32[2,256,512]{2,1,0:T(8,128)}, u32[]{:S(2)}, u32[]{:S(2)}) collective-permute-start(f32[2,256,512]{2,1,0:T(8,128)} %copy-done.20), channel_id=1, source_target_pairs={{0,4},{4,0},{8,12},{12,8},{16,20},{20,16},{24,28},{28,24},{1,5},{5... | collective-permute-start | bytes 3145736 | tf_op jit(solution)/shard_map/ppermute | solution.py:107
  102.3 43.5 %collective-permute-start.22 = (f32[6,128,256]{2,1,0:T(8,128)S(1)}, f32[6,128,256]{2,1,0:T(8,128)S(1)}, u32[]{:S(2)}, u32[]{:S(2)}) collective-permute-start(f32[6,128,256]{2,1,0:T(8,128)S(1)} %constant_dynamic-slice_fusion), channel_id=1, source_target_pairs={{8,0},{12,4},{16,24},{20,28},{9,1},{13,5},{17,25},{21,29},{10,2},{... | collective-permute-start | bytes 2359304 | tf_op jit(solution)/shard_map/ppermute | solution.py:103
  117.8 25.6 %collective-permute-start.31 = (f32[256,512]{1,0:T(8,128)S(1)}, f32[256,512]{1,0:T(8,128)S(1)}, u32[]{:S(2)}, u32[]{:S(2)}) collective-permute-start(f32[256,512]{1,0:T(8,128)S(1)} %dynamic-slice_bitcast_fusion), channel_id=1, source_target_pairs={{8,0},{12,4},{16,24},{20,28},{9,1},{13,5},{17,25},{21,29},{10,2},{... | collective-permute-start | bytes 1572872 | tf_op jit(solution)/shard_map/ppermute | solution.py:103
  136.2 40.7 %collective-permute-start.2 = (f32[6,128,256]{2,1,0:T(8,128)S(1)}, f32[6,128,256]{2,1,0:T(8,128)S(1)}, u32[]{:S(2)}, u32[]{:S(2)}) collective-permute-start(f32[6,128,256]{2,1,0:T(8,128)S(1)} %constant_dynamic-slice_fusion.1), channel_id=1, source_target_pairs={{8,0},{12,4},{16,24},{20,28},{9,1},{13,5},{17,25},{21,29},{10,2},{... | collective-permute-start | bytes 2359304 | tf_op jit(solution)/shard_map/ppermute | solution.py:103
  137.5 48.8 %collective-permute-start.29 = (f32[2,256,512]{2,1,0:T(8,128)S(1)}, f32[2,256,512]{2,1,0:T(8,128)S(1)}, u32[]{:S(2)}, u32[]{:S(2)}) collective-permute-start(f32[2,256,512]{2,1,0:T(8,128)S(1)} %collective-permute-done.8.inner.refs_3_), channel_id=1, source_target_pairs={{8,12},{12,8},{16,20},{20,16},{9,13},{13,9},{17,21},{21,17},{10,14... | collective-permute-start | bytes 3145736 | tf_op jit(solution)/shard_map/ppermute | solution.py:107
  142.3 31.2 %collective-permute-start.17 = (f32[3,128,256]{2,1,0:T(8,128)S(1)}, f32[3,128,256]{2,1,0:T(8,128)S(1)}, u32[]{:S(2)}, u32[]{:S(2)}) collective-permute-start(f32[3,128,256]{2,1,0:T(8,128)S(1)} %other_blocks.4), channel_id=1, source_target_pairs={{0,4},{4,0},{8,12},{12,8},{16,20},{20,16},{24,28},{28,24},{1,5},{5... | collective-permute-start | bytes 1179656 | tf_op jit(solution)/shard_map/ppermute | solution.py:107
  143.5 43.4 %collective-permute-start.9 = (f32[2,256,512]{2,1,0:T(8,128)S(1)}, f32[2,256,512]{2,1,0:T(8,128)S(1)}, u32[]{:S(2)}, u32[]{:S(2)}) collective-permute-start(f32[2,256,512]{2,1,0:T(8,128)S(1)} %relay_payload.1), channel_id=1, source_target_pairs={{8,16},{12,20},{16,8},{20,12},{9,17},{13,21},{17,9},{21,13},{10,18... | collective-permute-start | bytes 3145736 | tf_op jit(solution)/shard_map/ppermute | solution.py:103
  145.8 30.4 %collective-permute-start.32 = (f32[256,512]{1,0:T(8,128)S(1)}, f32[256,512]{1,0:T(8,128)S(1)}, u32[]{:S(2)}, u32[]{:S(2)}) collective-permute-start(f32[256,512]{1,0:T(8,128)S(1)} %collective-permute-done.31.refs_6_), channel_id=1, source_target_pairs={{0,4},{4,0},{24,28},{28,24},{1,5},{5,1},{25,29},{29,25},{2,6},{6,2... | collective-permute-start | bytes 1572872 | tf_op jit(solution)/shard_map/ppermute | solution.py:107
  186.3 27.3 %collective-permute-start.25 = (f32[6,128,256]{2,1,0:T(8,128)S(1)}, f32[6,128,256]{2,1,0:T(8,128)S(1)}, u32[]{:S(2)}, u32[]{:S(2)}) collective-permute-start(f32[6,128,256]{2,1,0:T(8,128)S(1)} %own_blocks.5.refs_9_), channel_id=1, source_target_pairs={{0,2},{1,3},{2,0},{3,1},{4,6},{5,7},{6,4},{7,5},{8,10},{9,11},{10,... | collective-permute-start | bytes 2359304 | tf_op jit(solution)/shard_map/ppermute | solution.py:111
  186.9 29.2 %collective-permute-start.24 = (f32[6,128,256]{2,1,0:T(8,128)S(1)}, f32[6,128,256]{2,1,0:T(8,128)}, u32[]{:S(2)}, u32[]{:S(2)}) collective-permute-start(f32[6,128,256]{2,1,0:T(8,128)S(1)} %own_blocks.5.refs_9_), channel_id=1, source_target_pairs={{0,1},{1,0},{2,3},{3,2},{4,5},{5,4},{6,7},{7,6},{8,9},{9,8},{10,11... | collective-permute-start | bytes 2359304 | tf_op jit(solution)/shard_map/ppermute | solution.py:112
  196.8 22.7 %collective-permute-start.20 = (f32[6,128,256]{2,1,0:T(8,128)S(1)}, f32[6,128,256]{2,1,0:T(8,128)S(1)}, u32[]{:S(2)}, u32[]{:S(2)}) collective-permute-start(f32[6,128,256]{2,1,0:T(8,128)S(1)} %collective-permute-done.19.refs_7_), channel_id=1, source_target_pairs={{0,1},{1,0},{2,3},{3,2},{4,5},{5,4},{6,7},{7,6},{8,9},{9,8},{10,11... | collective-permute-start | bytes 2359304 | tf_op jit(solution)/shard_map/ppermute | solution.py:113
  196.8 32.1 %collective-permute-start.5 = (f32[6,128,256]{2,1,0:T(8,128)S(1)}, f32[6,128,256]{2,1,0:T(8,128)S(1)}, u32[]{:S(2)}, u32[]{:S(2)}) collective-permute-start(f32[6,128,256]{2,1,0:T(8,128)S(1)} %own_blocks.3.refs_0_), channel_id=1, source_target_pairs={{0,2},{1,3},{2,0},{3,1},{4,6},{5,7},{6,4},{7,5},{8,10},{9,11},{10,... | collective-permute-start | bytes 2359304 | tf_op jit(solution)/shard_map/ppermute | solution.py:111
  213.7 28.2 %collective-permute-start.33 = (f32[2,256,512]{2,1,0:T(8,128)}, f32[2,256,512]{2,1,0:T(8,128)}, u32[]{:S(2)}, u32[]{:S(2)}) collective-permute-start(f32[2,256,512]{2,1,0:T(8,128)} %collective-permute-done.30.refs_7_), channel_id=1, source_target_pairs={{8,12},{12,8},{16,20},{20,16},{9,13},{13,9},{17,21},{21,17},{10,14... | collective-permute-start | bytes 3145736 | tf_op jit(solution)/shard_map/ppermute | solution.py:107
  216.1 47.7 %collective-permute-start.12 = (f32[2,256,512]{2,1,0:T(8,128)S(1)}, f32[2,256,512]{2,1,0:T(8,128)S(1)}, u32[]{:S(2)}, u32[]{:S(2)}) collective-permute-start(f32[2,256,512]{2,1,0:T(8,128)S(1)} %collective-permute-done.9.refs_1_), channel_id=1, source_target_pairs={{8,12},{12,8},{16,20},{20,16},{9,13},{13,9},{17,21},{21,17},{10,14... | collective-permute-start | bytes 3145736 | tf_op jit(solution)/shard_map/ppermute | solution.py:107
  219.5 29.8 %collective-permute-start.4 = (f32[6,128,256]{2,1,0:T(8,128)S(1)}, f32[6,128,256]{2,1,0:T(8,128)S(1)}, u32[]{:S(2)}, u32[]{:S(2)}) collective-permute-start(f32[6,128,256]{2,1,0:T(8,128)S(1)} %own_blocks.3.refs_0_), channel_id=1, source_target_pairs={{0,1},{1,0},{2,3},{3,2},{4,5},{5,4},{6,7},{7,6},{8,9},{9,8},{10,11... | collective-permute-start | bytes 2359304 | tf_op jit(solution)/shard_map/ppermute | solution.py:112
  228.9 34.9 %collective-permute-start.11 = (f32[256,512]{1,0:T(8,128)S(1)}, f32[256,512]{1,0:T(8,128)}, u32[]{:S(2)}, u32[]{:S(2)}) collective-permute-start(f32[256,512]{1,0:T(8,128)S(1)} %collective-permute-done.10.refs_0_), channel_id=1, source_target_pairs={{0,4},{4,0},{24,28},{28,24},{1,5},{5,1},{25,29},{29,25},{2,6},{6,2... | collective-permute-start | bytes 1572872 | tf_op jit(solution)/shard_map/ppermute | solution.py:107
  (42 other events, 558.3 us)
Sparse Core Ops, SparseCore 0:
  42.9 44.6 reduce-scatter.1

commit v6 on v5

--- a/solution.py
+++ b/solution.py
@@ -90,12 +90,26 @@
 VMEM = pl.BlockSpec(memory_space=pltpu.VMEM)
 SMEM = pl.BlockSpec(memory_space=pltpu.SMEM)
 PARAMS = pltpu.CompilerParams(vmem_limit_bytes=48 * 2**20)
+ANY = pl.BlockSpec(memory_space=pl.ANY)
 PAIRS = ((0, 1), (1, 0), (2, 3), (3, 2))
-INWARD = ((0, 1), (3, 2))
 MIDDLE = ((1, 2), (2, 1))
 OUTWARD = ((1, 0), (2, 3))
 ENDS = (0, 3)
 INNER = (1, 2)
+
+
+def ordered(body, arrays, in_specs, after=(), **call):
+    count = len(arrays)
+
+    def short(*refs):
+        body(*refs[:count], *refs[count + len(after) :])
+
+    return pl.pallas_call(
+        short,
+        in_specs=list(in_specs) + [ANY] * len(after),
+        compiler_params=PARAMS,
+        **call,
+    )(*arrays, *after)
 
 
 def lines(array, hops):
@@ -144,7 +158,7 @@
     )(place, tokens)
 
 
-def other_blocks(place, inner, ends=None):
+def other_blocks(place, inner, ends=None, after=()):
     def body(place, *refs):
         inner, out = refs[0], refs[-1]
         for i in range(HALF):
@@ -161,18 +175,19 @@
             def _():
                 out[i] = refs[1][HALF * (1 - place[1]) + i]
 
-    arrays = (inner,) if ends is None else (inner, ends)
-    return pl.pallas_call(
-        body,
+    arrays = (place, inner) if ends is None else (place, inner, ends)
+    return ordered(
+        body,
+        arrays,
+        [SMEM] + [VMEM] * (len(arrays) - 1),
+        after,
         out_shape=jax.ShapeDtypeStruct((HALF,) + inner.shape[1:], inner.dtype),
-        in_specs=[SMEM] + [VMEM] * len(arrays),
         out_specs=VMEM,
-        compiler_params=PARAMS,
         name="other_blocks",
-    )(place, *arrays)
-
-
-def own_blocks(place, got, inner, ends=None):
+    )
+
+
+def own_blocks(place, got, inner, ends=None, after=()):
     def body(place, got, *refs):
         inner, out = refs[0], refs[-1]
         for i in range(HALF):
@@ -190,18 +205,19 @@
             def _():
                 out[i] = refs[1][HALF * place[1] + i]
 
-    arrays = (inner,) if ends is None else (inner, ends)
-    return pl.pallas_call(
-        body,
+    arrays = (place, got, inner) if ends is None else (place, got, inner, ends)
+    return ordered(
+        body,
+        arrays,
+        [SMEM] + [VMEM] * (len(arrays) - 1),
+        after,
         out_shape=jax.ShapeDtypeStruct((OWN,) + inner.shape[1:], inner.dtype),
-        in_specs=[SMEM] + [VMEM] * (1 + len(arrays)),
         out_specs=VMEM,
-        compiler_params=PARAMS,
         name="own_blocks",
-    )(place, got, *arrays)
-
-
-def gate(place, tokens, in_weight, kernel, out_grad):
+    )
+
+
+def gate(place, tokens, in_weight, kernel, out_grad, after=()):
     rows, features = tokens.shape
     chans = in_weight.shape[2]
     taps = kernel.shape[0]
@@ -210,7 +226,7 @@
     deep = features // steps
     pad = 8
 
-    def body(place, tokens, weight, kernel, out_grad, own, grad, first, inner, middle, total, held, pads, back):
+    def body(place, tokens, weight, kernel, out_grad, own, grad, wide, inner, middle, total, held, pads, back):
         step = pl.program_id(1)
         for s in range(3):
             now = jnp.dot(tokens[...], weight[s], preferred_element_type=jnp.float32)
@@ -261,36 +277,38 @@
                         grad[j, s : s + 1, lanes] = jnp.sum(sums[s][j], axis=0, keepdims=True)
             for s in range(3):
                 own[s] = held[s].astype(jnp.bfloat16)
+                wide[s] = held[s]
             level = place[0]
-            first[...] = held[2 - 2 * lax.rem(level, 2)]
             low = jnp.where(level <= 1, 0, 1)
             for i in range(2):
                 inner[i] = held[low + i]
                 middle[i] = held[1 - low + i]
 
-    one = jax.ShapeDtypeStruct((rows, chans), jnp.float32)
+    three = jax.ShapeDtypeStruct((3, rows, chans), jnp.float32)
     two = jax.ShapeDtypeStruct((2, rows, chans), jnp.float32)
-    return pl.pallas_call(
-        body,
-        out_shape=(
-            jax.ShapeDtypeStruct((3, rows, chans), jnp.bfloat16),
-            jax.ShapeDtypeStruct((taps, 3, chans), jnp.float32),
-            one,
-            two,
-            two,
-        ),
-        grid=(chans // width, steps),
-        in_specs=[
+    return ordered(
+        body,
+        (place, tokens, in_weight, kernel, out_grad),
+        [
             SMEM,
             pl.BlockSpec((rows, deep), lambda c, k: (0, k)),
             pl.BlockSpec((3, deep, width), lambda c, k: (0, k, c)),
             pl.BlockSpec((taps, 3, width), lambda c, k: (0, 0, c)),
             pl.BlockSpec((rows, width), lambda c, k: (0, c)),
         ],
+        after,
+        out_shape=(
+            jax.ShapeDtypeStruct((3, rows, chans), jnp.bfloat16),
+            jax.ShapeDtypeStruct((taps, 3, chans), jnp.float32),
+            three,
+            two,
+            two,
+        ),
+        grid=(chans // width, steps),
         out_specs=(
             pl.BlockSpec((3, rows, width), lambda c, k: (0, 0, c)),
             pl.BlockSpec((taps, 3, width), lambda c, k: (0, 0, c)),
-            pl.BlockSpec((rows, width), lambda c, k: (0, c)),
+            pl.BlockSpec((3, rows, width), lambda c, k: (0, 0, c)),
             pl.BlockSpec((2, rows, width), lambda c, k: (0, 0, c)),
             pl.BlockSpec((2, rows, width), lambda c, k: (0, 0, c)),
         ),
@@ -300,39 +318,62 @@
             pltpu.VMEM((3, pad + SEQ, LANES), jnp.float32),
             pltpu.VMEM((3, SEQ + pad, LANES), jnp.float32),
         ],
-        compiler_params=PARAMS,
-        cost_estimate=pl.CostEstimate(
-            flops=2 * rows * features * 3 * chans,
-            bytes_accessed=2 * features * 3 * chans,
-            transcendentals=0,
-        ),
         name="gate",
-    )(place, tokens, in_weight, kernel, out_grad)
-
-
-def relay_payload(place, first, inner):
-    def body(place, first, inner, out):
-        @pl.when(place[0] <= 1)
-        def _():
-            out[0] = inner[1]
-            out[1] = first[...]
-
-        @pl.when(place[0] > 1)
-        def _():
-            out[0] = first[...]
-            out[1] = inner[0]
-
-    return pl.pallas_call(
-        body,
-        out_shape=jax.ShapeDtypeStruct(inner.shape, inner.dtype),
-        in_specs=[SMEM, VMEM, VMEM],
+    )
+
+
+def relay_payloads(place, pair, after=()):
+    def body(place, pair, across, side):
+        low = jnp.where(place[0] <= 1, 0, 1)
+        for i in range(2):
+            across[i] = pair[1 - low + i]
+            side[i] = pair[low + i]
+
+    two = jax.ShapeDtypeStruct((2,) + pair.shape[1:], pair.dtype)
+    return ordered(
+        body,
+        (place, pair),
+        [SMEM, VMEM],
+        after,
+        out_shape=(two, two),
+        out_specs=(VMEM, VMEM),
+        name="relay_payloads",
+    )
+
+
+def part_of(place, array, step, count, after=()):
+    def body(place, array, out):
+        start = jnp.where(place[0] <= 1, 0, step)
+        for i in range(count):
+            out[i] = array[start + i]
+
+    return ordered(
+        body,
+        (place, array),
+        [SMEM, VMEM],
+        after,
+        out_shape=jax.ShapeDtypeStruct((count,) + array.shape[1:], array.dtype),
         out_specs=VMEM,
-        compiler_params=PARAMS,
-        name="relay_payload",
-    )(place, first, inner)
-
-
-def arrange_tokens(place, own, slots):
+        name="part_of",
+    )
+
+
+def add(a, b, scale, after=()):
+    def body(a, b, out):
+        out[...] = (a[...] + b[...]) * scale
+
+    return ordered(
+        body,
+        (a, b),
+        [VMEM, VMEM],
+        after,
+        out_shape=jax.ShapeDtypeStruct(a.shape, a.dtype),
+        out_specs=VMEM,
+        name="add",
+    )
+
+
+def arrange_tokens(place, own, slots, after=()):
     slab = BLOCK // 4
     rows = slots[0][0].shape[2]
     counts = [slot[0].shape[0] // HALF for slot in slots]
@@ -358,60 +399,56 @@
                         ][HALF * c + i].astype(jnp.bfloat16)
             at += count
 
-    arrays = ([] if own is None else [own]) + [piece for slot in slots for piece in slot]
-    return pl.pallas_call(
-        body,
+    arrays = [place] + ([] if own is None else [own]) + [piece for slot in slots for piece in slot]
+    return ordered(
+        body,
+        arrays,
+        [SMEM] + [VMEM] * (len(arrays) - 1),
+        after,
         out_shape=jax.ShapeDtypeStruct((HALF, BLOCK, total * rows), jnp.bfloat16),
-        in_specs=[SMEM] + [VMEM] * len(arrays),
         out_specs=VMEM,
-        compiler_params=PARAMS,
         name="arrange_tokens",
-    )(place, *arrays)
-
-
-def weight_part(place, tok, own, slots, scale=None, so_far=None):
-    rows, chans = slots[0][1].shape[1:]
-    count = (0 if own is None else 1) + len(slots)
-    arrays = ([] if own is None else [own]) + [a for slot in slots for a in slot if a is not None]
-    last = scale is not None
+    )
+
+
+def weight_part(place, tok, slots, scale=None, so_far=None, after=()):
+    rows, chans = slots[0][0].shape[1:]
+    count = len(slots)
+    arrays = [a for slot in slots for a in slot if a is not None]
 
     def body(place, tok, *refs):
         out, held = refs[-2], refs[-1]
         level, column = place[0], place[1]
         i = pl.program_id(0)
         inside = jnp.logical_or(level == 1, level == 2)
-        at = 0
+        high = jnp.where(level <= 1, 0, 1)
 
         @pl.when(i == 0)
         def _():
-            at = 0
-            refs_left = list(refs)
-            if own is not None:
-                ref = refs_left.pop(0)
-                major = jnp.where(inside, level - 1 + column, jnp.where(level == 0, 0, 2))
-                held[0, 0:rows, :] = ref[major]
-                held[1, 0:rows, :] = ref[1]
-                at = 1
-            for ends, _inner in slots:
+            left = list(refs)
+            for at, (streams, ends) in enumerate(slots):
                 here = slice(at * rows, (at + 1) * rows)
+                ref = left.pop(0)
+                if streams.shape[0] == 3:
+                    major = jnp.where(inside, level - 1 + column, 2 * high)
+                    minor = 1
+                else:
+                    major = jnp.where(inside, column, high)
+                    minor = 1 - high
                 if ends is None:
-                    ref = refs_left.pop(0)
-                    major = jnp.where(inside, column, jnp.where(level == 0, 0, 1))
                     held[0, here, :] = ref[major].astype(jnp.bfloat16)
-                    held[1, here, :] = ref[jnp.where(level == 2, 0, 1)].astype(jnp.bfloat16)
                 else:
-                    end, ref = refs_left.pop(0), refs_left.pop(0)
+                    end = left.pop(0)
 
                     @pl.when(inside)
                     def _():
-                        held[0, here, :] = ref[column].astype(jnp.bfloat16)
-                        held[1, here, :] = ref[jnp.where(level == 2, 0, 1)].astype(jnp.bfloat16)
+                        held[0, here, :] = ref[major].astype(jnp.bfloat16)
 
                     @pl.when(jnp.logical_not(inside))
                     def _():
-                        held[0, here, :] = end[...].astype(jnp.bfloat16)
-
-                at += 1
+                        held[0, here, :] = end[0].astype(jnp.bfloat16)
+
+                held[1, here, :] = ref[minor].astype(jnp.bfloat16)
 
         second = jnp.logical_or(
             jnp.logical_and(jnp.logical_and(level == 1, column == 0), i == 2),
@@ -422,31 +459,27 @@
         )
         if so_far is not None:
             got = got + refs[-3][...]
-        out[...] = got * scale if last else got
+        out[...] = got if scale is None else got * scale
 
     whole = lambda a: pl.BlockSpec(a.shape, lambda i: (0,) * a.ndim)
     more = [] if so_far is None else [so_far]
     part = pl.BlockSpec((BLOCK, chans), lambda i: (i, 0))
-    return pl.pallas_call(
-        body,
+    return ordered(
+        body,
+        [place, tok] + arrays + more,
+        [SMEM, pl.BlockSpec((None, BLOCK, count * rows), lambda i: (i, 0, 0))]
+        + [whole(a) for a in arrays]
+        + [part] * len(more),
+        after,
         out_shape=jax.ShapeDtypeStruct((HALF * BLOCK, chans), jnp.float32),
         grid=(HALF,),
-        in_specs=[SMEM, pl.BlockSpec((None, BLOCK, count * rows), lambda i: (i, 0, 0))]
-        + [whole(a) for a in arrays]
-        + [part] * len(more),
         out_specs=part,
         scratch_shapes=[pltpu.VMEM((2, count * rows, chans), jnp.bfloat16)],
-        compiler_params=PARAMS,
-        cost_estimate=pl.CostEstimate(
-            flops=2 * HALF * BLOCK * count * rows * chans,
-            bytes_accessed=2 * HALF * BLOCK * count * rows + 8 * count * rows * chans,
-            transcendentals=0,
-        ),
         name="weight_part",
-    )(place, tok, *arrays, *more)
-
-
-def token_part(grads, weight):
+    )
+
+
+def token_part(grads, weight, after=()):
     rows, chans = grads.shape[1:]
     wide = weight.shape[1] // 4
 
@@ -463,23 +496,19 @@
         def _():
             out[...] += now
 
-    return pl.pallas_call(
-        body,
-        out_shape=jax.ShapeDtypeStruct((rows, 4 * wide), jnp.float32),
-        grid=(4, 3),
-        in_specs=[
+    return ordered(
+        body,
+        (grads, weight),
+        [
             pl.BlockSpec((None, rows, chans), lambda i, s: (s, 0, 0)),
             pl.BlockSpec((None, wide, chans), lambda i, s: (s, i, 0)),
         ],
+        after,
+        out_shape=jax.ShapeDtypeStruct((rows, 4 * wide), jnp.float32),
+        grid=(4, 3),
         out_specs=pl.BlockSpec((rows, wide), lambda i, s: (0, i)),
-        compiler_params=PARAMS,
-        cost_estimate=pl.CostEstimate(
-            flops=8 * rows * wide * 3 * chans,
-            bytes_accessed=8 * wide * 3 * chans + 16 * rows * wide,
-            transcendentals=0,
-        ),
         name="token_part",
-    )(grads, weight)
+    )
 
 
 def lined(tokens, in_weight, kernel, out_grad):
@@ -488,51 +517,73 @@
     level, column = rep // 2, rep % 2
     place = jnp.stack([level, column, lax.axis_index("shard")]).astype(jnp.int32)
     scale = 1.0 / math.sqrt(rows * lax.axis_size("rep"))
-    later = jnp.where(level <= 1, 0, 1)
+
+    def tap_step(taps, bit):
+        return lax.ppermute(taps, "rep", [(r, r ^ bit) for r in range(2 * LEVELS)])
 
     piece, theirs = turn_tokens(place, tokens)
     near = lines(piece, PAIRS)
     mid = lines(piece, MIDDLE)
-    slots = [share(sides(theirs))]
-
-    own, taps, first_out, inner_out, middle_out = gate(place, tokens, in_weight, kernel, out_grad)
-    partial = token_part(own, in_weight)
+    got0 = sides(theirs)
+    own, taps, wide, inner_out, middle_out = gate(
+        place, tokens, in_weight, kernel, out_grad, after=(theirs,)
+    )
+    pair = lines(wide, PAIRS)
+    own_y = sides(inner_out)
+    slots = [share(got0)]
+
+    far = lines(near, MIDDLE)
+    send1 = other_blocks(place, near, after=(inner_out,))
+    got1 = sides(send1)
+    send = part_of(place, mid, BLOCKS - OWN, OWN, after=(near, send1))
+    outer2 = lines(send, OUTWARD)
+    middle = lines(middle_out, MIDDLE)
+    partial = token_part(own, in_weight, after=(send, slots[0][1]))
     token_grad = lax.psum_scatter(partial, "shard", scatter_dimension=1, tiled=True)
 
-    def ended(array):
-        return lax.dynamic_slice_in_dim(array, 2 * later, OWN, 0)
-
-    far = lines(near, MIDDLE)
-    got = sides(other_blocks(place, near))
-    slots.append(share(own_blocks(place, got, near)))
-    for array in (mid, far):
-        outer = lines(ended(array), OUTWARD)
-        got = sides(other_blocks(place, array, outer))
-        slots.append(share(own_blocks(place, got, array, outer)))
-
-    own_y = sides(inner_out)
-    middle = lines(middle_out, MIDDLE)
-    inner = lines(inner_out, INWARD)
-    first = lines(first_out, PAIRS)
-    relayed = lines(relay_payload(place, first, inner), MIDDLE)
-    pick = lambda array: lax.dynamic_index_in_dim(array, later, 0, keepdims=False)
-    middle_end = lines(pick(middle), OUTWARD)
-    relayed_end = lines(pick(relayed), OUTWARD)
-
-    def both(ends, inner):
-        return [(ends, inner), (sides(ends, ENDS), sides(inner, INNER))]
-
-    early = [(None, own_y)] + both(first, inner) + both(middle_end, middle)
-    late = both(relayed_end, relayed)
-
-    for bit in (1, 2, 4):
-        taps = taps + lax.ppermute(taps, "rep", [(r, r ^ bit) for r in range(2 * LEVELS)])
-
-    so_far = weight_part(place, arrange_tokens(place, tokens, slots[:3]), own, early)
+    tap1 = tap_step(taps, 1)
+    send2 = other_blocks(place, mid, outer2, after=(partial, slots[0][3]))
+    got2 = sides(send2)
+    send = part_of(place, far, BLOCKS - OWN, OWN, after=(send2,))
+    outer3 = lines(send, OUTWARD)
+    own1 = own_blocks(place, got1, near, after=(send,))
+    slots.append(share(own1))
+    relay_out, side1_out = relay_payloads(place, pair, after=(own1,))
+    relayed = lines(relay_out, MIDDLE)
+    side1 = sides(side1_out)
+    taps = add(taps, tap1, 1.0, after=(relay_out,))
+    own2 = own_blocks(place, got2, mid, outer2, after=(taps, own_y))
+    slots.append(share(own2))
+    tap2 = tap_step(taps, 2)
+    send3 = other_blocks(place, far, outer3, after=(own2,))
+    got3 = sides(send3)
+    send = part_of(place, middle, 1, 1, after=(send3,))
+    middle_end = lines(send, OUTWARD)
+    side2 = sides(middle, INNER)
+    own3 = own_blocks(place, got3, far, outer3, after=(send,))
+    slots.append(share(own3))
+    taps = add(taps, tap2, 1.0, after=(own3,))
+    tap4 = tap_step(taps, 4)
+    side2_end = sides(middle_end, ENDS)
+    send = part_of(place, relayed, 1, 1, after=(taps,))
+    relayed_end = lines(send, OUTWARD)
+    side3 = sides(relayed, INNER)
+    tok = arrange_tokens(place, tokens, slots[:3], after=(send,))
+    early = [(own, None), (own_y, None), (pair, None), (side1, None)]
+    early += [(middle, middle_end), (side2, side2_end)]
+    so_far = weight_part(place, tok, early)
+    tok = arrange_tokens(place, None, slots[3:], after=(so_far,))
+    taps = add(taps, tap4, scale, after=(tok,))
+    side3_end = sides(relayed_end, ENDS)
     weight_grad = weight_part(
-        place, arrange_tokens(place, None, slots[3:]), None, late, scale, so_far
-    )
-    return (token_grad.astype(jnp.bfloat16), weight_grad, taps * scale)
+        place,
+        tok,
+        [(relayed, relayed_end), (side3, side3_end)],
+        scale,
+        so_far,
+        after=(taps,),
+    )
+    return (token_grad.astype(jnp.bfloat16), weight_grad, taps)
 
 
 def solution(mesh):

time: 279 us -> 272 us (0.975)
  the two profiles are of different devices: /device:TPU:18 before, /device:TPU:0 now
where the time goes in v6:
time: 272 us; the launch traced here: 271 us
  waiting for transfers between devices  128 us (47%)
  starting transfers between devices  60.7 us (22%)
  Pallas kernels  54.7 us (20%)
  between operations  14.5 us (5%)
  local copies, waits for them, and re-layouts  10.8 us (4%)
    ppermute x10, waiting for transfers between devices, lines(): return lax.ppermute(array, 'rep', perm)  58.6 us
    pallas_call x20, Pallas kernels, ordered(): pl.pallas_call(short, in_specs=list(in_specs) + [ANY] * len(after), compi...  53.9 us
    ppermute x4, waiting for transfers between devices, share(): across = lax.ppermute(array, 'shard', [(q, q ^ 2) for q in range(4)])  38.1 us
    ppermute x10, waiting for transfers between devices, sides(): lax.ppermute(array, 'rep', [(2 * z + y, 2 * z + 1 - y) for z in levels fo...  28.4 us
    ppermute x3, starting transfers between devices, tap_step(): return lax.ppermute(taps, 'rep', [(r, r ^ bit) for r in range(2 * LEVELS)])  21.5 us
    ppermute x10, starting transfers between devices, lines(): return lax.ppermute(array, 'rep', perm)  16.7 us
    ppermute x10, starting transfers between devices, sides(): lax.ppermute(array, 'rep', [(2 * z + y, 2 * z + 1 - y) for z in levels fo...  15.7 us
    unnamed x36, local copies, waits for them, and re-layouts  10.8 us
  transfers between devices with their start and end apart: 36, of which 13 were waited for; matrix products, arithmetic and copies ran while one was open for 1% of the time, Pallas kernels for 16%

profile of v6, /device:TPU:0, one launch (start us, length us, event | category | flops | bytes accessed | tf_op | source)
XLA Modules:
  0.0 270.9 jit_solution(11161542497740320851)
XLA Ops:
  9.7 3.1 %collective-permute-start.1 = (f32[8,128,256]{2,1,0:T(8,128)S(1)}, f32[8,128,256]{2,1,0:T(8,128)S(1)}, u32[]{:S(2)}, u32[]{:S(2)}) collective-permute-start(f32[8,128,256]{2,1,0:T(8,128)S(1)} %get-tuple-element.14), channel_id=1, source_target_pairs={{0,8},{4,12},{8,0},{12,4},{16,24},{20,28},{24,16},{28,20},{1,9},{5... | collective-permute-start | bytes 3145736 | tf_op jit(solution)/shard_map/ppermute | solution.py:117
  15.1 9.1 %collective-permute-done.2.refs_2_ = f32[3,128,256]{2,1,0:T(8,128)S(1)} collective-permute-done((f32[3,128,256]{2,1,0:T(8,128)S(1)}, f32[3,128,256]{2,1,0:T(8,128)S(1)}, u32[]{:S(2)}, u32[]{:S(2)}) %collective-permute-start.2) | collective-permute-done | bytes 393248 | tf_op jit(solution)/shard_map/ppermute | solution.py:121
  26.0 16.0 %gate.1 = (bf16[3,256,512]{2,1,0:T(8,128)(2,1)S(1)}, f32[7,3,512]{2,1,0:T(4,128)S(1)}, f32[3,256,512]{2,1,0:T(8,128)S(1)}, f32[2,256,512]{2,1,0:T(8,128)S(1)}, f32[2,256,512]{2,1,0:T(8,128)S(1)}) custom-call(s32[3]{0:T(128)S(1)} %pad_add_fusion.place.refs_0_, bf16[256,4096]{1,0:T(8,128)(2,1)} %refs_1_.5, bf16[3,4096,512]{2,1,0:T(8,128)(2,1)} %refs_1_.4, ...), custom_call_target="tpu_custom_call" | custom-call | tf_op jit(solution)/shard_map/gate/pallas_call | solution.py:107
  44.4 11.8 %token_part.1.refs_3_ = f32[256,4096]{1,0:T(8,128)S(1)} custom-call(bf16[3,256,512]{2,1,0:T(8,128)(2,1)S(1)} %get-tuple-element.13.refs_0_.refs_2_, bf16[3,4096,512]{2,1,0:T(8,128)(2,1)} %refs_1_.4, f32[6,128,256]{2,1,0:T(8,128)S(1)} %part_of.4.refs_2_, f32[3,128,256]{2,1,0:T(8,128)S(1)} %collective-permute-done.3.refs_3_), custom_call_target="tpu_custom_call" | custom-call | tf_op jit(solution)/shard_map/token_part/pallas_call | solution.py:107
  56.2 2.0 copy-done
  60.7 5.6 %collective-permute-start.11 = (f32[3,256,512]{2,1,0:T(8,128)}, f32[3,256,512]{2,1,0:T(8,128)S(1)}, u32[]{:S(2)}, u32[]{:S(2)}) collective-permute-start(f32[3,256,512]{2,1,0:T(8,128)} %copy-done.14), channel_id=1, source_target_pairs={{0,8},{4,12},{8,0},{12,4},{16,24},{20,28},{24,16},{28,20},{1,9},{5... | collective-permute-start | bytes 4718600 | tf_op jit(solution)/shard_map/ppermute | solution.py:117
  69.8 8.4 %collective-permute-done.6.refs_4_ = f32[3,128,256]{2,1,0:T(8,128)S(1)} collective-permute-done((f32[3,128,256]{2,1,0:T(8,128)}, f32[3,128,256]{2,1,0:T(8,128)S(1)}, u32[]{:S(2)}, u32[]{:S(2)}) %collective-permute-start.6) | collective-permute-done | bytes 393248 | tf_op jit(solution)/shard_map/ppermute | solution.py:125
  81.4 36.6 %collective-permute-done.5.refs_2_.refs_3_ = f32[6,128,256]{2,1,0:T(8,128)S(1)} collective-permute-done((f32[6,128,256]{2,1,0:T(8,128)}, f32[6,128,256]{2,1,0:T(8,128)S(1)}, u32[]{:S(2)}, u32[]{:S(2)}) %collective-permute-start.5) | collective-permute-done | bytes 786464 | tf_op jit(solution)/shard_map/ppermute | solution.py:117
  123.5 2.1 collective-permute-done.10.refs_1_
  127.2 1.7 relay_payloads.1
  128.9 8.3 %collective-permute-done.9.refs_1_ = f32[3,128,256]{2,1,0:T(8,128)S(1)} collective-permute-done((f32[3,128,256]{2,1,0:T(8,128)S(1)}, f32[3,128,256]{2,1,0:T(8,128)S(1)}, u32[]{:S(2)}, u32[]{:S(2)}) %collective-permute-start.9) | collective-permute-done | bytes 393248 | tf_op jit(solution)/shard_map/ppermute | solution.py:121
  137.8 3.3 %collective-permute-done.8.refs_2_.refs_3_ = f32[6,128,256]{2,1,0:T(8,128)S(1)} collective-permute-done((f32[6,128,256]{2,1,0:T(8,128)S(1)}, f32[6,128,256]{2,1,0:T(8,128)S(1)}, u32[]{:S(2)}, u32[]{:S(2)}) %collective-permute-start.8) | collective-permute-done | bytes 786464 | tf_op jit(solution)/shard_map/ppermute | solution.py:117
  143.3 19.9 %collective-permute-start.26 = (f32[7,3,512]{2,1,0:T(4,128)S(1)}, f32[7,3,512]{2,1,0:T(4,128)S(1)}, u32[]{:S(2)}, u32[]{:S(2)}) collective-permute-start(f32[7,3,512]{2,1,0:T(4,128)S(1)} %add.16.refs_4_.refs_0_), channel_id=1, source_target_pairs={{0,8},{4,12},{8,0},{12,4},{16,24},{20,28},{24,16},{28,20},{1,9},{5... | collective-permute-start | bytes 129032 | tf_op jit(solution)/shard_map/ppermute | solution.py:522
  169.4 14.3 %collective-permute-done.20.refs_8_ = f32[6,128,256]{2,1,0:T(8,128)S(1)} collective-permute-done((f32[6,128,256]{2,1,0:T(8,128)S(1)}, f32[6,128,256]{2,1,0:T(8,128)S(1)}, u32[]{:S(2)}, u32[]{:S(2)}) %collective-permute-start.20) | collective-permute-done | bytes 786464 | tf_op jit(solution)/shard_map/ppermute | solution.py:125
  185.3 15.4 %collective-permute-done.23.refs_12_ = f32[6,128,256]{2,1,0:T(8,128)} collective-permute-done((f32[6,128,256]{2,1,0:T(8,128)S(1)}, f32[6,128,256]{2,1,0:T(8,128)}, u32[]{:S(2)}, u32[]{:S(2)}) %collective-permute-start.23) | collective-permute-done | bytes 786464 | tf_op jit(solution)/shard_map/ppermute | solution.py:125
  204.0 12.6 %collective-permute-done.28.refs_7_ = f32[1,256,512]{2,1,0:T(8,128)} collective-permute-done((f32[1,256,512]{2,1,0:T(8,128)S(1)}, f32[1,256,512]{2,1,0:T(8,128)}, u32[]{:S(2)}, u32[]{:S(2)}) %collective-permute-start.28) | collective-permute-done | bytes 524320 | tf_op jit(solution)/shard_map/ppermute | solution.py:117
  217.9 6.0 %collective-permute-done.31.refs_3_ = f32[1,256,512]{2,1,0:T(8,128)} collective-permute-done((f32[1,256,512]{2,1,0:T(8,128)S(1)}, f32[1,256,512]{2,1,0:T(8,128)}, u32[]{:S(2)}, u32[]{:S(2)}) %collective-permute-start.31) | collective-permute-done | bytes 524320 | tf_op jit(solution)/shard_map/ppermute | solution.py:117
  224.0 2.4 collective-permute-start.30
  226.4 3.4 %collective-permute-start.33 = (f32[1,256,512]{2,1,0:T(8,128)}, f32[1,256,512]{2,1,0:T(8,128)}, u32[]{:S(2)}, u32[]{:S(2)}) collective-permute-start(f32[1,256,512]{2,1,0:T(8,128)} %collective-permute-done.31.refs_3_), channel_id=1, source_target_pairs={{0,4},{4,0},{24,28},{28,24},{1,5},{5,1},{25,29},{29,25},{2,6},{6,2... | collective-permute-start | bytes 1572872 | tf_op jit(solution)/shard_map/ppermute | solution.py:121
  229.8 11.1 %collective-permute-done.30.refs_9_ = f32[1,256,512]{2,1,0:T(8,128)S(1)} collective-permute-done((f32[1,256,512]{2,1,0:T(8,128)}, f32[1,256,512]{2,1,0:T(8,128)S(1)}, u32[]{:S(2)}, u32[]{:S(2)}) %collective-permute-start.30) | collective-permute-done | bytes 524320 | tf_op jit(solution)/shard_map/ppermute | solution.py:121
  241.7 5.1 %arrange_tokens.2.refs_1_ = bf16[3,512,1536]{2,1,0:T(8,128)(2,1)} custom-call(s32[3]{0:T(128)S(1)} %pad_add_fusion.place.refs_0_, bf16[256,4096]{1,0:T(8,128)(2,1)} %refs_1_.5, f32[3,128,256]{2,1,0:T(8,128)S(1)} %copy-done.10, f32[3,128,256]{2,1,0:T(8,128)S(1)} %copy-done.5, f32[3,128,256]{2,1,0:T(8,128)S(1)} %copy-done.12, ...), custom_call_target="tpu_custom_call" | custom-call | tf_op jit(solution)/shard_map/arrange_tokens/pallas_call | solution.py:107
  247.9 7.1 %weight_part.2.refs_5_.refs_6_ = f32[1536,512]{1,0:T(8,128)} custom-call(s32[3]{0:T(128)S(1)} %pad_add_fusion.place.refs_0_, bf16[3,512,1536]{2,1,0:T(8,128)(2,1)} %arrange_tokens.2.refs_1_, bf16[3,256,512]{2,1,0:T(8,128)(2,1)S(1)} %get-tuple-element.13.refs_0_.refs_2_, f32[2,256,512]{2,1,0:T(8,128)S(1)} %collective-permute-done.13.refs_5_.refs_3_, ...), custom_call_target="tpu_custom_call" | custom-call | tf_op jit(solution)/shard_map/weight_part/pallas_call | solution.py:107
  256.4 5.5 %weight_part.3 = f32[1536,512]{1,0:T(8,128)} custom-call(s32[3]{0:T(128)S(1)} %pad_add_fusion.place.refs_0_, bf16[3,512,512]{2,1,0:T(8,128)(2,1)S(1)} %arrange_tokens.3.refs_2_.refs_1_, f32[2,256,512]{2,1,0:T(8,128)S(1)} %collective-permute-done.25.refs_1_.refs_2_, f32[1,256,512]{2,1,0:T(8,128)} %collective-permute-done.31.refs_3_, ...), custom_call_target="tpu_custom_call" | custom-call | tf_op jit(solution)/shard_map/weight_part/pallas_call | solution.py:107
  261.9 2.1 convert_element_type.3
  (108 shorter events, 43.4 us)
Async XLA Ops:
  7.2 254.8 %reduce-scatter.2.cloned.1.call-start = ((), (), s32[]{:S(2)}) async-start(), calls=%async_computation.1 | async-start | bytes 5242880 | tf_op jit(solution)/shard_map/reduce_scatter | solution.py:542
  9.7 33.5 %collective-permute-start.1 = (f32[8,128,256]{2,1,0:T(8,128)S(1)}, f32[8,128,256]{2,1,0:T(8,128)S(1)}, u32[]{:S(2)}, u32[]{:S(2)}) collective-permute-start(f32[8,128,256]{2,1,0:T(8,128)S(1)} %get-tuple-element.14), channel_id=1, source_target_pairs={{0,8},{4,12},{8,0},{12,4},{16,24},{20,28},{24,16},{28,20},{1,9},{5... | collective-permute-start | bytes 3145736 | tf_op jit(solution)/shard_map/ppermute | solution.py:117
  12.8 31.0 %collective-permute-start = (f32[8,128,256]{2,1,0:T(8,128)S(1)}, f32[8,128,256]{2,1,0:T(8,128)S(1)}, u32[]{:S(2)}, u32[]{:S(2)}) collective-permute-start(f32[8,128,256]{2,1,0:T(8,128)S(1)} %get-tuple-element.14), channel_id=1, source_target_pairs={{8,16},{12,20},{16,8},{20,12},{9,17},{13,21},{17,9},{21,13},{10,18... | collective-permute-start | bytes 3145736 | tf_op jit(solution)/shard_map/ppermute | solution.py:117
  60.7 64.9 %collective-permute-start.11 = (f32[3,256,512]{2,1,0:T(8,128)}, f32[3,256,512]{2,1,0:T(8,128)S(1)}, u32[]{:S(2)}, u32[]{:S(2)}) collective-permute-start(f32[3,256,512]{2,1,0:T(8,128)} %copy-done.14), channel_id=1, source_target_pairs={{0,8},{4,12},{8,0},{12,4},{16,24},{20,28},{24,16},{28,20},{1,9},{5... | collective-permute-start | bytes 4718600 | tf_op jit(solution)/shard_map/ppermute | solution.py:117
  66.3 53.2 %collective-permute-start.4 = (f32[8,128,256]{2,1,0:T(8,128)S(1)}, f32[8,128,256]{2,1,0:T(8,128)S(1)}, u32[]{:S(2)}, u32[]{:S(2)}) collective-permute-start(f32[8,128,256]{2,1,0:T(8,128)S(1)} %collective-permute-done.1.refs_1_.refs_2_), channel_id=1, source_target_pairs={{8,16},{12,20},{16,8},{20,12},{9,17},{13,21},{17,9},{21,13},{10,18... | collective-permute-start | bytes 3145736 | tf_op jit(solution)/shard_map/ppermute | solution.py:117
  68.5 49.5 %collective-permute-start.5 = (f32[6,128,256]{2,1,0:T(8,128)}, f32[6,128,256]{2,1,0:T(8,128)S(1)}, u32[]{:S(2)}, u32[]{:S(2)}) collective-permute-start(f32[6,128,256]{2,1,0:T(8,128)} %copy-done.3), channel_id=1, source_target_pairs={{8,0},{12,4},{16,24},{20,28},{9,1},{13,5},{17,25},{21,29},{10,2},{... | collective-permute-start | bytes 2359304 | tf_op jit(solution)/shard_map/ppermute | solution.py:117
  78.2 50.7 %collective-permute-start.13 = (f32[2,256,512]{2,1,0:T(8,128)}, f32[2,256,512]{2,1,0:T(8,128)S(1)}, u32[]{:S(2)}, u32[]{:S(2)}) collective-permute-start(f32[2,256,512]{2,1,0:T(8,128)} %copy-done.6), channel_id=1, source_target_pairs={{0,4},{4,0},{8,12},{12,8},{16,20},{20,16},{24,28},{28,24},{1,5},{5... | collective-permute-start | bytes 3145736 | tf_op jit(solution)/shard_map/ppermute | solution.py:121
  79.9 41.4 %collective-permute-start.12 = (f32[3,128,256]{2,1,0:T(8,128)S(1)}, f32[3,128,256]{2,1,0:T(8,128)S(1)}, u32[]{:S(2)}, u32[]{:S(2)}) collective-permute-start(f32[3,128,256]{2,1,0:T(8,128)S(1)} %other_blocks.3.refs_3_), channel_id=1, source_target_pairs={{0,4},{4,0},{8,12},{12,8},{16,20},{20,16},{24,28},{28,24},{1,5},{5... | collective-permute-start | bytes 1179656 | tf_op jit(solution)/shard_map/ppermute | solution.py:121
  118.1 46.6 %collective-permute-start.29 = (f32[2,256,512]{2,1,0:T(8,128)S(1)}, f32[2,256,512]{2,1,0:T(8,128)S(1)}, u32[]{:S(2)}, u32[]{:S(2)}) collective-permute-start(f32[2,256,512]{2,1,0:T(8,128)S(1)} %collective-permute-done.15.refs_1_.refs_6_), channel_id=1, source_target_pairs={{8,12},{12,8},{16,20},{20,16},{9,13},{13,9},{17,21},{21,17},{10,14... | collective-permute-start | bytes 3145736 | tf_op jit(solution)/shard_map/ppermute | solution.py:121
  120.1 21.0 %collective-permute-start.8 = (f32[6,128,256]{2,1,0:T(8,128)S(1)}, f32[6,128,256]{2,1,0:T(8,128)S(1)}, u32[]{:S(2)}, u32[]{:S(2)}) collective-permute-start(f32[6,128,256]{2,1,0:T(8,128)S(1)} %part_of.5.refs_3_), channel_id=1, source_target_pairs={{8,0},{12,4},{16,24},{20,28},{9,1},{13,5},{17,25},{21,29},{10,2},{... | collective-permute-start | bytes 2359304 | tf_op jit(solution)/shard_map/ppermute | solution.py:117
  125.6 41.3 %collective-permute-start.19 = (f32[6,128,256]{2,1,0:T(8,128)S(1)}, f32[6,128,256]{2,1,0:T(8,128)S(1)}, u32[]{:S(2)}, u32[]{:S(2)}) collective-permute-start(f32[6,128,256]{2,1,0:T(8,128)S(1)} %own_blocks.3.refs_2_.refs_6_), channel_id=1, source_target_pairs={{0,1},{1,0},{2,3},{3,2},{4,5},{5,4},{6,7},{7,6},{8,9},{9,8},{10,11... | collective-permute-start | bytes 2359304 | tf_op jit(solution)/shard_map/ppermute | solution.py:126
  141.7 25.9 %collective-permute-start.14 = (f32[3,128,256]{2,1,0:T(8,128)S(1)}, f32[3,128,256]{2,1,0:T(8,128)S(1)}, u32[]{:S(2)}, u32[]{:S(2)}) collective-permute-start(f32[3,128,256]{2,1,0:T(8,128)S(1)} %other_blocks.5.refs_2_), channel_id=1, source_target_pairs={{0,4},{4,0},{8,12},{12,8},{16,20},{20,16},{24,28},{28,24},{1,5},{5... | collective-permute-start | bytes 1179656 | tf_op jit(solution)/shard_map/ppermute | solution.py:121
  143.3 22.1 %collective-permute-start.26 = (f32[7,3,512]{2,1,0:T(4,128)S(1)}, f32[7,3,512]{2,1,0:T(4,128)S(1)}, u32[]{:S(2)}, u32[]{:S(2)}) collective-permute-start(f32[7,3,512]{2,1,0:T(4,128)S(1)} %add.16.refs_4_.refs_0_), channel_id=1, source_target_pairs={{0,8},{4,12},{8,0},{12,4},{16,24},{20,28},{24,16},{28,20},{1,9},{5... | collective-permute-start | bytes 129032 | tf_op jit(solution)/shard_map/ppermute | solution.py:522
  165.4 35.3 %collective-permute-start.23 = (f32[6,128,256]{2,1,0:T(8,128)S(1)}, f32[6,128,256]{2,1,0:T(8,128)}, u32[]{:S(2)}, u32[]{:S(2)}) collective-permute-start(f32[6,128,256]{2,1,0:T(8,128)S(1)} %own_blocks.4.refs_3_.refs_10_), channel_id=1, source_target_pairs={{0,2},{1,3},{2,0},{3,1},{4,6},{5,7},{6,4},{7,5},{8,10},{9,11},{10,... | collective-permute-start | bytes 2359304 | tf_op jit(solution)/shard_map/ppermute | solution.py:125
  166.9 35.1 %collective-permute-start.25 = (f32[2,256,512]{2,1,0:T(8,128)S(1)}, f32[2,256,512]{2,1,0:T(8,128)S(1)}, u32[]{:S(2)}, u32[]{:S(2)}) collective-permute-start(f32[2,256,512]{2,1,0:T(8,128)S(1)} %get-tuple-element.18.refs_2_), channel_id=1, source_target_pairs={{8,16},{12,20},{16,8},{20,12},{9,17},{13,21},{17,9},{21,13},{10,18... | collective-permute-start | bytes 3145736 | tf_op jit(solution)/shard_map/ppermute | solution.py:117
  167.6 35.1 %collective-permute-start.27 = (f32[2,256,512]{2,1,0:T(8,128)}, f32[2,256,512]{2,1,0:T(8,128)S(1)}, u32[]{:S(2)}, u32[]{:S(2)}) collective-permute-start(f32[2,256,512]{2,1,0:T(8,128)} %get-tuple-element.20), channel_id=1, source_target_pairs={{0,4},{4,0},{8,12},{12,8},{16,20},{20,16},{24,28},{28,24},{1,5},{5... | collective-permute-start | bytes 3145736 | tf_op jit(solution)/shard_map/ppermute | solution.py:121
  183.7 33.6 %collective-permute-start.21 = (f32[6,128,256]{2,1,0:T(8,128)S(1)}, f32[6,128,256]{2,1,0:T(8,128)S(1)}, u32[]{:S(2)}, u32[]{:S(2)}) collective-permute-start(f32[6,128,256]{2,1,0:T(8,128)S(1)} %collective-permute-done.20.refs_8_), channel_id=1, source_target_pairs={{0,1},{1,0},{2,3},{3,2},{4,5},{5,4},{6,7},{7,6},{8,9},{9,8},{10,11... | collective-permute-start | bytes 2359304 | tf_op jit(solution)/shard_map/ppermute | solution.py:127
  183.7 33.7 %collective-permute-start.17 = (f32[6,128,256]{2,1,0:T(8,128)S(1)}, f32[6,128,256]{2,1,0:T(8,128)S(1)}, u32[]{:S(2)}, u32[]{:S(2)}) collective-permute-start(f32[6,128,256]{2,1,0:T(8,128)S(1)} %own_blocks.5.refs_2_.refs_1_), channel_id=1, source_target_pairs={{0,2},{1,3},{2,0},{3,1},{4,6},{5,7},{6,4},{7,5},{8,10},{9,11},{10,... | collective-permute-start | bytes 2359304 | tf_op jit(solution)/shard_map/ppermute | solution.py:125
  202.0 24.4 %collective-permute-start.24 = (f32[6,128,256]{2,1,0:T(8,128)}, f32[6,128,256]{2,1,0:T(8,128)}, u32[]{:S(2)}, u32[]{:S(2)}) collective-permute-start(f32[6,128,256]{2,1,0:T(8,128)} %collective-permute-done.23.refs_12_), channel_id=1, source_target_pairs={{0,1},{1,0},{2,3},{3,2},{4,5},{5,4},{6,7},{7,6},{8,9},{9,8},{10,11... | collective-permute-start | bytes 2359304 | tf_op jit(solution)/shard_map/ppermute | solution.py:127
  202.7 21.3 %collective-permute-start.31 = (f32[1,256,512]{2,1,0:T(8,128)S(1)}, f32[1,256,512]{2,1,0:T(8,128)}, u32[]{:S(2)}, u32[]{:S(2)}) collective-permute-start(f32[1,256,512]{2,1,0:T(8,128)S(1)} %part_of.7.refs_14_), channel_id=1, source_target_pairs={{8,0},{12,4},{16,24},{20,28},{9,1},{13,5},{17,25},{21,29},{10,2},{... | collective-permute-start | bytes 1572872 | tf_op jit(solution)/shard_map/ppermute | solution.py:117
  216.6 39.8 %collective-permute-start.32 = (f32[2,256,512]{2,1,0:T(8,128)S(1)}, f32[2,256,512]{2,1,0:T(8,128)S(1)}, u32[]{:S(2)}, u32[]{:S(2)}) collective-permute-start(f32[2,256,512]{2,1,0:T(8,128)S(1)} %collective-permute-done.25.refs_1_.refs_2_), channel_id=1, source_target_pairs={{8,12},{12,8},{16,20},{20,16},{9,13},{13,9},{17,21},{21,17},{10,14... | collective-permute-start | bytes 3145736 | tf_op jit(solution)/shard_map/ppermute | solution.py:121
  217.4 37.6 %collective-permute-start.16 = (f32[6,128,256]{2,1,0:T(8,128)S(1)}, f32[6,128,256]{2,1,0:T(8,128)S(1)}, u32[]{:S(2)}, u32[]{:S(2)}) collective-permute-start(f32[6,128,256]{2,1,0:T(8,128)S(1)} %own_blocks.5.refs_2_.refs_1_), channel_id=1, source_target_pairs={{0,1},{1,0},{2,3},{3,2},{4,5},{5,4},{6,7},{7,6},{8,9},{9,8},{10,11... | collective-permute-start | bytes 2359304 | tf_op jit(solution)/shard_map/ppermute | solution.py:126
  217.4 37.6 %collective-permute-start.18 = (f32[6,128,256]{2,1,0:T(8,128)S(1)}, f32[6,128,256]{2,1,0:T(8,128)S(1)}, u32[]{:S(2)}, u32[]{:S(2)}) collective-permute-start(f32[6,128,256]{2,1,0:T(8,128)S(1)} %collective-permute-done.17.refs_3_), channel_id=1, source_target_pairs={{0,1},{1,0},{2,3},{3,2},{4,5},{5,4},{6,7},{7,6},{8,9},{9,8},{10,11... | collective-permute-start | bytes 2359304 | tf_op jit(solution)/shard_map/ppermute | solution.py:127
  226.4 30.0 %collective-permute-start.33 = (f32[1,256,512]{2,1,0:T(8,128)}, f32[1,256,512]{2,1,0:T(8,128)}, u32[]{:S(2)}, u32[]{:S(2)}) collective-permute-start(f32[1,256,512]{2,1,0:T(8,128)} %collective-permute-done.31.refs_3_), channel_id=1, source_target_pairs={{0,4},{4,0},{24,28},{28,24},{1,5},{5,1},{25,29},{29,25},{2,6},{6,2... | collective-permute-start | bytes 1572872 | tf_op jit(solution)/shard_map/ppermute | solution.py:121
  (29 other events, 499.5 us)
Sparse Core Ops, SparseCore 0:
  60.0 46.3 reduce-scatter.1

commit v7 on v6

--- a/solution.py
+++ b/solution.py
@@ -89,27 +89,64 @@
 LANES = 128
 VMEM = pl.BlockSpec(memory_space=pltpu.VMEM)
 SMEM = pl.BlockSpec(memory_space=pltpu.SMEM)
+ANY = pl.BlockSpec(memory_space=pl.ANY)
 PARAMS = pltpu.CompilerParams(vmem_limit_bytes=48 * 2**20)
-ANY = pl.BlockSpec(memory_space=pl.ANY)
+NOTHING = pl.CostEstimate(flops=128, bytes_accessed=128, transcendentals=0)
 PAIRS = ((0, 1), (1, 0), (2, 3), (3, 2))
+INWARD = ((0, 1), (3, 2))
 MIDDLE = ((1, 2), (2, 1))
 OUTWARD = ((1, 0), (2, 3))
-ENDS = (0, 3)
-INNER = (1, 2)
-
-
-def ordered(body, arrays, in_specs, after=(), **call):
-    count = len(arrays)
-
-    def short(*refs):
-        body(*refs[:count], *refs[count + len(after) :])
-
-    return pl.pallas_call(
-        short,
-        in_specs=list(in_specs) + [ANY] * len(after),
-        compiler_params=PARAMS,
-        **call,
-    )(*arrays, *after)
+
+
+class Order:
+    def __init__(self, clock):
+        self.clock = clock
+
+    def call(self, body, arrays, in_specs, *, out_shape, out_specs, scalars=(), grid=(), scratch_shapes=(), name):
+        several = isinstance(out_shape, tuple)
+        shapes = out_shape if several else (out_shape,)
+        specs = tuple(out_specs) if several else (out_specs,)
+        held, count, outs = len(scalars), len(arrays), len(shapes)
+
+        def short(*refs):
+            ins = refs[: held + count]
+            rest = refs[held + count + 1 :]
+            body(*ins, *rest[:outs], *rest[outs + 1 :])
+
+        result = pl.pallas_call(
+            short,
+            out_shape=shapes + (jax.ShapeDtypeStruct(self.clock.shape, self.clock.dtype),),
+            grid_spec=pltpu.PrefetchScalarGridSpec(
+                num_scalar_prefetch=held,
+                grid=grid,
+                in_specs=list(in_specs) + [ANY],
+                out_specs=specs + (ANY,),
+                scratch_shapes=scratch_shapes,
+            ),
+            input_output_aliases={held + count: outs},
+            compiler_params=PARAMS,
+            cost_estimate=NOTHING,
+            name=name,
+        )(*scalars, *arrays, self.clock)
+        self.clock = result[-1]
+        return result[:-1] if several else result[0]
+
+    def wait(self, *arrays):
+        def body(*refs):
+            pass
+
+        every = arrays + (self.clock,)
+        result = pl.pallas_call(
+            body,
+            out_shape=tuple(jax.ShapeDtypeStruct(a.shape, a.dtype) for a in every),
+            in_specs=[ANY] * len(every),
+            out_specs=(ANY,) * len(every),
+            input_output_aliases={i: i for i in range(len(every))},
+            cost_estimate=NOTHING,
+            name="wait",
+        )(*every)
+        self.clock = result[-1]
+        return result[0] if len(arrays) == 1 else result[:-1]
 
 
 def lines(array, hops):
@@ -117,107 +154,77 @@
     return lax.ppermute(array, "rep", perm)
 
 
-def sides(array, levels=range(LEVELS)):
-    return lax.ppermute(array, "rep", [(2 * z + y, 2 * z + 1 - y) for z in levels for y in range(2)])
-
-
-def share(array):
-    across = lax.ppermute(array, "shard", [(q, q ^ 2) for q in range(4)])
-    beside = lax.ppermute(array, "shard", [(q, q ^ 1) for q in range(4)])
-    both = lax.ppermute(across, "shard", [(q, q ^ 1) for q in range(4)])
-    return (array, beside, across, both)
+def flipped(array, axis, flip):
+    return lax.ppermute(array, axis, [(r, r ^ flip) for r in range(lax.axis_size(axis))])
 
 
 def device_block(level, column, i):
     return lax.rem(OWN * level + HALF * column + i, BLOCKS)
 
 
-def turn_tokens(place, tokens):
+def turn_tokens(order, place, tokens):
     rows = tokens.shape[0]
     slab = BLOCK // 4
 
-    def body(place, tokens, piece, theirs):
+    def body(place, tokens, piece):
         start = pl.multiple_of(place[2] * slab, slab)
         for b in range(BLOCKS):
             piece[b] = tokens[:, pl.ds(pl.multiple_of(BLOCK * b + start, slab), slab)].astype(
                 jnp.float32
             ).T
-        for i in range(HALF):
-            theirs[i] = piece[device_block(place[0], 1 - place[1], i)]
-
-    return pl.pallas_call(
-        body,
-        out_shape=(
-            jax.ShapeDtypeStruct((BLOCKS, slab, rows), jnp.float32),
-            jax.ShapeDtypeStruct((HALF, slab, rows), jnp.float32),
-        ),
-        in_specs=[SMEM, VMEM],
-        out_specs=(VMEM, VMEM),
-        compiler_params=PARAMS,
+
+    return order.call(
+        body,
+        (place, tokens),
+        [SMEM, VMEM],
+        out_shape=jax.ShapeDtypeStruct((BLOCKS, slab, rows), jnp.float32),
+        out_specs=VMEM,
         name="turn_tokens",
-    )(place, tokens)
-
-
-def other_blocks(place, inner, ends=None, after=()):
+    )
+
+
+def column_blocks(order, place, slots, own, got=None, part=(0, 0)):
+    arrays = [a for slot in slots for a in slot if a is not None]
+    begin, extra = part
+    first = slots[0][0]
+    count = HALF * len(slots)
+
     def body(place, *refs):
-        inner, out = refs[0], refs[-1]
-        for i in range(HALF):
-            if ends is None:
-                out[i] = inner[device_block(place[0], 1 - place[1], i)]
-                continue
-            inside = jnp.logical_or(place[0] == 1, place[0] == 2)
-
-            @pl.when(inside)
-            def _():
-                out[i] = inner[device_block(place[0], 1 - place[1], i)]
-
-            @pl.when(jnp.logical_not(inside))
-            def _():
-                out[i] = refs[1][HALF * (1 - place[1]) + i]
-
-    arrays = (place, inner) if ends is None else (place, inner, ends)
-    return ordered(
-        body,
-        arrays,
-        [SMEM] + [VMEM] * (len(arrays) - 1),
-        after,
-        out_shape=jax.ShapeDtypeStruct((HALF,) + inner.shape[1:], inner.dtype),
+        out = refs[-1]
+        left = list(refs)
+        column = place[1] if own else 1 - place[1]
+        inside = jnp.logical_or(place[0] == 1, place[0] == 2)
+        for n, (_, ends) in enumerate(slots):
+            inner = left.pop(0)
+            end = None if ends is None else left.pop(0)
+            for i in range(HALF):
+                block = device_block(place[0], column, i)
+                if end is None:
+                    out[HALF * n + i] = inner[block]
+                    continue
+
+                @pl.when(inside)
+                def _():
+                    out[HALF * n + i] = inner[block]
+
+                @pl.when(jnp.logical_not(inside))
+                def _():
+                    out[HALF * n + i] = end[HALF * column + i]
+
+        for i in range(extra):
+            out[count + i] = left[0][begin + i]
+
+    return order.call(
+        body,
+        [place] + arrays + ([] if got is None else [got]),
+        [SMEM] + [VMEM] * (len(arrays) + (extra > 0)),
+        out_shape=jax.ShapeDtypeStruct((count + extra,) + first.shape[1:], first.dtype),
         out_specs=VMEM,
-        name="other_blocks",
-    )
-
-
-def own_blocks(place, got, inner, ends=None, after=()):
-    def body(place, got, *refs):
-        inner, out = refs[0], refs[-1]
-        for i in range(HALF):
-            out[HALF + i] = got[i]
-            if ends is None:
-                out[i] = inner[device_block(place[0], place[1], i)]
-                continue
-            inside = jnp.logical_or(place[0] == 1, place[0] == 2)
-
-            @pl.when(inside)
-            def _():
-                out[i] = inner[device_block(place[0], place[1], i)]
-
-            @pl.when(jnp.logical_not(inside))
-            def _():
-                out[i] = refs[1][HALF * place[1] + i]
-
-    arrays = (place, got, inner) if ends is None else (place, got, inner, ends)
-    return ordered(
-        body,
-        arrays,
-        [SMEM] + [VMEM] * (len(arrays) - 1),
-        after,
-        out_shape=jax.ShapeDtypeStruct((OWN,) + inner.shape[1:], inner.dtype),
-        out_specs=VMEM,
-        name="own_blocks",
-    )
-
-
-def gate(place, tokens, in_weight, kernel, out_grad, after=()):
+        name="own_blocks" if own else "other_blocks",
+    )
+
+
+def gate(order, place, tokens, in_weight, kernel, out_grad):
     rows, features = tokens.shape
     chans = in_weight.shape[2]
     taps = kernel.shape[0]
@@ -226,7 +233,7 @@
     deep = features // steps
     pad = 8
 
-    def body(place, tokens, weight, kernel, out_grad, own, grad, wide, inner, middle, total, held, pads, back):
+    def body(place, tokens, weight, kernel, out_grad, own, grad, first, inner, middle, total, held, pads, back):
         step = pl.program_id(1)
         for s in range(3):
             now = jnp.dot(tokens[...], weight[s], preferred_element_type=jnp.float32)
@@ -277,16 +284,16 @@
                         grad[j, s : s + 1, lanes] = jnp.sum(sums[s][j], axis=0, keepdims=True)
             for s in range(3):
                 own[s] = held[s].astype(jnp.bfloat16)
-                wide[s] = held[s]
             level = place[0]
+            first[0] = held[2 - 2 * lax.rem(level, 2)]
             low = jnp.where(level <= 1, 0, 1)
             for i in range(2):
                 inner[i] = held[low + i]
                 middle[i] = held[1 - low + i]
 
-    three = jax.ShapeDtypeStruct((3, rows, chans), jnp.float32)
+    one = jax.ShapeDtypeStruct((1, rows, chans), jnp.float32)
     two = jax.ShapeDtypeStruct((2, rows, chans), jnp.float32)
-    return ordered(
+    return order.call(
         body,
         (place, tokens, in_weight, kernel, out_grad),
         [
@@ -296,11 +303,10 @@
             pl.BlockSpec((taps, 3, width), lambda c, k: (0, 0, c)),
             pl.BlockSpec((rows, width), lambda c, k: (0, c)),
         ],
-        after,
         out_shape=(
             jax.ShapeDtypeStruct((3, rows, chans), jnp.bfloat16),
             jax.ShapeDtypeStruct((taps, 3, chans), jnp.float32),
-            three,
+            one,
             two,
             two,
         ),
@@ -308,7 +314,7 @@
         out_specs=(
             pl.BlockSpec((3, rows, width), lambda c, k: (0, 0, c)),
             pl.BlockSpec((taps, 3, width), lambda c, k: (0, 0, c)),
-            pl.BlockSpec((3, rows, width), lambda c, k: (0, 0, c)),
+            pl.BlockSpec((1, rows, width), lambda c, k: (0, 0, c)),
             pl.BlockSpec((2, rows, width), lambda c, k: (0, 0, c)),
             pl.BlockSpec((2, rows, width), lambda c, k: (0, 0, c)),
         ),
@@ -322,58 +328,95 @@
     )
 
 
-def relay_payloads(place, pair, after=()):
-    def body(place, pair, across, side):
-        low = jnp.where(place[0] <= 1, 0, 1)
-        for i in range(2):
-            across[i] = pair[1 - low + i]
-            side[i] = pair[low + i]
-
-    two = jax.ShapeDtypeStruct((2,) + pair.shape[1:], pair.dtype)
-    return ordered(
-        body,
-        (place, pair),
-        [SMEM, VMEM],
-        after,
+def relay_payload(order, place, first, inner):
+    def body(place, first, inner, out, side):
+        @pl.when(place[0] <= 1)
+        def _():
+            out[0] = inner[1]
+            out[1] = first[0]
+
+        @pl.when(place[0] > 1)
+        def _():
+            out[0] = first[0]
+            out[1] = inner[0]
+
+        level_own(place, inner, first, side)
+
+    two = jax.ShapeDtypeStruct(inner.shape, inner.dtype)
+    return order.call(
+        body,
+        (place, first, inner),
+        [SMEM, VMEM, VMEM],
         out_shape=(two, two),
         out_specs=(VMEM, VMEM),
-        name="relay_payloads",
-    )
-
-
-def part_of(place, array, step, count, after=()):
+        name="relay_payload",
+    )
+
+
+def level_own(place, inner, ends, out):
+    inside = jnp.logical_or(place[0] == 1, place[0] == 2)
+
+    @pl.when(inside)
+    def _():
+        out[...] = inner[...]
+
+    @pl.when(jnp.logical_not(inside))
+    def _():
+        out[jnp.where(place[0] == 0, 0, 1)] = ends[0]
+        out[jnp.where(place[0] == 0, 1, 0)] = ends[0]
+
+
+def side_payload(order, place, inner, ends):
+    return order.call(
+        level_own,
+        (place, inner, ends),
+        [SMEM, VMEM, VMEM],
+        out_shape=jax.ShapeDtypeStruct(inner.shape, inner.dtype),
+        out_specs=VMEM,
+        name="side_payload",
+    )
+
+
+def part_of(order, place, array, step, count):
     def body(place, array, out):
         start = jnp.where(place[0] <= 1, 0, step)
         for i in range(count):
             out[i] = array[start + i]
 
-    return ordered(
+    return order.call(
         body,
         (place, array),
         [SMEM, VMEM],
-        after,
         out_shape=jax.ShapeDtypeStruct((count,) + array.shape[1:], array.dtype),
         out_specs=VMEM,
         name="part_of",
     )
 
 
-def add(a, b, scale, after=()):
-    def body(a, b, out):
-        out[...] = (a[...] + b[...]) * scale
-
-    return ordered(
-        body,
-        (a, b),
-        [VMEM, VMEM],
-        after,
-        out_shape=jax.ShapeDtypeStruct(a.shape, a.dtype),
-        out_specs=VMEM,
+def add(order, mine, other, scale=1.0):
+    pair = mine.ndim == 3 and mine.shape[0] == 2
+
+    def body(mine, other, out, again):
+        if pair:
+            out[...] = mine[1] + other[1]
+            again[...] = mine[0] + other[0]
+        else:
+            total = (mine[...] + other[...]) * scale
+            out[...] = total
+            again[...] = total
+
+    shape = jax.ShapeDtypeStruct(mine.shape[1:] if pair else mine.shape, mine.dtype)
+    return order.call(
+        body,
+        (mine, other),
+        [VMEM] * 2,
+        out_shape=(shape, shape),
+        out_specs=(VMEM,) * 2,
         name="add",
     )
 
 
-def arrange_tokens(place, own, slots, after=()):
+def arrange_tokens(order, place, own, slots):
     slab = BLOCK // 4
     rows = slots[0][0].shape[2]
     counts = [slot[0].shape[0] // HALF for slot in slots]
@@ -400,18 +443,17 @@
             at += count
 
     arrays = [place] + ([] if own is None else [own]) + [piece for slot in slots for piece in slot]
-    return ordered(
+    return order.call(
         body,
         arrays,
         [SMEM] + [VMEM] * (len(arrays) - 1),
-        after,
         out_shape=jax.ShapeDtypeStruct((HALF, BLOCK, total * rows), jnp.bfloat16),
         out_specs=VMEM,
         name="arrange_tokens",
     )
 
 
-def weight_part(place, tok, slots, scale=None, so_far=None, after=()):
+def weight_part(order, place, tok, slots, scale=None, so_far=None):
     rows, chans = slots[0][0].shape[1:]
     count = len(slots)
     arrays = [a for slot in slots for a in slot if a is not None]
@@ -464,13 +506,12 @@
     whole = lambda a: pl.BlockSpec(a.shape, lambda i: (0,) * a.ndim)
     more = [] if so_far is None else [so_far]
     part = pl.BlockSpec((BLOCK, chans), lambda i: (i, 0))
-    return ordered(
+    return order.call(
         body,
         [place, tok] + arrays + more,
         [SMEM, pl.BlockSpec((None, BLOCK, count * rows), lambda i: (i, 0, 0))]
         + [whole(a) for a in arrays]
         + [part] * len(more),
-        after,
         out_shape=jax.ShapeDtypeStruct((HALF * BLOCK, chans), jnp.float32),
         grid=(HALF,),
         out_specs=part,
@@ -479,11 +520,12 @@
     )
 
 
-def token_part(grads, weight, after=()):
+def token_part(order, quarters, grads, weight):
     rows, chans = grads.shape[1:]
     wide = weight.shape[1] // 4
-
-    def body(grads, weight, out):
+    count = quarters.shape[0]
+
+    def body(quarters, grads, weight, out):
         now = lax.dot_general(
             grads[...], weight[...], (((1,), (1,)), ((), ())), preferred_element_type=jnp.float32
         )
@@ -496,94 +538,109 @@
         def _():
             out[...] += now
 
-    return ordered(
+    return order.call(
         body,
         (grads, weight),
         [
-            pl.BlockSpec((None, rows, chans), lambda i, s: (s, 0, 0)),
-            pl.BlockSpec((None, wide, chans), lambda i, s: (s, i, 0)),
+            pl.BlockSpec((None, rows, chans), lambda i, s, quarters: (s, 0, 0)),
+            pl.BlockSpec((None, wide, chans), lambda i, s, quarters: (s, quarters[i], 0)),
         ],
-        after,
-        out_shape=jax.ShapeDtypeStruct((rows, 4 * wide), jnp.float32),
-        grid=(4, 3),
-        out_specs=pl.BlockSpec((rows, wide), lambda i, s: (0, i)),
+        scalars=(quarters,),
+        out_shape=jax.ShapeDtypeStruct((count, rows, wide), jnp.float32),
+        grid=(count, 3),
+        out_specs=pl.BlockSpec((None, rows, wide), lambda i, s, quarters: (i, 0, 0)),
         name="token_part",
     )
 
 
 def lined(tokens, in_weight, kernel, out_grad):
-    rows, features = tokens.shape
-    rep = lax.axis_index("rep")
+    rows = tokens.shape[0]
+    rep, quarter = lax.axis_index("rep"), lax.axis_index("shard")
     level, column = rep // 2, rep % 2
-    place = jnp.stack([level, column, lax.axis_index("shard")]).astype(jnp.int32)
+    place = jnp.stack([level, column, quarter]).astype(jnp.int32)
     scale = 1.0 / math.sqrt(rows * lax.axis_size("rep"))
-
-    def tap_step(taps, bit):
-        return lax.ppermute(taps, "rep", [(r, r ^ bit) for r in range(2 * LEVELS)])
-
-    piece, theirs = turn_tokens(place, tokens)
+    order = Order(jnp.zeros((8, LANES), jnp.float32))
+    quarters = [jnp.bitwise_xor(quarter, k).astype(jnp.int32) for k in (3, 1, 2, 0)]
+    piece = turn_tokens(order, place, tokens)
     near = lines(piece, PAIRS)
     mid = lines(piece, MIDDLE)
-    got0 = sides(theirs)
-    own, taps, wide, inner_out, middle_out = gate(
-        place, tokens, in_weight, kernel, out_grad, after=(theirs,)
-    )
-    pair = lines(wide, PAIRS)
-    own_y = sides(inner_out)
-    slots = [share(got0)]
-
+    own, taps, first_out, inner_out, middle_out = gate(
+        order, place, tokens, in_weight, kernel, out_grad
+    )
+    own_y = flipped(inner_out, "rep", 1)
+    inner = lines(inner_out, INWARD)
+    first = lines(first_out, PAIRS)
+    middle = lines(middle_out, MIDDLE)
+    taps1 = flipped(taps, "rep", 1)
+    near = order.wait(near)
     far = lines(near, MIDDLE)
-    send1 = other_blocks(place, near, after=(inner_out,))
-    got1 = sides(send1)
-    send = part_of(place, mid, BLOCKS - OWN, OWN, after=(near, send1))
-    outer2 = lines(send, OUTWARD)
-    middle = lines(middle_out, MIDDLE)
-    partial = token_part(own, in_weight, after=(send, slots[0][1]))
-    token_grad = lax.psum_scatter(partial, "shard", scatter_dimension=1, tiled=True)
-
-    tap1 = tap_step(taps, 1)
-    send2 = other_blocks(place, mid, outer2, after=(partial, slots[0][3]))
-    got2 = sides(send2)
-    send = part_of(place, far, BLOCKS - OWN, OWN, after=(send2,))
-    outer3 = lines(send, OUTWARD)
-    own1 = own_blocks(place, got1, near, after=(send,))
-    slots.append(share(own1))
-    relay_out, side1_out = relay_payloads(place, pair, after=(own1,))
-    relayed = lines(relay_out, MIDDLE)
-    side1 = sides(side1_out)
-    taps = add(taps, tap1, 1.0, after=(relay_out,))
-    own2 = own_blocks(place, got2, mid, outer2, after=(taps, own_y))
-    slots.append(share(own2))
-    tap2 = tap_step(taps, 2)
-    send3 = other_blocks(place, far, outer3, after=(own2,))
-    got3 = sides(send3)
-    send = part_of(place, middle, 1, 1, after=(send3,))
-    middle_end = lines(send, OUTWARD)
-    side2 = sides(middle, INNER)
-    own3 = own_blocks(place, got3, far, outer3, after=(send,))
-    slots.append(share(own3))
-    taps = add(taps, tap2, 1.0, after=(own3,))
-    tap4 = tap_step(taps, 4)
-    side2_end = sides(middle_end, ENDS)
-    send = part_of(place, relayed, 1, 1, after=(taps,))
-    relayed_end = lines(send, OUTWARD)
-    side3 = sides(relayed, INNER)
-    tok = arrange_tokens(place, tokens, slots[:3], after=(send,))
-    early = [(own, None), (own_y, None), (pair, None), (side1, None)]
-    early += [(middle, middle_end), (side2, side2_end)]
-    so_far = weight_part(place, tok, early)
-    tok = arrange_tokens(place, None, slots[3:], after=(so_far,))
-    taps = add(taps, tap4, scale, after=(tok,))
-    side3_end = sides(relayed_end, ENDS)
-    weight_grad = weight_part(
-        place,
-        tok,
-        [(relayed, relayed_end), (side3, side3_end)],
-        scale,
-        so_far,
-        after=(taps,),
-    )
-    return (token_grad.astype(jnp.bfloat16), weight_grad, taps)
+    over = column_blocks(order, place, [(piece, None), (near, None)], False)
+    got1 = flipped(over, "rep", 1)
+    mid = order.wait(mid)
+    outer2 = lines(part_of(order, place, mid, BLOCKS - OWN, OWN), OUTWARD)
+    send = token_part(order, jnp.stack(quarters[:2]), own, in_weight)
+    summed = flipped(send, "shard", 1)
+    keep = token_part(order, jnp.stack(quarters[2:]), own, in_weight)
+    own_y, inner, outer2 = order.wait(own_y, inner, outer2)
+    over = column_blocks(order, place, [(mid, outer2)], False)
+    got2 = flipped(over, "rep", 1)
+    far = order.wait(far)
+    outer3 = lines(part_of(order, place, far, BLOCKS - OWN, OWN), OUTWARD)
+    first = order.wait(first)
+    relay, side1 = relay_payload(order, place, first, inner)
+    relayed = lines(relay, MIDDLE)
+    side1 = flipped(side1, "rep", 1)
+    middle, got2 = order.wait(middle, got2)
+    own2 = column_blocks(order, place, [(mid, outer2)], True, got2, (0, HALF))
+    across2 = flipped(own2, "shard", 2)
+    beside2 = flipped(own2, "shard", 1)
+    got1 = order.wait(got1)
+    own1 = column_blocks(order, place, [(near, None)], True, got1, (0, OWN))
+    across1 = flipped(own1, "shard", 2)
+    beside1 = flipped(own1, "shard", 1)
+    middle_end = lines(part_of(order, place, middle, 1, 1), OUTWARD)
+    summed = order.wait(summed)
+    token_grad, away = add(order, keep, summed)
+    last = flipped(away, "shard", 2)
+    across1, beside1, side1, outer3, relayed = order.wait(
+        across1, beside1, side1, outer3, relayed
+    )
+    both1 = flipped(across1, "shard", 1)
+    over = column_blocks(order, place, [(far, outer3)], False)
+    got3 = flipped(over, "rep", 1)
+    middle_end = order.wait(middle_end)
+    relayed_end = lines(part_of(order, place, relayed, 1, 1), OUTWARD)
+    beside2, taps1 = order.wait(beside2, taps1)
+    taps, taps_out = add(order, taps, taps1)
+    taps2 = flipped(taps_out, "rep", 2)
+    relayed_end = order.wait(relayed_end)
+    side2 = flipped(side_payload(order, place, middle, middle_end), "rep", 1)
+    across2, got3 = order.wait(across2, got3)
+    both2 = flipped(across2, "shard", 1)
+    own3 = column_blocks(order, place, [(far, outer3)], True, got3, (0, HALF))
+    across3 = flipped(own3, "shard", 2)
+    beside3 = flipped(own3, "shard", 1)
+    both2, both1 = order.wait(both2, both1)
+    side3 = flipped(side_payload(order, place, relayed, relayed_end), "rep", 1)
+    tok = arrange_tokens(order, place, tokens, [(own1, beside1, across1, both1)])
+    early = [(own, None), (inner, first), (own_y, None), (side1, None)]
+    so_far = weight_part(order, place, tok, early)
+    side2, across3, beside3 = order.wait(side2, across3, beside3)
+    both3 = flipped(across3, "shard", 1)
+    both3 = order.wait(both3)
+    tok = arrange_tokens(order, place, None, [(own2, beside2, across2, both2)])
+    taps2 = order.wait(taps2)
+    taps, taps_out = add(order, taps, taps2)
+    taps4 = flipped(taps_out, "rep", 4)
+    so_far = weight_part(order, place, tok, [(middle, middle_end), (side2, None)], None, so_far)
+    last = order.wait(last)
+    token_grad = (token_grad + last).astype(jnp.bfloat16)
+    tok = arrange_tokens(order, place, None, [(own3, beside3, across3, both3)])
+    side3, taps4 = order.wait(side3, taps4)
+    taps, _ = add(order, taps, taps4, scale=scale)
+    late = [(relayed, relayed_end), (side3, None)]
+    weight_grad = weight_part(order, place, tok, late, scale, so_far)
+    return (token_grad, weight_grad, taps)
 
 
 def solution(mesh):

time: 272 us -> 241 us (0.89)
  waiting for transfers between devices: 128 us -> 41.9 us
  local copies, waits for them, and re-layouts: 10.8 us -> 67.2 us
  Pallas kernels: 54.7 us -> 86.2 us
  starting transfers between devices: 60.7 us -> 39.8 us
  between operations: 14.5 us -> 1.09 us
    unnamed x36 -> x196, local copies, waits for them, and re-layouts: 10.8 us -> 67.2 us
    ppermute x25 -> x21, waiting for transfers between devices: 69.4 us -> 19.4 us  [flipped(): lax.ppermute(array, axis, [(r, r ^ flip) for r in range(lax.axis_size(axi...]
    ppermute x10 -> x11, waiting for transfers between devices: 58.6 us -> 22.4 us  [lines(): return lax.ppermute(array, 'rep', perm)]
    pallas_call x21 -> x46, Pallas kernels: 54.7 us -> 86.2 us  [the longest x27 86.2 us: call(): pl.pallas_call(short, out_shape=shapes + (jax.ShapeDtypeStruct(self.clock...]
    ppermute x25 -> x21, starting transfers between devices: 44 us -> 16.7 us  [flipped(): lax.ppermute(array, axis, [(r, r ^ flip) for r in range(lax.axis_size(axi...]
    ppermute x10 -> x11, starting transfers between devices: 16.7 us -> 23 us  [lines(): return lax.ppermute(array, 'rep', perm)]
  transfers between devices with their start and end apart: 36 -> 32, of which waited for: 13 -> 9; matrix products, arithmetic and copies ran while one was open for 1% -> 1% of each run, Pallas kernels for 16% -> 33%
where the time goes in v7:
time: 241 us; the launch traced here: 239 us
  Pallas kernels  86.2 us (36%)
  local copies, waits for them, and re-layouts  67.2 us (28%)
  waiting for transfers between devices  41.9 us (17%)
  starting transfers between devices  39.8 us (17%)
  other arithmetic  2.71 us (1%)
    pallas_call x27, Pallas kernels, call(): pl.pallas_call(short, out_shape=shapes + (jax.ShapeDtypeStruct(self.clock...  86.2 us
    unnamed x196, local copies, waits for them, and re-layouts  67.2 us
    ppermute x11, starting transfers between devices, lines(): return lax.ppermute(array, 'rep', perm)  23 us
    ppermute x11, waiting for transfers between devices, lines(): return lax.ppermute(array, 'rep', perm)  22.4 us
    ppermute x21, waiting for transfers between devices, flipped(): lax.ppermute(array, axis, [(r, r ^ flip) for r in range(lax.axis_size(axi...  19.4 us
    ppermute x21, starting transfers between devices, flipped(): lax.ppermute(array, axis, [(r, r ^ flip) for r in range(lax.axis_size(axi...  16.7 us
  transfers between devices with their start and end apart: 32, of which 9 were waited for; matrix products, arithmetic and copies ran while one was open for 1% of the time, Pallas kernels for 33%

profile of v7, /device:TPU:0, one launch (start us, length us, event | category | flops | bytes accessed | tf_op | source)
XLA Modules:
  0.0 238.8 jit_solution(205254195547850457)
XLA Ops:
  4.1 3.0 %collective-permute-start.1 = (f32[8,128,256]{2,1,0:T(8,128)}, f32[8,128,256]{2,1,0:T(8,128)S(1)}, u32[]{:S(2)}, u32[]{:S(2)}) collective-permute-start(f32[8,128,256]{2,1,0:T(8,128)} %get-tuple-element.117.refs_1_), channel_id=1, source_target_pairs={{0,8},{4,12},{8,0},{12,4},{16,24},{20,28},{24,16},{28,20},{1,9},{5... | collective-permute-start | bytes 3145736 | tf_op jit(solution)/shard_map/ppermute | solution.py:154
  7.9 16.6 %gate.1 = (bf16[3,256,512]{2,1,0:T(8,128)(2,1)S(1)}, f32[7,3,512]{2,1,0:T(4,128)S(1)}, f32[1,256,512]{2,1,0:T(8,128)}, f32[2,256,512]{2,1,0:T(8,128)}, f32[2,256,512]{2,1,0:T(8,128)}, /*index=5*/f32[8,128]{1,0:T(8,128)S(1)}) custom-call(s32[3]{0:T(128)S(1)} %pad_add_fusion.1.refs_0_, bf16[256,4096]{1,0:T(8,128)(2,1)S(1)} %copy-done, ...), custom_call_target="tpu_custom_call", output_to_operand_aliasing={{5}: (5, {})} | custom-call | flops 128 | bytes 128 | tf_op jit(solution)/shard_map/gate/pallas_call | solution.py:116
  28.1 7.2 %collective-permute-start.5 = (f32[2,256,512]{2,1,0:T(8,128)}, f32[2,256,512]{2,1,0:T(8,128)}, u32[]{:S(2)}, u32[]{:S(2)}) collective-permute-start(f32[2,256,512]{2,1,0:T(8,128)} %get-tuple-element.129), channel_id=1, source_target_pairs={{0,8},{4,12},{24,16},{28,20},{1,9},{5,13},{25,17},{29,21},{2,10},{... | collective-permute-start | bytes 3145736 | tf_op jit(solution)/shard_map/ppermute | solution.py:154
  39.0 2.3 other_blocks.3
  48.9 7.9 %token_part.2 = (f32[2,256,1024]{2,1,0:T(8,128)}, f32[8,128]{1,0:T(8,128)S(1)}) custom-call(s32[2]{0:T(128)S(1)} %pad_add_fusion.2.refs_0_, bf16[3,256,512]{2,1,0:T(8,128)(2,1)S(1)} %copy-done.61, bf16[3,4096,512]{2,1,0:T(8,128)(2,1)} %refs_2_.5, f32[8,128]{1,0:T(8,128)S(1)} %copy-done.19), custom_call_target="tpu_custom_call", output_to_operand_aliasing={{1}: (3, {})} | custom-call | flops 128 | bytes 128 | tf_op jit(solution)/shard_map/token_part/pallas_call | solution.py:116
  58.2 4.8 %collective-permute-start.8 = (f32[1,256,512]{2,1,0:T(8,128)}, f32[1,256,512]{2,1,0:T(8,128)}, u32[]{:S(2)}, u32[]{:S(2)}) collective-permute-start(f32[1,256,512]{2,1,0:T(8,128)} %get-tuple-element.135), channel_id=1, source_target_pairs={{0,8},{4,12},{8,0},{12,4},{16,24},{20,28},{24,16},{28,20},{1,9},{5... | collective-permute-start | bytes 1572872 | tf_op jit(solution)/shard_map/ppermute | solution.py:154
  63.0 6.6 %collective-permute-done.6.refs_2_ = f32[6,128,256]{2,1,0:T(8,128)} collective-permute-done((f32[6,128,256]{2,1,0:T(8,128)}, f32[6,128,256]{2,1,0:T(8,128)}, u32[]{:S(2)}, u32[]{:S(2)}) %collective-permute-start.6) | collective-permute-done | bytes 786464 | tf_op jit(solution)/shard_map/ppermute | solution.py:154
  70.8 6.6 %token_part.3 = (f32[2,256,1024]{2,1,0:T(8,128)S(1)}, f32[8,128]{1,0:T(8,128)S(1)}) custom-call(s32[2]{0:T(128)S(1)} %pad_add_fusion.refs_0_, bf16[3,256,512]{2,1,0:T(8,128)(2,1)S(1)} %copy-done.61, bf16[3,4096,512]{2,1,0:T(8,128)(2,1)} %refs_2_.5, f32[8,128]{1,0:T(8,128)S(1)} %copy-done.21), custom_call_target="tpu_custom_call", output_to_operand_aliasing={{1}: (3, {})} | custom-call | flops 128 | bytes 128 | tf_op jit(solution)/shard_map/token_part/pallas_call | solution.py:116
  92.5 2.6 %relay_payload.1 = (f32[2,256,512]{2,1,0:T(8,128)S(1)}, f32[2,256,512]{2,1,0:T(8,128)}, f32[8,128]{1,0:T(8,128)S(1)}) custom-call(s32[3]{0:T(128)S(1)} %pad_add_fusion.1.refs_0_, f32[1,256,512]{2,1,0:T(8,128)} %get-tuple-element.140.refs_1_.refs_4_, f32[2,256,512]{2,1,0:T(8,128)} %get-tuple-element.141.refs_2_.refs_3_, ...), custom_call_target="tpu_custom_call", output_to_operand_aliasing={{2}: (3, {})} | custom-call | flops 128 | bytes 128 | tf_op jit(solution)/shard_map/relay_payload/pallas_call | solution.py:116
  97.2 5.0 %collective-permute-done.7.refs_1_ = f32[3,128,256]{2,1,0:T(8,128)S(1)} collective-permute-done((f32[3,128,256]{2,1,0:T(8,128)}, f32[3,128,256]{2,1,0:T(8,128)S(1)}, u32[]{:S(2)}, u32[]{:S(2)}) %collective-permute-start.7) | collective-permute-done | bytes 393248 | tf_op jit(solution)/shard_map/ppermute | solution.py:158
  104.7 2.2 own_blocks.3
  109.3 2.2 own_blocks.4
  117.1 3.8 %collective-permute-done.16.refs_2_ = f32[2,256,512]{2,1,0:T(8,128)} collective-permute-done((f32[2,256,512]{2,1,0:T(8,128)}, f32[2,256,512]{2,1,0:T(8,128)}, u32[]{:S(2)}, u32[]{:S(2)}) %collective-permute-start.16) | collective-permute-done | bytes 1048608 | tf_op jit(solution)/shard_map/ppermute | solution.py:158
  123.1 2.8 %add.23 = (f32[256,1024]{1,0:T(8,128)S(1)}, f32[256,1024]{1,0:T(8,128)}, f32[8,128]{1,0:T(8,128)S(1)}) custom-call(f32[2,256,1024]{2,1,0:T(8,128)S(1)} %copy-done.68, f32[2,256,1024]{2,1,0:T(8,128)} %get-tuple-element.153.refs_1_, f32[8,128]{1,0:T(8,128)S(1)} %copy-done.33), custom_call_target="tpu_custom_call", output_to_operand_aliasing={{2}: (2, {})} | custom-call | flops 128 | bytes 128 | tf_op jit(solution)/shard_map/add/pallas_call | solution.py:116
  141.7 2.5 %collective-permute-done.13.refs_1_ = f32[7,3,512]{2,1,0:T(4,128)S(1)} collective-permute-done((f32[7,3,512]{2,1,0:T(4,128)S(1)}, f32[7,3,512]{2,1,0:T(4,128)S(1)}, u32[]{:S(2)}, u32[]{:S(2)}) %collective-permute-start.13) | collective-permute-done | bytes 43040 | tf_op jit(solution)/shard_map/ppermute | solution.py:158
  150.8 15.8 %collective-permute-done.22.refs_0_ = f32[1,256,512]{2,1,0:T(8,128)} collective-permute-done((f32[1,256,512]{2,1,0:T(8,128)}, f32[1,256,512]{2,1,0:T(8,128)}, u32[]{:S(2)}, u32[]{:S(2)}) %collective-permute-start.22) | collective-permute-done | bytes 524320 | tf_op jit(solution)/shard_map/ppermute | solution.py:154
  167.3 2.1 side_payload.2
  174.0 2.2 own_blocks.5
  183.3 5.1 %arrange_tokens.3 = (bf16[3,512,1024]{2,1,0:T(8,128)(2,1)}, f32[8,128]{1,0:T(8,128)S(1)}) custom-call(s32[3]{0:T(128)S(1)} %pad_add_fusion.1.refs_0_, bf16[256,4096]{1,0:T(8,128)(2,1)} %refs_1_.5, f32[9,128,256]{2,1,0:T(8,128)} %get-tuple-element.159.refs_2_, f32[9,128,256]{2,1,0:T(8,128)} %get-tuple-element.188.refs_3_, ...), custom_call_target="tpu_custom_call", output_to_operand_aliasing={{1}: (6, {})} | custom-call | flops 128 | bytes 128 | tf_op jit(solution)/shard_map/arrange_tokens/pallas_call | solution.py:116
  188.4 6.6 %weight_part.3 = (f32[1536,512]{1,0:T(8,128)}, f32[8,128]{1,0:T(8,128)S(1)}) custom-call(s32[3]{0:T(128)S(1)} %pad_add_fusion.1.refs_0_, bf16[3,512,1024]{2,1,0:T(8,128)(2,1)} %get-tuple-element.193.refs_1_, bf16[3,256,512]{2,1,0:T(8,128)(2,1)S(1)} %copy-done.62, f32[2,256,512]{2,1,0:T(8,128)} %get-tuple-element.141.refs_2_.refs_3_, ...), custom_call_target="tpu_custom_call", output_to_operand_aliasing={{1}: (7, {})} | custom-call | flops 128 | bytes 128 | tf_op jit(solution)/shard_map/weight_part/pallas_call | solution.py:116
  209.4 5.7 %weight_part.4 = (f32[1536,512]{1,0:T(8,128)}, f32[8,128]{1,0:T(8,128)S(1)}) custom-call(s32[3]{0:T(128)S(1)} %pad_add_fusion.1.refs_0_, bf16[3,512,512]{2,1,0:T(8,128)(2,1)S(1)} %copy-done.72, f32[2,256,512]{2,1,0:T(8,128)S(1)} %copy-done.2, f32[1,256,512]{2,1,0:T(8,128)} %get-tuple-element.173.refs_2_.refs_3_, ...), custom_call_target="tpu_custom_call", output_to_operand_aliasing={{1}: (6, {})} | custom-call | flops 128 | bytes 128 | tf_op jit(solution)/shard_map/weight_part/pallas_call | solution.py:116
  215.8 3.8 %collective-permute-done.11.refs_0_ = f32[256,1024]{1,0:T(8,128)} collective-permute-done((f32[256,1024]{1,0:T(8,128)}, f32[256,1024]{1,0:T(8,128)}, u32[]{:S(2)}, u32[]{:S(2)}) %collective-permute-start.11) | collective-permute-done | bytes 1048608 | tf_op jit(solution)/shard_map/ppermute | solution.py:158
  219.5 2.5 %add_convert_fusion = bf16[256,1024]{1,0:T(8,128)(2,1)} fusion(f32[256,1024]{1,0:T(8,128)} %copy-done.77, f32[256,1024]{1,0:T(8,128)} %get-tuple-element.211), kind=kLoop, calls=%fused_computation | loop fusion | flops 524288 | bytes 2621440 | tf_op jit(solution)/shard_map/convert_element_type | solution.py:637
  233.5 5.4 %weight_part.5 = (f32[1536,512]{1,0:T(8,128)}, f32[8,128]{1,0:T(8,128)S(1)}) custom-call(s32[3]{0:T(128)S(1)} %pad_add_fusion.1.refs_0_, bf16[3,512,512]{2,1,0:T(8,128)(2,1)S(1)} %copy-done.70, f32[2,256,512]{2,1,0:T(8,128)S(1)} %copy-done.7, f32[1,256,512]{2,1,0:T(8,128)} %get-tuple-element.190.refs_2_.refs_3_, ...), custom_call_target="tpu_custom_call", output_to_operand_aliasing={{1}: (6, {})} | custom-call | flops 128 | bytes 128 | tf_op jit(solution)/shard_map/weight_part/pallas_call | solution.py:116
  (287 shorter events, 112.4 us)
Async XLA Ops:
  4.1 31.3 %collective-permute-start.1 = (f32[8,128,256]{2,1,0:T(8,128)}, f32[8,128,256]{2,1,0:T(8,128)S(1)}, u32[]{:S(2)}, u32[]{:S(2)}) collective-permute-start(f32[8,128,256]{2,1,0:T(8,128)} %get-tuple-element.117.refs_1_), channel_id=1, source_target_pairs={{0,8},{4,12},{8,0},{12,4},{16,24},{20,28},{24,16},{28,20},{1,9},{5... | collective-permute-start | bytes 3145736 | tf_op jit(solution)/shard_map/ppermute | solution.py:154
  7.1 34.8 %collective-permute-start = (f32[8,128,256]{2,1,0:T(8,128)}, f32[8,128,256]{2,1,0:T(8,128)S(1)}, u32[]{:S(2)}, u32[]{:S(2)}) collective-permute-start(f32[8,128,256]{2,1,0:T(8,128)} %get-tuple-element.117.refs_1_), channel_id=1, source_target_pairs={{8,16},{12,20},{16,8},{20,12},{9,17},{13,21},{17,9},{21,13},{10,18... | collective-permute-start | bytes 3145736 | tf_op jit(solution)/shard_map/ppermute | solution.py:154
  26.6 30.8 %collective-permute-start.4 = (f32[2,256,512]{2,1,0:T(8,128)}, f32[2,256,512]{2,1,0:T(8,128)}, u32[]{:S(2)}, u32[]{:S(2)}) collective-permute-start(f32[2,256,512]{2,1,0:T(8,128)} %get-tuple-element.129), channel_id=1, source_target_pairs={{0,4},{4,0},{8,12},{12,8},{16,20},{20,16},{24,28},{28,24},{1,5},{5... | collective-permute-start | bytes 3145736 | tf_op jit(solution)/shard_map/ppermute | solution.py:158
  28.1 30.1 %collective-permute-start.5 = (f32[2,256,512]{2,1,0:T(8,128)}, f32[2,256,512]{2,1,0:T(8,128)}, u32[]{:S(2)}, u32[]{:S(2)}) collective-permute-start(f32[2,256,512]{2,1,0:T(8,128)} %get-tuple-element.129), channel_id=1, source_target_pairs={{0,8},{4,12},{24,16},{28,20},{1,9},{5,13},{25,17},{29,21},{2,10},{... | collective-permute-start | bytes 3145736 | tf_op jit(solution)/shard_map/ppermute | solution.py:154
  36.3 47.5 %collective-permute-start.9 = (f32[8,128,256]{2,1,0:T(8,128)}, f32[8,128,256]{2,1,0:T(8,128)S(1)}, u32[]{:S(2)}, u32[]{:S(2)}) collective-permute-start(f32[8,128,256]{2,1,0:T(8,128)} %get-tuple-element.119.refs_2_.refs_1_), channel_id=1, source_target_pairs={{8,16},{12,20},{16,8},{20,12},{9,17},{13,21},{17,9},{21,13},{10,18... | collective-permute-start | bytes 3145736 | tf_op jit(solution)/shard_map/ppermute | solution.py:154
  46.9 22.7 %collective-permute-start.6 = (f32[6,128,256]{2,1,0:T(8,128)}, f32[6,128,256]{2,1,0:T(8,128)}, u32[]{:S(2)}, u32[]{:S(2)}) collective-permute-start(f32[6,128,256]{2,1,0:T(8,128)} %get-tuple-element.130), channel_id=1, source_target_pairs={{8,0},{12,4},{16,24},{20,28},{9,1},{13,5},{17,25},{21,29},{10,2},{... | collective-permute-start | bytes 2359304 | tf_op jit(solution)/shard_map/ppermute | solution.py:154
  57.4 58.3 %collective-permute-start.2 = (f32[2,256,1024]{2,1,0:T(8,128)}, f32[2,256,1024]{2,1,0:T(8,128)}, u32[]{:S(2)}, u32[]{:S(2)}) collective-permute-start(f32[2,256,1024]{2,1,0:T(8,128)} %get-tuple-element.127), channel_id=1, source_target_pairs={{0,1},{1,0},{2,3},{3,2},{4,5},{5,4},{6,7},{7,6},{8,9},{9,8},{10,11... | collective-permute-start | bytes 6291464 | tf_op jit(solution)/shard_map/ppermute | solution.py:158
  57.4 39.3 %collective-permute-start.3 = (f32[2,256,512]{2,1,0:T(8,128)}, f32[2,256,512]{2,1,0:T(8,128)S(1)}, u32[]{:S(2)}, u32[]{:S(2)}) collective-permute-start(f32[2,256,512]{2,1,0:T(8,128)} %get-tuple-element.128), channel_id=1, source_target_pairs={{8,16},{12,20},{16,8},{20,12},{9,17},{13,21},{17,9},{21,13},{10,18... | collective-permute-start | bytes 3145736 | tf_op jit(solution)/shard_map/ppermute | solution.py:154
  58.2 32.0 %collective-permute-start.8 = (f32[1,256,512]{2,1,0:T(8,128)}, f32[1,256,512]{2,1,0:T(8,128)}, u32[]{:S(2)}, u32[]{:S(2)}) collective-permute-start(f32[1,256,512]{2,1,0:T(8,128)} %get-tuple-element.135), channel_id=1, source_target_pairs={{0,8},{4,12},{8,0},{12,4},{16,24},{20,28},{24,16},{28,20},{1,9},{5... | collective-permute-start | bytes 1572872 | tf_op jit(solution)/shard_map/ppermute | solution.py:154
  69.6 37.9 %collective-permute-start.10 = (f32[6,128,256]{2,1,0:T(8,128)}, f32[6,128,256]{2,1,0:T(8,128)}, u32[]{:S(2)}, u32[]{:S(2)}) collective-permute-start(f32[6,128,256]{2,1,0:T(8,128)} %get-tuple-element.145), channel_id=1, source_target_pairs={{0,4},{4,0},{8,12},{12,8},{16,20},{20,16},{24,28},{28,24},{1,5},{5... | collective-permute-start | bytes 2359304 | tf_op jit(solution)/shard_map/ppermute | solution.py:158
  88.9 24.1 %collective-permute-start.17 = (f32[6,128,256]{2,1,0:T(8,128)}, f32[6,128,256]{2,1,0:T(8,128)}, u32[]{:S(2)}, u32[]{:S(2)}) collective-permute-start(f32[6,128,256]{2,1,0:T(8,128)} %get-tuple-element.161), channel_id=1, source_target_pairs={{8,0},{12,4},{16,24},{20,28},{9,1},{13,5},{17,25},{21,29},{10,2},{... | collective-permute-start | bytes 2359304 | tf_op jit(solution)/shard_map/ppermute | solution.py:154
  96.7 24.1 %collective-permute-start.16 = (f32[2,256,512]{2,1,0:T(8,128)}, f32[2,256,512]{2,1,0:T(8,128)}, u32[]{:S(2)}, u32[]{:S(2)}) collective-permute-start(f32[2,256,512]{2,1,0:T(8,128)} %get-tuple-element.160), channel_id=1, source_target_pairs={{0,4},{4,0},{8,12},{12,8},{16,20},{20,16},{24,28},{28,24},{1,5},{5... | collective-permute-start | bytes 3145736 | tf_op jit(solution)/shard_map/ppermute | solution.py:158
  115.8 19.8 %collective-permute-start.19 = (f32[1,256,512]{2,1,0:T(8,128)}, f32[1,256,512]{2,1,0:T(8,128)}, u32[]{:S(2)}, u32[]{:S(2)}) collective-permute-start(f32[1,256,512]{2,1,0:T(8,128)} %get-tuple-element.165), channel_id=1, source_target_pairs={{8,0},{12,4},{16,24},{20,28},{9,1},{13,5},{17,25},{21,29},{10,2},{... | collective-permute-start | bytes 1572872 | tf_op jit(solution)/shard_map/ppermute | solution.py:154
  120.8 25.7 %collective-permute-start.12 = (f32[6,128,256]{2,1,0:T(8,128)}, f32[6,128,256]{2,1,0:T(8,128)}, u32[]{:S(2)}, u32[]{:S(2)}) collective-permute-start(f32[6,128,256]{2,1,0:T(8,128)} %get-tuple-element.157.refs_1_), channel_id=1, source_target_pairs={{0,1},{1,0},{2,3},{3,2},{4,5},{5,4},{6,7},{7,6},{8,9},{9,8},{10,11... | collective-permute-start | bytes 2359304 | tf_op jit(solution)/shard_map/ppermute | solution.py:158
  126.5 45.1 %collective-permute-start.20 = (f32[6,128,256]{2,1,0:T(8,128)}, f32[6,128,256]{2,1,0:T(8,128)}, u32[]{:S(2)}, u32[]{:S(2)}) collective-permute-start(f32[6,128,256]{2,1,0:T(8,128)} %get-tuple-element.157.refs_1_), channel_id=1, source_target_pairs={{0,2},{1,3},{2,0},{3,1},{4,6},{5,7},{6,4},{7,5},{8,10},{9,11},{10,... | collective-permute-start | bytes 2359304 | tf_op jit(solution)/shard_map/ppermute | solution.py:158
  138.2 28.4 %collective-permute-start.22 = (f32[1,256,512]{2,1,0:T(8,128)}, f32[1,256,512]{2,1,0:T(8,128)}, u32[]{:S(2)}, u32[]{:S(2)}) collective-permute-start(f32[1,256,512]{2,1,0:T(8,128)} %get-tuple-element.174), channel_id=1, source_target_pairs={{8,0},{12,4},{16,24},{20,28},{9,1},{13,5},{17,25},{21,29},{10,2},{... | collective-permute-start | bytes 1572872 | tf_op jit(solution)/shard_map/ppermute | solution.py:154
  139.5 38.9 %collective-permute-start.24 = (f32[9,128,256]{2,1,0:T(8,128)}, f32[9,128,256]{2,1,0:T(8,128)}, u32[]{:S(2)}, u32[]{:S(2)}) collective-permute-start(f32[9,128,256]{2,1,0:T(8,128)} %get-tuple-element.181.refs_4_), channel_id=1, source_target_pairs={{0,1},{1,0},{2,3},{3,2},{4,5},{5,4},{6,7},{7,6},{8,9},{9,8},{10,11... | collective-permute-start | bytes 3538952 | tf_op jit(solution)/shard_map/ppermute | solution.py:158
  144.8 26.8 %collective-permute-start.21 = (f32[3,128,256]{2,1,0:T(8,128)}, f32[3,128,256]{2,1,0:T(8,128)S(1)}, u32[]{:S(2)}, u32[]{:S(2)}) collective-permute-start(f32[3,128,256]{2,1,0:T(8,128)} %copy-done.92), channel_id=1, source_target_pairs={{0,4},{4,0},{8,12},{12,8},{16,20},{20,16},{24,28},{28,24},{1,5},{5... | collective-permute-start | bytes 1179656 | tf_op jit(solution)/shard_map/ppermute | solution.py:158
  170.0 27.4 %collective-permute-start.25 = (f32[2,256,512]{2,1,0:T(8,128)}, f32[2,256,512]{2,1,0:T(8,128)}, u32[]{:S(2)}, u32[]{:S(2)}) collective-permute-start(f32[2,256,512]{2,1,0:T(8,128)} %get-tuple-element.186), channel_id=1, source_target_pairs={{0,4},{4,0},{8,12},{12,8},{16,20},{20,16},{24,28},{28,24},{1,5},{5... | collective-permute-start | bytes 3145736 | tf_op jit(solution)/shard_map/ppermute | solution.py:158
  176.8 20.7 %collective-permute-start.26 = (f32[6,128,256]{2,1,0:T(8,128)}, f32[6,128,256]{2,1,0:T(8,128)}, u32[]{:S(2)}, u32[]{:S(2)}) collective-permute-start(f32[6,128,256]{2,1,0:T(8,128)} %get-tuple-element.187.refs_1_), channel_id=1, source_target_pairs={{0,2},{1,3},{2,0},{3,1},{4,6},{5,7},{6,4},{7,5},{8,10},{9,11},{10,... | collective-permute-start | bytes 2359304 | tf_op jit(solution)/shard_map/ppermute | solution.py:158
  178.2 19.2 %collective-permute-start.27 = (f32[6,128,256]{2,1,0:T(8,128)}, f32[6,128,256]{2,1,0:T(8,128)}, u32[]{:S(2)}, u32[]{:S(2)}) collective-permute-start(f32[6,128,256]{2,1,0:T(8,128)} %get-tuple-element.187.refs_1_), channel_id=1, source_target_pairs={{0,1},{1,0},{2,3},{3,2},{4,5},{5,4},{6,7},{7,6},{8,9},{9,8},{10,11... | collective-permute-start | bytes 2359304 | tf_op jit(solution)/shard_map/ppermute | solution.py:158
  178.4 41.1 %collective-permute-start.11 = (f32[256,1024]{1,0:T(8,128)}, f32[256,1024]{1,0:T(8,128)}, u32[]{:S(2)}, u32[]{:S(2)}) collective-permute-start(f32[256,1024]{1,0:T(8,128)} %get-tuple-element.156), channel_id=1, source_target_pairs={{0,2},{1,3},{2,0},{3,1},{4,6},{5,7},{6,4},{7,5},{8,10},{9,11},{10,... | collective-permute-start | bytes 3145736 | tf_op jit(solution)/shard_map/ppermute | solution.py:158
  197.5 28.2 %collective-permute-start.30 = (f32[2,256,512]{2,1,0:T(8,128)}, f32[2,256,512]{2,1,0:T(8,128)S(1)}, u32[]{:S(2)}, u32[]{:S(2)}) collective-permute-start(f32[2,256,512]{2,1,0:T(8,128)} %copy-done.90), channel_id=1, source_target_pairs={{0,4},{4,0},{8,12},{12,8},{16,20},{20,16},{24,28},{28,24},{1,5},{5... | collective-permute-start | bytes 3145736 | tf_op jit(solution)/shard_map/ppermute | solution.py:158
  207.3 18.4 %collective-permute-start.31 = (f32[7,3,512]{2,1,0:T(4,128)S(1)}, f32[7,3,512]{2,1,0:T(4,128)S(1)}, u32[]{:S(2)}, u32[]{:S(2)}) collective-permute-start(f32[7,3,512]{2,1,0:T(4,128)S(1)} %get-tuple-element.217), channel_id=1, source_target_pairs={{0,16},{4,20},{8,24},{12,28},{16,0},{20,4},{24,8},{28,12},{1,17},{... | collective-permute-start | bytes 129032 | tf_op jit(solution)/shard_map/ppermute | solution.py:158
  (105 other events, 229.8 us)

commit v8 on v7

--- a/solution.py
+++ b/solution.py
@@ -99,54 +99,36 @@
 
 
 class Order:
-    def __init__(self, clock):
-        self.clock = clock
+    def __init__(self):
+        self.after = []
 
     def call(self, body, arrays, in_specs, *, out_shape, out_specs, scalars=(), grid=(), scratch_shapes=(), name):
-        several = isinstance(out_shape, tuple)
-        shapes = out_shape if several else (out_shape,)
-        specs = tuple(out_specs) if several else (out_specs,)
-        held, count, outs = len(scalars), len(arrays), len(shapes)
+        held, count = len(scalars), len(arrays)
+        after = [a for a in self.after if not any(a is b for b in arrays)]
 
         def short(*refs):
-            ins = refs[: held + count]
-            rest = refs[held + count + 1 :]
-            body(*ins, *rest[:outs], *rest[outs + 1 :])
+            body(*refs[: held + count], *refs[held + count + len(after) :])
 
         result = pl.pallas_call(
             short,
-            out_shape=shapes + (jax.ShapeDtypeStruct(self.clock.shape, self.clock.dtype),),
+            out_shape=out_shape,
             grid_spec=pltpu.PrefetchScalarGridSpec(
                 num_scalar_prefetch=held,
                 grid=grid,
-                in_specs=list(in_specs) + [ANY],
-                out_specs=specs + (ANY,),
+                in_specs=list(in_specs) + [ANY] * len(after),
+                out_specs=out_specs,
                 scratch_shapes=scratch_shapes,
             ),
-            input_output_aliases={held + count: outs},
             compiler_params=PARAMS,
             cost_estimate=NOTHING,
             name=name,
-        )(*scalars, *arrays, self.clock)
-        self.clock = result[-1]
-        return result[:-1] if several else result[0]
+        )(*scalars, *arrays, *after)
+        self.after = [result[0] if isinstance(result, (list, tuple)) else result]
+        return result
 
     def wait(self, *arrays):
-        def body(*refs):
-            pass
-
-        every = arrays + (self.clock,)
-        result = pl.pallas_call(
-            body,
-            out_shape=tuple(jax.ShapeDtypeStruct(a.shape, a.dtype) for a in every),
-            in_specs=[ANY] * len(every),
-            out_specs=(ANY,) * len(every),
-            input_output_aliases={i: i for i in range(len(every))},
-            cost_estimate=NOTHING,
-            name="wait",
-        )(*every)
-        self.clock = result[-1]
-        return result[0] if len(arrays) == 1 else result[:-1]
+        self.after.extend(arrays)
+        return arrays[0] if len(arrays) == 1 else arrays
 
 
 def lines(array, hops):
@@ -559,7 +541,7 @@
     level, column = rep // 2, rep % 2
     place = jnp.stack([level, column, quarter]).astype(jnp.int32)
     scale = 1.0 / math.sqrt(rows * lax.axis_size("rep"))
-    order = Order(jnp.zeros((8, LANES), jnp.float32))
+    order = Order()
     quarters = [jnp.bitwise_xor(quarter, k).astype(jnp.int32) for k in (3, 1, 2, 0)]
     piece = turn_tokens(order, place, tokens)
     near = lines(piece, PAIRS)
@@ -580,66 +562,65 @@
     outer2 = lines(part_of(order, place, mid, BLOCKS - OWN, OWN), OUTWARD)
     send = token_part(order, jnp.stack(quarters[:2]), own, in_weight)
     summed = flipped(send, "shard", 1)
+    inner, own_y, far = order.wait(inner, own_y, far)
     keep = token_part(order, jnp.stack(quarters[2:]), own, in_weight)
-    own_y, inner, outer2 = order.wait(own_y, inner, outer2)
+    outer3 = lines(part_of(order, place, far, BLOCKS - OWN, OWN), OUTWARD)
+    outer2 = order.wait(outer2)
     over = column_blocks(order, place, [(mid, outer2)], False)
     got2 = flipped(over, "rep", 1)
-    far = order.wait(far)
-    outer3 = lines(part_of(order, place, far, BLOCKS - OWN, OWN), OUTWARD)
     first = order.wait(first)
     relay, side1 = relay_payload(order, place, first, inner)
     relayed = lines(relay, MIDDLE)
     side1 = flipped(side1, "rep", 1)
-    middle, got2 = order.wait(middle, got2)
+    middle, got1 = order.wait(middle, got1)
+    own1 = column_blocks(order, place, [(near, None)], True, got1, (0, OWN))
+    across1 = flipped(own1, "shard", 2)
+    beside1 = flipped(own1, "shard", 1)
+    beside1, outer3, side1 = order.wait(beside1, outer3, side1)
+    middle_end = lines(part_of(order, place, middle, 1, 1), OUTWARD)
+    summed, got2 = order.wait(summed, got2)
     own2 = column_blocks(order, place, [(mid, outer2)], True, got2, (0, HALF))
     across2 = flipped(own2, "shard", 2)
     beside2 = flipped(own2, "shard", 1)
-    got1 = order.wait(got1)
-    own1 = column_blocks(order, place, [(near, None)], True, got1, (0, OWN))
-    across1 = flipped(own1, "shard", 2)
-    beside1 = flipped(own1, "shard", 1)
-    middle_end = lines(part_of(order, place, middle, 1, 1), OUTWARD)
-    summed = order.wait(summed)
-    token_grad, away = add(order, keep, summed)
-    last = flipped(away, "shard", 2)
-    across1, beside1, side1, outer3, relayed = order.wait(
-        across1, beside1, side1, outer3, relayed
-    )
-    both1 = flipped(across1, "shard", 1)
     over = column_blocks(order, place, [(far, outer3)], False)
     got3 = flipped(over, "rep", 1)
     middle_end = order.wait(middle_end)
+    side2 = flipped(side_payload(order, place, middle, middle_end), "rep", 1)
+    across1 = order.wait(across1)
+    both1 = flipped(across1, "shard", 1)
+    token_grad, away = add(order, keep, summed)
+    last = flipped(away, "shard", 2)
+    relayed = order.wait(relayed)
     relayed_end = lines(part_of(order, place, relayed, 1, 1), OUTWARD)
     beside2, taps1 = order.wait(beside2, taps1)
     taps, taps_out = add(order, taps, taps1)
     taps2 = flipped(taps_out, "rep", 2)
-    relayed_end = order.wait(relayed_end)
-    side2 = flipped(side_payload(order, place, middle, middle_end), "rep", 1)
-    across2, got3 = order.wait(across2, got3)
+    across2, relayed_end, got3 = order.wait(across2, relayed_end, got3)
     both2 = flipped(across2, "shard", 1)
     own3 = column_blocks(order, place, [(far, outer3)], True, got3, (0, HALF))
     across3 = flipped(own3, "shard", 2)
     beside3 = flipped(own3, "shard", 1)
-    both2, both1 = order.wait(both2, both1)
-    side3 = flipped(side_payload(order, place, relayed, relayed_end), "rep", 1)
+    both1 = order.wait(both1)
     tok = arrange_tokens(order, place, tokens, [(own1, beside1, across1, both1)])
+    both2 = order.wait(both2)
     early = [(own, None), (inner, first), (own_y, None), (side1, None)]
     so_far = weight_part(order, place, tok, early)
-    side2, across3, beside3 = order.wait(side2, across3, beside3)
+    side3 = flipped(side_payload(order, place, relayed, relayed_end), "rep", 1)
+    side2, across3 = order.wait(side2, across3)
     both3 = flipped(across3, "shard", 1)
     both3 = order.wait(both3)
     tok = arrange_tokens(order, place, None, [(own2, beside2, across2, both2)])
+    so_far = weight_part(order, place, tok, [(middle, middle_end), (side2, None)], None, so_far)
     taps2 = order.wait(taps2)
     taps, taps_out = add(order, taps, taps2)
     taps4 = flipped(taps_out, "rep", 4)
-    so_far = weight_part(order, place, tok, [(middle, middle_end), (side2, None)], None, so_far)
-    last = order.wait(last)
+    taps4, beside3, last = order.wait(taps4, beside3, last)
     token_grad = (token_grad + last).astype(jnp.bfloat16)
     tok = arrange_tokens(order, place, None, [(own3, beside3, across3, both3)])
-    side3, taps4 = order.wait(side3, taps4)
-    taps, _ = add(order, taps, taps4, scale=scale)
+    side3 = order.wait(side3)
     late = [(relayed, relayed_end), (side3, None)]
     weight_grad = weight_part(order, place, tok, late, scale, so_far)
+    taps, _ = add(order, taps, taps4, scale=scale)
     return (token_grad, weight_grad, taps)
 
 

time: 241 us -> 195 us (0.81)
  local copies, waits for them, and re-layouts: 67.2 us -> 17.3 us
  waiting for transfers between devices: 41.9 us -> 56.9 us
  Pallas kernels: 86.2 us -> 76.7 us
    unnamed x196 -> x58, local copies, waits for them, and re-layouts: 67.2 us -> 17.3 us
    ppermute x21, waiting for transfers between devices: 19.4 us -> 34.9 us  [flipped(): lax.ppermute(array, axis, [(r, r ^ flip) for r in range(lax.axis_size(axi...]
    pallas_call x46 -> x27, Pallas kernels: 86.2 us -> 76.7 us  [call(): pl.pallas_call(short, out_shape=out_shape, grid_spec=pltpu.PrefetchScalar...]
    ppermute x11, starting transfers between devices: 23 us -> 20.6 us  [lines(): return lax.ppermute(array, 'rep', perm)]
  transfers between devices with their start and end apart: 32 -> 32, of which waited for: 9 -> 12; matrix products, arithmetic and copies ran while one was open for 1% -> 0% of each run, Pallas kernels for 33% -> 36%
where the time goes in v8:
time: 195 us; the launch traced here: 194 us
  Pallas kernels  76.7 us (39%)
  waiting for transfers between devices  56.9 us (29%)
  starting transfers between devices  39.4 us (20%)
  local copies, waits for them, and re-layouts  17.3 us (9%)
  other arithmetic  2.39 us (1%)
    pallas_call x27, Pallas kernels, call(): pl.pallas_call(short, out_shape=out_shape, grid_spec=pltpu.PrefetchScalar...  76.7 us
    ppermute x21, waiting for transfers between devices, flipped(): lax.ppermute(array, axis, [(r, r ^ flip) for r in range(lax.axis_size(axi...  34.9 us
    ppermute x11, waiting for transfers between devices, lines(): return lax.ppermute(array, 'rep', perm)  22 us
    ppermute x11, starting transfers between devices, lines(): return lax.ppermute(array, 'rep', perm)  20.6 us
    ppermute x21, starting transfers between devices, flipped(): lax.ppermute(array, axis, [(r, r ^ flip) for r in range(lax.axis_size(axi...  18.8 us
    unnamed x58, local copies, waits for them, and re-layouts  17.3 us
  transfers between devices with their start and end apart: 32, of which 12 were waited for; matrix products, arithmetic and copies ran while one was open for 0% of the time, Pallas kernels for 36%

profile of v8, /device:TPU:0, one launch (start us, length us, event | category | flops | bytes accessed | tf_op | source)
XLA Modules:
  0.0 193.8 jit_solution(10064352286243157458)
XLA Ops:
  3.1 3.1 %collective-permute-start.1 = (f32[8,128,256]{2,1,0:T(8,128)S(1)}, f32[8,128,256]{2,1,0:T(8,128)}, u32[]{:S(2)}, u32[]{:S(2)}) collective-permute-start(f32[8,128,256]{2,1,0:T(8,128)S(1)} %turn_tokens.1.refs_5_.refs_1_), channel_id=1, source_target_pairs={{0,8},{4,12},{8,0},{12,4},{16,24},{20,28},{24,16},{28,20},{1,9},{5... | collective-permute-start | bytes 3145736 | tf_op jit(solution)/shard_map/ppermute | solution.py:136
  7.0 17.2 %gate.1 = (bf16[3,256,512]{2,1,0:T(8,128)(2,1)S(1)}, f32[7,3,512]{2,1,0:T(4,128)S(1)}, f32[1,256,512]{2,1,0:T(8,128)}, f32[2,256,512]{2,1,0:T(8,128)}, f32[2,256,512]{2,1,0:T(8,128)}) custom-call(s32[3]{0:T(128)S(1)} %pad_add_fusion.1.refs_0_, bf16[256,4096]{1,0:T(8,128)(2,1)} %refs_1_.5, bf16[3,4096,512]{2,1,0:T(8,128)(2,1)} %refs_2_.5, ...), custom_call_target="tpu_custom_call" | custom-call | flops 128 | bytes 128 | tf_op jit(solution)/shard_map/gate/pallas_call | solution.py:112
  24.2 7.3 %collective-permute-start.2 = (f32[2,256,512]{2,1,0:T(8,128)}, f32[2,256,512]{2,1,0:T(8,128)}, u32[]{:S(2)}, u32[]{:S(2)}) collective-permute-start(f32[2,256,512]{2,1,0:T(8,128)} %get-tuple-element.18), channel_id=1, source_target_pairs={{0,8},{4,12},{24,16},{28,20},{1,9},{5,13},{25,17},{29,21},{2,10},{... | collective-permute-start | bytes 3145736 | tf_op jit(solution)/shard_map/ppermute | solution.py:136
  34.4 2.3 %other_blocks.3.refs_2_ = f32[6,128,256]{2,1,0:T(8,128)} custom-call(s32[3]{0:T(128)S(1)} %pad_add_fusion.1.refs_0_, f32[8,128,256]{2,1,0:T(8,128)S(1)} %turn_tokens.1.refs_5_.refs_1_, f32[8,128,256]{2,1,0:T(8,128)} %collective-permute-done.1.refs_2_.refs_1_, bf16[3,256,512]{2,1,0:T(8,128)(2,1)S(1)} %get-tuple-element.17.refs_3_.refs_1_.refs_2_), custom_call_target="tpu_custom_call" | custom-call | flops 128 | bytes 128 | tf_op jit(solution)/shard_map/other_blocks/pallas_call | solution.py:112
  40.6 7.9 %token_part.2.refs_3_ = f32[2,256,1024]{2,1,0:T(8,128)} custom-call(s32[2]{0:T(128)S(1)} %pad_add_fusion.2.refs_0_, bf16[3,256,512]{2,1,0:T(8,128)(2,1)S(1)} %get-tuple-element.17.refs_3_.refs_1_.refs_2_, bf16[3,4096,512]{2,1,0:T(8,128)(2,1)} %refs_2_.5, f32[6,128,256]{2,1,0:T(8,128)} %part_of.4.refs_3_), custom_call_target="tpu_custom_call" | custom-call | flops 128 | bytes 128 | tf_op jit(solution)/shard_map/token_part/pallas_call | solution.py:112
  48.5 4.1 %collective-permute-done.2.refs_4_.refs_2_.refs_3_ = f32[2,256,512]{2,1,0:T(8,128)} collective-permute-done((f32[2,256,512]{2,1,0:T(8,128)}, f32[2,256,512]{2,1,0:T(8,128)}, u32[]{:S(2)}, u32[]{:S(2)}) %collective-permute-start.2) | collective-permute-done | bytes 1048608 | tf_op jit(solution)/shard_map/ppermute | solution.py:136
  52.6 3.2 %collective-permute-done.3.refs_5_ = f32[2,256,512]{2,1,0:T(8,128)} collective-permute-done((f32[2,256,512]{2,1,0:T(8,128)}, f32[2,256,512]{2,1,0:T(8,128)}, u32[]{:S(2)}, u32[]{:S(2)}) %collective-permute-start.3) | collective-permute-done | bytes 1048608 | tf_op jit(solution)/shard_map/ppermute | solution.py:140
  59.7 6.6 %token_part.3.refs_2_.refs_0_ = f32[2,256,1024]{2,1,0:T(8,128)S(1)} custom-call(s32[2]{0:T(128)S(1)} %pad_add_fusion.refs_0_, bf16[3,256,512]{2,1,0:T(8,128)(2,1)S(1)} %get-tuple-element.17.refs_3_.refs_1_.refs_2_, bf16[3,4096,512]{2,1,0:T(8,128)(2,1)} %refs_2_.5, f32[2,256,1024]{2,1,0:T(8,128)} %token_part.2.refs_3_, ...), custom_call_target="tpu_custom_call" | custom-call | flops 128 | bytes 128 | tf_op jit(solution)/shard_map/token_part/pallas_call | solution.py:112
  70.9 2.6 %relay_payload.1 = (f32[2,256,512]{2,1,0:T(8,128)}, f32[2,256,512]{2,1,0:T(8,128)S(1)}) custom-call(s32[3]{0:T(128)S(1)} %pad_add_fusion.1.refs_0_, f32[1,256,512]{2,1,0:T(8,128)S(1)} %collective-permute-done.8.refs_1_.refs_4_, f32[2,256,512]{2,1,0:T(8,128)} %collective-permute-done.2.refs_4_.refs_2_.refs_3_, f32[3,128,256]{2,1,0:T(8,128)S(1)} %other_blocks.4.refs_3_), custom_call_target="tpu_custom_call" | custom-call | flops 128 | bytes 128 | tf_op jit(solution)/shard_map/relay_payload/pallas_call | solution.py:112
  79.3 14.4 %collective-permute-done.11.refs_4_.refs_2_ = f32[6,128,256]{2,1,0:T(8,128)S(1)} collective-permute-done((f32[6,128,256]{2,1,0:T(8,128)S(1)}, f32[6,128,256]{2,1,0:T(8,128)S(1)}, u32[]{:S(2)}, u32[]{:S(2)}) %collective-permute-start.11) | collective-permute-done | bytes 786464 | tf_op jit(solution)/shard_map/ppermute | solution.py:136
  94.5 2.6 %collective-permute-done.12.refs_5_.refs_6_ = f32[2,256,512]{2,1,0:T(8,128)S(1)} collective-permute-done((f32[2,256,512]{2,1,0:T(8,128)S(1)}, f32[2,256,512]{2,1,0:T(8,128)S(1)}, u32[]{:S(2)}, u32[]{:S(2)}) %collective-permute-start.12) | collective-permute-done | bytes 1048608 | tf_op jit(solution)/shard_map/ppermute | solution.py:140
  99.8 5.9 %collective-permute-done.14.refs_3_ = f32[3,128,256]{2,1,0:T(8,128)S(1)} collective-permute-done((f32[3,128,256]{2,1,0:T(8,128)S(1)}, f32[3,128,256]{2,1,0:T(8,128)S(1)}, u32[]{:S(2)}, u32[]{:S(2)}) %collective-permute-start.14) | collective-permute-done | bytes 393248 | tf_op jit(solution)/shard_map/ppermute | solution.py:140
  114.2 3.3 %add.23 = (f32[256,1024]{1,0:T(8,128)S(1)}, f32[256,1024]{1,0:T(8,128)}) custom-call(f32[2,256,1024]{2,1,0:T(8,128)} %copy-done.2, f32[2,256,1024]{2,1,0:T(8,128)} %collective-permute-done.5.refs_5_.refs_1_, f32[2,256,512]{2,1,0:T(8,128)} %side_payload.2.refs_2_, f32[9,128,256]{2,1,0:T(8,128)S(1)} %collective-permute-done.15.refs_3_.refs_4_), custom_call_target="tpu_custom_call" | custom-call | flops 128 | bytes 128 | tf_op jit(solution)/shard_map/add/pallas_call | solution.py:112
  120.5 3.5 %collective-permute-done.18.refs_1_ = f32[7,3,512]{2,1,0:T(4,128)S(1)} collective-permute-done((f32[7,3,512]{2,1,0:T(4,128)S(1)}, f32[7,3,512]{2,1,0:T(4,128)S(1)}, u32[]{:S(2)}, u32[]{:S(2)}) %collective-permute-start.18) | collective-permute-done | bytes 43040 | tf_op jit(solution)/shard_map/ppermute | solution.py:140
  126.1 6.1 %collective-permute-done.17.refs_3_ = f32[3,128,256]{2,1,0:T(8,128)S(1)} collective-permute-done((f32[3,128,256]{2,1,0:T(8,128)S(1)}, f32[3,128,256]{2,1,0:T(8,128)S(1)}, u32[]{:S(2)}, u32[]{:S(2)}) %collective-permute-start.17) | collective-permute-done | bytes 393248 | tf_op jit(solution)/shard_map/ppermute | solution.py:140
  135.8 4.3 %arrange_tokens.3.refs_1_ = bf16[3,512,1024]{2,1,0:T(8,128)(2,1)} custom-call(s32[3]{0:T(128)S(1)} %pad_add_fusion.1.refs_0_, bf16[256,4096]{1,0:T(8,128)(2,1)} %refs_1_.5, f32[9,128,256]{2,1,0:T(8,128)S(1)} %own_blocks.3.refs_2_, f32[9,128,256]{2,1,0:T(8,128)S(1)} %collective-permute-done.10.refs_3_, ...), custom_call_target="tpu_custom_call" | custom-call | flops 128 | bytes 128 | tf_op jit(solution)/shard_map/arrange_tokens/pallas_call | solution.py:112
  140.2 6.2 %weight_part.3.refs_3_.refs_5_ = f32[1536,512]{1,0:T(8,128)} custom-call(s32[3]{0:T(128)S(1)} %pad_add_fusion.1.refs_0_, bf16[3,512,1024]{2,1,0:T(8,128)(2,1)} %arrange_tokens.3.refs_1_, bf16[3,256,512]{2,1,0:T(8,128)(2,1)S(1)} %get-tuple-element.17.refs_3_.refs_1_.refs_2_, f32[2,256,512]{2,1,0:T(8,128)} %collective-permute-done.2.refs_4_.refs_2_.refs_3_, ...), custom_call_target="tpu_custom_call" | custom-call | flops 128 | bytes 128 | tf_op jit(solution)/shard_map/weight_part/pallas_call | solution.py:112
  150.8 2.5 %collective-permute-done.24.refs_7_.refs_3_ = f32[6,128,256]{2,1,0:T(8,128)S(1)} collective-permute-done((f32[6,128,256]{2,1,0:T(8,128)S(1)}, f32[6,128,256]{2,1,0:T(8,128)S(1)}, u32[]{:S(2)}, u32[]{:S(2)}) %collective-permute-start.24) | collective-permute-done | bytes 786464 | tf_op jit(solution)/shard_map/ppermute | solution.py:140
  153.8 6.8 %collective-permute-done.29.refs_6_.refs_4_ = f32[2,256,512]{2,1,0:T(8,128)} collective-permute-done((f32[2,256,512]{2,1,0:T(8,128)}, f32[2,256,512]{2,1,0:T(8,128)}, u32[]{:S(2)}, u32[]{:S(2)}) %collective-permute-start.29) | collective-permute-done | bytes 1048608 | tf_op jit(solution)/shard_map/ppermute | solution.py:140
  160.7 2.9 %collective-permute-start.26 = (f32[7,3,512]{2,1,0:T(4,128)S(1)}, f32[7,3,512]{2,1,0:T(4,128)S(1)}, u32[]{:S(2)}, u32[]{:S(2)}) collective-permute-start(f32[7,3,512]{2,1,0:T(4,128)S(1)} %copy-done.26), channel_id=1, source_target_pairs={{0,8},{4,12},{8,0},{12,4},{16,24},{20,28},{24,16},{28,20},{1,9},{5... | collective-permute-start | bytes 129032 | tf_op jit(solution)/shard_map/ppermute | solution.py:140
  164.7 2.5 %arrange_tokens.4.refs_1_ = bf16[3,512,512]{2,1,0:T(8,128)(2,1)} custom-call(s32[3]{0:T(128)S(1)} %pad_add_fusion.1.refs_0_, f32[6,128,256]{2,1,0:T(8,128)S(1)} %own_blocks.4.refs_3_.refs_1_, f32[6,128,256]{2,1,0:T(8,128)S(1)} %copy-done.17, f32[6,128,256]{2,1,0:T(8,128)} %collective-permute-done.21.refs_5_.refs_3_, f32[6,128,256]{2,1,0:T(8,128)S(1)} %copy-done.15, ...), custom_call_target="tpu_custom_call" | custom-call | flops 128 | bytes 128 | tf_op jit(solution)/shard_map/arrange_tokens/pallas_call | solution.py:112
  168.6 5.6 %weight_part.4.refs_2_.refs_5_ = f32[1536,512]{1,0:T(8,128)} custom-call(s32[3]{0:T(128)S(1)} %pad_add_fusion.1.refs_0_, bf16[3,512,512]{2,1,0:T(8,128)(2,1)S(1)} %copy-done.7, f32[2,256,512]{2,1,0:T(8,128)S(1)} %collective-permute-done.6.refs_4_.refs_1_.refs_2_, f32[1,256,512]{2,1,0:T(8,128)S(1)} %copy-done.21, ...), custom_call_target="tpu_custom_call" | custom-call | flops 128 | bytes 128 | tf_op jit(solution)/shard_map/weight_part/pallas_call | solution.py:112
  177.1 4.2 %collective-permute-done.30.refs_6_.refs_1_ = f32[7,3,512]{2,1,0:T(4,128)S(1)} collective-permute-done((f32[7,3,512]{2,1,0:T(4,128)S(1)}, f32[7,3,512]{2,1,0:T(4,128)S(1)}, u32[]{:S(2)}, u32[]{:S(2)}) %collective-permute-start.30) | collective-permute-done | bytes 43040 | tf_op jit(solution)/shard_map/ppermute | solution.py:140
  183.1 5.3 %weight_part.5.refs_2_ = f32[1536,512]{1,0:T(8,128)} custom-call(s32[3]{0:T(128)S(1)} %pad_add_fusion.1.refs_0_, bf16[3,512,512]{2,1,0:T(8,128)(2,1)S(1)} %arrange_tokens.5.refs_1_, f32[2,256,512]{2,1,0:T(8,128)S(1)} %collective-permute-done.19.refs_1_.refs_2_, f32[1,256,512]{2,1,0:T(8,128)S(1)} %collective-permute-done.22.refs_6_.refs_2_.refs_3_, ...), custom_call_target="tpu_custom_call" | custom-call | flops 128 | bytes 128 | tf_op jit(solution)/shard_map/weight_part/pallas_call | solution.py:112
  (129 shorter events, 62.4 us)
Async XLA Ops:
  3.1 29.9 %collective-permute-start.1 = (f32[8,128,256]{2,1,0:T(8,128)S(1)}, f32[8,128,256]{2,1,0:T(8,128)}, u32[]{:S(2)}, u32[]{:S(2)}) collective-permute-start(f32[8,128,256]{2,1,0:T(8,128)S(1)} %turn_tokens.1.refs_5_.refs_1_), channel_id=1, source_target_pairs={{0,8},{4,12},{8,0},{12,4},{16,24},{20,28},{24,16},{28,20},{1,9},{5... | collective-permute-start | bytes 3145736 | tf_op jit(solution)/shard_map/ppermute | solution.py:136
  6.2 30.5 %collective-permute-start = (f32[8,128,256]{2,1,0:T(8,128)S(1)}, f32[8,128,256]{2,1,0:T(8,128)S(1)}, u32[]{:S(2)}, u32[]{:S(2)}) collective-permute-start(f32[8,128,256]{2,1,0:T(8,128)S(1)} %turn_tokens.1.refs_5_.refs_1_), channel_id=1, source_target_pairs={{8,16},{12,20},{16,8},{20,12},{9,17},{13,21},{17,9},{21,13},{10,18... | collective-permute-start | bytes 3145736 | tf_op jit(solution)/shard_map/ppermute | solution.py:136
  24.2 28.4 %collective-permute-start.2 = (f32[2,256,512]{2,1,0:T(8,128)}, f32[2,256,512]{2,1,0:T(8,128)}, u32[]{:S(2)}, u32[]{:S(2)}) collective-permute-start(f32[2,256,512]{2,1,0:T(8,128)} %get-tuple-element.18), channel_id=1, source_target_pairs={{0,8},{4,12},{24,16},{28,20},{1,9},{5,13},{25,17},{29,21},{2,10},{... | collective-permute-start | bytes 3145736 | tf_op jit(solution)/shard_map/ppermute | solution.py:136
  31.5 24.4 %collective-permute-start.3 = (f32[2,256,512]{2,1,0:T(8,128)}, f32[2,256,512]{2,1,0:T(8,128)}, u32[]{:S(2)}, u32[]{:S(2)}) collective-permute-start(f32[2,256,512]{2,1,0:T(8,128)} %get-tuple-element.18), channel_id=1, source_target_pairs={{0,4},{4,0},{8,12},{12,8},{16,20},{20,16},{24,28},{28,24},{1,5},{5... | collective-permute-start | bytes 3145736 | tf_op jit(solution)/shard_map/ppermute | solution.py:140
  33.0 24.4 %collective-permute-start.4 = (f32[8,128,256]{2,1,0:T(8,128)}, f32[8,128,256]{2,1,0:T(8,128)S(1)}, u32[]{:S(2)}, u32[]{:S(2)}) collective-permute-start(f32[8,128,256]{2,1,0:T(8,128)} %collective-permute-done.1.refs_2_.refs_1_), channel_id=1, source_target_pairs={{8,16},{12,20},{16,8},{20,12},{9,17},{13,21},{17,9},{21,13},{10,18... | collective-permute-start | bytes 3145736 | tf_op jit(solution)/shard_map/ppermute | solution.py:136
  33.7 42.4 %collective-permute-start.6 = (f32[2,256,512]{2,1,0:T(8,128)}, f32[2,256,512]{2,1,0:T(8,128)S(1)}, u32[]{:S(2)}, u32[]{:S(2)}) collective-permute-start(f32[2,256,512]{2,1,0:T(8,128)} %get-tuple-element.19), channel_id=1, source_target_pairs={{8,16},{12,20},{16,8},{20,12},{9,17},{13,21},{17,9},{21,13},{10,18... | collective-permute-start | bytes 3145736 | tf_op jit(solution)/shard_map/ppermute | solution.py:136
  39.2 27.7 %collective-permute-start.9 = (f32[6,128,256]{2,1,0:T(8,128)}, f32[6,128,256]{2,1,0:T(8,128)}, u32[]{:S(2)}, u32[]{:S(2)}) collective-permute-start(f32[6,128,256]{2,1,0:T(8,128)} %part_of.4.refs_3_), channel_id=1, source_target_pairs={{8,0},{12,4},{16,24},{20,28},{9,1},{13,5},{17,25},{21,29},{10,2},{... | collective-permute-start | bytes 2359304 | tf_op jit(solution)/shard_map/ppermute | solution.py:136
  52.6 53.1 %collective-permute-start.5 = (f32[2,256,1024]{2,1,0:T(8,128)}, f32[2,256,1024]{2,1,0:T(8,128)}, u32[]{:S(2)}, u32[]{:S(2)}) collective-permute-start(f32[2,256,1024]{2,1,0:T(8,128)} %token_part.2.refs_3_), channel_id=1, source_target_pairs={{0,1},{1,0},{2,3},{3,2},{4,5},{5,4},{6,7},{7,6},{8,9},{9,8},{10,11... | collective-permute-start | bytes 6291464 | tf_op jit(solution)/shard_map/ppermute | solution.py:140
  55.8 20.3 %collective-permute-start.7 = (f32[6,128,256]{2,1,0:T(8,128)}, f32[6,128,256]{2,1,0:T(8,128)}, u32[]{:S(2)}, u32[]{:S(2)}) collective-permute-start(f32[6,128,256]{2,1,0:T(8,128)} %other_blocks.3.refs_2_), channel_id=1, source_target_pairs={{0,4},{4,0},{8,12},{12,8},{16,20},{20,16},{24,28},{28,24},{1,5},{5... | collective-permute-start | bytes 2359304 | tf_op jit(solution)/shard_map/ppermute | solution.py:140
  73.5 23.5 %collective-permute-start.12 = (f32[2,256,512]{2,1,0:T(8,128)S(1)}, f32[2,256,512]{2,1,0:T(8,128)S(1)}, u32[]{:S(2)}, u32[]{:S(2)}) collective-permute-start(f32[2,256,512]{2,1,0:T(8,128)S(1)} %get-tuple-element.22), channel_id=1, source_target_pairs={{0,4},{4,0},{8,12},{12,8},{16,20},{20,16},{24,28},{28,24},{1,5},{5... | collective-permute-start | bytes 3145736 | tf_op jit(solution)/shard_map/ppermute | solution.py:140
  74.8 18.9 %collective-permute-start.11 = (f32[6,128,256]{2,1,0:T(8,128)S(1)}, f32[6,128,256]{2,1,0:T(8,128)S(1)}, u32[]{:S(2)}, u32[]{:S(2)}) collective-permute-start(f32[6,128,256]{2,1,0:T(8,128)S(1)} %part_of.5.refs_3_), channel_id=1, source_target_pairs={{8,0},{12,4},{16,24},{20,28},{9,1},{13,5},{17,25},{21,29},{10,2},{... | collective-permute-start | bytes 2359304 | tf_op jit(solution)/shard_map/ppermute | solution.py:136
  77.7 20.2 %collective-permute-start.10 = (f32[9,128,256]{2,1,0:T(8,128)S(1)}, f32[9,128,256]{2,1,0:T(8,128)S(1)}, u32[]{:S(2)}, u32[]{:S(2)}) collective-permute-start(f32[9,128,256]{2,1,0:T(8,128)S(1)} %own_blocks.3.refs_2_), channel_id=1, source_target_pairs={{0,1},{1,0},{2,3},{3,2},{4,5},{5,4},{6,7},{7,6},{8,9},{9,8},{10,11... | collective-permute-start | bytes 3538952 | tf_op jit(solution)/shard_map/ppermute | solution.py:140
  77.8 30.7 %collective-permute-start.15 = (f32[9,128,256]{2,1,0:T(8,128)S(1)}, f32[9,128,256]{2,1,0:T(8,128)S(1)}, u32[]{:S(2)}, u32[]{:S(2)}) collective-permute-start(f32[9,128,256]{2,1,0:T(8,128)S(1)} %own_blocks.3.refs_2_), channel_id=1, source_target_pairs={{0,2},{1,3},{2,0},{3,1},{4,6},{5,7},{6,4},{7,5},{8,10},{9,11},{10,... | collective-permute-start | bytes 3538952 | tf_op jit(solution)/shard_map/ppermute | solution.py:140
  93.7 23.8 %collective-permute-start.19 = (f32[2,256,512]{2,1,0:T(8,128)}, f32[2,256,512]{2,1,0:T(8,128)S(1)}, u32[]{:S(2)}, u32[]{:S(2)}) collective-permute-start(f32[2,256,512]{2,1,0:T(8,128)} %get-tuple-element.21.refs_3_), channel_id=1, source_target_pairs={{8,16},{12,20},{16,8},{20,12},{9,17},{13,21},{17,9},{21,13},{10,18... | collective-permute-start | bytes 3145736 | tf_op jit(solution)/shard_map/ppermute | solution.py:136
  106.9 18.4 %collective-permute-start.21 = (f32[6,128,256]{2,1,0:T(8,128)S(1)}, f32[6,128,256]{2,1,0:T(8,128)}, u32[]{:S(2)}, u32[]{:S(2)}) collective-permute-start(f32[6,128,256]{2,1,0:T(8,128)S(1)} %own_blocks.4.refs_3_.refs_1_), channel_id=1, source_target_pairs={{0,2},{1,3},{2,0},{3,1},{4,6},{5,7},{6,4},{7,5},{8,10},{9,11},{10,... | collective-permute-start | bytes 2359304 | tf_op jit(solution)/shard_map/ppermute | solution.py:140
  108.5 16.9 %collective-permute-start.20 = (f32[6,128,256]{2,1,0:T(8,128)S(1)}, f32[6,128,256]{2,1,0:T(8,128)S(1)}, u32[]{:S(2)}, u32[]{:S(2)}) collective-permute-start(f32[6,128,256]{2,1,0:T(8,128)S(1)} %own_blocks.4.refs_3_.refs_1_), channel_id=1, source_target_pairs={{0,1},{1,0},{2,3},{3,2},{4,5},{5,4},{6,7},{7,6},{8,9},{9,8},{10,11... | collective-permute-start | bytes 2359304 | tf_op jit(solution)/shard_map/ppermute | solution.py:140
  108.5 27.4 %collective-permute-start.28 = (f32[9,128,256]{2,1,0:T(8,128)S(1)}, f32[9,128,256]{2,1,0:T(8,128)}, u32[]{:S(2)}, u32[]{:S(2)}) collective-permute-start(f32[9,128,256]{2,1,0:T(8,128)S(1)} %collective-permute-done.15.refs_3_.refs_4_), channel_id=1, source_target_pairs={{0,1},{1,0},{2,3},{3,2},{4,5},{5,4},{6,7},{7,6},{8,9},{9,8},{10,11... | collective-permute-start | bytes 3538952 | tf_op jit(solution)/shard_map/ppermute | solution.py:140
  118.1 14.0 %collective-permute-start.22 = (f32[1,256,512]{2,1,0:T(8,128)S(1)}, f32[1,256,512]{2,1,0:T(8,128)S(1)}, u32[]{:S(2)}, u32[]{:S(2)}) collective-permute-start(f32[1,256,512]{2,1,0:T(8,128)S(1)} %part_of.7.refs_2_), channel_id=1, source_target_pairs={{8,0},{12,4},{16,24},{20,28},{9,1},{13,5},{17,25},{21,29},{10,2},{... | collective-permute-start | bytes 1572872 | tf_op jit(solution)/shard_map/ppermute | solution.py:136
  125.3 14.8 %collective-permute-start.27 = (f32[6,128,256]{2,1,0:T(8,128)}, f32[6,128,256]{2,1,0:T(8,128)S(1)}, u32[]{:S(2)}, u32[]{:S(2)}) collective-permute-start(f32[6,128,256]{2,1,0:T(8,128)} %collective-permute-done.21.refs_5_.refs_3_), channel_id=1, source_target_pairs={{0,1},{1,0},{2,3},{3,2},{4,5},{5,4},{6,7},{7,6},{8,9},{9,8},{10,11... | collective-permute-start | bytes 2359304 | tf_op jit(solution)/shard_map/ppermute | solution.py:140
  132.8 20.5 %collective-permute-start.24 = (f32[6,128,256]{2,1,0:T(8,128)S(1)}, f32[6,128,256]{2,1,0:T(8,128)S(1)}, u32[]{:S(2)}, u32[]{:S(2)}) collective-permute-start(f32[6,128,256]{2,1,0:T(8,128)S(1)} %own_blocks.5.refs_6_.refs_1_), channel_id=1, source_target_pairs={{0,2},{1,3},{2,0},{3,1},{4,6},{5,7},{6,4},{7,5},{8,10},{9,11},{10,... | collective-permute-start | bytes 2359304 | tf_op jit(solution)/shard_map/ppermute | solution.py:140
  134.2 26.4 %collective-permute-start.29 = (f32[2,256,512]{2,1,0:T(8,128)}, f32[2,256,512]{2,1,0:T(8,128)}, u32[]{:S(2)}, u32[]{:S(2)}) collective-permute-start(f32[2,256,512]{2,1,0:T(8,128)} %side_payload.2.refs_2_), channel_id=1, source_target_pairs={{0,4},{4,0},{8,12},{12,8},{16,20},{20,16},{24,28},{28,24},{1,5},{5... | collective-permute-start | bytes 3145736 | tf_op jit(solution)/shard_map/ppermute | solution.py:140
  135.3 40.8 %collective-permute-start.16 = (f32[256,1024]{1,0:T(8,128)}, f32[256,1024]{1,0:T(8,128)}, u32[]{:S(2)}, u32[]{:S(2)}) collective-permute-start(f32[256,1024]{1,0:T(8,128)} %get-tuple-element.24), channel_id=1, source_target_pairs={{0,2},{1,3},{2,0},{3,1},{4,6},{5,7},{6,4},{7,5},{8,10},{9,11},{10,... | collective-permute-start | bytes 3145736 | tf_op jit(solution)/shard_map/ppermute | solution.py:140
  149.7 33.4 %collective-permute-start.31 = (f32[2,256,512]{2,1,0:T(8,128)S(1)}, f32[2,256,512]{2,1,0:T(8,128)S(1)}, u32[]{:S(2)}, u32[]{:S(2)}) collective-permute-start(f32[2,256,512]{2,1,0:T(8,128)S(1)} %side_payload.3.refs_5_), channel_id=1, source_target_pairs={{0,4},{4,0},{8,12},{12,8},{16,20},{20,16},{24,28},{28,24},{1,5},{5... | collective-permute-start | bytes 3145736 | tf_op jit(solution)/shard_map/ppermute | solution.py:140
  153.3 22.9 %collective-permute-start.23 = (f32[6,128,256]{2,1,0:T(8,128)S(1)}, f32[6,128,256]{2,1,0:T(8,128)S(1)}, u32[]{:S(2)}, u32[]{:S(2)}) collective-permute-start(f32[6,128,256]{2,1,0:T(8,128)S(1)} %own_blocks.5.refs_6_.refs_1_), channel_id=1, source_target_pairs={{0,1},{1,0},{2,3},{3,2},{4,5},{5,4},{6,7},{7,6},{8,9},{9,8},{10,11... | collective-permute-start | bytes 2359304 | tf_op jit(solution)/shard_map/ppermute | solution.py:140
  (36 other events, 193.7 us)

commit v9 on v8

--- a/solution.py
+++ b/solution.py
@@ -90,7 +90,6 @@
 VMEM = pl.BlockSpec(memory_space=pltpu.VMEM)
 SMEM = pl.BlockSpec(memory_space=pltpu.SMEM)
 ANY = pl.BlockSpec(memory_space=pl.ANY)
-PARAMS = pltpu.CompilerParams(vmem_limit_bytes=48 * 2**20)
 NOTHING = pl.CostEstimate(flops=128, bytes_accessed=128, transcendentals=0)
 PAIRS = ((0, 1), (1, 0), (2, 3), (3, 2))
 INWARD = ((0, 1), (3, 2))
@@ -102,7 +101,7 @@
     def __init__(self):
         self.after = []
 
-    def call(self, body, arrays, in_specs, *, out_shape, out_specs, scalars=(), grid=(), scratch_shapes=(), name):
+    def call(self, body, arrays, in_specs, *, out_shape, out_specs, scalars=(), grid=(), scratch_shapes=(), name, vmem=10):
         held, count = len(scalars), len(arrays)
         after = [a for a in self.after if not any(a is b for b in arrays)]
 
@@ -119,7 +118,7 @@
                 out_specs=out_specs,
                 scratch_shapes=scratch_shapes,
             ),
-            compiler_params=PARAMS,
+            compiler_params=pltpu.CompilerParams(vmem_limit_bytes=vmem * 2**20),
             cost_estimate=NOTHING,
             name=name,
         )(*scalars, *arrays, *after)
@@ -307,6 +306,7 @@
             pltpu.VMEM((3, SEQ + pad, LANES), jnp.float32),
         ],
         name="gate",
+        vmem=24,
     )
 
 
@@ -395,6 +395,20 @@
         out_shape=(shape, shape),
         out_specs=(VMEM,) * 2,
         name="add",
+    )
+
+
+def add_rounded(order, mine, other):
+    def body(mine, other, out):
+        out[...] = (mine[...] + other[...]).astype(jnp.bfloat16)
+
+    return order.call(
+        body,
+        (mine, other),
+        [VMEM] * 2,
+        out_shape=jax.ShapeDtypeStruct(mine.shape, jnp.bfloat16),
+        out_specs=VMEM,
+        name="add_rounded",
     )
 
 
@@ -432,6 +446,7 @@
         out_shape=jax.ShapeDtypeStruct((HALF, BLOCK, total * rows), jnp.bfloat16),
         out_specs=VMEM,
         name="arrange_tokens",
+        vmem=20,
     )
 
 
@@ -499,6 +514,7 @@
         out_specs=part,
         scratch_shapes=[pltpu.VMEM((2, count * rows, chans), jnp.bfloat16)],
         name="weight_part",
+        vmem=56,
     )
 
 
@@ -532,6 +548,7 @@
         grid=(count, 3),
         out_specs=pl.BlockSpec((None, rows, wide), lambda i, s, quarters: (i, 0, 0)),
         name="token_part",
+        vmem=12,
     )
 
 
@@ -582,6 +599,8 @@
     own2 = column_blocks(order, place, [(mid, outer2)], True, got2, (0, HALF))
     across2 = flipped(own2, "shard", 2)
     beside2 = flipped(own2, "shard", 1)
+    relayed = order.wait(relayed)
+    relayed_end = lines(part_of(order, place, relayed, 1, 1), OUTWARD)
     over = column_blocks(order, place, [(far, outer3)], False)
     got3 = flipped(over, "rep", 1)
     middle_end = order.wait(middle_end)
@@ -590,37 +609,39 @@
     both1 = flipped(across1, "shard", 1)
     token_grad, away = add(order, keep, summed)
     last = flipped(away, "shard", 2)
-    relayed = order.wait(relayed)
-    relayed_end = lines(part_of(order, place, relayed, 1, 1), OUTWARD)
-    beside2, taps1 = order.wait(beside2, taps1)
+    beside2, across2, taps1 = order.wait(beside2, across2, taps1)
+    both2 = flipped(across2, "shard", 1)
     taps, taps_out = add(order, taps, taps1)
     taps2 = flipped(taps_out, "rep", 2)
-    across2, relayed_end, got3 = order.wait(across2, relayed_end, got3)
-    both2 = flipped(across2, "shard", 1)
+    relayed_end, got3 = order.wait(relayed_end, got3)
     own3 = column_blocks(order, place, [(far, outer3)], True, got3, (0, HALF))
     across3 = flipped(own3, "shard", 2)
     beside3 = flipped(own3, "shard", 1)
     both1 = order.wait(both1)
-    tok = arrange_tokens(order, place, tokens, [(own1, beside1, across1, both1)])
-    both2 = order.wait(both2)
-    early = [(own, None), (inner, first), (own_y, None), (side1, None)]
-    so_far = weight_part(order, place, tok, early)
     side3 = flipped(side_payload(order, place, relayed, relayed_end), "rep", 1)
     side2, across3 = order.wait(side2, across3)
     both3 = flipped(across3, "shard", 1)
-    both3 = order.wait(both3)
-    tok = arrange_tokens(order, place, None, [(own2, beside2, across2, both2)])
-    so_far = weight_part(order, place, tok, [(middle, middle_end), (side2, None)], None, so_far)
-    taps2 = order.wait(taps2)
+    both3, both2, taps2 = order.wait(both3, both2, taps2)
     taps, taps_out = add(order, taps, taps2)
     taps4 = flipped(taps_out, "rep", 4)
-    taps4, beside3, last = order.wait(taps4, beside3, last)
-    token_grad = (token_grad + last).astype(jnp.bfloat16)
-    tok = arrange_tokens(order, place, None, [(own3, beside3, across3, both3)])
+    beside3 = order.wait(beside3)
+    tok3 = arrange_tokens(order, place, None, [(own3, beside3, across3, both3)])
+    tok = arrange_tokens(
+        order,
+        place,
+        tokens,
+        [(own1, beside1, across1, both1), (own2, beside2, across2, both2)],
+    )
+    taps4 = order.wait(taps4)
+    early = [(own, None), (inner, first), (own_y, None), (side1, None)]
+    early += [(middle, middle_end), (side2, None)]
+    so_far = weight_part(order, place, tok, early)
+    last = order.wait(last)
+    token_grad = add_rounded(order, token_grad, last)
+    taps, _ = add(order, taps, taps4, scale=scale)
     side3 = order.wait(side3)
     late = [(relayed, relayed_end), (side3, None)]
-    weight_grad = weight_part(order, place, tok, late, scale, so_far)
-    taps, _ = add(order, taps, taps4, scale=scale)
+    weight_grad = weight_part(order, place, tok3, late, scale, so_far)
     return (token_grad, weight_grad, taps)
 
 

time: 195 us -> 193 us (0.990)
  Pallas kernels: 76.7 us -> 64.6 us
  local copies, waits for them, and re-layouts: 17.3 us -> 26 us
  starting transfers between devices: 39.4 us -> 42.1 us
  other arithmetic: 2.39 us -> 0.23 us
    pallas_call x27 -> x26, Pallas kernels: 76.7 us -> 64.6 us  [call(): pl.pallas_call(short, out_shape=out_shape, grid_spec=pltpu.PrefetchScalar...]
    unnamed x58 -> x60, local copies, waits for them, and re-layouts: 17.3 us -> 26 us
    ppermute x21, waiting for transfers between devices: 34.9 us -> 41.6 us  [flipped(): lax.ppermute(array, axis, [(r, r ^ flip) for r in range(lax.axis_size(axi...]
    ppermute x11, waiting for transfers between devices: 22 us -> 16.7 us  [lines(): return lax.ppermute(array, 'rep', perm)]
    ppermute x11, starting transfers between devices: 20.6 us -> 25.1 us  [lines(): return lax.ppermute(array, 'rep', perm)]
    convert_element_type x1 -> x0, other arithmetic: 2.16 us -> none  [lined(): token_grad = (token_grad + last).astype(jnp.bfloat16)]
  transfers between devices with their start and end apart: 32 -> 32, of which waited for: 12 -> 11; matrix products, arithmetic and copies ran while one was open for 0% -> 0% of each run, Pallas kernels for 36% -> 30%
where the time goes in v9:
time: 193 us; the launch traced here: 192 us
  Pallas kernels  64.6 us (33%)
  waiting for transfers between devices  58.3 us (30%)
  starting transfers between devices  42.1 us (22%)
  local copies, waits for them, and re-layouts  26 us (13%)
    pallas_call x26, Pallas kernels, call(): pl.pallas_call(short, out_shape=out_shape, grid_spec=pltpu.PrefetchScalar...  64.6 us
    ppermute x21, waiting for transfers between devices, flipped(): lax.ppermute(array, axis, [(r, r ^ flip) for r in range(lax.axis_size(axi...  41.6 us
    unnamed x60, local copies, waits for them, and re-layouts  26 us
    ppermute x11, starting transfers between devices, lines(): return lax.ppermute(array, 'rep', perm)  25.1 us
    ppermute x21, starting transfers between devices, flipped(): lax.ppermute(array, axis, [(r, r ^ flip) for r in range(lax.axis_size(axi...  17 us
    ppermute x11, waiting for transfers between devices, lines(): return lax.ppermute(array, 'rep', perm)  16.7 us
  transfers between devices with their start and end apart: 32, of which 11 were waited for; matrix products, arithmetic and copies ran while one was open for 0% of the time, Pallas kernels for 30%

profile of v9, /device:TPU:0, one launch (start us, length us, event | category | flops | bytes accessed | tf_op | source)
XLA Modules:
  0.0 192.3 jit_solution(2931764872217942603)
XLA Ops:
  3.1 3.1 %collective-permute-start.1 = (f32[8,128,256]{2,1,0:T(8,128)S(1)}, f32[8,128,256]{2,1,0:T(8,128)}, u32[]{:S(2)}, u32[]{:S(2)}) collective-permute-start(f32[8,128,256]{2,1,0:T(8,128)S(1)} %turn_tokens.1.refs_5_.refs_1_), channel_id=1, source_target_pairs={{0,8},{4,12},{8,0},{12,4},{16,24},{20,28},{24,16},{28,20},{1,9},{5... | collective-permute-start | bytes 3145736 | tf_op jit(solution)/shard_map/ppermute | solution.py:135
  7.0 4.6 %copy-done = bf16[3,4096,512]{2,1,0:T(8,128)(2,1)S(1)} copy-done((bf16[3,4096,512]{2,1,0:T(8,128)(2,1)S(1)}, bf16[3,4096,512]{2,1,0:T(8,128)(2,1)}, u32[]{:S(2)}) %copy-start) | copy-done | bytes 12582936
  11.6 15.5 %gate.1 = (bf16[3,256,512]{2,1,0:T(8,128)(2,1)S(1)}, f32[7,3,512]{2,1,0:T(4,128)S(1)}, f32[1,256,512]{2,1,0:T(8,128)}, f32[2,256,512]{2,1,0:T(8,128)}, f32[2,256,512]{2,1,0:T(8,128)}) custom-call(s32[3]{0:T(128)S(1)} %pad_add_fusion.1.refs_0_, bf16[256,4096]{1,0:T(8,128)(2,1)S(1)} %copy-done.6, bf16[3,4096,512]{2,1,0:T(8,128)(2,1)S(1)} %copy-done, ...), custom_call_target="tpu_custom_call" | custom-call | flops 128 | bytes 128 | tf_op jit(solution)/shard_map/gate/pallas_call | solution.py:111
  28.6 7.2 %collective-permute-start.2 = (f32[2,256,512]{2,1,0:T(8,128)}, f32[2,256,512]{2,1,0:T(8,128)}, u32[]{:S(2)}, u32[]{:S(2)}) collective-permute-start(f32[2,256,512]{2,1,0:T(8,128)} %get-tuple-element.18), channel_id=1, source_target_pairs={{0,8},{4,12},{24,16},{28,20},{1,9},{5,13},{25,17},{29,21},{2,10},{... | collective-permute-start | bytes 3145736 | tf_op jit(solution)/shard_map/ppermute | solution.py:135
  37.5 2.2 %other_blocks.3.refs_2_ = f32[6,128,256]{2,1,0:T(8,128)} custom-call(s32[3]{0:T(128)S(1)} %pad_add_fusion.1.refs_0_, f32[8,128,256]{2,1,0:T(8,128)S(1)} %turn_tokens.1.refs_5_.refs_1_, f32[8,128,256]{2,1,0:T(8,128)} %collective-permute-done.1.refs_2_.refs_1_, bf16[3,256,512]{2,1,0:T(8,128)(2,1)S(1)} %get-tuple-element.17.refs_3_.refs_1_.refs_2_), custom_call_target="tpu_custom_call" | custom-call | flops 128 | bytes 128 | tf_op jit(solution)/shard_map/other_blocks/pallas_call | solution.py:111
  43.3 4.6 %copy-done.1 = bf16[3,4096,512]{2,1,0:T(8,128)(2,1)S(1)} copy-done((bf16[3,4096,512]{2,1,0:T(8,128)(2,1)S(1)}, bf16[3,4096,512]{2,1,0:T(8,128)(2,1)}, u32[]{:S(2)}) %copy-start.1) | copy-done | bytes 12582936
  49.0 5.3 %token_part.2.refs_3_ = f32[2,256,1024]{2,1,0:T(8,128)} custom-call(s32[2]{0:T(128)S(1)} %pad_add_fusion.2.refs_0_, bf16[3,256,512]{2,1,0:T(8,128)(2,1)S(1)} %copy-done.10, bf16[3,4096,512]{2,1,0:T(8,128)(2,1)S(1)} %copy-done.1, f32[6,128,256]{2,1,0:T(8,128)} %part_of.4.refs_3_), custom_call_target="tpu_custom_call" | custom-call | flops 128 | bytes 128 | tf_op jit(solution)/shard_map/token_part/pallas_call | solution.py:111
  56.7 5.8 %collective-permute-start.8 = (f32[1,256,512]{2,1,0:T(8,128)}, f32[1,256,512]{2,1,0:T(8,128)}, u32[]{:S(2)}, u32[]{:S(2)}) collective-permute-start(f32[1,256,512]{2,1,0:T(8,128)} %get-tuple-element.20), channel_id=1, source_target_pairs={{0,8},{4,12},{8,0},{12,4},{16,24},{20,28},{24,16},{28,20},{1,9},{5... | collective-permute-start | bytes 1572872 | tf_op jit(solution)/shard_map/ppermute | solution.py:135
  62.6 4.6 %copy-done.2 = bf16[3,4096,512]{2,1,0:T(8,128)(2,1)S(1)} copy-done((bf16[3,4096,512]{2,1,0:T(8,128)(2,1)S(1)}, bf16[3,4096,512]{2,1,0:T(8,128)(2,1)}, u32[]{:S(2)}) %copy-start.2) | copy-done | bytes 12582936
  68.3 4.0 %token_part.3.refs_2_.refs_0_ = f32[2,256,1024]{2,1,0:T(8,128)S(1)} custom-call(s32[2]{0:T(128)S(1)} %pad_add_fusion.refs_0_, bf16[3,256,512]{2,1,0:T(8,128)(2,1)S(1)} %copy-done.11, bf16[3,4096,512]{2,1,0:T(8,128)(2,1)S(1)} %copy-done.2, f32[2,256,1024]{2,1,0:T(8,128)} %token_part.2.refs_3_, f32[2,256,512]{2,1,0:T(8,128)} %collective-permute-done.2.refs_4_.refs_2_.refs_3_, ...), custom_call_target="tpu_custom_call" | custom-call | flops 128 | bytes 128 | tf_op jit(solution)/shard_map/token_part/pallas_call | solution.py:111
  82.0 10.3 %collective-permute-done.11.refs_4_.refs_2_ = f32[6,128,256]{2,1,0:T(8,128)S(1)} collective-permute-done((f32[6,128,256]{2,1,0:T(8,128)S(1)}, f32[6,128,256]{2,1,0:T(8,128)S(1)}, u32[]{:S(2)}, u32[]{:S(2)}) %collective-permute-start.11) | collective-permute-done | bytes 786464 | tf_op jit(solution)/shard_map/ppermute | solution.py:135
  93.0 7.4 %collective-permute-done.12.refs_5_.refs_6_ = f32[2,256,512]{2,1,0:T(8,128)S(1)} collective-permute-done((f32[2,256,512]{2,1,0:T(8,128)S(1)}, f32[2,256,512]{2,1,0:T(8,128)S(1)}, u32[]{:S(2)}, u32[]{:S(2)}) %collective-permute-start.12) | collective-permute-done | bytes 1048608 | tf_op jit(solution)/shard_map/ppermute | solution.py:139
  103.7 5.0 %collective-permute-done.15.refs_3_ = f32[3,128,256]{2,1,0:T(8,128)S(1)} collective-permute-done((f32[3,128,256]{2,1,0:T(8,128)S(1)}, f32[3,128,256]{2,1,0:T(8,128)S(1)}, u32[]{:S(2)}, u32[]{:S(2)}) %collective-permute-start.15) | collective-permute-done | bytes 393248 | tf_op jit(solution)/shard_map/ppermute | solution.py:139
  114.1 2.1 %collective-permute-done.23.refs_1_ = f32[7,3,512]{2,1,0:T(4,128)S(1)} collective-permute-done((f32[7,3,512]{2,1,0:T(4,128)S(1)}, f32[7,3,512]{2,1,0:T(4,128)S(1)}, u32[]{:S(2)}, u32[]{:S(2)}) %collective-permute-start.23) | collective-permute-done | bytes 43040 | tf_op jit(solution)/shard_map/ppermute | solution.py:139
  121.0 2.8 %add.18 = (f32[256,1024]{1,0:T(8,128)S(1)}, f32[256,1024]{1,0:T(8,128)}) custom-call(f32[2,256,1024]{2,1,0:T(8,128)S(1)} %token_part.3.refs_2_.refs_0_, f32[2,256,1024]{2,1,0:T(8,128)} %collective-permute-done.5.refs_5_.refs_1_, f32[2,256,512]{2,1,0:T(8,128)S(1)} %side_payload.2.refs_2_, f32[9,128,256]{2,1,0:T(8,128)S(1)} %collective-permute-done.16.refs_3_.refs_4_), custom_call_target="tpu_custom_call" | custom-call | flops 128 | bytes 128 | tf_op jit(solution)/shard_map/add/pallas_call | solution.py:111
  125.7 3.4 %collective-permute-done.22.refs_3_ = f32[3,128,256]{2,1,0:T(8,128)S(1)} collective-permute-done((f32[3,128,256]{2,1,0:T(8,128)S(1)}, f32[3,128,256]{2,1,0:T(8,128)S(1)}, u32[]{:S(2)}, u32[]{:S(2)}) %collective-permute-start.22) | collective-permute-done | bytes 393248 | tf_op jit(solution)/shard_map/ppermute | solution.py:139
  129.1 4.5 %collective-permute-done.24.refs_5_.refs_2_.refs_3_ = f32[1,256,512]{2,1,0:T(8,128)S(1)} collective-permute-done((f32[1,256,512]{2,1,0:T(8,128)S(1)}, f32[1,256,512]{2,1,0:T(8,128)S(1)}, u32[]{:S(2)}, u32[]{:S(2)}) %collective-permute-start.24) | collective-permute-done | bytes 524320 | tf_op jit(solution)/shard_map/ppermute | solution.py:135
  140.0 2.6 %collective-permute-done.28.refs_1_ = f32[7,3,512]{2,1,0:T(4,128)S(1)} collective-permute-done((f32[7,3,512]{2,1,0:T(4,128)S(1)}, f32[7,3,512]{2,1,0:T(4,128)S(1)}, u32[]{:S(2)}, u32[]{:S(2)}) %collective-permute-start.28) | collective-permute-done | bytes 43040 | tf_op jit(solution)/shard_map/ppermute | solution.py:139
  142.8 12.8 %collective-permute-done.26.refs_4_.refs_3_ = f32[6,128,256]{2,1,0:T(8,128)S(1)} collective-permute-done((f32[6,128,256]{2,1,0:T(8,128)S(1)}, f32[6,128,256]{2,1,0:T(8,128)S(1)}, u32[]{:S(2)}, u32[]{:S(2)}) %collective-permute-start.26) | collective-permute-done | bytes 786464 | tf_op jit(solution)/shard_map/ppermute | solution.py:139
  156.2 6.5 %collective-permute-done.29.refs_3_.refs_9_ = f32[2,256,512]{2,1,0:T(8,128)S(1)} collective-permute-done((f32[2,256,512]{2,1,0:T(8,128)S(1)}, f32[2,256,512]{2,1,0:T(8,128)S(1)}, u32[]{:S(2)}, u32[]{:S(2)}) %collective-permute-start.29) | collective-permute-done | bytes 1048608 | tf_op jit(solution)/shard_map/ppermute | solution.py:139
  167.2 2.2 %copy-done.4 = bf16[3,512,1536]{2,1,0:T(8,128)(2,1)} copy-done((bf16[3,512,1536]{2,1,0:T(8,128)(2,1)}, bf16[3,512,1536]{2,1,0:T(8,128)(2,1)S(1)}, u32[]{:S(2)}) %copy-start.4) | copy-done | bytes 4718616
  170.0 8.6 %weight_part.2.refs_2_.refs_5_ = f32[1536,512]{1,0:T(8,128)} custom-call(s32[3]{0:T(128)} %copy-done.26, bf16[3,512,1536]{2,1,0:T(8,128)(2,1)} %copy-done.4, bf16[3,256,512]{2,1,0:T(8,128)(2,1)} %copy-done.9, f32[2,256,512]{2,1,0:T(8,128)} %collective-permute-done.2.refs_4_.refs_2_.refs_3_, f32[1,256,512]{2,1,0:T(8,128)} %collective-permute-done.8.refs_1_.refs_4_, ...), custom_call_target="tpu_custom_call" | custom-call | flops 128 | bytes 128 | tf_op jit(solution)/shard_map/weight_part/pallas_call | solution.py:111
  180.6 2.1 %add_rounded.1.refs_2_ = bf16[256,1024]{1,0:T(8,128)(2,1)} custom-call(f32[256,1024]{1,0:T(8,128)S(1)} %copy-done.19, f32[256,1024]{1,0:T(8,128)} %collective-permute-done.17.refs_1_, f32[1536,512]{1,0:T(8,128)S(1)} %copy-done.3), custom_call_target="tpu_custom_call" | custom-call | flops 128 | bytes 128 | tf_op jit(solution)/shard_map/add_rounded/pallas_call | solution.py:111
  186.0 6.3 %weight_part.3 = f32[1536,512]{1,0:T(8,128)} custom-call(s32[3]{0:T(128)} %copy-done.26, bf16[3,512,512]{2,1,0:T(8,128)(2,1)} %copy-done.8, f32[2,256,512]{2,1,0:T(8,128)} %copy-done.12, f32[1,256,512]{2,1,0:T(8,128)} %copy-done.15, f32[2,256,512]{2,1,0:T(8,128)} %copy-done.27, f32[1536,512]{1,0:T(8,128)} %weight_part.2.refs_2_.refs_5_, f32[7,3,512]{2,1,0:T(4,128)} %copy-done.25), custom_call_target="tpu_custom_call" | custom-call | flops 128 | bytes 128 | tf_op jit(solution)/shard_map/weight_part/pallas_call | solution.py:111
  (129 shorter events, 57.9 us)
Async XLA Ops:
  3.1 32.7 %collective-permute-start.1 = (f32[8,128,256]{2,1,0:T(8,128)S(1)}, f32[8,128,256]{2,1,0:T(8,128)}, u32[]{:S(2)}, u32[]{:S(2)}) collective-permute-start(f32[8,128,256]{2,1,0:T(8,128)S(1)} %turn_tokens.1.refs_5_.refs_1_), channel_id=1, source_target_pairs={{0,8},{4,12},{8,0},{12,4},{16,24},{20,28},{24,16},{28,20},{1,9},{5... | collective-permute-start | bytes 3145736 | tf_op jit(solution)/shard_map/ppermute | solution.py:135
  6.2 33.5 %collective-permute-start = (f32[8,128,256]{2,1,0:T(8,128)S(1)}, f32[8,128,256]{2,1,0:T(8,128)S(1)}, u32[]{:S(2)}, u32[]{:S(2)}) collective-permute-start(f32[8,128,256]{2,1,0:T(8,128)S(1)} %turn_tokens.1.refs_5_.refs_1_), channel_id=1, source_target_pairs={{8,16},{12,20},{16,8},{20,12},{9,17},{13,21},{17,9},{21,13},{10,18... | collective-permute-start | bytes 3145736 | tf_op jit(solution)/shard_map/ppermute | solution.py:135
  27.1 27.2 %collective-permute-start.3 = (f32[2,256,512]{2,1,0:T(8,128)}, f32[2,256,512]{2,1,0:T(8,128)}, u32[]{:S(2)}, u32[]{:S(2)}) collective-permute-start(f32[2,256,512]{2,1,0:T(8,128)} %get-tuple-element.18), channel_id=1, source_target_pairs={{0,4},{4,0},{8,12},{12,8},{16,20},{20,16},{24,28},{28,24},{1,5},{5... | collective-permute-start | bytes 3145736 | tf_op jit(solution)/shard_map/ppermute | solution.py:139
  28.6 28.1 %collective-permute-start.2 = (f32[2,256,512]{2,1,0:T(8,128)}, f32[2,256,512]{2,1,0:T(8,128)}, u32[]{:S(2)}, u32[]{:S(2)}) collective-permute-start(f32[2,256,512]{2,1,0:T(8,128)} %get-tuple-element.18), channel_id=1, source_target_pairs={{0,8},{4,12},{24,16},{28,20},{1,9},{5,13},{25,17},{29,21},{2,10},{... | collective-permute-start | bytes 3145736 | tf_op jit(solution)/shard_map/ppermute | solution.py:135
  35.8 20.9 %collective-permute-start.4 = (f32[8,128,256]{2,1,0:T(8,128)}, f32[8,128,256]{2,1,0:T(8,128)}, u32[]{:S(2)}, u32[]{:S(2)}) collective-permute-start(f32[8,128,256]{2,1,0:T(8,128)} %collective-permute-done.1.refs_2_.refs_1_), channel_id=1, source_target_pairs={{8,16},{12,20},{16,8},{20,12},{9,17},{13,21},{17,9},{21,13},{10,18... | collective-permute-start | bytes 3145736 | tf_op jit(solution)/shard_map/ppermute | solution.py:135
  41.2 32.5 %collective-permute-start.9 = (f32[6,128,256]{2,1,0:T(8,128)}, f32[6,128,256]{2,1,0:T(8,128)}, u32[]{:S(2)}, u32[]{:S(2)}) collective-permute-start(f32[6,128,256]{2,1,0:T(8,128)} %part_of.4.refs_3_), channel_id=1, source_target_pairs={{8,0},{12,4},{16,24},{20,28},{9,1},{13,5},{17,25},{21,29},{10,2},{... | collective-permute-start | bytes 2359304 | tf_op jit(solution)/shard_map/ppermute | solution.py:135
  42.5 35.9 %collective-permute-start.6 = (f32[2,256,512]{2,1,0:T(8,128)}, f32[2,256,512]{2,1,0:T(8,128)S(1)}, u32[]{:S(2)}, u32[]{:S(2)}) collective-permute-start(f32[2,256,512]{2,1,0:T(8,128)} %get-tuple-element.19), channel_id=1, source_target_pairs={{8,16},{12,20},{16,8},{20,12},{9,17},{13,21},{17,9},{21,13},{10,18... | collective-permute-start | bytes 3145736 | tf_op jit(solution)/shard_map/ppermute | solution.py:135
  54.3 24.1 %collective-permute-start.7 = (f32[6,128,256]{2,1,0:T(8,128)}, f32[6,128,256]{2,1,0:T(8,128)}, u32[]{:S(2)}, u32[]{:S(2)}) collective-permute-start(f32[6,128,256]{2,1,0:T(8,128)} %other_blocks.3.refs_2_), channel_id=1, source_target_pairs={{0,4},{4,0},{8,12},{12,8},{16,20},{20,16},{24,28},{28,24},{1,5},{5... | collective-permute-start | bytes 2359304 | tf_op jit(solution)/shard_map/ppermute | solution.py:139
  56.7 51.9 %collective-permute-start.5 = (f32[2,256,1024]{2,1,0:T(8,128)}, f32[2,256,1024]{2,1,0:T(8,128)}, u32[]{:S(2)}, u32[]{:S(2)}) collective-permute-start(f32[2,256,1024]{2,1,0:T(8,128)} %token_part.2.refs_3_), channel_id=1, source_target_pairs={{0,1},{1,0},{2,3},{3,2},{4,5},{5,4},{6,7},{7,6},{8,9},{9,8},{10,11... | collective-permute-start | bytes 6291464 | tf_op jit(solution)/shard_map/ppermute | solution.py:139
  56.7 19.5 %collective-permute-start.8 = (f32[1,256,512]{2,1,0:T(8,128)}, f32[1,256,512]{2,1,0:T(8,128)}, u32[]{:S(2)}, u32[]{:S(2)}) collective-permute-start(f32[1,256,512]{2,1,0:T(8,128)} %get-tuple-element.20), channel_id=1, source_target_pairs={{0,8},{4,12},{8,0},{12,4},{16,24},{20,28},{24,16},{28,20},{1,9},{5... | collective-permute-start | bytes 1572872 | tf_op jit(solution)/shard_map/ppermute | solution.py:135
  73.7 18.6 %collective-permute-start.11 = (f32[6,128,256]{2,1,0:T(8,128)S(1)}, f32[6,128,256]{2,1,0:T(8,128)S(1)}, u32[]{:S(2)}, u32[]{:S(2)}) collective-permute-start(f32[6,128,256]{2,1,0:T(8,128)S(1)} %part_of.5.refs_3_), channel_id=1, source_target_pairs={{8,0},{12,4},{16,24},{20,28},{9,1},{13,5},{17,25},{21,29},{10,2},{... | collective-permute-start | bytes 2359304 | tf_op jit(solution)/shard_map/ppermute | solution.py:135
  77.8 22.6 %collective-permute-start.12 = (f32[2,256,512]{2,1,0:T(8,128)S(1)}, f32[2,256,512]{2,1,0:T(8,128)S(1)}, u32[]{:S(2)}, u32[]{:S(2)}) collective-permute-start(f32[2,256,512]{2,1,0:T(8,128)S(1)} %get-tuple-element.22), channel_id=1, source_target_pairs={{0,4},{4,0},{8,12},{12,8},{16,20},{20,16},{24,28},{28,24},{1,5},{5... | collective-permute-start | bytes 3145736 | tf_op jit(solution)/shard_map/ppermute | solution.py:139
  80.3 21.4 %collective-permute-start.10 = (f32[9,128,256]{2,1,0:T(8,128)S(1)}, f32[9,128,256]{2,1,0:T(8,128)S(1)}, u32[]{:S(2)}, u32[]{:S(2)}) collective-permute-start(f32[9,128,256]{2,1,0:T(8,128)S(1)} %own_blocks.3.refs_2_), channel_id=1, source_target_pairs={{0,1},{1,0},{2,3},{3,2},{4,5},{5,4},{6,7},{7,6},{8,9},{9,8},{10,11... | collective-permute-start | bytes 3538952 | tf_op jit(solution)/shard_map/ppermute | solution.py:139
  80.4 31.1 %collective-permute-start.16 = (f32[9,128,256]{2,1,0:T(8,128)S(1)}, f32[9,128,256]{2,1,0:T(8,128)S(1)}, u32[]{:S(2)}, u32[]{:S(2)}) collective-permute-start(f32[9,128,256]{2,1,0:T(8,128)S(1)} %own_blocks.3.refs_2_), channel_id=1, source_target_pairs={{0,2},{1,3},{2,0},{3,1},{4,6},{5,7},{6,4},{7,5},{8,10},{9,11},{10,... | collective-permute-start | bytes 3538952 | tf_op jit(solution)/shard_map/ppermute | solution.py:139
  92.3 19.7 %collective-permute-start.14 = (f32[2,256,512]{2,1,0:T(8,128)S(1)}, f32[2,256,512]{2,1,0:T(8,128)S(1)}, u32[]{:S(2)}, u32[]{:S(2)}) collective-permute-start(f32[2,256,512]{2,1,0:T(8,128)S(1)} %get-tuple-element.21.refs_3_), channel_id=1, source_target_pairs={{8,16},{12,20},{16,8},{20,12},{9,17},{13,21},{17,9},{21,13},{10,18... | collective-permute-start | bytes 3145736 | tf_op jit(solution)/shard_map/ppermute | solution.py:135
  102.3 16.4 %collective-permute-start.13 = (f32[1,256,512]{2,1,0:T(8,128)S(1)}, f32[1,256,512]{2,1,0:T(8,128)S(1)}, u32[]{:S(2)}, u32[]{:S(2)}) collective-permute-start(f32[1,256,512]{2,1,0:T(8,128)S(1)} %part_of.6.refs_4_), channel_id=1, source_target_pairs={{8,0},{12,4},{16,24},{20,28},{9,1},{13,5},{17,25},{21,29},{10,2},{... | collective-permute-start | bytes 1572872 | tf_op jit(solution)/shard_map/ppermute | solution.py:135
  109.9 15.8 %collective-permute-start.20 = (f32[6,128,256]{2,1,0:T(8,128)S(1)}, f32[6,128,256]{2,1,0:T(8,128)S(1)}, u32[]{:S(2)}, u32[]{:S(2)}) collective-permute-start(f32[6,128,256]{2,1,0:T(8,128)S(1)} %own_blocks.4.refs_2_.refs_6_), channel_id=1, source_target_pairs={{0,2},{1,3},{2,0},{3,1},{4,6},{5,7},{6,4},{7,5},{8,10},{9,11},{10,... | collective-permute-start | bytes 2359304 | tf_op jit(solution)/shard_map/ppermute | solution.py:139
  111.5 27.3 %collective-permute-start.18 = (f32[9,128,256]{2,1,0:T(8,128)S(1)}, f32[9,128,256]{2,1,0:T(8,128)S(1)}, u32[]{:S(2)}, u32[]{:S(2)}) collective-permute-start(f32[9,128,256]{2,1,0:T(8,128)S(1)} %collective-permute-done.16.refs_3_.refs_4_), channel_id=1, source_target_pairs={{0,1},{1,0},{2,3},{3,2},{4,5},{5,4},{6,7},{7,6},{8,9},{9,8},{10,11... | collective-permute-start | bytes 3538952 | tf_op jit(solution)/shard_map/ppermute | solution.py:139
  116.2 17.4 %collective-permute-start.24 = (f32[1,256,512]{2,1,0:T(8,128)S(1)}, f32[1,256,512]{2,1,0:T(8,128)S(1)}, u32[]{:S(2)}, u32[]{:S(2)}) collective-permute-start(f32[1,256,512]{2,1,0:T(8,128)S(1)} %part_of.7.refs_3_), channel_id=1, source_target_pairs={{8,0},{12,4},{16,24},{20,28},{9,1},{13,5},{17,25},{21,29},{10,2},{... | collective-permute-start | bytes 1572872 | tf_op jit(solution)/shard_map/ppermute | solution.py:135
  135.1 20.5 %collective-permute-start.26 = (f32[6,128,256]{2,1,0:T(8,128)S(1)}, f32[6,128,256]{2,1,0:T(8,128)S(1)}, u32[]{:S(2)}, u32[]{:S(2)}) collective-permute-start(f32[6,128,256]{2,1,0:T(8,128)S(1)} %own_blocks.5.refs_3_.refs_1_), channel_id=1, source_target_pairs={{0,2},{1,3},{2,0},{3,1},{4,6},{5,7},{6,4},{7,5},{8,10},{9,11},{10,... | collective-permute-start | bytes 2359304 | tf_op jit(solution)/shard_map/ppermute | solution.py:139
  136.6 19.0 %collective-permute-start.21 = (f32[6,128,256]{2,1,0:T(8,128)S(1)}, f32[6,128,256]{2,1,0:T(8,128)S(1)}, u32[]{:S(2)}, u32[]{:S(2)}) collective-permute-start(f32[6,128,256]{2,1,0:T(8,128)S(1)} %collective-permute-done.20.refs_4_.refs_8_), channel_id=1, source_target_pairs={{0,1},{1,0},{2,3},{3,2},{4,5},{5,4},{6,7},{7,6},{8,9},{9,8},{10,11... | collective-permute-start | bytes 2359304 | tf_op jit(solution)/shard_map/ppermute | solution.py:139
  136.6 26.0 %collective-permute-start.29 = (f32[2,256,512]{2,1,0:T(8,128)S(1)}, f32[2,256,512]{2,1,0:T(8,128)S(1)}, u32[]{:S(2)}, u32[]{:S(2)}) collective-permute-start(f32[2,256,512]{2,1,0:T(8,128)S(1)} %side_payload.2.refs_2_), channel_id=1, source_target_pairs={{0,4},{4,0},{8,12},{12,8},{16,20},{20,16},{24,28},{28,24},{1,5},{5... | collective-permute-start | bytes 3145736 | tf_op jit(solution)/shard_map/ppermute | solution.py:139
  138.8 39.9 %collective-permute-start.17 = (f32[256,1024]{1,0:T(8,128)}, f32[256,1024]{1,0:T(8,128)}, u32[]{:S(2)}, u32[]{:S(2)}) collective-permute-start(f32[256,1024]{1,0:T(8,128)} %get-tuple-element.24), channel_id=1, source_target_pairs={{0,2},{1,3},{2,0},{3,1},{4,6},{5,7},{6,4},{7,5},{8,10},{9,11},{10,... | collective-permute-start | bytes 3145736 | tf_op jit(solution)/shard_map/ppermute | solution.py:139
  142.6 42.5 %collective-permute-start.31 = (f32[2,256,512]{2,1,0:T(8,128)S(1)}, f32[2,256,512]{2,1,0:T(8,128)S(1)}, u32[]{:S(2)}, u32[]{:S(2)}) collective-permute-start(f32[2,256,512]{2,1,0:T(8,128)S(1)} %side_payload.3.refs_2_), channel_id=1, source_target_pairs={{0,4},{4,0},{8,12},{12,8},{16,20},{20,16},{24,28},{28,24},{1,5},{5... | collective-permute-start | bytes 3145736 | tf_op jit(solution)/shard_map/ppermute | solution.py:139
  (37 other events, 393.0 us)

commit v10 on v9

--- a/solution.py
+++ b/solution.py
@@ -306,7 +306,7 @@
             pltpu.VMEM((3, SEQ + pad, LANES), jnp.float32),
         ],
         name="gate",
-        vmem=24,
+        vmem=50,
     )
 
 
@@ -514,7 +514,7 @@
         out_specs=part,
         scratch_shapes=[pltpu.VMEM((2, count * rows, chans), jnp.bfloat16)],
         name="weight_part",
-        vmem=56,
+        vmem=58,
     )
 
 
@@ -548,7 +548,7 @@
         grid=(count, 3),
         out_specs=pl.BlockSpec((None, rows, wide), lambda i, s, quarters: (i, 0, 0)),
         name="token_part",
-        vmem=12,
+        vmem=50,
     )
 
 
@@ -575,10 +575,10 @@
     far = lines(near, MIDDLE)
     over = column_blocks(order, place, [(piece, None), (near, None)], False)
     got1 = flipped(over, "rep", 1)
+    send = token_part(order, jnp.stack(quarters[:2]), own, in_weight)
+    summed = flipped(send, "shard", 1)
     mid = order.wait(mid)
     outer2 = lines(part_of(order, place, mid, BLOCKS - OWN, OWN), OUTWARD)
-    send = token_part(order, jnp.stack(quarters[:2]), own, in_weight)
-    summed = flipped(send, "shard", 1)
     inner, own_y, far = order.wait(inner, own_y, far)
     keep = token_part(order, jnp.stack(quarters[2:]), own, in_weight)
     outer3 = lines(part_of(order, place, far, BLOCKS - OWN, OWN), OUTWARD)
@@ -590,58 +590,54 @@
     relayed = lines(relay, MIDDLE)
     side1 = flipped(side1, "rep", 1)
     middle, got1 = order.wait(middle, got1)
+    middle_end = lines(part_of(order, place, middle, 1, 1), OUTWARD)
     own1 = column_blocks(order, place, [(near, None)], True, got1, (0, OWN))
     across1 = flipped(own1, "shard", 2)
     beside1 = flipped(own1, "shard", 1)
-    beside1, outer3, side1 = order.wait(beside1, outer3, side1)
-    middle_end = lines(part_of(order, place, middle, 1, 1), OUTWARD)
+    outer3 = order.wait(outer3)
+    over = column_blocks(order, place, [(far, outer3)], False)
+    got3 = flipped(over, "rep", 1)
     summed, got2 = order.wait(summed, got2)
     own2 = column_blocks(order, place, [(mid, outer2)], True, got2, (0, HALF))
     across2 = flipped(own2, "shard", 2)
     beside2 = flipped(own2, "shard", 1)
     relayed = order.wait(relayed)
     relayed_end = lines(part_of(order, place, relayed, 1, 1), OUTWARD)
-    over = column_blocks(order, place, [(far, outer3)], False)
-    got3 = flipped(over, "rep", 1)
     middle_end = order.wait(middle_end)
     side2 = flipped(side_payload(order, place, middle, middle_end), "rep", 1)
-    across1 = order.wait(across1)
+    across1, relayed_end = order.wait(across1, relayed_end)
     both1 = flipped(across1, "shard", 1)
     token_grad, away = add(order, keep, summed)
     last = flipped(away, "shard", 2)
-    beside2, across2, taps1 = order.wait(beside2, across2, taps1)
+    beside2, beside1, side1, across2, got3, taps1 = order.wait(
+        beside2, beside1, side1, across2, got3, taps1
+    )
     both2 = flipped(across2, "shard", 1)
     taps, taps_out = add(order, taps, taps1)
     taps2 = flipped(taps_out, "rep", 2)
-    relayed_end, got3 = order.wait(relayed_end, got3)
     own3 = column_blocks(order, place, [(far, outer3)], True, got3, (0, HALF))
     across3 = flipped(own3, "shard", 2)
     beside3 = flipped(own3, "shard", 1)
     both1 = order.wait(both1)
+    tok = arrange_tokens(order, place, tokens, [(own1, beside1, across1, both1)])
+    taps2 = order.wait(taps2)
     side3 = flipped(side_payload(order, place, relayed, relayed_end), "rep", 1)
-    side2, across3 = order.wait(side2, across3)
+    early = [(own, None), (inner, first), (own_y, None), (side1, None)]
+    so_far = weight_part(order, place, tok, early)
+    beside3, across3, side2, both2 = order.wait(beside3, across3, side2, both2)
     both3 = flipped(across3, "shard", 1)
-    both3, both2, taps2 = order.wait(both3, both2, taps2)
     taps, taps_out = add(order, taps, taps2)
     taps4 = flipped(taps_out, "rep", 4)
-    beside3 = order.wait(beside3)
-    tok3 = arrange_tokens(order, place, None, [(own3, beside3, across3, both3)])
-    tok = arrange_tokens(
-        order,
-        place,
-        tokens,
-        [(own1, beside1, across1, both1), (own2, beside2, across2, both2)],
-    )
-    taps4 = order.wait(taps4)
-    early = [(own, None), (inner, first), (own_y, None), (side1, None)]
-    early += [(middle, middle_end), (side2, None)]
-    so_far = weight_part(order, place, tok, early)
+    both3 = order.wait(both3)
+    late = [(own2, beside2, across2, both2), (own3, beside3, across3, both3)]
+    tok = arrange_tokens(order, place, None, late)
+    side3 = order.wait(side3)
+    late = [(middle, middle_end), (side2, None), (relayed, relayed_end), (side3, None)]
+    weight_grad = weight_part(order, place, tok, late, scale, so_far)
     last = order.wait(last)
     token_grad = add_rounded(order, token_grad, last)
+    taps4 = order.wait(taps4)
     taps, _ = add(order, taps, taps4, scale=scale)
-    side3 = order.wait(side3)
-    late = [(relayed, relayed_end), (side3, None)]
-    weight_grad = weight_part(order, place, tok3, late, scale, so_far)
     return (token_grad, weight_grad, taps)
 
 

time: 193 us -> 190 us (0.984)
  local copies, waits for them, and re-layouts: 26 us -> 14.5 us
  Pallas kernels: 64.6 us -> 75.2 us
  waiting for transfers between devices: 58.3 us -> 54.6 us
    unnamed x60, local copies, waits for them, and re-layouts: 26 us -> 14.5 us
    pallas_call x26, Pallas kernels: 64.6 us -> 75.2 us  [call(): pl.pallas_call(short, out_shape=out_shape, grid_spec=pltpu.PrefetchScalar...]
    ppermute x21, waiting for transfers between devices: 41.6 us -> 31.7 us  [flipped(): lax.ppermute(array, axis, [(r, r ^ flip) for r in range(lax.axis_size(axi...]
    ppermute x11, waiting for transfers between devices: 16.7 us -> 22.9 us  [lines(): return lax.ppermute(array, 'rep', perm)]
    ppermute x21, starting transfers between devices: 17 us -> 22.3 us  [flipped(): lax.ppermute(array, axis, [(r, r ^ flip) for r in range(lax.axis_size(axi...]
    ppermute x11, starting transfers between devices: 25.1 us -> 20.7 us  [lines(): return lax.ppermute(array, 'rep', perm)]
  transfers between devices with their start and end apart: 32 -> 32, of which waited for: 11 -> 12; matrix products, arithmetic and copies ran while one was open for 0% -> 0% of each run, Pallas kernels for 30% -> 39%
where the time goes in v10:
time: 190 us; the launch traced here: 189 us
  Pallas kernels  75.2 us (40%)
  waiting for transfers between devices  54.6 us (29%)
  starting transfers between devices  42.9 us (23%)
  local copies, waits for them, and re-layouts  14.5 us (8%)
    pallas_call x26, Pallas kernels, call(): pl.pallas_call(short, out_shape=out_shape, grid_spec=pltpu.PrefetchScalar...  75.2 us
    ppermute x21, waiting for transfers between devices, flipped(): lax.ppermute(array, axis, [(r, r ^ flip) for r in range(lax.axis_size(axi...  31.7 us
    ppermute x11, waiting for transfers between devices, lines(): return lax.ppermute(array, 'rep', perm)  22.9 us
    ppermute x21, starting transfers between devices, flipped(): lax.ppermute(array, axis, [(r, r ^ flip) for r in range(lax.axis_size(axi...  22.3 us
    ppermute x11, starting transfers between devices, lines(): return lax.ppermute(array, 'rep', perm)  20.7 us
    unnamed x60, local copies, waits for them, and re-layouts  14.5 us
  transfers between devices with their start and end apart: 32, of which 12 were waited for; matrix products, arithmetic and copies ran while one was open for 0% of the time, Pallas kernels for 39%

profile of v10, /device:TPU:0, one launch (start us, length us, event | category | flops | bytes accessed | tf_op | source)
XLA Modules:
  0.0 188.5 jit_solution(9161437612975763149)
XLA Ops:
  4.1 3.0 %collective-permute-start.1 = (f32[8,128,256]{2,1,0:T(8,128)}, f32[8,128,256]{2,1,0:T(8,128)}, u32[]{:S(2)}, u32[]{:S(2)}) collective-permute-start(f32[8,128,256]{2,1,0:T(8,128)} %turn_tokens.1.refs_5_.refs_1_), channel_id=1, source_target_pairs={{0,8},{4,12},{8,0},{12,4},{16,24},{20,28},{24,16},{28,20},{1,9},{5... | collective-permute-start | bytes 3145736 | tf_op jit(solution)/shard_map/ppermute | solution.py:135
  8.8 17.2 %gate.1 = (bf16[3,256,512]{2,1,0:T(8,128)(2,1)S(1)}, f32[7,3,512]{2,1,0:T(4,128)S(1)}, f32[1,256,512]{2,1,0:T(8,128)}, f32[2,256,512]{2,1,0:T(8,128)}, f32[2,256,512]{2,1,0:T(8,128)}) custom-call(s32[3]{0:T(128)S(1)} %pad_add_fusion.1.refs_0_, bf16[256,4096]{1,0:T(8,128)(2,1)} %refs_1_.5, bf16[3,4096,512]{2,1,0:T(8,128)(2,1)} %refs_2_.5, ...), custom_call_target="tpu_custom_call" | custom-call | flops 128 | bytes 128 | tf_op jit(solution)/shard_map/gate/pallas_call | solution.py:111
  26.0 5.4 %collective-permute-start.2 = (f32[2,256,512]{2,1,0:T(8,128)}, f32[2,256,512]{2,1,0:T(8,128)S(1)}, u32[]{:S(2)}, u32[]{:S(2)}) collective-permute-start(f32[2,256,512]{2,1,0:T(8,128)} %get-tuple-element.18), channel_id=1, source_target_pairs={{0,8},{4,12},{24,16},{28,20},{1,9},{5,13},{25,17},{29,21},{2,10},{... | collective-permute-start | bytes 3145736 | tf_op jit(solution)/shard_map/ppermute | solution.py:135
  33.8 2.5 %other_blocks.3.refs_3_ = f32[6,128,256]{2,1,0:T(8,128)} custom-call(s32[3]{0:T(128)S(1)} %pad_add_fusion.1.refs_0_, f32[8,128,256]{2,1,0:T(8,128)} %turn_tokens.1.refs_5_.refs_1_, f32[8,128,256]{2,1,0:T(8,128)} %collective-permute-done.1.refs_2_.refs_1_, bf16[3,256,512]{2,1,0:T(8,128)(2,1)S(1)} %get-tuple-element.17.refs_3_.refs_1_.refs_2_), custom_call_target="tpu_custom_call" | custom-call | flops 128 | bytes 128 | tf_op jit(solution)/shard_map/other_blocks/pallas_call | solution.py:111
  36.3 7.9 %token_part.2.refs_2_ = f32[2,256,1024]{2,1,0:T(8,128)} custom-call(s32[2]{0:T(128)S(1)} %pad_add_fusion.2.refs_0_, bf16[3,256,512]{2,1,0:T(8,128)(2,1)S(1)} %get-tuple-element.17.refs_3_.refs_1_.refs_2_, bf16[3,4096,512]{2,1,0:T(8,128)(2,1)} %refs_2_.5, f32[6,128,256]{2,1,0:T(8,128)} %other_blocks.3.refs_3_), custom_call_target="tpu_custom_call" | custom-call | flops 128 | bytes 128 | tf_op jit(solution)/shard_map/token_part/pallas_call | solution.py:111
  44.2 2.2 %part_of.4.refs_3_ = f32[6,128,256]{2,1,0:T(8,128)} custom-call(s32[3]{0:T(128)S(1)} %pad_add_fusion.1.refs_0_, f32[8,128,256]{2,1,0:T(8,128)} %collective-permute-done.refs_1_, f32[2,256,1024]{2,1,0:T(8,128)} %token_part.2.refs_2_), custom_call_target="tpu_custom_call" | custom-call | flops 128 | bytes 128 | tf_op jit(solution)/shard_map/part_of/pallas_call | solution.py:111
  47.6 5.8 %collective-permute-done.2.refs_4_.refs_2_.refs_3_ = f32[2,256,512]{2,1,0:T(8,128)S(1)} collective-permute-done((f32[2,256,512]{2,1,0:T(8,128)}, f32[2,256,512]{2,1,0:T(8,128)S(1)}, u32[]{:S(2)}, u32[]{:S(2)}) %collective-permute-start.2) | collective-permute-done | bytes 1048608 | tf_op jit(solution)/shard_map/ppermute | solution.py:135
  55.8 2.4 %collective-permute-start.7 = (f32[1,256,512]{2,1,0:T(8,128)}, f32[1,256,512]{2,1,0:T(8,128)S(1)}, u32[]{:S(2)}, u32[]{:S(2)}) collective-permute-start(f32[1,256,512]{2,1,0:T(8,128)} %get-tuple-element.20), channel_id=1, source_target_pairs={{0,8},{4,12},{8,0},{12,4},{16,24},{20,28},{24,16},{28,20},{1,9},{5... | collective-permute-start | bytes 1572872 | tf_op jit(solution)/shard_map/ppermute | solution.py:135
  59.8 7.9 %token_part.3.refs_2_.refs_0_ = f32[2,256,1024]{2,1,0:T(8,128)} custom-call(s32[2]{0:T(128)S(1)} %pad_add_fusion.refs_0_, bf16[3,256,512]{2,1,0:T(8,128)(2,1)S(1)} %get-tuple-element.17.refs_3_.refs_1_.refs_2_, bf16[3,4096,512]{2,1,0:T(8,128)(2,1)} %refs_2_.5, f32[6,128,256]{2,1,0:T(8,128)} %part_of.4.refs_3_, ...), custom_call_target="tpu_custom_call" | custom-call | flops 128 | bytes 128 | tf_op jit(solution)/shard_map/token_part/pallas_call | solution.py:111
  74.0 6.0 %collective-permute-done.7.refs_1_.refs_4_ = f32[1,256,512]{2,1,0:T(8,128)S(1)} collective-permute-done((f32[1,256,512]{2,1,0:T(8,128)}, f32[1,256,512]{2,1,0:T(8,128)S(1)}, u32[]{:S(2)}, u32[]{:S(2)}) %collective-permute-start.7) | collective-permute-done | bytes 524320 | tf_op jit(solution)/shard_map/ppermute | solution.py:135
  87.5 4.6 %collective-permute-done.12.refs_3_ = f32[3,128,256]{2,1,0:T(8,128)S(1)} collective-permute-done((f32[3,128,256]{2,1,0:T(8,128)S(1)}, f32[3,128,256]{2,1,0:T(8,128)S(1)}, u32[]{:S(2)}, u32[]{:S(2)}) %collective-permute-start.12) | collective-permute-done | bytes 393248 | tf_op jit(solution)/shard_map/ppermute | solution.py:139
  93.6 2.9 %collective-permute-done.13.refs_2_ = f32[6,128,256]{2,1,0:T(8,128)S(1)} collective-permute-done((f32[6,128,256]{2,1,0:T(8,128)S(1)}, f32[6,128,256]{2,1,0:T(8,128)S(1)}, u32[]{:S(2)}, u32[]{:S(2)}) %collective-permute-start.13) | collective-permute-done | bytes 786464 | tf_op jit(solution)/shard_map/ppermute | solution.py:135
  101.9 12.1 %collective-permute-done.21.refs_1_ = f32[7,3,512]{2,1,0:T(4,128)S(1)} collective-permute-done((f32[7,3,512]{2,1,0:T(4,128)S(1)}, f32[7,3,512]{2,1,0:T(4,128)S(1)}, u32[]{:S(2)}, u32[]{:S(2)}) %collective-permute-start.21) | collective-permute-done | bytes 43040 | tf_op jit(solution)/shard_map/ppermute | solution.py:139
  120.1 8.1 %collective-permute-done.15.refs_4_.refs_2_.refs_6_ = f32[1,256,512]{2,1,0:T(8,128)S(1)} collective-permute-done((f32[1,256,512]{2,1,0:T(8,128)S(1)}, f32[1,256,512]{2,1,0:T(8,128)S(1)}, u32[]{:S(2)}, u32[]{:S(2)}) %collective-permute-start.15) | collective-permute-done | bytes 524320 | tf_op jit(solution)/shard_map/ppermute | solution.py:135
  128.2 2.0 %collective-permute-start.29 = (f32[2,256,512]{2,1,0:T(8,128)S(1)}, f32[2,256,512]{2,1,0:T(8,128)S(1)}, u32[]{:S(2)}, u32[]{:S(2)}) collective-permute-start(f32[2,256,512]{2,1,0:T(8,128)S(1)} %side_payload.2.refs_2_), channel_id=1, source_target_pairs={{0,4},{4,0},{8,12},{12,8},{16,20},{20,16},{24,28},{28,24},{1,5},{5... | collective-permute-start | bytes 3145736 | tf_op jit(solution)/shard_map/ppermute | solution.py:139
  130.2 2.8 %add.18 = (f32[256,1024]{1,0:T(8,128)S(1)}, f32[256,1024]{1,0:T(8,128)}) custom-call(f32[2,256,1024]{2,1,0:T(8,128)S(1)} %copy-done.5, f32[2,256,1024]{2,1,0:T(8,128)} %collective-permute-done.5.refs_5_.refs_1_, f32[2,256,512]{2,1,0:T(8,128)S(1)} %side_payload.2.refs_2_, f32[9,128,256]{2,1,0:T(8,128)S(1)} %collective-permute-done.14.refs_3_.refs_4_, ...), custom_call_target="tpu_custom_call" | custom-call | flops 128 | bytes 128 | tf_op jit(solution)/shard_map/add/pallas_call | solution.py:111
  132.9 2.6 %collective-permute-done.18.refs_6_.refs_3_ = f32[6,128,256]{2,1,0:T(8,128)} collective-permute-done((f32[6,128,256]{2,1,0:T(8,128)S(1)}, f32[6,128,256]{2,1,0:T(8,128)}, u32[]{:S(2)}, u32[]{:S(2)}) %collective-permute-start.18) | collective-permute-done | bytes 786464 | tf_op jit(solution)/shard_map/ppermute | solution.py:139
  138.6 2.7 %collective-permute-start.27 = (f32[7,3,512]{2,1,0:T(4,128)S(1)}, f32[7,3,512]{2,1,0:T(4,128)S(1)}, u32[]{:S(2)}, u32[]{:S(2)}) collective-permute-start(f32[7,3,512]{2,1,0:T(4,128)S(1)} %get-tuple-element.27), channel_id=1, source_target_pairs={{0,8},{4,12},{8,0},{12,4},{16,24},{20,28},{24,16},{28,20},{1,9},{5... | collective-permute-start | bytes 129032 | tf_op jit(solution)/shard_map/ppermute | solution.py:139
  147.1 7.2 %collective-permute-done.29.refs_5_.refs_4_ = f32[2,256,512]{2,1,0:T(8,128)S(1)} collective-permute-done((f32[2,256,512]{2,1,0:T(8,128)S(1)}, f32[2,256,512]{2,1,0:T(8,128)S(1)}, u32[]{:S(2)}, u32[]{:S(2)}) %collective-permute-start.29) | collective-permute-done | bytes 1048608 | tf_op jit(solution)/shard_map/ppermute | solution.py:139
  155.3 2.4 %collective-permute-done.25.refs_4_.refs_7_ = f32[6,128,256]{2,1,0:T(8,128)} collective-permute-done((f32[6,128,256]{2,1,0:T(8,128)S(1)}, f32[6,128,256]{2,1,0:T(8,128)}, u32[]{:S(2)}, u32[]{:S(2)}) %collective-permute-start.25) | collective-permute-done | bytes 786464 | tf_op jit(solution)/shard_map/ppermute | solution.py:139
  157.7 6.9 %weight_part.2.refs_2_.refs_8_ = f32[1536,512]{1,0:T(8,128)} custom-call(s32[3]{0:T(128)} %copy-done.26, bf16[3,512,1024]{2,1,0:T(8,128)(2,1)} %copy-done.1, bf16[3,256,512]{2,1,0:T(8,128)(2,1)} %copy-done.9, f32[2,256,512]{2,1,0:T(8,128)} %copy-done.12, f32[1,256,512]{2,1,0:T(8,128)} %copy-done.22, f32[2,256,512]{2,1,0:T(8,128)} %collective-permute-done.3.refs_5_, ...), custom_call_target="tpu_custom_call" | custom-call | flops 128 | bytes 128 | tf_op jit(solution)/shard_map/weight_part/pallas_call | solution.py:111
  166.5 2.7 %collective-permute-start.31 = (f32[7,3,512]{2,1,0:T(4,128)S(1)}, f32[7,3,512]{2,1,0:T(4,128)S(1)}, u32[]{:S(2)}, u32[]{:S(2)}) collective-permute-start(f32[7,3,512]{2,1,0:T(4,128)S(1)} %get-tuple-element.29), channel_id=1, source_target_pairs={{0,16},{4,20},{8,24},{12,28},{16,0},{20,4},{24,8},{28,12},{1,17},{... | collective-permute-start | bytes 129032 | tf_op jit(solution)/shard_map/ppermute | solution.py:139
  174.1 8.1 %weight_part.3.refs_2_ = f32[1536,512]{1,0:T(8,128)} custom-call(s32[3]{0:T(128)} %copy-done.26, bf16[3,512,1024]{2,1,0:T(8,128)(2,1)} %copy-done.11, f32[2,256,512]{2,1,0:T(8,128)} %collective-permute-done.6.refs_1_.refs_2_, f32[1,256,512]{2,1,0:T(8,128)} %copy-done.23, f32[2,256,512]{2,1,0:T(8,128)} %copy-done.15, f32[2,256,512]{2,1,0:T(8,128)} %copy-done.13, ...), custom_call_target="tpu_custom_call" | custom-call | flops 128 | bytes 128 | tf_op jit(solution)/shard_map/weight_part/pallas_call | solution.py:111
  184.1 2.1 %add_rounded.1.refs_2_ = bf16[256,1024]{1,0:T(8,128)(2,1)} custom-call(f32[256,1024]{1,0:T(8,128)S(1)} %copy-done.19, f32[256,1024]{1,0:T(8,128)} %collective-permute-done.16.refs_1_, f32[1536,512]{1,0:T(8,128)S(1)} %copy-done.10), custom_call_target="tpu_custom_call" | custom-call | flops 128 | bytes 128 | tf_op jit(solution)/shard_map/add_rounded/pallas_call | solution.py:111
  (129 shorter events, 60.1 us)
Async XLA Ops:
  4.1 28.9 %collective-permute-start.1 = (f32[8,128,256]{2,1,0:T(8,128)}, f32[8,128,256]{2,1,0:T(8,128)}, u32[]{:S(2)}, u32[]{:S(2)}) collective-permute-start(f32[8,128,256]{2,1,0:T(8,128)} %turn_tokens.1.refs_5_.refs_1_), channel_id=1, source_target_pairs={{0,8},{4,12},{8,0},{12,4},{16,24},{20,28},{24,16},{28,20},{1,9},{5... | collective-permute-start | bytes 3145736 | tf_op jit(solution)/shard_map/ppermute | solution.py:135
  7.1 37.1 %collective-permute-start = (f32[8,128,256]{2,1,0:T(8,128)}, f32[8,128,256]{2,1,0:T(8,128)}, u32[]{:S(2)}, u32[]{:S(2)}) collective-permute-start(f32[8,128,256]{2,1,0:T(8,128)} %turn_tokens.1.refs_5_.refs_1_), channel_id=1, source_target_pairs={{8,16},{12,20},{16,8},{20,12},{9,17},{13,21},{17,9},{21,13},{10,18... | collective-permute-start | bytes 3145736 | tf_op jit(solution)/shard_map/ppermute | solution.py:135
  26.0 27.5 %collective-permute-start.2 = (f32[2,256,512]{2,1,0:T(8,128)}, f32[2,256,512]{2,1,0:T(8,128)S(1)}, u32[]{:S(2)}, u32[]{:S(2)}) collective-permute-start(f32[2,256,512]{2,1,0:T(8,128)} %get-tuple-element.18), channel_id=1, source_target_pairs={{0,8},{4,12},{24,16},{28,20},{1,9},{5,13},{25,17},{29,21},{2,10},{... | collective-permute-start | bytes 3145736 | tf_op jit(solution)/shard_map/ppermute | solution.py:135
  31.4 24.4 %collective-permute-start.3 = (f32[2,256,512]{2,1,0:T(8,128)}, f32[2,256,512]{2,1,0:T(8,128)}, u32[]{:S(2)}, u32[]{:S(2)}) collective-permute-start(f32[2,256,512]{2,1,0:T(8,128)} %get-tuple-element.18), channel_id=1, source_target_pairs={{0,4},{4,0},{8,12},{12,8},{16,20},{20,16},{24,28},{28,24},{1,5},{5... | collective-permute-start | bytes 3145736 | tf_op jit(solution)/shard_map/ppermute | solution.py:139
  33.0 25.3 %collective-permute-start.4 = (f32[8,128,256]{2,1,0:T(8,128)}, f32[8,128,256]{2,1,0:T(8,128)S(1)}, u32[]{:S(2)}, u32[]{:S(2)}) collective-permute-start(f32[8,128,256]{2,1,0:T(8,128)} %collective-permute-done.1.refs_2_.refs_1_), channel_id=1, source_target_pairs={{8,16},{12,20},{16,8},{20,12},{9,17},{13,21},{17,9},{21,13},{10,18... | collective-permute-start | bytes 3145736 | tf_op jit(solution)/shard_map/ppermute | solution.py:135
  44.2 52.3 %collective-permute-start.5 = (f32[2,256,1024]{2,1,0:T(8,128)}, f32[2,256,1024]{2,1,0:T(8,128)}, u32[]{:S(2)}, u32[]{:S(2)}) collective-permute-start(f32[2,256,1024]{2,1,0:T(8,128)} %token_part.2.refs_2_), channel_id=1, source_target_pairs={{0,1},{1,0},{2,3},{3,2},{4,5},{5,4},{6,7},{7,6},{8,9},{9,8},{10,11... | collective-permute-start | bytes 6291464 | tf_op jit(solution)/shard_map/ppermute | solution.py:139
  46.3 24.8 %collective-permute-start.8 = (f32[6,128,256]{2,1,0:T(8,128)}, f32[6,128,256]{2,1,0:T(8,128)}, u32[]{:S(2)}, u32[]{:S(2)}) collective-permute-start(f32[6,128,256]{2,1,0:T(8,128)} %part_of.4.refs_3_), channel_id=1, source_target_pairs={{8,0},{12,4},{16,24},{20,28},{9,1},{13,5},{17,25},{21,29},{10,2},{... | collective-permute-start | bytes 2359304 | tf_op jit(solution)/shard_map/ppermute | solution.py:135
  53.5 29.4 %collective-permute-start.6 = (f32[2,256,512]{2,1,0:T(8,128)}, f32[2,256,512]{2,1,0:T(8,128)}, u32[]{:S(2)}, u32[]{:S(2)}) collective-permute-start(f32[2,256,512]{2,1,0:T(8,128)} %get-tuple-element.19), channel_id=1, source_target_pairs={{8,16},{12,20},{16,8},{20,12},{9,17},{13,21},{17,9},{21,13},{10,18... | collective-permute-start | bytes 3145736 | tf_op jit(solution)/shard_map/ppermute | solution.py:135
  55.8 24.2 %collective-permute-start.7 = (f32[1,256,512]{2,1,0:T(8,128)}, f32[1,256,512]{2,1,0:T(8,128)S(1)}, u32[]{:S(2)}, u32[]{:S(2)}) collective-permute-start(f32[1,256,512]{2,1,0:T(8,128)} %get-tuple-element.20), channel_id=1, source_target_pairs={{0,8},{4,12},{8,0},{12,4},{16,24},{20,28},{24,16},{28,20},{1,9},{5... | collective-permute-start | bytes 1572872 | tf_op jit(solution)/shard_map/ppermute | solution.py:135
  58.2 25.3 %collective-permute-start.9 = (f32[6,128,256]{2,1,0:T(8,128)}, f32[6,128,256]{2,1,0:T(8,128)}, u32[]{:S(2)}, u32[]{:S(2)}) collective-permute-start(f32[6,128,256]{2,1,0:T(8,128)} %other_blocks.3.refs_3_), channel_id=1, source_target_pairs={{0,4},{4,0},{8,12},{12,8},{16,20},{20,16},{24,28},{28,24},{1,5},{5... | collective-permute-start | bytes 2359304 | tf_op jit(solution)/shard_map/ppermute | solution.py:139
  71.2 25.3 %collective-permute-start.13 = (f32[6,128,256]{2,1,0:T(8,128)S(1)}, f32[6,128,256]{2,1,0:T(8,128)S(1)}, u32[]{:S(2)}, u32[]{:S(2)}) collective-permute-start(f32[6,128,256]{2,1,0:T(8,128)S(1)} %part_of.5.refs_3_), channel_id=1, source_target_pairs={{8,0},{12,4},{16,24},{20,28},{9,1},{13,5},{17,25},{21,29},{10,2},{... | collective-permute-start | bytes 2359304 | tf_op jit(solution)/shard_map/ppermute | solution.py:135
  83.6 31.9 %collective-permute-start.23 = (f32[2,256,512]{2,1,0:T(8,128)S(1)}, f32[2,256,512]{2,1,0:T(8,128)S(1)}, u32[]{:S(2)}, u32[]{:S(2)}) collective-permute-start(f32[2,256,512]{2,1,0:T(8,128)S(1)} %get-tuple-element.25), channel_id=1, source_target_pairs={{0,4},{4,0},{8,12},{12,8},{16,20},{20,16},{24,28},{28,24},{1,5},{5... | collective-permute-start | bytes 3145736 | tf_op jit(solution)/shard_map/ppermute | solution.py:139
  92.1 25.0 %collective-permute-start.14 = (f32[9,128,256]{2,1,0:T(8,128)S(1)}, f32[9,128,256]{2,1,0:T(8,128)S(1)}, u32[]{:S(2)}, u32[]{:S(2)}) collective-permute-start(f32[9,128,256]{2,1,0:T(8,128)S(1)} %own_blocks.3.refs_3_.refs_2_), channel_id=1, source_target_pairs={{0,2},{1,3},{2,0},{3,1},{4,6},{5,7},{6,4},{7,5},{8,10},{9,11},{10,... | collective-permute-start | bytes 3538952 | tf_op jit(solution)/shard_map/ppermute | solution.py:139
  96.5 20.7 %collective-permute-start.22 = (f32[9,128,256]{2,1,0:T(8,128)S(1)}, f32[9,128,256]{2,1,0:T(8,128)S(1)}, u32[]{:S(2)}, u32[]{:S(2)}) collective-permute-start(f32[9,128,256]{2,1,0:T(8,128)S(1)} %own_blocks.3.refs_3_.refs_2_), channel_id=1, source_target_pairs={{0,1},{1,0},{2,3},{3,2},{4,5},{5,4},{6,7},{7,6},{8,9},{9,8},{10,11... | collective-permute-start | bytes 3538952 | tf_op jit(solution)/shard_map/ppermute | solution.py:139
  96.5 18.9 %collective-permute-start.10 = (f32[1,256,512]{2,1,0:T(8,128)S(1)}, f32[1,256,512]{2,1,0:T(8,128)S(1)}, u32[]{:S(2)}, u32[]{:S(2)}) collective-permute-start(f32[1,256,512]{2,1,0:T(8,128)S(1)} %part_of.6.refs_3_), channel_id=1, source_target_pairs={{8,0},{12,4},{16,24},{20,28},{9,1},{13,5},{17,25},{21,29},{10,2},{... | collective-permute-start | bytes 1572872 | tf_op jit(solution)/shard_map/ppermute | solution.py:135
  115.4 17.6 %collective-permute-start.17 = (f32[6,128,256]{2,1,0:T(8,128)S(1)}, f32[6,128,256]{2,1,0:T(8,128)S(1)}, u32[]{:S(2)}, u32[]{:S(2)}) collective-permute-start(f32[6,128,256]{2,1,0:T(8,128)S(1)} %own_blocks.4.refs_2_.refs_1_), channel_id=1, source_target_pairs={{0,1},{1,0},{2,3},{3,2},{4,5},{5,4},{6,7},{7,6},{8,9},{9,8},{10,11... | collective-permute-start | bytes 2359304 | tf_op jit(solution)/shard_map/ppermute | solution.py:139
  115.5 20.0 %collective-permute-start.18 = (f32[6,128,256]{2,1,0:T(8,128)S(1)}, f32[6,128,256]{2,1,0:T(8,128)}, u32[]{:S(2)}, u32[]{:S(2)}) collective-permute-start(f32[6,128,256]{2,1,0:T(8,128)S(1)} %own_blocks.4.refs_2_.refs_1_), channel_id=1, source_target_pairs={{0,2},{1,3},{2,0},{3,1},{4,6},{5,7},{6,4},{7,5},{8,10},{9,11},{10,... | collective-permute-start | bytes 2359304 | tf_op jit(solution)/shard_map/ppermute | solution.py:139
  117.0 24.3 %collective-permute-start.28 = (f32[9,128,256]{2,1,0:T(8,128)S(1)}, f32[9,128,256]{2,1,0:T(8,128)S(1)}, u32[]{:S(2)}, u32[]{:S(2)}) collective-permute-start(f32[9,128,256]{2,1,0:T(8,128)S(1)} %collective-permute-done.14.refs_3_.refs_4_), channel_id=1, source_target_pairs={{0,1},{1,0},{2,3},{3,2},{4,5},{5,4},{6,7},{7,6},{8,9},{9,8},{10,11... | collective-permute-start | bytes 3538952 | tf_op jit(solution)/shard_map/ppermute | solution.py:139
  128.2 26.1 %collective-permute-start.29 = (f32[2,256,512]{2,1,0:T(8,128)S(1)}, f32[2,256,512]{2,1,0:T(8,128)S(1)}, u32[]{:S(2)}, u32[]{:S(2)}) collective-permute-start(f32[2,256,512]{2,1,0:T(8,128)S(1)} %side_payload.2.refs_2_), channel_id=1, source_target_pairs={{0,4},{4,0},{8,12},{12,8},{16,20},{20,16},{24,28},{28,24},{1,5},{5... | collective-permute-start | bytes 3145736 | tf_op jit(solution)/shard_map/ppermute | solution.py:139
  137.1 20.6 %collective-permute-start.25 = (f32[6,128,256]{2,1,0:T(8,128)S(1)}, f32[6,128,256]{2,1,0:T(8,128)}, u32[]{:S(2)}, u32[]{:S(2)}) collective-permute-start(f32[6,128,256]{2,1,0:T(8,128)S(1)} %own_blocks.5.refs_6_.refs_5_), channel_id=1, source_target_pairs={{0,2},{1,3},{2,0},{3,1},{4,6},{5,7},{6,4},{7,5},{8,10},{9,11},{10,... | collective-permute-start | bytes 2359304 | tf_op jit(solution)/shard_map/ppermute | solution.py:139
  145.1 29.0 %collective-permute-start.30 = (f32[2,256,512]{2,1,0:T(8,128)}, f32[2,256,512]{2,1,0:T(8,128)}, u32[]{:S(2)}, u32[]{:S(2)}) collective-permute-start(f32[2,256,512]{2,1,0:T(8,128)} %side_payload.3.refs_7_), channel_id=1, source_target_pairs={{0,4},{4,0},{8,12},{12,8},{16,20},{20,16},{24,28},{28,24},{1,5},{5... | collective-permute-start | bytes 3145736 | tf_op jit(solution)/shard_map/ppermute | solution.py:139
  146.6 35.6 %collective-permute-start.16 = (f32[256,1024]{1,0:T(8,128)}, f32[256,1024]{1,0:T(8,128)}, u32[]{:S(2)}, u32[]{:S(2)}) collective-permute-start(f32[256,1024]{1,0:T(8,128)} %get-tuple-element.23), channel_id=1, source_target_pairs={{0,2},{1,3},{2,0},{3,1},{4,6},{5,7},{6,4},{7,5},{8,10},{9,11},{10,... | collective-permute-start | bytes 3145736 | tf_op jit(solution)/shard_map/ppermute | solution.py:139
  147.1 17.4 %collective-permute-start.24 = (f32[6,128,256]{2,1,0:T(8,128)S(1)}, f32[6,128,256]{2,1,0:T(8,128)S(1)}, u32[]{:S(2)}, u32[]{:S(2)}) collective-permute-start(f32[6,128,256]{2,1,0:T(8,128)S(1)} %own_blocks.5.refs_6_.refs_5_), channel_id=1, source_target_pairs={{0,1},{1,0},{2,3},{3,2},{4,5},{5,4},{6,7},{7,6},{8,9},{9,8},{10,11... | collective-permute-start | bytes 2359304 | tf_op jit(solution)/shard_map/ppermute | solution.py:139
  166.5 19.7 %collective-permute-start.31 = (f32[7,3,512]{2,1,0:T(4,128)S(1)}, f32[7,3,512]{2,1,0:T(4,128)S(1)}, u32[]{:S(2)}, u32[]{:S(2)}) collective-permute-start(f32[7,3,512]{2,1,0:T(4,128)S(1)} %get-tuple-element.29), channel_id=1, source_target_pairs={{0,16},{4,20},{8,24},{12,28},{16,0},{20,4},{24,8},{28,12},{1,17},{... | collective-permute-start | bytes 129032 | tf_op jit(solution)/shard_map/ppermute | solution.py:139
  (37 other events, 501.3 us)

commit v11 on v10

--- a/solution.py
+++ b/solution.py
@@ -147,26 +147,31 @@
     rows = tokens.shape[0]
     slab = BLOCK // 4
 
-    def body(place, tokens, piece):
+    def body(place, tokens, piece, theirs):
         start = pl.multiple_of(place[2] * slab, slab)
         for b in range(BLOCKS):
             piece[b] = tokens[:, pl.ds(pl.multiple_of(BLOCK * b + start, slab), slab)].astype(
                 jnp.float32
             ).T
+        for i in range(HALF):
+            theirs[i] = piece[device_block(place[0], 1 - place[1], i)]
 
     return order.call(
         body,
         (place, tokens),
         [SMEM, VMEM],
-        out_shape=jax.ShapeDtypeStruct((BLOCKS, slab, rows), jnp.float32),
-        out_specs=VMEM,
+        out_shape=(
+            jax.ShapeDtypeStruct((BLOCKS, slab, rows), jnp.float32),
+            jax.ShapeDtypeStruct((HALF, slab, rows), jnp.float32),
+        ),
+        out_specs=(VMEM, VMEM),
         name="turn_tokens",
     )
 
 
-def column_blocks(order, place, slots, own, got=None, part=(0, 0)):
+def column_blocks(order, place, slots, own, *got):
     arrays = [a for slot in slots for a in slot if a is not None]
-    begin, extra = part
+    extra = sum(a.shape[0] for a in got)
     first = slots[0][0]
     count = HALF * len(slots)
 
@@ -192,13 +197,15 @@
                 def _():
                     out[HALF * n + i] = end[HALF * column + i]
 
-        for i in range(extra):
-            out[count + i] = left[0][begin + i]
-
-    return order.call(
-        body,
-        [place] + arrays + ([] if got is None else [got]),
-        [SMEM] + [VMEM] * (len(arrays) + (extra > 0)),
+        at = count
+        for ref in left[: len(got)]:
+            out[at : at + ref.shape[0]] = ref[...]
+            at += ref.shape[0]
+
+    return order.call(
+        body,
+        [place] + arrays + list(got),
+        [SMEM] + [VMEM] * (len(arrays) + len(got)),
         out_shape=jax.ShapeDtypeStruct((count + extra,) + first.shape[1:], first.dtype),
         out_specs=VMEM,
         name="own_blocks" if own else "other_blocks",
@@ -214,7 +221,7 @@
     deep = features // steps
     pad = 8
 
-    def body(place, tokens, weight, kernel, out_grad, own, grad, first, inner, middle, total, held, pads, back):
+    def body(place, tokens, weight, kernel, out_grad, own, stored, grad, first, inner, middle, total, held, pads, back):
         step = pl.program_id(1)
         for s in range(3):
             now = jnp.dot(tokens[...], weight[s], preferred_element_type=jnp.float32)
@@ -232,12 +239,12 @@
             blank = jnp.zeros((pad, LANES), jnp.float32)
             for lane in range(0, width, LANES):
                 lanes = slice(lane, lane + LANES)
-                sums = [[None] * taps for _ in range(3)]
                 for q in range(rows // SEQ):
                     here = slice(q * SEQ, (q + 1) * SEQ)
                     conv = []
                     for s in range(3):
-                        values = total[s, here, lanes].astype(jnp.bfloat16).astype(jnp.float32)
+                        stored[s, here, lanes] = total[s, here, lanes].astype(jnp.bfloat16)
+                        values = stored[s, here, lanes].astype(jnp.float32)
                         pads[s, 0:pad, :] = blank
                         pads[s, pad : pad + SEQ, :] = values
                         mix = kernel[0, s : s + 1, lanes] * values
@@ -249,20 +256,14 @@
                     grads = (up * keyed * valued, up * query * valued, up * query * keyed)
                     for s in range(3):
                         back[s, 0:SEQ, :] = grads[s]
+                        grad[s, here, lanes] = grads[s]
                         back[s, SEQ : SEQ + pad, :] = blank
                     for s in range(3):
-                        values = pads[s, pad : pad + SEQ, :]
                         mixed = None
                         for j in range(taps):
-                            moved = back[s, j : j + SEQ, :]
-                            term = kernel[j, s : s + 1, lanes] * moved
+                            term = kernel[j, s : s + 1, lanes] * back[s, j : j + SEQ, :]
                             mixed = term if mixed is None else mixed + term
-                            folded = jnp.sum((values * moved).reshape(SEQ // 8, 8, LANES), axis=0)
-                            sums[s][j] = folded if q == 0 else sums[s][j] + folded
                         held[s, here, lanes] = mixed
-                for s in range(3):
-                    for j in range(taps):
-                        grad[j, s : s + 1, lanes] = jnp.sum(sums[s][j], axis=0, keepdims=True)
             for s in range(3):
                 own[s] = held[s].astype(jnp.bfloat16)
             level = place[0]
@@ -286,7 +287,8 @@
         ],
         out_shape=(
             jax.ShapeDtypeStruct((3, rows, chans), jnp.bfloat16),
-            jax.ShapeDtypeStruct((taps, 3, chans), jnp.float32),
+            jax.ShapeDtypeStruct((3, rows, chans), jnp.bfloat16),
+            jax.ShapeDtypeStruct((3, rows, chans), jnp.float32),
             one,
             two,
             two,
@@ -294,7 +296,8 @@
         grid=(chans // width, steps),
         out_specs=(
             pl.BlockSpec((3, rows, width), lambda c, k: (0, 0, c)),
-            pl.BlockSpec((taps, 3, width), lambda c, k: (0, 0, c)),
+            pl.BlockSpec((3, rows, width), lambda c, k: (0, 0, c)),
+            pl.BlockSpec((3, rows, width), lambda c, k: (0, 0, c)),
             pl.BlockSpec((1, rows, width), lambda c, k: (0, 0, c)),
             pl.BlockSpec((2, rows, width), lambda c, k: (0, 0, c)),
             pl.BlockSpec((2, rows, width), lambda c, k: (0, 0, c)),
@@ -307,6 +310,38 @@
         ],
         name="gate",
         vmem=50,
+    )
+
+
+def tap_part(order, stored, grads, taps):
+    rows, chans = grads.shape[1:]
+    pad = 8
+
+    def body(stored, grads, out, back):
+        for s in range(3):
+            sums = [None] * taps
+            for q in range(rows // SEQ):
+                here = slice(q * SEQ, (q + 1) * SEQ)
+                values = stored[s, here, :].astype(jnp.float32)
+                back[0:SEQ, :] = grads[s, here, :]
+                back[SEQ : SEQ + pad, :] = jnp.zeros((pad, LANES), jnp.float32)
+                for j in range(taps):
+                    term = values * back[j : j + SEQ, :]
+                    folded = jnp.sum(term.reshape(SEQ // 8, 8, LANES), axis=0)
+                    sums[j] = folded if q == 0 else sums[j] + folded
+            for j in range(taps):
+                out[j, s : s + 1, :] = jnp.sum(sums[j], axis=0, keepdims=True)
+
+    part = pl.BlockSpec((3, rows, LANES), lambda c: (0, 0, c))
+    return order.call(
+        body,
+        (stored, grads),
+        [part, part],
+        out_shape=jax.ShapeDtypeStruct((taps, 3, chans), jnp.float32),
+        grid=(chans // LANES,),
+        out_specs=pl.BlockSpec((taps, 3, LANES), lambda c: (0, 0, c)),
+        scratch_shapes=[pltpu.VMEM((SEQ + pad, LANES), jnp.float32)],
+        name="tap_part",
     )
 
 
@@ -560,26 +595,26 @@
     scale = 1.0 / math.sqrt(rows * lax.axis_size("rep"))
     order = Order()
     quarters = [jnp.bitwise_xor(quarter, k).astype(jnp.int32) for k in (3, 1, 2, 0)]
-    piece = turn_tokens(order, place, tokens)
+    piece, theirs = turn_tokens(order, place, tokens)
+    got0 = flipped(theirs, "rep", 1)
     near = lines(piece, PAIRS)
     mid = lines(piece, MIDDLE)
-    own, taps, first_out, inner_out, middle_out = gate(
+    own, stored, grads, first_out, inner_out, middle_out = gate(
         order, place, tokens, in_weight, kernel, out_grad
     )
     own_y = flipped(inner_out, "rep", 1)
     inner = lines(inner_out, INWARD)
     first = lines(first_out, PAIRS)
     middle = lines(middle_out, MIDDLE)
-    taps1 = flipped(taps, "rep", 1)
     near = order.wait(near)
     far = lines(near, MIDDLE)
-    over = column_blocks(order, place, [(piece, None), (near, None)], False)
+    over = column_blocks(order, place, [(near, None)], False)
     got1 = flipped(over, "rep", 1)
+    mid = order.wait(mid)
+    outer2 = lines(part_of(order, place, mid, BLOCKS - OWN, OWN), OUTWARD)
     send = token_part(order, jnp.stack(quarters[:2]), own, in_weight)
     summed = flipped(send, "shard", 1)
-    mid = order.wait(mid)
-    outer2 = lines(part_of(order, place, mid, BLOCKS - OWN, OWN), OUTWARD)
-    inner, own_y, far = order.wait(inner, own_y, far)
+    own_y, inner, far = order.wait(own_y, inner, far)
     keep = token_part(order, jnp.stack(quarters[2:]), own, in_weight)
     outer3 = lines(part_of(order, place, far, BLOCKS - OWN, OWN), OUTWARD)
     outer2 = order.wait(outer2)
@@ -589,33 +624,36 @@
     relay, side1 = relay_payload(order, place, first, inner)
     relayed = lines(relay, MIDDLE)
     side1 = flipped(side1, "rep", 1)
-    middle, got1 = order.wait(middle, got1)
+    middle = order.wait(middle)
     middle_end = lines(part_of(order, place, middle, 1, 1), OUTWARD)
-    own1 = column_blocks(order, place, [(near, None)], True, got1, (0, OWN))
+    got0, got1 = order.wait(got0, got1)
+    own1 = column_blocks(order, place, [(near, None)], True, got0, got1)
     across1 = flipped(own1, "shard", 2)
     beside1 = flipped(own1, "shard", 1)
+    summed, got2 = order.wait(summed, got2)
+    own2 = column_blocks(order, place, [(mid, outer2)], True, got2)
+    across2 = flipped(own2, "shard", 2)
+    beside2 = flipped(own2, "shard", 1)
     outer3 = order.wait(outer3)
     over = column_blocks(order, place, [(far, outer3)], False)
     got3 = flipped(over, "rep", 1)
-    summed, got2 = order.wait(summed, got2)
-    own2 = column_blocks(order, place, [(mid, outer2)], True, got2, (0, HALF))
-    across2 = flipped(own2, "shard", 2)
-    beside2 = flipped(own2, "shard", 1)
+    taps = tap_part(order, stored, grads, kernel.shape[0])
+    taps1 = flipped(taps, "rep", 1)
     relayed = order.wait(relayed)
     relayed_end = lines(part_of(order, place, relayed, 1, 1), OUTWARD)
-    middle_end = order.wait(middle_end)
+    relayed_end, middle_end = order.wait(relayed_end, middle_end)
     side2 = flipped(side_payload(order, place, middle, middle_end), "rep", 1)
-    across1, relayed_end = order.wait(across1, relayed_end)
-    both1 = flipped(across1, "shard", 1)
     token_grad, away = add(order, keep, summed)
     last = flipped(away, "shard", 2)
-    beside2, beside1, side1, across2, got3, taps1 = order.wait(
-        beside2, beside1, side1, across2, got3, taps1
-    )
-    both2 = flipped(across2, "shard", 1)
+    beside2, across1, beside1, side1, got3, taps1 = order.wait(
+        beside2, across1, beside1, side1, got3, taps1
+    )
+    both1 = flipped(across1, "shard", 1)
     taps, taps_out = add(order, taps, taps1)
     taps2 = flipped(taps_out, "rep", 2)
-    own3 = column_blocks(order, place, [(far, outer3)], True, got3, (0, HALF))
+    across2 = order.wait(across2)
+    both2 = flipped(across2, "shard", 1)
+    own3 = column_blocks(order, place, [(far, outer3)], True, got3)
     across3 = flipped(own3, "shard", 2)
     beside3 = flipped(own3, "shard", 1)
     both1 = order.wait(both1)
@@ -624,20 +662,19 @@
     side3 = flipped(side_payload(order, place, relayed, relayed_end), "rep", 1)
     early = [(own, None), (inner, first), (own_y, None), (side1, None)]
     so_far = weight_part(order, place, tok, early)
-    beside3, across3, side2, both2 = order.wait(beside3, across3, side2, both2)
+    side2, beside3, across3, both2 = order.wait(side2, beside3, across3, both2)
     both3 = flipped(across3, "shard", 1)
     taps, taps_out = add(order, taps, taps2)
     taps4 = flipped(taps_out, "rep", 4)
     both3 = order.wait(both3)
     late = [(own2, beside2, across2, both2), (own3, beside3, across3, both3)]
     tok = arrange_tokens(order, place, None, late)
-    side3 = order.wait(side3)
+    taps4 = order.wait(taps4)
+    taps, _ = add(order, taps, taps4, scale=scale)
+    side3, last = order.wait(side3, last)
+    token_grad = add_rounded(order, token_grad, last)
     late = [(middle, middle_end), (side2, None), (relayed, relayed_end), (side3, None)]
     weight_grad = weight_part(order, place, tok, late, scale, so_far)
-    last = order.wait(last)
-    token_grad = add_rounded(order, token_grad, last)
-    taps4 = order.wait(taps4)
-    taps, _ = add(order, taps, taps4, scale=scale)
     return (token_grad, weight_grad, taps)
 
 

time: 190 us -> 196 us (1.032)
  waiting for transfers between devices: 54.6 us -> 66.1 us
  starting transfers between devices: 42.9 us -> 38.2 us
    ppermute x11, waiting for transfers between devices: 22.9 us -> 31.5 us  [lines(): return lax.ppermute(array, 'rep', perm)]
    ppermute x21 -> x22, starting transfers between devices: 22.3 us -> 16.4 us  [flipped(): lax.ppermute(array, axis, [(r, r ^ flip) for r in range(lax.axis_size(axi...]
    ppermute x21 -> x22, waiting for transfers between devices: 31.7 us -> 34.7 us  [flipped(): lax.ppermute(array, axis, [(r, r ^ flip) for r in range(lax.axis_size(axi...]
    pallas_call x26 -> x27, Pallas kernels: 75.2 us -> 74.7 us  [call(): pl.pallas_call(short, out_shape=out_shape, grid_spec=pltpu.PrefetchScalar...]
    unnamed x60 -> x68, local copies, waits for them, and re-layouts: 14.5 us -> 14.4 us
  transfers between devices with their start and end apart: 32 -> 33, of which waited for: 12 -> 15; matrix products, arithmetic and copies ran while one was open for 0% -> 0% of each run, Pallas kernels for 39% -> 32%
where the time goes in v11:
time: 196 us; the launch traced here: 195 us
  Pallas kernels  74.7 us (38%)
  waiting for transfers between devices  66.1 us (34%)
  starting transfers between devices  38.2 us (19%)
  local copies, waits for them, and re-layouts  14.4 us (7%)
    pallas_call x27, Pallas kernels, call(): pl.pallas_call(short, out_shape=out_shape, grid_spec=pltpu.PrefetchScalar...  74.7 us
    ppermute x22, waiting for transfers between devices, flipped(): lax.ppermute(array, axis, [(r, r ^ flip) for r in range(lax.axis_size(axi...  34.7 us
    ppermute x11, waiting for transfers between devices, lines(): return lax.ppermute(array, 'rep', perm)  31.5 us
    ppermute x11, starting transfers between devices, lines(): return lax.ppermute(array, 'rep', perm)  21.8 us
    ppermute x22, starting transfers between devices, flipped(): lax.ppermute(array, axis, [(r, r ^ flip) for r in range(lax.axis_size(axi...  16.4 us
    unnamed x68, local copies, waits for them, and re-layouts  14.4 us
  transfers between devices with their start and end apart: 33, of which 15 were waited for; matrix products, arithmetic and copies ran while one was open for 0% of the time, Pallas kernels for 32%

profile of v11, /device:TPU:0, one launch (start us, length us, event | category | flops | bytes accessed | tf_op | source)
XLA Modules:
  0.0 194.8 jit_solution(4585534885663542324)
XLA Ops:
  4.2 3.0 %collective-permute-start.1 = (f32[8,128,256]{2,1,0:T(8,128)}, f32[8,128,256]{2,1,0:T(8,128)}, u32[]{:S(2)}, u32[]{:S(2)}) collective-permute-start(f32[8,128,256]{2,1,0:T(8,128)} %get-tuple-element.20.refs_5_), channel_id=1, source_target_pairs={{0,8},{4,12},{8,0},{12,4},{16,24},{20,28},{24,16},{28,20},{1,9},{5... | collective-permute-start | bytes 3145736 | tf_op jit(solution)/shard_map/ppermute | solution.py:135
  8.0 17.0 %gate.1 = (bf16[3,256,512]{2,1,0:T(8,128)(2,1)S(1)}, bf16[3,256,512]{2,1,0:T(8,128)(2,1)S(1)}, f32[3,256,512]{2,1,0:T(8,128)}, f32[1,256,512]{2,1,0:T(8,128)S(1)...) custom-call(s32[3]{0:T(128)S(1)} %pad_add_fusion.1.refs_0_, bf16[256,4096]{1,0:T(8,128)(2,1)} %refs_1_.5, ...), custom_call_target="tpu_custom_call" | custom-call | flops 128 | bytes 128 | tf_op jit(solution)/shard_map/gate/pallas_call | solution.py:111
  27.5 7.2 %collective-permute-start.3 = (f32[2,256,512]{2,1,0:T(8,128)}, f32[2,256,512]{2,1,0:T(8,128)}, u32[]{:S(2)}, u32[]{:S(2)}) collective-permute-start(f32[2,256,512]{2,1,0:T(8,128)} %get-tuple-element.22), channel_id=1, source_target_pairs={{0,8},{4,12},{24,16},{28,20},{1,9},{5,13},{25,17},{29,21},{2,10},{... | collective-permute-start | bytes 3145736 | tf_op jit(solution)/shard_map/ppermute | solution.py:135
  39.0 7.9 %token_part.2.refs_3_ = f32[2,256,1024]{2,1,0:T(8,128)} custom-call(s32[2]{0:T(128)S(1)} %pad_add_fusion.2.refs_0_, bf16[3,256,512]{2,1,0:T(8,128)(2,1)S(1)} %get-tuple-element.21.refs_2_.refs_1_, bf16[3,4096,512]{2,1,0:T(8,128)(2,1)} %refs_2_.5, f32[6,128,256]{2,1,0:T(8,128)} %part_of.4.refs_3_), custom_call_target="tpu_custom_call" | custom-call | flops 128 | bytes 128 | tf_op jit(solution)/shard_map/token_part/pallas_call | solution.py:111
  48.6 2.3 %collective-permute-done.2.refs_4_.refs_5_ = f32[2,256,512]{2,1,0:T(8,128)} collective-permute-done((f32[2,256,512]{2,1,0:T(8,128)}, f32[2,256,512]{2,1,0:T(8,128)}, u32[]{:S(2)}, u32[]{:S(2)}) %collective-permute-start.2) | collective-permute-done | bytes 1048608 | tf_op jit(solution)/shard_map/ppermute | solution.py:139
  52.2 3.4 %collective-permute-done.3.refs_5_.refs_2_.refs_3_ = f32[2,256,512]{2,1,0:T(8,128)} collective-permute-done((f32[2,256,512]{2,1,0:T(8,128)}, f32[2,256,512]{2,1,0:T(8,128)}, u32[]{:S(2)}, u32[]{:S(2)}) %collective-permute-start.3) | collective-permute-done | bytes 1048608 | tf_op jit(solution)/shard_map/ppermute | solution.py:135
  55.6 2.5 %collective-permute-start.7 = (f32[1,256,512]{2,1,0:T(8,128)}, f32[1,256,512]{2,1,0:T(8,128)S(1)}, u32[]{:S(2)}, u32[]{:S(2)}) collective-permute-start(f32[1,256,512]{2,1,0:T(8,128)} %copy-done.31), channel_id=1, source_target_pairs={{0,8},{4,12},{8,0},{12,4},{16,24},{20,28},{24,16},{28,20},{1,9},{5... | collective-permute-start | bytes 1572872 | tf_op jit(solution)/shard_map/ppermute | solution.py:135
  58.7 7.9 %token_part.3.refs_2_.refs_0_ = f32[2,256,1024]{2,1,0:T(8,128)} custom-call(s32[2]{0:T(128)S(1)} %pad_add_fusion.refs_0_, bf16[3,256,512]{2,1,0:T(8,128)(2,1)S(1)} %get-tuple-element.21.refs_2_.refs_1_, bf16[3,4096,512]{2,1,0:T(8,128)(2,1)} %refs_2_.5, f32[2,256,1024]{2,1,0:T(8,128)} %token_part.2.refs_3_, ...), custom_call_target="tpu_custom_call" | custom-call | flops 128 | bytes 128 | tf_op jit(solution)/shard_map/token_part/pallas_call | solution.py:111
  70.1 4.8 %collective-permute-done.8.refs_2_ = f32[6,128,256]{2,1,0:T(8,128)} collective-permute-done((f32[6,128,256]{2,1,0:T(8,128)}, f32[6,128,256]{2,1,0:T(8,128)}, u32[]{:S(2)}, u32[]{:S(2)}) %collective-permute-start.8) | collective-permute-done | bytes 786464 | tf_op jit(solution)/shard_map/ppermute | solution.py:135
  77.7 8.4 %collective-permute-done.7.refs_1_.refs_4_ = f32[1,256,512]{2,1,0:T(8,128)S(1)} collective-permute-done((f32[1,256,512]{2,1,0:T(8,128)}, f32[1,256,512]{2,1,0:T(8,128)S(1)}, u32[]{:S(2)}, u32[]{:S(2)}) %collective-permute-start.7) | collective-permute-done | bytes 524320 | tf_op jit(solution)/shard_map/ppermute | solution.py:135
  93.1 5.1 %collective-permute-done.12.refs_3_ = f32[3,128,256]{2,1,0:T(8,128)S(1)} collective-permute-done((f32[3,128,256]{2,1,0:T(8,128)S(1)}, f32[3,128,256]{2,1,0:T(8,128)S(1)}, u32[]{:S(2)}, u32[]{:S(2)}) %collective-permute-start.12) | collective-permute-done | bytes 393248 | tf_op jit(solution)/shard_map/ppermute | solution.py:139
  108.4 8.7 %collective-permute-done.9.refs_2_.refs_3_ = f32[1,256,512]{2,1,0:T(8,128)S(1)} collective-permute-done((f32[1,256,512]{2,1,0:T(8,128)S(1)}, f32[1,256,512]{2,1,0:T(8,128)S(1)}, u32[]{:S(2)}, u32[]{:S(2)}) %collective-permute-start.9) | collective-permute-done | bytes 524320 | tf_op jit(solution)/shard_map/ppermute | solution.py:135
  118.7 2.6 %collective-permute-done.17.refs_1_ = f32[7,3,512]{2,1,0:T(4,128)S(1)} collective-permute-done((f32[7,3,512]{2,1,0:T(4,128)S(1)}, f32[7,3,512]{2,1,0:T(4,128)S(1)}, u32[]{:S(2)}, u32[]{:S(2)}) %collective-permute-start.17) | collective-permute-done | bytes 43040 | tf_op jit(solution)/shard_map/ppermute | solution.py:139
  122.9 5.2 %collective-permute-done.15.refs_4_.refs_2_.refs_6_ = f32[1,256,512]{2,1,0:T(8,128)S(1)} collective-permute-done((f32[1,256,512]{2,1,0:T(8,128)S(1)}, f32[1,256,512]{2,1,0:T(8,128)S(1)}, u32[]{:S(2)}, u32[]{:S(2)}) %collective-permute-start.15) | collective-permute-done | bytes 524320 | tf_op jit(solution)/shard_map/ppermute | solution.py:135
  131.5 2.8 %add.18 = (f32[256,1024]{1,0:T(8,128)S(1)}, f32[256,1024]{1,0:T(8,128)}) custom-call(f32[2,256,1024]{2,1,0:T(8,128)S(1)} %copy-done.4, f32[2,256,1024]{2,1,0:T(8,128)} %collective-permute-done.5.refs_5_.refs_1_, f32[2,256,512]{2,1,0:T(8,128)S(1)} %side_payload.2.refs_2_), custom_call_target="tpu_custom_call" | custom-call | flops 128 | bytes 128 | tf_op jit(solution)/shard_map/add/pallas_call | solution.py:111
  134.3 5.8 %collective-permute-done.22.refs_7_.refs_3_ = f32[3,128,256]{2,1,0:T(8,128)S(1)} collective-permute-done((f32[3,128,256]{2,1,0:T(8,128)S(1)}, f32[3,128,256]{2,1,0:T(8,128)S(1)}, u32[]{:S(2)}, u32[]{:S(2)}) %collective-permute-start.22) | collective-permute-done | bytes 393248 | tf_op jit(solution)/shard_map/ppermute | solution.py:139
  145.0 2.3 %collective-permute-done.23.refs_4_.refs_1_ = f32[7,3,512]{2,1,0:T(4,128)S(1)} collective-permute-done((f32[7,3,512]{2,1,0:T(4,128)S(1)}, f32[7,3,512]{2,1,0:T(4,128)S(1)}, u32[]{:S(2)}, u32[]{:S(2)}) %collective-permute-start.23) | collective-permute-done | bytes 43040 | tf_op jit(solution)/shard_map/ppermute | solution.py:139
  150.5 12.0 %collective-permute-done.26.refs_3_.refs_4_ = f32[2,256,512]{2,1,0:T(8,128)S(1)} collective-permute-done((f32[2,256,512]{2,1,0:T(8,128)S(1)}, f32[2,256,512]{2,1,0:T(8,128)S(1)}, u32[]{:S(2)}, u32[]{:S(2)}) %collective-permute-start.26) | collective-permute-done | bytes 1048608 | tf_op jit(solution)/shard_map/ppermute | solution.py:139
  164.0 6.8 %weight_part.2.refs_2_.refs_8_ = f32[1536,512]{1,0:T(8,128)} custom-call(s32[3]{0:T(128)} %copy-done.29, bf16[3,512,1024]{2,1,0:T(8,128)(2,1)} %copy-done.2, bf16[3,256,512]{2,1,0:T(8,128)(2,1)} %copy-done.7, f32[2,256,512]{2,1,0:T(8,128)} %collective-permute-done.3.refs_5_.refs_2_.refs_3_, f32[1,256,512]{2,1,0:T(8,128)} %copy-done.19, ...), custom_call_target="tpu_custom_call" | custom-call | flops 128 | bytes 128 | tf_op jit(solution)/shard_map/weight_part/pallas_call | solution.py:111
  170.9 1.9 copy-done
  179.6 2.0 %collective-permute-done.16.refs_1_ = f32[256,1024]{1,0:T(8,128)} collective-permute-done((f32[256,1024]{1,0:T(8,128)}, f32[256,1024]{1,0:T(8,128)}, u32[]{:S(2)}, u32[]{:S(2)}) %collective-permute-start.16) | collective-permute-done | bytes 1048608 | tf_op jit(solution)/shard_map/ppermute | solution.py:139
  181.6 2.4 %collective-permute-done.32.refs_3_.refs_7_ = f32[2,256,512]{2,1,0:T(8,128)} collective-permute-done((f32[2,256,512]{2,1,0:T(8,128)}, f32[2,256,512]{2,1,0:T(8,128)}, u32[]{:S(2)}, u32[]{:S(2)}) %collective-permute-start.32) | collective-permute-done | bytes 1048608 | tf_op jit(solution)/shard_map/ppermute | solution.py:139
  183.9 2.1 %add_rounded.1.refs_9_ = bf16[256,1024]{1,0:T(8,128)(2,1)} custom-call(f32[256,1024]{1,0:T(8,128)S(1)} %copy-done.14, f32[256,1024]{1,0:T(8,128)} %collective-permute-done.16.refs_1_, f32[7,3,512]{2,1,0:T(4,128)S(1)} %get-tuple-element.39.refs_2_, f32[2,256,512]{2,1,0:T(8,128)} %collective-permute-done.32.refs_3_.refs_7_), custom_call_target="tpu_custom_call" | custom-call | flops 128 | bytes 128 | tf_op jit(solution)/shard_map/add_rounded/pallas_call | solution.py:111
  186.7 8.1 %weight_part.3 = f32[1536,512]{1,0:T(8,128)} custom-call(s32[3]{0:T(128)} %copy-done.29, bf16[3,512,1024]{2,1,0:T(8,128)(2,1)} %copy-done.1, f32[2,256,512]{2,1,0:T(8,128)} %collective-permute-done.6.refs_1_.refs_2_, f32[1,256,512]{2,1,0:T(8,128)} %copy-done.20, f32[2,256,512]{2,1,0:T(8,128)} %copy-done.10, f32[2,256,512]{2,1,0:T(8,128)} %copy-done.8, ...), custom_call_target="tpu_custom_call" | custom-call | flops 128 | bytes 128 | tf_op jit(solution)/shard_map/weight_part/pallas_call | solution.py:111
  (140 shorter events, 61.5 us)
Async XLA Ops:
  4.2 30.5 %collective-permute-start.1 = (f32[8,128,256]{2,1,0:T(8,128)}, f32[8,128,256]{2,1,0:T(8,128)}, u32[]{:S(2)}, u32[]{:S(2)}) collective-permute-start(f32[8,128,256]{2,1,0:T(8,128)} %get-tuple-element.20.refs_5_), channel_id=1, source_target_pairs={{0,8},{4,12},{8,0},{12,4},{16,24},{20,28},{24,16},{28,20},{1,9},{5... | collective-permute-start | bytes 3145736 | tf_op jit(solution)/shard_map/ppermute | solution.py:135
  7.2 29.5 %collective-permute-start = (f32[8,128,256]{2,1,0:T(8,128)}, f32[8,128,256]{2,1,0:T(8,128)S(1)}, u32[]{:S(2)}, u32[]{:S(2)}) collective-permute-start(f32[8,128,256]{2,1,0:T(8,128)} %get-tuple-element.20.refs_5_), channel_id=1, source_target_pairs={{8,16},{12,20},{16,8},{20,12},{9,17},{13,21},{17,9},{21,13},{10,18... | collective-permute-start | bytes 3145736 | tf_op jit(solution)/shard_map/ppermute | solution.py:135
  26.0 24.9 %collective-permute-start.2 = (f32[2,256,512]{2,1,0:T(8,128)}, f32[2,256,512]{2,1,0:T(8,128)}, u32[]{:S(2)}, u32[]{:S(2)}) collective-permute-start(f32[2,256,512]{2,1,0:T(8,128)} %get-tuple-element.22), channel_id=1, source_target_pairs={{0,4},{4,0},{8,12},{12,8},{16,20},{20,16},{24,28},{28,24},{1,5},{5... | collective-permute-start | bytes 3145736 | tf_op jit(solution)/shard_map/ppermute | solution.py:139
  27.5 28.1 %collective-permute-start.3 = (f32[2,256,512]{2,1,0:T(8,128)}, f32[2,256,512]{2,1,0:T(8,128)}, u32[]{:S(2)}, u32[]{:S(2)}) collective-permute-start(f32[2,256,512]{2,1,0:T(8,128)} %get-tuple-element.22), channel_id=1, source_target_pairs={{0,8},{4,12},{24,16},{28,20},{1,9},{5,13},{25,17},{29,21},{2,10},{... | collective-permute-start | bytes 3145736 | tf_op jit(solution)/shard_map/ppermute | solution.py:135
  34.7 23.4 %collective-permute-start.4 = (f32[8,128,256]{2,1,0:T(8,128)}, f32[8,128,256]{2,1,0:T(8,128)S(1)}, u32[]{:S(2)}, u32[]{:S(2)}) collective-permute-start(f32[8,128,256]{2,1,0:T(8,128)} %collective-permute-done.1.refs_1_), channel_id=1, source_target_pairs={{8,16},{12,20},{16,8},{20,12},{9,17},{13,21},{17,9},{21,13},{10,18... | collective-permute-start | bytes 3145736 | tf_op jit(solution)/shard_map/ppermute | solution.py:135
  46.9 53.6 %collective-permute-start.5 = (f32[2,256,1024]{2,1,0:T(8,128)}, f32[2,256,1024]{2,1,0:T(8,128)}, u32[]{:S(2)}, u32[]{:S(2)}) collective-permute-start(f32[2,256,1024]{2,1,0:T(8,128)} %token_part.2.refs_3_), channel_id=1, source_target_pairs={{0,1},{1,0},{2,3},{3,2},{4,5},{5,4},{6,7},{7,6},{8,9},{9,8},{10,11... | collective-permute-start | bytes 6291464 | tf_op jit(solution)/shard_map/ppermute | solution.py:139
  46.9 42.1 %collective-permute-start.6 = (f32[2,256,512]{2,1,0:T(8,128)}, f32[2,256,512]{2,1,0:T(8,128)}, u32[]{:S(2)}, u32[]{:S(2)}) collective-permute-start(f32[2,256,512]{2,1,0:T(8,128)} %get-tuple-element.23), channel_id=1, source_target_pairs={{8,16},{12,20},{16,8},{20,12},{9,17},{13,21},{17,9},{21,13},{10,18... | collective-permute-start | bytes 3145736 | tf_op jit(solution)/shard_map/ppermute | solution.py:135
  50.9 24.1 %collective-permute-start.8 = (f32[6,128,256]{2,1,0:T(8,128)}, f32[6,128,256]{2,1,0:T(8,128)}, u32[]{:S(2)}, u32[]{:S(2)}) collective-permute-start(f32[6,128,256]{2,1,0:T(8,128)} %part_of.4.refs_3_), channel_id=1, source_target_pairs={{8,0},{12,4},{16,24},{20,28},{9,1},{13,5},{17,25},{21,29},{10,2},{... | collective-permute-start | bytes 2359304 | tf_op jit(solution)/shard_map/ppermute | solution.py:135
  55.6 30.5 %collective-permute-start.7 = (f32[1,256,512]{2,1,0:T(8,128)}, f32[1,256,512]{2,1,0:T(8,128)S(1)}, u32[]{:S(2)}, u32[]{:S(2)}) collective-permute-start(f32[1,256,512]{2,1,0:T(8,128)} %copy-done.31), channel_id=1, source_target_pairs={{0,8},{4,12},{8,0},{12,4},{16,24},{20,28},{24,16},{28,20},{1,9},{5... | collective-permute-start | bytes 1572872 | tf_op jit(solution)/shard_map/ppermute | solution.py:135
  68.8 31.7 %collective-permute-start.11 = (f32[6,128,256]{2,1,0:T(8,128)S(1)}, f32[6,128,256]{2,1,0:T(8,128)S(1)}, u32[]{:S(2)}, u32[]{:S(2)}) collective-permute-start(f32[6,128,256]{2,1,0:T(8,128)S(1)} %part_of.5.refs_3_), channel_id=1, source_target_pairs={{8,0},{12,4},{16,24},{20,28},{9,1},{13,5},{17,25},{21,29},{10,2},{... | collective-permute-start | bytes 2359304 | tf_op jit(solution)/shard_map/ppermute | solution.py:135
  89.1 17.3 %collective-permute-start.10 = (f32[2,256,512]{2,1,0:T(8,128)S(1)}, f32[2,256,512]{2,1,0:T(8,128)S(1)}, u32[]{:S(2)}, u32[]{:S(2)}) collective-permute-start(f32[2,256,512]{2,1,0:T(8,128)S(1)} %get-tuple-element.25.refs_2_), channel_id=1, source_target_pairs={{8,16},{12,20},{16,8},{20,12},{9,17},{13,21},{17,9},{21,13},{10,18... | collective-permute-start | bytes 3145736 | tf_op jit(solution)/shard_map/ppermute | solution.py:135
  89.8 28.9 %collective-permute-start.21 = (f32[2,256,512]{2,1,0:T(8,128)S(1)}, f32[2,256,512]{2,1,0:T(8,128)S(1)}, u32[]{:S(2)}, u32[]{:S(2)}) collective-permute-start(f32[2,256,512]{2,1,0:T(8,128)S(1)} %get-tuple-element.31), channel_id=1, source_target_pairs={{0,4},{4,0},{8,12},{12,8},{16,20},{20,16},{24,28},{28,24},{1,5},{5... | collective-permute-start | bytes 3145736 | tf_op jit(solution)/shard_map/ppermute | solution.py:139
  98.2 24.7 %collective-permute-start.19 = (f32[9,128,256]{2,1,0:T(8,128)S(1)}, f32[9,128,256]{2,1,0:T(8,128)S(1)}, u32[]{:S(2)}, u32[]{:S(2)}) collective-permute-start(f32[9,128,256]{2,1,0:T(8,128)S(1)} %own_blocks.3.refs_4_.refs_2_), channel_id=1, source_target_pairs={{0,2},{1,3},{2,0},{3,1},{4,6},{5,7},{6,4},{7,5},{8,10},{9,11},{10,... | collective-permute-start | bytes 3538952 | tf_op jit(solution)/shard_map/ppermute | solution.py:139
  100.6 30.3 %collective-permute-start.20 = (f32[9,128,256]{2,1,0:T(8,128)S(1)}, f32[9,128,256]{2,1,0:T(8,128)S(1)}, u32[]{:S(2)}, u32[]{:S(2)}) collective-permute-start(f32[9,128,256]{2,1,0:T(8,128)S(1)} %own_blocks.3.refs_4_.refs_2_), channel_id=1, source_target_pairs={{0,1},{1,0},{2,3},{3,2},{4,5},{5,4},{6,7},{7,6},{8,9},{9,8},{10,11... | collective-permute-start | bytes 3538952 | tf_op jit(solution)/shard_map/ppermute | solution.py:139
  100.6 16.6 %collective-permute-start.9 = (f32[1,256,512]{2,1,0:T(8,128)S(1)}, f32[1,256,512]{2,1,0:T(8,128)S(1)}, u32[]{:S(2)}, u32[]{:S(2)}) collective-permute-start(f32[1,256,512]{2,1,0:T(8,128)S(1)} %part_of.6.refs_4_), channel_id=1, source_target_pairs={{8,0},{12,4},{16,24},{20,28},{9,1},{13,5},{17,25},{21,29},{10,2},{... | collective-permute-start | bytes 1572872 | tf_op jit(solution)/shard_map/ppermute | solution.py:135
  107.0 21.0 %collective-permute-start.15 = (f32[1,256,512]{2,1,0:T(8,128)S(1)}, f32[1,256,512]{2,1,0:T(8,128)S(1)}, u32[]{:S(2)}, u32[]{:S(2)}) collective-permute-start(f32[1,256,512]{2,1,0:T(8,128)S(1)} %part_of.7.refs_3_), channel_id=1, source_target_pairs={{8,0},{12,4},{16,24},{20,28},{9,1},{13,5},{17,25},{21,29},{10,2},{... | collective-permute-start | bytes 1572872 | tf_op jit(solution)/shard_map/ppermute | solution.py:135
  118.7 21.3 %collective-permute-start.18 = (f32[6,128,256]{2,1,0:T(8,128)S(1)}, f32[6,128,256]{2,1,0:T(8,128)S(1)}, u32[]{:S(2)}, u32[]{:S(2)}) collective-permute-start(f32[6,128,256]{2,1,0:T(8,128)S(1)} %own_blocks.4.refs_3_.refs_1_), channel_id=1, source_target_pairs={{0,1},{1,0},{2,3},{3,2},{4,5},{5,4},{6,7},{7,6},{8,9},{9,8},{10,11... | collective-permute-start | bytes 2359304 | tf_op jit(solution)/shard_map/ppermute | solution.py:139
  121.4 19.6 %collective-permute-start.25 = (f32[6,128,256]{2,1,0:T(8,128)S(1)}, f32[6,128,256]{2,1,0:T(8,128)}, u32[]{:S(2)}, u32[]{:S(2)}) collective-permute-start(f32[6,128,256]{2,1,0:T(8,128)S(1)} %own_blocks.4.refs_3_.refs_1_), channel_id=1, source_target_pairs={{0,2},{1,3},{2,0},{3,1},{4,6},{5,7},{6,4},{7,5},{8,10},{9,11},{10,... | collective-permute-start | bytes 2359304 | tf_op jit(solution)/shard_map/ppermute | solution.py:139
  122.8 20.8 %collective-permute-start.24 = (f32[9,128,256]{2,1,0:T(8,128)S(1)}, f32[9,128,256]{2,1,0:T(8,128)S(1)}, u32[]{:S(2)}, u32[]{:S(2)}) collective-permute-start(f32[9,128,256]{2,1,0:T(8,128)S(1)} %collective-permute-done.19.refs_4_), channel_id=1, source_target_pairs={{0,1},{1,0},{2,3},{3,2},{4,5},{5,4},{6,7},{7,6},{8,9},{9,8},{10,11... | collective-permute-start | bytes 3538952 | tf_op jit(solution)/shard_map/ppermute | solution.py:139
  130.9 31.6 %collective-permute-start.26 = (f32[2,256,512]{2,1,0:T(8,128)S(1)}, f32[2,256,512]{2,1,0:T(8,128)S(1)}, u32[]{:S(2)}, u32[]{:S(2)}) collective-permute-start(f32[2,256,512]{2,1,0:T(8,128)S(1)} %side_payload.2.refs_2_), channel_id=1, source_target_pairs={{0,4},{4,0},{8,12},{12,8},{16,20},{20,16},{24,28},{28,24},{1,5},{5... | collective-permute-start | bytes 3145736 | tf_op jit(solution)/shard_map/ppermute | solution.py:139
  141.6 21.9 %collective-permute-start.28 = (f32[6,128,256]{2,1,0:T(8,128)S(1)}, f32[6,128,256]{2,1,0:T(8,128)}, u32[]{:S(2)}, u32[]{:S(2)}) collective-permute-start(f32[6,128,256]{2,1,0:T(8,128)S(1)} %own_blocks.5.refs_6_.refs_5_), channel_id=1, source_target_pairs={{0,2},{1,3},{2,0},{3,1},{4,6},{5,7},{6,4},{7,5},{8,10},{9,11},{10,... | collective-permute-start | bytes 2359304 | tf_op jit(solution)/shard_map/ppermute | solution.py:139
  143.1 38.4 %collective-permute-start.16 = (f32[256,1024]{1,0:T(8,128)}, f32[256,1024]{1,0:T(8,128)}, u32[]{:S(2)}, u32[]{:S(2)}) collective-permute-start(f32[256,1024]{1,0:T(8,128)} %get-tuple-element.30), channel_id=1, source_target_pairs={{0,2},{1,3},{2,0},{3,1},{4,6},{5,7},{6,4},{7,5},{8,10},{9,11},{10,... | collective-permute-start | bytes 3145736 | tf_op jit(solution)/shard_map/ppermute | solution.py:139
  148.9 35.0 %collective-permute-start.32 = (f32[2,256,512]{2,1,0:T(8,128)}, f32[2,256,512]{2,1,0:T(8,128)}, u32[]{:S(2)}, u32[]{:S(2)}) collective-permute-start(f32[2,256,512]{2,1,0:T(8,128)} %side_payload.3.refs_7_), channel_id=1, source_target_pairs={{0,4},{4,0},{8,12},{12,8},{16,20},{20,16},{24,28},{28,24},{1,5},{5... | collective-permute-start | bytes 3145736 | tf_op jit(solution)/shard_map/ppermute | solution.py:139
  150.5 20.4 %collective-permute-start.27 = (f32[6,128,256]{2,1,0:T(8,128)S(1)}, f32[6,128,256]{2,1,0:T(8,128)S(1)}, u32[]{:S(2)}, u32[]{:S(2)}) collective-permute-start(f32[6,128,256]{2,1,0:T(8,128)S(1)} %own_blocks.5.refs_6_.refs_5_), channel_id=1, source_target_pairs={{0,1},{1,0},{2,3},{3,2},{4,5},{5,4},{6,7},{7,6},{8,9},{9,8},{10,11... | collective-permute-start | bytes 2359304 | tf_op jit(solution)/shard_map/ppermute | solution.py:139
  (42 other events, 476.2 us)

commit v12 on v11

--- a/solution.py
+++ b/solution.py
@@ -216,7 +216,7 @@
     rows, features = tokens.shape
     chans = in_weight.shape[2]
     taps = kernel.shape[0]
-    steps = 4
+    steps = 2
     width = min(chans, 2 * LANES)
     deep = features // steps
     pad = 8
@@ -606,15 +606,15 @@
     inner = lines(inner_out, INWARD)
     first = lines(first_out, PAIRS)
     middle = lines(middle_out, MIDDLE)
-    near = order.wait(near)
+    near, mid = order.wait(near, mid)
     far = lines(near, MIDDLE)
+    send = token_part(order, jnp.stack(quarters[:2]), own, in_weight)
+    summed = flipped(send, "shard", 1)
+    outer2 = lines(part_of(order, place, mid, BLOCKS - OWN, OWN), OUTWARD)
+    own_y, inner = order.wait(own_y, inner)
     over = column_blocks(order, place, [(near, None)], False)
     got1 = flipped(over, "rep", 1)
-    mid = order.wait(mid)
-    outer2 = lines(part_of(order, place, mid, BLOCKS - OWN, OWN), OUTWARD)
-    send = token_part(order, jnp.stack(quarters[:2]), own, in_weight)
-    summed = flipped(send, "shard", 1)
-    own_y, inner, far = order.wait(own_y, inner, far)
+    far = order.wait(far)
     keep = token_part(order, jnp.stack(quarters[2:]), own, in_weight)
     outer3 = lines(part_of(order, place, far, BLOCKS - OWN, OWN), OUTWARD)
     outer2 = order.wait(outer2)
@@ -630,34 +630,32 @@
     own1 = column_blocks(order, place, [(near, None)], True, got0, got1)
     across1 = flipped(own1, "shard", 2)
     beside1 = flipped(own1, "shard", 1)
-    summed, got2 = order.wait(summed, got2)
+    summed, outer3, got2 = order.wait(summed, outer3, got2)
     own2 = column_blocks(order, place, [(mid, outer2)], True, got2)
     across2 = flipped(own2, "shard", 2)
     beside2 = flipped(own2, "shard", 1)
-    outer3 = order.wait(outer3)
     over = column_blocks(order, place, [(far, outer3)], False)
     got3 = flipped(over, "rep", 1)
     taps = tap_part(order, stored, grads, kernel.shape[0])
     taps1 = flipped(taps, "rep", 1)
     relayed = order.wait(relayed)
     relayed_end = lines(part_of(order, place, relayed, 1, 1), OUTWARD)
-    relayed_end, middle_end = order.wait(relayed_end, middle_end)
+    across1, relayed_end, middle_end = order.wait(across1, relayed_end, middle_end)
+    both1 = flipped(across1, "shard", 1)
     side2 = flipped(side_payload(order, place, middle, middle_end), "rep", 1)
     token_grad, away = add(order, keep, summed)
     last = flipped(away, "shard", 2)
-    beside2, across1, beside1, side1, got3, taps1 = order.wait(
-        beside2, across1, beside1, side1, got3, taps1
-    )
-    both1 = flipped(across1, "shard", 1)
-    taps, taps_out = add(order, taps, taps1)
-    taps2 = flipped(taps_out, "rep", 2)
-    across2 = order.wait(across2)
+    beside2, beside1, side1, got3, taps1, across2 = order.wait(
+        beside2, beside1, side1, got3, taps1, across2
+    )
     both2 = flipped(across2, "shard", 1)
     own3 = column_blocks(order, place, [(far, outer3)], True, got3)
     across3 = flipped(own3, "shard", 2)
     beside3 = flipped(own3, "shard", 1)
     both1 = order.wait(both1)
     tok = arrange_tokens(order, place, tokens, [(own1, beside1, across1, both1)])
+    taps, taps_out = add(order, taps, taps1)
+    taps2 = flipped(taps_out, "rep", 2)
     taps2 = order.wait(taps2)
     side3 = flipped(side_payload(order, place, relayed, relayed_end), "rep", 1)
     early = [(own, None), (inner, first), (own_y, None), (side1, None)]
@@ -669,9 +667,9 @@
     both3 = order.wait(both3)
     late = [(own2, beside2, across2, both2), (own3, beside3, across3, both3)]
     tok = arrange_tokens(order, place, None, late)
-    taps4 = order.wait(taps4)
+    side3, taps4 = order.wait(side3, taps4)
     taps, _ = add(order, taps, taps4, scale=scale)
-    side3, last = order.wait(side3, last)
+    last = order.wait(last)
     token_grad = add_rounded(order, token_grad, last)
     late = [(middle, middle_end), (side2, None), (relayed, relayed_end), (side3, None)]
     weight_grad = weight_part(order, place, tok, late, scale, so_far)

time: 196 us -> 192 us (0.980)
  Pallas kernels: 74.7 us -> 71 us
  local copies, waits for them, and re-layouts: 14.4 us -> 10.7 us
  starting transfers between devices: 38.2 us -> 41.4 us
    ppermute x22, starting transfers between devices: 16.4 us -> 20.5 us  [flipped(): lax.ppermute(array, axis, [(r, r ^ flip) for r in range(lax.axis_size(axi...]
    ppermute x11, waiting for transfers between devices: 31.5 us -> 27.8 us  [lines(): return lax.ppermute(array, 'rep', perm)]
    pallas_call x27, Pallas kernels: 74.7 us -> 71 us  [call(): pl.pallas_call(short, out_shape=out_shape, grid_spec=pltpu.PrefetchScalar...]
    unnamed x68 -> x54, local copies, waits for them, and re-layouts: 14.4 us -> 10.7 us
    ppermute x22, waiting for transfers between devices: 34.7 us -> 38.3 us  [flipped(): lax.ppermute(array, axis, [(r, r ^ flip) for r in range(lax.axis_size(axi...]
  transfers between devices with their start and end apart: 33 -> 33, of which waited for: 15 -> 14; matrix products, arithmetic and copies ran while one was open for 0% -> 0% of each run, Pallas kernels for 32% -> 31%
where the time goes in v12:
time: 192 us; the launch traced here: 191 us
  Pallas kernels  71 us (37%)
  waiting for transfers between devices  66.1 us (34%)
  starting transfers between devices  41.4 us (22%)
  local copies, waits for them, and re-layouts  10.7 us (6%)
    pallas_call x27, Pallas kernels, call(): pl.pallas_call(short, out_shape=out_shape, grid_spec=pltpu.PrefetchScalar...  71 us
    ppermute x22, waiting for transfers between devices, flipped(): lax.ppermute(array, axis, [(r, r ^ flip) for r in range(lax.axis_size(axi...  38.3 us
    ppermute x11, waiting for transfers between devices, lines(): return lax.ppermute(array, 'rep', perm)  27.8 us
    ppermute x11, starting transfers between devices, lines(): return lax.ppermute(array, 'rep', perm)  20.9 us
    ppermute x22, starting transfers between devices, flipped(): lax.ppermute(array, axis, [(r, r ^ flip) for r in range(lax.axis_size(axi...  20.5 us
    unnamed x54, local copies, waits for them, and re-layouts  10.7 us
  transfers between devices with their start and end apart: 33, of which 14 were waited for; matrix products, arithmetic and copies ran while one was open for 0% of the time, Pallas kernels for 31%

profile of v12, /device:TPU:0, one launch (start us, length us, event | category | flops | bytes accessed | tf_op | source)
XLA Modules:
  0.0 190.5 jit_solution(3703120567871128747)
XLA Ops:
  4.2 3.0 %collective-permute-start = (f32[8,128,256]{2,1,0:T(8,128)}, f32[8,128,256]{2,1,0:T(8,128)}, u32[]{:S(2)}, u32[]{:S(2)}) collective-permute-start(f32[8,128,256]{2,1,0:T(8,128)} %get-tuple-element.20.refs_5_), channel_id=1, source_target_pairs={{0,8},{4,12},{8,0},{12,4},{16,24},{20,28},{24,16},{28,20},{1,9},{5... | collective-permute-start | bytes 3145736 | tf_op jit(solution)/shard_map/ppermute | solution.py:135
  8.0 14.6 %gate.1 = (bf16[3,256,512]{2,1,0:T(8,128)(2,1)S(1)}, bf16[3,256,512]{2,1,0:T(8,128)(2,1)S(1)}, f32[3,256,512]{2,1,0:T(8,128)}, f32[1,256,512]{2,1,0:T(8,128)}, f...) custom-call(s32[3]{0:T(128)S(1)} %pad_add_fusion.1.refs_0_, bf16[256,4096]{1,0:T(8,128)(2,1)} %refs_1_.5, ...), custom_call_target="tpu_custom_call" | custom-call | flops 128 | bytes 128 | tf_op jit(solution)/shard_map/gate/pallas_call | solution.py:111
  25.1 7.2 %collective-permute-start.3 = (f32[2,256,512]{2,1,0:T(8,128)}, f32[2,256,512]{2,1,0:T(8,128)}, u32[]{:S(2)}, u32[]{:S(2)}) collective-permute-start(f32[2,256,512]{2,1,0:T(8,128)} %get-tuple-element.22), channel_id=1, source_target_pairs={{0,8},{4,12},{24,16},{28,20},{1,9},{5,13},{25,17},{29,21},{2,10},{... | collective-permute-start | bytes 3145736 | tf_op jit(solution)/shard_map/ppermute | solution.py:135
  33.2 7.9 %token_part.2.refs_2_ = f32[2,256,1024]{2,1,0:T(8,128)} custom-call(s32[2]{0:T(128)S(1)} %pad_add_fusion.2.refs_0_, bf16[3,256,512]{2,1,0:T(8,128)(2,1)S(1)} %get-tuple-element.21.refs_1_.refs_2_, bf16[3,4096,512]{2,1,0:T(8,128)(2,1)} %refs_2_.5, f32[8,128,256]{2,1,0:T(8,128)} %collective-permute-done.refs_3_.refs_1_, ...), custom_call_target="tpu_custom_call" | custom-call | flops 128 | bytes 128 | tf_op jit(solution)/shard_map/token_part/pallas_call | solution.py:111
  45.5 3.1 %collective-permute-done.2.refs_3_.refs_5_ = f32[2,256,512]{2,1,0:T(8,128)} collective-permute-done((f32[2,256,512]{2,1,0:T(8,128)}, f32[2,256,512]{2,1,0:T(8,128)}, u32[]{:S(2)}, u32[]{:S(2)}) %collective-permute-start.2) | collective-permute-done | bytes 1048608 | tf_op jit(solution)/shard_map/ppermute | solution.py:139
  49.3 4.0 %collective-permute-done.3.refs_4_.refs_2_.refs_3_ = f32[2,256,512]{2,1,0:T(8,128)} collective-permute-done((f32[2,256,512]{2,1,0:T(8,128)}, f32[2,256,512]{2,1,0:T(8,128)}, u32[]{:S(2)}, u32[]{:S(2)}) %collective-permute-start.3) | collective-permute-done | bytes 1048608 | tf_op jit(solution)/shard_map/ppermute | solution.py:135
  53.2 2.5 %collective-permute-start.7 = (f32[1,256,512]{2,1,0:T(8,128)}, f32[1,256,512]{2,1,0:T(8,128)}, u32[]{:S(2)}, u32[]{:S(2)}) collective-permute-start(f32[1,256,512]{2,1,0:T(8,128)} %get-tuple-element.24), channel_id=1, source_target_pairs={{0,8},{4,12},{8,0},{12,4},{16,24},{20,28},{24,16},{28,20},{1,9},{5... | collective-permute-start | bytes 1572872 | tf_op jit(solution)/shard_map/ppermute | solution.py:135
  57.9 8.0 %token_part.3.refs_2_.refs_0_ = f32[2,256,1024]{2,1,0:T(8,128)} custom-call(s32[2]{0:T(128)S(1)} %pad_add_fusion.refs_0_, bf16[3,256,512]{2,1,0:T(8,128)(2,1)S(1)} %copy-done.11, bf16[3,4096,512]{2,1,0:T(8,128)(2,1)} %refs_2_.5, f32[3,128,256]{2,1,0:T(8,128)S(1)} %other_blocks.3.refs_3_, f32[8,128,256]{2,1,0:T(8,128)S(1)} %collective-permute-done.4.refs_4_.refs_1_), custom_call_target="tpu_custom_call" | custom-call | flops 128 | bytes 128 | tf_op jit(solution)/shard_map/token_part/pallas_call | solution.py:111
  72.0 6.6 %collective-permute-done.7.refs_1_.refs_4_ = f32[1,256,512]{2,1,0:T(8,128)} collective-permute-done((f32[1,256,512]{2,1,0:T(8,128)}, f32[1,256,512]{2,1,0:T(8,128)}, u32[]{:S(2)}, u32[]{:S(2)}) %collective-permute-start.7) | collective-permute-done | bytes 524320 | tf_op jit(solution)/shard_map/ppermute | solution.py:135
  78.6 2.3 %collective-permute-start.12 = (f32[3,128,256]{2,1,0:T(8,128)S(1)}, f32[3,128,256]{2,1,0:T(8,128)S(1)}, u32[]{:S(2)}, u32[]{:S(2)}) collective-permute-start(f32[3,128,256]{2,1,0:T(8,128)S(1)} %other_blocks.4.refs_3_), channel_id=1, source_target_pairs={{0,4},{4,0},{8,12},{12,8},{16,20},{20,16},{24,28},{28,24},{1,5},{5... | collective-permute-start | bytes 1179656 | tf_op jit(solution)/shard_map/ppermute | solution.py:139
  86.7 3.2 %collective-permute-done.12.refs_3_ = f32[3,128,256]{2,1,0:T(8,128)S(1)} collective-permute-done((f32[3,128,256]{2,1,0:T(8,128)S(1)}, f32[3,128,256]{2,1,0:T(8,128)S(1)}, u32[]{:S(2)}, u32[]{:S(2)}) %collective-permute-start.12) | collective-permute-done | bytes 393248 | tf_op jit(solution)/shard_map/ppermute | solution.py:139
  91.6 3.5 %collective-permute-done.11.refs_6_.refs_2_ = f32[6,128,256]{2,1,0:T(8,128)S(1)} collective-permute-done((f32[6,128,256]{2,1,0:T(8,128)S(1)}, f32[6,128,256]{2,1,0:T(8,128)S(1)}, u32[]{:S(2)}, u32[]{:S(2)}) %collective-permute-start.11) | collective-permute-done | bytes 786464 | tf_op jit(solution)/shard_map/ppermute | solution.py:135
  103.0 8.7 %collective-permute-done.9.refs_2_.refs_3_ = f32[1,256,512]{2,1,0:T(8,128)S(1)} collective-permute-done((f32[1,256,512]{2,1,0:T(8,128)S(1)}, f32[1,256,512]{2,1,0:T(8,128)S(1)}, u32[]{:S(2)}, u32[]{:S(2)}) %collective-permute-start.9) | collective-permute-done | bytes 524320 | tf_op jit(solution)/shard_map/ppermute | solution.py:135
  111.8 2.3 %collective-permute-start.18 = (f32[7,3,512]{2,1,0:T(4,128)S(1)}, f32[7,3,512]{2,1,0:T(4,128)S(1)}, u32[]{:S(2)}, u32[]{:S(2)}) collective-permute-start(f32[7,3,512]{2,1,0:T(4,128)S(1)} %tap_part.1.refs_2_.refs_0_), channel_id=1, source_target_pairs={{0,4},{4,0},{8,12},{12,8},{16,20},{20,16},{24,28},{28,24},{1,5},{5... | collective-permute-start | bytes 129032 | tf_op jit(solution)/shard_map/ppermute | solution.py:139
  117.7 4.9 %collective-permute-done.16.refs_5_.refs_2_.refs_6_ = f32[1,256,512]{2,1,0:T(8,128)S(1)} collective-permute-done((f32[1,256,512]{2,1,0:T(8,128)S(1)}, f32[1,256,512]{2,1,0:T(8,128)S(1)}, u32[]{:S(2)}, u32[]{:S(2)}) %collective-permute-start.16) | collective-permute-done | bytes 524320 | tf_op jit(solution)/shard_map/ppermute | solution.py:135
  122.6 2.3 %collective-permute-start.21 = (f32[3,128,256]{2,1,0:T(8,128)S(1)}, f32[3,128,256]{2,1,0:T(8,128)S(1)}, u32[]{:S(2)}, u32[]{:S(2)}) collective-permute-start(f32[3,128,256]{2,1,0:T(8,128)S(1)} %other_blocks.5.refs_2_), channel_id=1, source_target_pairs={{0,4},{4,0},{8,12},{12,8},{16,20},{20,16},{24,28},{28,24},{1,5},{5... | collective-permute-start | bytes 1179656 | tf_op jit(solution)/shard_map/ppermute | solution.py:139
  125.6 2.8 %add.18 = (f32[256,1024]{1,0:T(8,128)S(1)}, f32[256,1024]{1,0:T(8,128)}) custom-call(f32[2,256,1024]{2,1,0:T(8,128)S(1)} %copy-done.4, f32[2,256,1024]{2,1,0:T(8,128)} %collective-permute-done.5.refs_5_.refs_1_, f32[2,256,512]{2,1,0:T(8,128)S(1)} %side_payload.2.refs_2_), custom_call_target="tpu_custom_call" | custom-call | flops 128 | bytes 128 | tf_op jit(solution)/shard_map/add/pallas_call | solution.py:111
  128.5 6.3 %collective-permute-done.21.refs_3_ = f32[3,128,256]{2,1,0:T(8,128)S(1)} collective-permute-done((f32[3,128,256]{2,1,0:T(8,128)S(1)}, f32[3,128,256]{2,1,0:T(8,128)S(1)}, u32[]{:S(2)}, u32[]{:S(2)}) %collective-permute-start.21) | collective-permute-done | bytes 393248 | tf_op jit(solution)/shard_map/ppermute | solution.py:139
  138.7 4.2 %collective-permute-done.25.refs_4_.refs_1_ = f32[7,3,512]{2,1,0:T(4,128)S(1)} collective-permute-done((f32[7,3,512]{2,1,0:T(4,128)S(1)}, f32[7,3,512]{2,1,0:T(4,128)S(1)}, u32[]{:S(2)}, u32[]{:S(2)}) %collective-permute-start.25) | collective-permute-done | bytes 43040 | tf_op jit(solution)/shard_map/ppermute | solution.py:139
  146.7 10.6 %collective-permute-done.26.refs_3_.refs_4_ = f32[2,256,512]{2,1,0:T(8,128)S(1)} collective-permute-done((f32[2,256,512]{2,1,0:T(8,128)S(1)}, f32[2,256,512]{2,1,0:T(8,128)S(1)}, u32[]{:S(2)}, u32[]{:S(2)}) %collective-permute-start.26) | collective-permute-done | bytes 1048608 | tf_op jit(solution)/shard_map/ppermute | solution.py:139
  157.8 6.9 %weight_part.2.refs_2_.refs_8_ = f32[1536,512]{1,0:T(8,128)} custom-call(s32[3]{0:T(128)} %copy-done.23, bf16[3,512,1024]{2,1,0:T(8,128)(2,1)} %copy-done.1, bf16[3,256,512]{2,1,0:T(8,128)(2,1)} %copy-done.10, f32[2,256,512]{2,1,0:T(8,128)} %collective-permute-done.3.refs_4_.refs_2_.refs_3_, f32[1,256,512]{2,1,0:T(8,128)} %collective-permute-done.7.refs_1_.refs_4_, ...), custom_call_target="tpu_custom_call" | custom-call | flops 128 | bytes 128 | tf_op jit(solution)/shard_map/weight_part/pallas_call | solution.py:111
  167.7 2.6 %arrange_tokens.3.refs_2_.refs_1_ = bf16[3,512,1024]{2,1,0:T(8,128)(2,1)S(1)} custom-call(s32[3]{0:T(128)S(1)} %copy-done.24, f32[6,128,256]{2,1,0:T(8,128)S(1)} %own_blocks.4.refs_3_.refs_1_, f32[6,128,256]{2,1,0:T(8,128)S(1)} %copy-done.17, f32[6,128,256]{2,1,0:T(8,128)} %collective-permute-done.24.refs_9_.refs_3_, ...), custom_call_target="tpu_custom_call" | custom-call | flops 128 | bytes 128 | tf_op jit(solution)/shard_map/arrange_tokens/pallas_call | solution.py:111
  172.0 7.0 %collective-permute-done.32.refs_3_.refs_7_ = f32[2,256,512]{2,1,0:T(8,128)} collective-permute-done((f32[2,256,512]{2,1,0:T(8,128)S(1)}, f32[2,256,512]{2,1,0:T(8,128)}, u32[]{:S(2)}, u32[]{:S(2)}) %collective-permute-start.32) | collective-permute-done | bytes 1048608 | tf_op jit(solution)/shard_map/ppermute | solution.py:139
  182.4 8.1 %weight_part.3 = f32[1536,512]{1,0:T(8,128)} custom-call(s32[3]{0:T(128)} %copy-done.23, bf16[3,512,1024]{2,1,0:T(8,128)(2,1)} %copy-done.2, f32[2,256,512]{2,1,0:T(8,128)} %copy-done.7, f32[1,256,512]{2,1,0:T(8,128)} %copy-done.18, f32[2,256,512]{2,1,0:T(8,128)} %copy-done.14, f32[2,256,512]{2,1,0:T(8,128)} %copy-done.8, f32[1,256,512]{2,1,0:T(8,128)} %copy-done.12, ...), custom_call_target="tpu_custom_call" | custom-call | flops 128 | bytes 128 | tf_op jit(solution)/shard_map/weight_part/pallas_call | solution.py:111
  (126 shorter events, 56.7 us)
Async XLA Ops:
  4.2 28.2 %collective-permute-start = (f32[8,128,256]{2,1,0:T(8,128)}, f32[8,128,256]{2,1,0:T(8,128)}, u32[]{:S(2)}, u32[]{:S(2)}) collective-permute-start(f32[8,128,256]{2,1,0:T(8,128)} %get-tuple-element.20.refs_5_), channel_id=1, source_target_pairs={{0,8},{4,12},{8,0},{12,4},{16,24},{20,28},{24,16},{28,20},{1,9},{5... | collective-permute-start | bytes 3145736 | tf_op jit(solution)/shard_map/ppermute | solution.py:135
  7.2 26.0 %collective-permute-start.1 = (f32[8,128,256]{2,1,0:T(8,128)}, f32[8,128,256]{2,1,0:T(8,128)S(1)}, u32[]{:S(2)}, u32[]{:S(2)}) collective-permute-start(f32[8,128,256]{2,1,0:T(8,128)} %get-tuple-element.20.refs_5_), channel_id=1, source_target_pairs={{8,16},{12,20},{16,8},{20,12},{9,17},{13,21},{17,9},{21,13},{10,18... | collective-permute-start | bytes 3145736 | tf_op jit(solution)/shard_map/ppermute | solution.py:135
  23.6 24.9 %collective-permute-start.2 = (f32[2,256,512]{2,1,0:T(8,128)}, f32[2,256,512]{2,1,0:T(8,128)}, u32[]{:S(2)}, u32[]{:S(2)}) collective-permute-start(f32[2,256,512]{2,1,0:T(8,128)} %get-tuple-element.22), channel_id=1, source_target_pairs={{0,4},{4,0},{8,12},{12,8},{16,20},{20,16},{24,28},{28,24},{1,5},{5... | collective-permute-start | bytes 3145736 | tf_op jit(solution)/shard_map/ppermute | solution.py:139
  25.1 28.1 %collective-permute-start.3 = (f32[2,256,512]{2,1,0:T(8,128)}, f32[2,256,512]{2,1,0:T(8,128)}, u32[]{:S(2)}, u32[]{:S(2)}) collective-permute-start(f32[2,256,512]{2,1,0:T(8,128)} %get-tuple-element.22), channel_id=1, source_target_pairs={{0,8},{4,12},{24,16},{28,20},{1,9},{5,13},{25,17},{29,21},{2,10},{... | collective-permute-start | bytes 3145736 | tf_op jit(solution)/shard_map/ppermute | solution.py:135
  32.4 23.4 %collective-permute-start.4 = (f32[8,128,256]{2,1,0:T(8,128)}, f32[8,128,256]{2,1,0:T(8,128)S(1)}, u32[]{:S(2)}, u32[]{:S(2)}) collective-permute-start(f32[8,128,256]{2,1,0:T(8,128)} %collective-permute-done.refs_3_.refs_1_), channel_id=1, source_target_pairs={{8,16},{12,20},{16,8},{20,12},{9,17},{13,21},{17,9},{21,13},{10,18... | collective-permute-start | bytes 3145736 | tf_op jit(solution)/shard_map/ppermute | solution.py:135
  41.1 54.1 %collective-permute-start.5 = (f32[2,256,1024]{2,1,0:T(8,128)}, f32[2,256,1024]{2,1,0:T(8,128)}, u32[]{:S(2)}, u32[]{:S(2)}) collective-permute-start(f32[2,256,1024]{2,1,0:T(8,128)} %token_part.2.refs_2_), channel_id=1, source_target_pairs={{0,1},{1,0},{2,3},{3,2},{4,5},{5,4},{6,7},{7,6},{8,9},{9,8},{10,11... | collective-permute-start | bytes 6291464 | tf_op jit(solution)/shard_map/ppermute | solution.py:139
  44.2 25.3 %collective-permute-start.8 = (f32[6,128,256]{2,1,0:T(8,128)}, f32[6,128,256]{2,1,0:T(8,128)}, u32[]{:S(2)}, u32[]{:S(2)}) collective-permute-start(f32[6,128,256]{2,1,0:T(8,128)} %part_of.4.refs_2_), channel_id=1, source_target_pairs={{8,0},{12,4},{16,24},{20,28},{9,1},{13,5},{17,25},{21,29},{10,2},{... | collective-permute-start | bytes 2359304 | tf_op jit(solution)/shard_map/ppermute | solution.py:135
  48.5 33.9 %collective-permute-start.6 = (f32[2,256,512]{2,1,0:T(8,128)}, f32[2,256,512]{2,1,0:T(8,128)S(1)}, u32[]{:S(2)}, u32[]{:S(2)}) collective-permute-start(f32[2,256,512]{2,1,0:T(8,128)} %get-tuple-element.23), channel_id=1, source_target_pairs={{8,16},{12,20},{16,8},{20,12},{9,17},{13,21},{17,9},{21,13},{10,18... | collective-permute-start | bytes 3145736 | tf_op jit(solution)/shard_map/ppermute | solution.py:135
  53.2 25.3 %collective-permute-start.7 = (f32[1,256,512]{2,1,0:T(8,128)}, f32[1,256,512]{2,1,0:T(8,128)}, u32[]{:S(2)}, u32[]{:S(2)}) collective-permute-start(f32[1,256,512]{2,1,0:T(8,128)} %get-tuple-element.24), channel_id=1, source_target_pairs={{0,8},{4,12},{8,0},{12,4},{16,24},{20,28},{24,16},{28,20},{1,9},{5... | collective-permute-start | bytes 1572872 | tf_op jit(solution)/shard_map/ppermute | solution.py:135
  65.9 17.8 %collective-permute-start.14 = (f32[3,128,256]{2,1,0:T(8,128)S(1)}, f32[3,128,256]{2,1,0:T(8,128)S(1)}, u32[]{:S(2)}, u32[]{:S(2)}) collective-permute-start(f32[3,128,256]{2,1,0:T(8,128)S(1)} %other_blocks.3.refs_3_), channel_id=1, source_target_pairs={{0,4},{4,0},{8,12},{12,8},{16,20},{20,16},{24,28},{28,24},{1,5},{5... | collective-permute-start | bytes 1179656 | tf_op jit(solution)/shard_map/ppermute | solution.py:139
  69.5 25.7 %collective-permute-start.11 = (f32[6,128,256]{2,1,0:T(8,128)S(1)}, f32[6,128,256]{2,1,0:T(8,128)S(1)}, u32[]{:S(2)}, u32[]{:S(2)}) collective-permute-start(f32[6,128,256]{2,1,0:T(8,128)S(1)} %part_of.5.refs_3_), channel_id=1, source_target_pairs={{8,0},{12,4},{16,24},{20,28},{9,1},{13,5},{17,25},{21,29},{10,2},{... | collective-permute-start | bytes 2359304 | tf_op jit(solution)/shard_map/ppermute | solution.py:135
  82.5 18.5 %collective-permute-start.10 = (f32[2,256,512]{2,1,0:T(8,128)S(1)}, f32[2,256,512]{2,1,0:T(8,128)S(1)}, u32[]{:S(2)}, u32[]{:S(2)}) collective-permute-start(f32[2,256,512]{2,1,0:T(8,128)S(1)} %get-tuple-element.25.refs_2_), channel_id=1, source_target_pairs={{8,16},{12,20},{16,8},{20,12},{9,17},{13,21},{17,9},{21,13},{10,18... | collective-permute-start | bytes 3145736 | tf_op jit(solution)/shard_map/ppermute | solution.py:135
  85.1 32.6 %collective-permute-start.15 = (f32[9,128,256]{2,1,0:T(8,128)S(1)}, f32[9,128,256]{2,1,0:T(8,128)S(1)}, u32[]{:S(2)}, u32[]{:S(2)}) collective-permute-start(f32[9,128,256]{2,1,0:T(8,128)S(1)} %own_blocks.3.refs_4_.refs_2_), channel_id=1, source_target_pairs={{0,2},{1,3},{2,0},{3,1},{4,6},{5,7},{6,4},{7,5},{8,10},{9,11},{10,... | collective-permute-start | bytes 3538952 | tf_op jit(solution)/shard_map/ppermute | solution.py:139
  89.9 24.2 %collective-permute-start.23 = (f32[2,256,512]{2,1,0:T(8,128)S(1)}, f32[2,256,512]{2,1,0:T(8,128)S(1)}, u32[]{:S(2)}, u32[]{:S(2)}) collective-permute-start(f32[2,256,512]{2,1,0:T(8,128)S(1)} %get-tuple-element.31), channel_id=1, source_target_pairs={{0,4},{4,0},{8,12},{12,8},{16,20},{20,16},{24,28},{28,24},{1,5},{5... | collective-permute-start | bytes 3145736 | tf_op jit(solution)/shard_map/ppermute | solution.py:139
  95.1 30.4 %collective-permute-start.19 = (f32[9,128,256]{2,1,0:T(8,128)S(1)}, f32[9,128,256]{2,1,0:T(8,128)S(1)}, u32[]{:S(2)}, u32[]{:S(2)}) collective-permute-start(f32[9,128,256]{2,1,0:T(8,128)S(1)} %own_blocks.3.refs_4_.refs_2_), channel_id=1, source_target_pairs={{0,1},{1,0},{2,3},{3,2},{4,5},{5,4},{6,7},{7,6},{8,9},{9,8},{10,11... | collective-permute-start | bytes 3538952 | tf_op jit(solution)/shard_map/ppermute | solution.py:139
  101.6 21.0 %collective-permute-start.16 = (f32[1,256,512]{2,1,0:T(8,128)S(1)}, f32[1,256,512]{2,1,0:T(8,128)S(1)}, u32[]{:S(2)}, u32[]{:S(2)}) collective-permute-start(f32[1,256,512]{2,1,0:T(8,128)S(1)} %part_of.7.refs_3_), channel_id=1, source_target_pairs={{8,0},{12,4},{16,24},{20,28},{9,1},{13,5},{17,25},{21,29},{10,2},{... | collective-permute-start | bytes 1572872 | tf_op jit(solution)/shard_map/ppermute | solution.py:135
  114.1 20.7 %collective-permute-start.22 = (f32[6,128,256]{2,1,0:T(8,128)S(1)}, f32[6,128,256]{2,1,0:T(8,128)S(1)}, u32[]{:S(2)}, u32[]{:S(2)}) collective-permute-start(f32[6,128,256]{2,1,0:T(8,128)S(1)} %own_blocks.4.refs_3_.refs_1_), channel_id=1, source_target_pairs={{0,1},{1,0},{2,3},{3,2},{4,5},{5,4},{6,7},{7,6},{8,9},{9,8},{10,11... | collective-permute-start | bytes 2359304 | tf_op jit(solution)/shard_map/ppermute | solution.py:139
  116.2 18.6 %collective-permute-start.24 = (f32[6,128,256]{2,1,0:T(8,128)S(1)}, f32[6,128,256]{2,1,0:T(8,128)}, u32[]{:S(2)}, u32[]{:S(2)}) collective-permute-start(f32[6,128,256]{2,1,0:T(8,128)S(1)} %own_blocks.4.refs_3_.refs_1_), channel_id=1, source_target_pairs={{0,2},{1,3},{2,0},{3,1},{4,6},{5,7},{6,4},{7,5},{8,10},{9,11},{10,... | collective-permute-start | bytes 2359304 | tf_op jit(solution)/shard_map/ppermute | solution.py:139
  117.7 19.5 %collective-permute-start.20 = (f32[9,128,256]{2,1,0:T(8,128)S(1)}, f32[9,128,256]{2,1,0:T(8,128)S(1)}, u32[]{:S(2)}, u32[]{:S(2)}) collective-permute-start(f32[9,128,256]{2,1,0:T(8,128)S(1)} %collective-permute-done.15.refs_4_), channel_id=1, source_target_pairs={{0,1},{1,0},{2,3},{3,2},{4,5},{5,4},{6,7},{7,6},{8,9},{9,8},{10,11... | collective-permute-start | bytes 3538952 | tf_op jit(solution)/shard_map/ppermute | solution.py:139
  125.6 31.7 %collective-permute-start.26 = (f32[2,256,512]{2,1,0:T(8,128)S(1)}, f32[2,256,512]{2,1,0:T(8,128)S(1)}, u32[]{:S(2)}, u32[]{:S(2)}) collective-permute-start(f32[2,256,512]{2,1,0:T(8,128)S(1)} %side_payload.2.refs_2_), channel_id=1, source_target_pairs={{0,4},{4,0},{8,12},{12,8},{16,20},{20,16},{24,28},{28,24},{1,5},{5... | collective-permute-start | bytes 3145736 | tf_op jit(solution)/shard_map/ppermute | solution.py:139
  135.7 21.6 %collective-permute-start.28 = (f32[6,128,256]{2,1,0:T(8,128)S(1)}, f32[6,128,256]{2,1,0:T(8,128)}, u32[]{:S(2)}, u32[]{:S(2)}) collective-permute-start(f32[6,128,256]{2,1,0:T(8,128)S(1)} %own_blocks.5.refs_6_.refs_5_), channel_id=1, source_target_pairs={{0,2},{1,3},{2,0},{3,1},{4,6},{5,7},{6,4},{7,5},{8,10},{9,11},{10,... | collective-permute-start | bytes 2359304 | tf_op jit(solution)/shard_map/ppermute | solution.py:139
  143.5 35.5 %collective-permute-start.32 = (f32[2,256,512]{2,1,0:T(8,128)S(1)}, f32[2,256,512]{2,1,0:T(8,128)}, u32[]{:S(2)}, u32[]{:S(2)}) collective-permute-start(f32[2,256,512]{2,1,0:T(8,128)S(1)} %side_payload.3.refs_7_), channel_id=1, source_target_pairs={{0,4},{4,0},{8,12},{12,8},{16,20},{20,16},{24,28},{28,24},{1,5},{5... | collective-permute-start | bytes 3145736 | tf_op jit(solution)/shard_map/ppermute | solution.py:139
  145.7 34.0 %collective-permute-start.17 = (f32[256,1024]{1,0:T(8,128)}, f32[256,1024]{1,0:T(8,128)}, u32[]{:S(2)}, u32[]{:S(2)}) collective-permute-start(f32[256,1024]{1,0:T(8,128)} %get-tuple-element.30), channel_id=1, source_target_pairs={{0,2},{1,3},{2,0},{3,1},{4,6},{5,7},{6,4},{7,5},{8,10},{9,11},{10,... | collective-permute-start | bytes 3145736 | tf_op jit(solution)/shard_map/ppermute | solution.py:139
  146.7 18.0 %collective-permute-start.27 = (f32[6,128,256]{2,1,0:T(8,128)S(1)}, f32[6,128,256]{2,1,0:T(8,128)}, u32[]{:S(2)}, u32[]{:S(2)}) collective-permute-start(f32[6,128,256]{2,1,0:T(8,128)S(1)} %own_blocks.5.refs_6_.refs_5_), channel_id=1, source_target_pairs={{0,1},{1,0},{2,3},{3,2},{4,5},{5,4},{6,7},{7,6},{8,9},{9,8},{10,11... | collective-permute-start | bytes 2359304 | tf_op jit(solution)/shard_map/ppermute | solution.py:139
  (35 other events, 476.7 us)

commit v13 on v10

--- a/solution.py
+++ b/solution.py
@@ -209,7 +209,7 @@
     rows, features = tokens.shape
     chans = in_weight.shape[2]
     taps = kernel.shape[0]
-    steps = 4
+    steps = 2
     width = min(chans, 2 * LANES)
     deep = features // steps
     pad = 8
@@ -514,7 +514,7 @@
         out_specs=part,
         scratch_shapes=[pltpu.VMEM((2, count * rows, chans), jnp.bfloat16)],
         name="weight_part",
-        vmem=58,
+        vmem=61,
     )
 
 

time: 190 us -> 191 us (level)
  waiting for transfers between devices: 54.6 us -> 57.1 us
    ppermute x11, waiting for transfers between devices: 22.9 us -> 25.6 us  [lines(): return lax.ppermute(array, 'rep', perm)]
  transfers between devices with their start and end apart: 32 -> 32, of which waited for: 12 -> 13; matrix products, arithmetic and copies ran while one was open for 0% -> 0% of each run, Pallas kernels for 39% -> 37%
where the time goes in v13:
time: 191 us; the launch traced here: 190 us
  Pallas kernels  73.5 us (38%)
  waiting for transfers between devices  57.1 us (30%)
  starting transfers between devices  44.5 us (23%)
  local copies, waits for them, and re-layouts  13.5 us (7%)
    pallas_call x26, Pallas kernels, call(): pl.pallas_call(short, out_shape=out_shape, grid_spec=pltpu.PrefetchScalar...  73.5 us
    ppermute x21, waiting for transfers between devices, flipped(): lax.ppermute(array, axis, [(r, r ^ flip) for r in range(lax.axis_size(axi...  31.5 us
    ppermute x11, waiting for transfers between devices, lines(): return lax.ppermute(array, 'rep', perm)  25.6 us
    ppermute x11, starting transfers between devices, lines(): return lax.ppermute(array, 'rep', perm)  22.5 us
    ppermute x21, starting transfers between devices, flipped(): lax.ppermute(array, axis, [(r, r ^ flip) for r in range(lax.axis_size(axi...  22 us
    unnamed x60, local copies, waits for them, and re-layouts  13.5 us
  transfers between devices with their start and end apart: 32, of which 13 were waited for; matrix products, arithmetic and copies ran while one was open for 0% of the time, Pallas kernels for 37%

profile of v13, /device:TPU:0, one launch (start us, length us, event | category | flops | bytes accessed | tf_op | source)
XLA Modules:
  0.0 190.0 jit_solution(12006597826961194206)
XLA Ops:
  4.1 3.0 %collective-permute-start.1 = (f32[8,128,256]{2,1,0:T(8,128)}, f32[8,128,256]{2,1,0:T(8,128)}, u32[]{:S(2)}, u32[]{:S(2)}) collective-permute-start(f32[8,128,256]{2,1,0:T(8,128)} %turn_tokens.1.refs_5_.refs_1_), channel_id=1, source_target_pairs={{0,8},{4,12},{8,0},{12,4},{16,24},{20,28},{24,16},{28,20},{1,9},{5... | collective-permute-start | bytes 3145736 | tf_op jit(solution)/shard_map/ppermute | solution.py:135
  8.8 14.7 %gate.1 = (bf16[3,256,512]{2,1,0:T(8,128)(2,1)S(1)}, f32[7,3,512]{2,1,0:T(4,128)S(1)}, f32[1,256,512]{2,1,0:T(8,128)}, f32[2,256,512]{2,1,0:T(8,128)}, f32[2,256,512]{2,1,0:T(8,128)}) custom-call(s32[3]{0:T(128)S(1)} %pad_add_fusion.1.refs_0_, bf16[256,4096]{1,0:T(8,128)(2,1)} %refs_1_.5, bf16[3,4096,512]{2,1,0:T(8,128)(2,1)} %refs_2_.5, ...), custom_call_target="tpu_custom_call" | custom-call | flops 128 | bytes 128 | tf_op jit(solution)/shard_map/gate/pallas_call | solution.py:111
  23.5 5.4 %collective-permute-start.2 = (f32[2,256,512]{2,1,0:T(8,128)}, f32[2,256,512]{2,1,0:T(8,128)S(1)}, u32[]{:S(2)}, u32[]{:S(2)}) collective-permute-start(f32[2,256,512]{2,1,0:T(8,128)} %get-tuple-element.18), channel_id=1, source_target_pairs={{0,8},{4,12},{24,16},{28,20},{1,9},{5,13},{25,17},{29,21},{2,10},{... | collective-permute-start | bytes 3145736 | tf_op jit(solution)/shard_map/ppermute | solution.py:135
  31.8 2.5 %other_blocks.3.refs_3_ = f32[6,128,256]{2,1,0:T(8,128)} custom-call(s32[3]{0:T(128)S(1)} %pad_add_fusion.1.refs_0_, f32[8,128,256]{2,1,0:T(8,128)} %turn_tokens.1.refs_5_.refs_1_, f32[8,128,256]{2,1,0:T(8,128)} %collective-permute-done.1.refs_2_.refs_1_, bf16[3,256,512]{2,1,0:T(8,128)(2,1)S(1)} %get-tuple-element.17.refs_3_.refs_1_.refs_2_), custom_call_target="tpu_custom_call" | custom-call | flops 128 | bytes 128 | tf_op jit(solution)/shard_map/other_blocks/pallas_call | solution.py:111
  34.3 7.9 %token_part.2.refs_2_ = f32[2,256,1024]{2,1,0:T(8,128)} custom-call(s32[2]{0:T(128)S(1)} %pad_add_fusion.2.refs_0_, bf16[3,256,512]{2,1,0:T(8,128)(2,1)S(1)} %get-tuple-element.17.refs_3_.refs_1_.refs_2_, bf16[3,4096,512]{2,1,0:T(8,128)(2,1)} %refs_2_.5, f32[6,128,256]{2,1,0:T(8,128)} %other_blocks.3.refs_3_), custom_call_target="tpu_custom_call" | custom-call | flops 128 | bytes 128 | tf_op jit(solution)/shard_map/token_part/pallas_call | solution.py:111
  42.2 2.2 %part_of.4.refs_3_ = f32[6,128,256]{2,1,0:T(8,128)} custom-call(s32[3]{0:T(128)S(1)} %pad_add_fusion.1.refs_0_, f32[8,128,256]{2,1,0:T(8,128)} %collective-permute-done.refs_1_, f32[2,256,1024]{2,1,0:T(8,128)} %token_part.2.refs_2_), custom_call_target="tpu_custom_call" | custom-call | flops 128 | bytes 128 | tf_op jit(solution)/shard_map/part_of/pallas_call | solution.py:111
  45.8 6.6 %collective-permute-done.2.refs_4_.refs_2_.refs_3_ = f32[2,256,512]{2,1,0:T(8,128)S(1)} collective-permute-done((f32[2,256,512]{2,1,0:T(8,128)}, f32[2,256,512]{2,1,0:T(8,128)S(1)}, u32[]{:S(2)}, u32[]{:S(2)}) %collective-permute-start.2) | collective-permute-done | bytes 1048608 | tf_op jit(solution)/shard_map/ppermute | solution.py:135
  54.0 4.3 %collective-permute-start.7 = (f32[1,256,512]{2,1,0:T(8,128)}, f32[1,256,512]{2,1,0:T(8,128)S(1)}, u32[]{:S(2)}, u32[]{:S(2)}) collective-permute-start(f32[1,256,512]{2,1,0:T(8,128)} %get-tuple-element.20), channel_id=1, source_target_pairs={{0,8},{4,12},{8,0},{12,4},{16,24},{20,28},{24,16},{28,20},{1,9},{5... | collective-permute-start | bytes 1572872 | tf_op jit(solution)/shard_map/ppermute | solution.py:135
  59.9 7.9 %token_part.3.refs_2_.refs_0_ = f32[2,256,1024]{2,1,0:T(8,128)} custom-call(s32[2]{0:T(128)S(1)} %pad_add_fusion.refs_0_, bf16[3,256,512]{2,1,0:T(8,128)(2,1)S(1)} %get-tuple-element.17.refs_3_.refs_1_.refs_2_, bf16[3,4096,512]{2,1,0:T(8,128)(2,1)} %refs_2_.5, f32[6,128,256]{2,1,0:T(8,128)} %part_of.4.refs_3_, ...), custom_call_target="tpu_custom_call" | custom-call | flops 128 | bytes 128 | tf_op jit(solution)/shard_map/token_part/pallas_call | solution.py:111
  74.1 6.7 %collective-permute-done.7.refs_1_.refs_4_ = f32[1,256,512]{2,1,0:T(8,128)S(1)} collective-permute-done((f32[1,256,512]{2,1,0:T(8,128)}, f32[1,256,512]{2,1,0:T(8,128)S(1)}, u32[]{:S(2)}, u32[]{:S(2)}) %collective-permute-start.7) | collective-permute-done | bytes 524320 | tf_op jit(solution)/shard_map/ppermute | solution.py:135
  88.3 4.6 %collective-permute-done.12.refs_3_ = f32[3,128,256]{2,1,0:T(8,128)S(1)} collective-permute-done((f32[3,128,256]{2,1,0:T(8,128)S(1)}, f32[3,128,256]{2,1,0:T(8,128)S(1)}, u32[]{:S(2)}, u32[]{:S(2)}) %collective-permute-start.12) | collective-permute-done | bytes 393248 | tf_op jit(solution)/shard_map/ppermute | solution.py:139
  94.3 3.2 %collective-permute-done.13.refs_2_ = f32[6,128,256]{2,1,0:T(8,128)S(1)} collective-permute-done((f32[6,128,256]{2,1,0:T(8,128)S(1)}, f32[6,128,256]{2,1,0:T(8,128)S(1)}, u32[]{:S(2)}, u32[]{:S(2)}) %collective-permute-start.13) | collective-permute-done | bytes 786464 | tf_op jit(solution)/shard_map/ppermute | solution.py:135
  103.2 12.1 %collective-permute-done.21.refs_1_ = f32[7,3,512]{2,1,0:T(4,128)S(1)} collective-permute-done((f32[7,3,512]{2,1,0:T(4,128)S(1)}, f32[7,3,512]{2,1,0:T(4,128)S(1)}, u32[]{:S(2)}, u32[]{:S(2)}) %collective-permute-start.21) | collective-permute-done | bytes 43040 | tf_op jit(solution)/shard_map/ppermute | solution.py:139
  121.3 8.6 %collective-permute-done.15.refs_4_.refs_2_.refs_6_ = f32[1,256,512]{2,1,0:T(8,128)S(1)} collective-permute-done((f32[1,256,512]{2,1,0:T(8,128)S(1)}, f32[1,256,512]{2,1,0:T(8,128)S(1)}, u32[]{:S(2)}, u32[]{:S(2)}) %collective-permute-start.15) | collective-permute-done | bytes 524320 | tf_op jit(solution)/shard_map/ppermute | solution.py:135
  131.4 2.8 %add.18 = (f32[256,1024]{1,0:T(8,128)S(1)}, f32[256,1024]{1,0:T(8,128)}) custom-call(f32[2,256,1024]{2,1,0:T(8,128)S(1)} %copy-done.5, f32[2,256,1024]{2,1,0:T(8,128)} %collective-permute-done.5.refs_5_.refs_1_, f32[2,256,512]{2,1,0:T(8,128)S(1)} %side_payload.2.refs_2_, f32[9,128,256]{2,1,0:T(8,128)S(1)} %collective-permute-done.14.refs_3_.refs_4_, ...), custom_call_target="tpu_custom_call" | custom-call | flops 128 | bytes 128 | tf_op jit(solution)/shard_map/add/pallas_call | solution.py:111
  134.2 2.5 %collective-permute-done.18.refs_6_.refs_3_ = f32[6,128,256]{2,1,0:T(8,128)} collective-permute-done((f32[6,128,256]{2,1,0:T(8,128)S(1)}, f32[6,128,256]{2,1,0:T(8,128)}, u32[]{:S(2)}, u32[]{:S(2)}) %collective-permute-start.18) | collective-permute-done | bytes 786464 | tf_op jit(solution)/shard_map/ppermute | solution.py:139
  139.0 2.7 %collective-permute-start.27 = (f32[7,3,512]{2,1,0:T(4,128)S(1)}, f32[7,3,512]{2,1,0:T(4,128)S(1)}, u32[]{:S(2)}, u32[]{:S(2)}) collective-permute-start(f32[7,3,512]{2,1,0:T(4,128)S(1)} %get-tuple-element.27), channel_id=1, source_target_pairs={{0,8},{4,12},{8,0},{12,4},{16,24},{20,28},{24,16},{28,20},{1,9},{5... | collective-permute-start | bytes 129032 | tf_op jit(solution)/shard_map/ppermute | solution.py:139
  147.5 8.4 %collective-permute-done.29.refs_5_.refs_4_ = f32[2,256,512]{2,1,0:T(8,128)S(1)} collective-permute-done((f32[2,256,512]{2,1,0:T(8,128)S(1)}, f32[2,256,512]{2,1,0:T(8,128)S(1)}, u32[]{:S(2)}, u32[]{:S(2)}) %collective-permute-start.29) | collective-permute-done | bytes 1048608 | tf_op jit(solution)/shard_map/ppermute | solution.py:139
  158.1 6.8 %weight_part.2.refs_2_.refs_8_ = f32[1536,512]{1,0:T(8,128)} custom-call(s32[3]{0:T(128)} %copy-done.26, bf16[3,512,1024]{2,1,0:T(8,128)(2,1)} %copy-done.1, bf16[3,256,512]{2,1,0:T(8,128)(2,1)} %copy-done.9, f32[2,256,512]{2,1,0:T(8,128)} %copy-done.12, f32[1,256,512]{2,1,0:T(8,128)} %copy-done.22, f32[2,256,512]{2,1,0:T(8,128)} %collective-permute-done.3.refs_5_, ...), custom_call_target="tpu_custom_call" | custom-call | flops 128 | bytes 128 | tf_op jit(solution)/shard_map/weight_part/pallas_call | solution.py:111
  164.9 1.9 copy-done
  166.8 2.6 %collective-permute-start.31 = (f32[7,3,512]{2,1,0:T(4,128)S(1)}, f32[7,3,512]{2,1,0:T(4,128)S(1)}, u32[]{:S(2)}, u32[]{:S(2)}) collective-permute-start(f32[7,3,512]{2,1,0:T(4,128)S(1)} %get-tuple-element.29), channel_id=1, source_target_pairs={{0,16},{4,20},{8,24},{12,28},{16,0},{20,4},{24,8},{28,12},{1,17},{... | collective-permute-start | bytes 129032 | tf_op jit(solution)/shard_map/ppermute | solution.py:139
  169.5 2.6 %arrange_tokens.3.refs_1_ = bf16[3,512,1024]{2,1,0:T(8,128)(2,1)S(1)} custom-call(s32[3]{0:T(128)S(1)} %copy-done.27, f32[6,128,256]{2,1,0:T(8,128)S(1)} %own_blocks.4.refs_2_.refs_1_, f32[6,128,256]{2,1,0:T(8,128)S(1)} %copy-done.21, f32[6,128,256]{2,1,0:T(8,128)} %collective-permute-done.18.refs_6_.refs_3_, ...), custom_call_target="tpu_custom_call" | custom-call | flops 128 | bytes 128 | tf_op jit(solution)/shard_map/arrange_tokens/pallas_call | solution.py:111
  175.5 8.1 %weight_part.3.refs_2_ = f32[1536,512]{1,0:T(8,128)} custom-call(s32[3]{0:T(128)} %copy-done.26, bf16[3,512,1024]{2,1,0:T(8,128)(2,1)} %copy-done.11, f32[2,256,512]{2,1,0:T(8,128)} %collective-permute-done.6.refs_1_.refs_2_, f32[1,256,512]{2,1,0:T(8,128)} %copy-done.23, f32[2,256,512]{2,1,0:T(8,128)} %copy-done.15, f32[2,256,512]{2,1,0:T(8,128)} %copy-done.13, ...), custom_call_target="tpu_custom_call" | custom-call | flops 128 | bytes 128 | tf_op jit(solution)/shard_map/weight_part/pallas_call | solution.py:111
  185.5 2.1 %add_rounded.1.refs_2_ = bf16[256,1024]{1,0:T(8,128)(2,1)} custom-call(f32[256,1024]{1,0:T(8,128)S(1)} %copy-done.19, f32[256,1024]{1,0:T(8,128)} %collective-permute-done.16.refs_1_, f32[1536,512]{1,0:T(8,128)S(1)} %copy-done.10), custom_call_target="tpu_custom_call" | custom-call | flops 128 | bytes 128 | tf_op jit(solution)/shard_map/add_rounded/pallas_call | solution.py:111
  (129 shorter events, 58.6 us)
Async XLA Ops:
  4.1 26.9 %collective-permute-start.1 = (f32[8,128,256]{2,1,0:T(8,128)}, f32[8,128,256]{2,1,0:T(8,128)}, u32[]{:S(2)}, u32[]{:S(2)}) collective-permute-start(f32[8,128,256]{2,1,0:T(8,128)} %turn_tokens.1.refs_5_.refs_1_), channel_id=1, source_target_pairs={{0,8},{4,12},{8,0},{12,4},{16,24},{20,28},{24,16},{28,20},{1,9},{5... | collective-permute-start | bytes 3145736 | tf_op jit(solution)/shard_map/ppermute | solution.py:135
  7.1 35.1 %collective-permute-start = (f32[8,128,256]{2,1,0:T(8,128)}, f32[8,128,256]{2,1,0:T(8,128)}, u32[]{:S(2)}, u32[]{:S(2)}) collective-permute-start(f32[8,128,256]{2,1,0:T(8,128)} %turn_tokens.1.refs_5_.refs_1_), channel_id=1, source_target_pairs={{8,16},{12,20},{16,8},{20,12},{9,17},{13,21},{17,9},{21,13},{10,18... | collective-permute-start | bytes 3145736 | tf_op jit(solution)/shard_map/ppermute | solution.py:135
  23.5 28.8 %collective-permute-start.2 = (f32[2,256,512]{2,1,0:T(8,128)}, f32[2,256,512]{2,1,0:T(8,128)S(1)}, u32[]{:S(2)}, u32[]{:S(2)}) collective-permute-start(f32[2,256,512]{2,1,0:T(8,128)} %get-tuple-element.18), channel_id=1, source_target_pairs={{0,8},{4,12},{24,16},{28,20},{1,9},{5,13},{25,17},{29,21},{2,10},{... | collective-permute-start | bytes 3145736 | tf_op jit(solution)/shard_map/ppermute | solution.py:135
  28.9 25.1 %collective-permute-start.3 = (f32[2,256,512]{2,1,0:T(8,128)}, f32[2,256,512]{2,1,0:T(8,128)}, u32[]{:S(2)}, u32[]{:S(2)}) collective-permute-start(f32[2,256,512]{2,1,0:T(8,128)} %get-tuple-element.18), channel_id=1, source_target_pairs={{0,4},{4,0},{8,12},{12,8},{16,20},{20,16},{24,28},{28,24},{1,5},{5... | collective-permute-start | bytes 3145736 | tf_op jit(solution)/shard_map/ppermute | solution.py:139
  31.0 27.3 %collective-permute-start.4 = (f32[8,128,256]{2,1,0:T(8,128)}, f32[8,128,256]{2,1,0:T(8,128)S(1)}, u32[]{:S(2)}, u32[]{:S(2)}) collective-permute-start(f32[8,128,256]{2,1,0:T(8,128)} %collective-permute-done.1.refs_2_.refs_1_), channel_id=1, source_target_pairs={{8,16},{12,20},{16,8},{20,12},{9,17},{13,21},{17,9},{21,13},{10,18... | collective-permute-start | bytes 3145736 | tf_op jit(solution)/shard_map/ppermute | solution.py:135
  42.2 55.2 %collective-permute-start.5 = (f32[2,256,1024]{2,1,0:T(8,128)}, f32[2,256,1024]{2,1,0:T(8,128)}, u32[]{:S(2)}, u32[]{:S(2)}) collective-permute-start(f32[2,256,1024]{2,1,0:T(8,128)} %token_part.2.refs_2_), channel_id=1, source_target_pairs={{0,1},{1,0},{2,3},{3,2},{4,5},{5,4},{6,7},{7,6},{8,9},{9,8},{10,11... | collective-permute-start | bytes 6291464 | tf_op jit(solution)/shard_map/ppermute | solution.py:139
  44.5 26.8 %collective-permute-start.8 = (f32[6,128,256]{2,1,0:T(8,128)}, f32[6,128,256]{2,1,0:T(8,128)}, u32[]{:S(2)}, u32[]{:S(2)}) collective-permute-start(f32[6,128,256]{2,1,0:T(8,128)} %part_of.4.refs_3_), channel_id=1, source_target_pairs={{8,0},{12,4},{16,24},{20,28},{9,1},{13,5},{17,25},{21,29},{10,2},{... | collective-permute-start | bytes 2359304 | tf_op jit(solution)/shard_map/ppermute | solution.py:135
  52.3 31.7 %collective-permute-start.6 = (f32[2,256,512]{2,1,0:T(8,128)}, f32[2,256,512]{2,1,0:T(8,128)}, u32[]{:S(2)}, u32[]{:S(2)}) collective-permute-start(f32[2,256,512]{2,1,0:T(8,128)} %get-tuple-element.19), channel_id=1, source_target_pairs={{8,16},{12,20},{16,8},{20,12},{9,17},{13,21},{17,9},{21,13},{10,18... | collective-permute-start | bytes 3145736 | tf_op jit(solution)/shard_map/ppermute | solution.py:135
  54.0 26.8 %collective-permute-start.7 = (f32[1,256,512]{2,1,0:T(8,128)}, f32[1,256,512]{2,1,0:T(8,128)S(1)}, u32[]{:S(2)}, u32[]{:S(2)}) collective-permute-start(f32[1,256,512]{2,1,0:T(8,128)} %get-tuple-element.20), channel_id=1, source_target_pairs={{0,8},{4,12},{8,0},{12,4},{16,24},{20,28},{24,16},{28,20},{1,9},{5... | collective-permute-start | bytes 1572872 | tf_op jit(solution)/shard_map/ppermute | solution.py:135
  58.3 26.5 %collective-permute-start.9 = (f32[6,128,256]{2,1,0:T(8,128)}, f32[6,128,256]{2,1,0:T(8,128)}, u32[]{:S(2)}, u32[]{:S(2)}) collective-permute-start(f32[6,128,256]{2,1,0:T(8,128)} %other_blocks.3.refs_3_), channel_id=1, source_target_pairs={{0,4},{4,0},{8,12},{12,8},{16,20},{20,16},{24,28},{28,24},{1,5},{5... | collective-permute-start | bytes 2359304 | tf_op jit(solution)/shard_map/ppermute | solution.py:139
  71.2 26.2 %collective-permute-start.13 = (f32[6,128,256]{2,1,0:T(8,128)S(1)}, f32[6,128,256]{2,1,0:T(8,128)S(1)}, u32[]{:S(2)}, u32[]{:S(2)}) collective-permute-start(f32[6,128,256]{2,1,0:T(8,128)S(1)} %part_of.5.refs_3_), channel_id=1, source_target_pairs={{8,0},{12,4},{16,24},{20,28},{9,1},{13,5},{17,25},{21,29},{10,2},{... | collective-permute-start | bytes 2359304 | tf_op jit(solution)/shard_map/ppermute | solution.py:135
  84.8 31.9 %collective-permute-start.23 = (f32[2,256,512]{2,1,0:T(8,128)S(1)}, f32[2,256,512]{2,1,0:T(8,128)S(1)}, u32[]{:S(2)}, u32[]{:S(2)}) collective-permute-start(f32[2,256,512]{2,1,0:T(8,128)S(1)} %get-tuple-element.25), channel_id=1, source_target_pairs={{0,4},{4,0},{8,12},{12,8},{16,20},{20,16},{24,28},{28,24},{1,5},{5... | collective-permute-start | bytes 3145736 | tf_op jit(solution)/shard_map/ppermute | solution.py:139
  92.8 25.5 %collective-permute-start.14 = (f32[9,128,256]{2,1,0:T(8,128)S(1)}, f32[9,128,256]{2,1,0:T(8,128)S(1)}, u32[]{:S(2)}, u32[]{:S(2)}) collective-permute-start(f32[9,128,256]{2,1,0:T(8,128)S(1)} %own_blocks.3.refs_3_.refs_2_), channel_id=1, source_target_pairs={{0,2},{1,3},{2,0},{3,1},{4,6},{5,7},{6,4},{7,5},{8,10},{9,11},{10,... | collective-permute-start | bytes 3538952 | tf_op jit(solution)/shard_map/ppermute | solution.py:139
  97.5 20.9 %collective-permute-start.22 = (f32[9,128,256]{2,1,0:T(8,128)S(1)}, f32[9,128,256]{2,1,0:T(8,128)S(1)}, u32[]{:S(2)}, u32[]{:S(2)}) collective-permute-start(f32[9,128,256]{2,1,0:T(8,128)S(1)} %own_blocks.3.refs_3_.refs_2_), channel_id=1, source_target_pairs={{0,1},{1,0},{2,3},{3,2},{4,5},{5,4},{6,7},{7,6},{8,9},{9,8},{10,11... | collective-permute-start | bytes 3538952 | tf_op jit(solution)/shard_map/ppermute | solution.py:139
  97.5 19.1 %collective-permute-start.10 = (f32[1,256,512]{2,1,0:T(8,128)S(1)}, f32[1,256,512]{2,1,0:T(8,128)S(1)}, u32[]{:S(2)}, u32[]{:S(2)}) collective-permute-start(f32[1,256,512]{2,1,0:T(8,128)S(1)} %part_of.6.refs_3_), channel_id=1, source_target_pairs={{8,0},{12,4},{16,24},{20,28},{9,1},{13,5},{17,25},{21,29},{10,2},{... | collective-permute-start | bytes 1572872 | tf_op jit(solution)/shard_map/ppermute | solution.py:135
  116.6 17.6 %collective-permute-start.17 = (f32[6,128,256]{2,1,0:T(8,128)S(1)}, f32[6,128,256]{2,1,0:T(8,128)S(1)}, u32[]{:S(2)}, u32[]{:S(2)}) collective-permute-start(f32[6,128,256]{2,1,0:T(8,128)S(1)} %own_blocks.4.refs_2_.refs_1_), channel_id=1, source_target_pairs={{0,1},{1,0},{2,3},{3,2},{4,5},{5,4},{6,7},{7,6},{8,9},{9,8},{10,11... | collective-permute-start | bytes 2359304 | tf_op jit(solution)/shard_map/ppermute | solution.py:139
  116.7 20.0 %collective-permute-start.18 = (f32[6,128,256]{2,1,0:T(8,128)S(1)}, f32[6,128,256]{2,1,0:T(8,128)}, u32[]{:S(2)}, u32[]{:S(2)}) collective-permute-start(f32[6,128,256]{2,1,0:T(8,128)S(1)} %own_blocks.4.refs_2_.refs_1_), channel_id=1, source_target_pairs={{0,2},{1,3},{2,0},{3,1},{4,6},{5,7},{6,4},{7,5},{8,10},{9,11},{10,... | collective-permute-start | bytes 2359304 | tf_op jit(solution)/shard_map/ppermute | solution.py:139
  118.3 23.3 %collective-permute-start.28 = (f32[9,128,256]{2,1,0:T(8,128)S(1)}, f32[9,128,256]{2,1,0:T(8,128)S(1)}, u32[]{:S(2)}, u32[]{:S(2)}) collective-permute-start(f32[9,128,256]{2,1,0:T(8,128)S(1)} %collective-permute-done.14.refs_3_.refs_4_), channel_id=1, source_target_pairs={{0,1},{1,0},{2,3},{3,2},{4,5},{5,4},{6,7},{7,6},{8,9},{9,8},{10,11... | collective-permute-start | bytes 3538952 | tf_op jit(solution)/shard_map/ppermute | solution.py:139
  129.9 26.1 %collective-permute-start.29 = (f32[2,256,512]{2,1,0:T(8,128)S(1)}, f32[2,256,512]{2,1,0:T(8,128)S(1)}, u32[]{:S(2)}, u32[]{:S(2)}) collective-permute-start(f32[2,256,512]{2,1,0:T(8,128)S(1)} %side_payload.2.refs_2_), channel_id=1, source_target_pairs={{0,4},{4,0},{8,12},{12,8},{16,20},{20,16},{24,28},{28,24},{1,5},{5... | collective-permute-start | bytes 3145736 | tf_op jit(solution)/shard_map/ppermute | solution.py:139
  137.4 20.6 %collective-permute-start.25 = (f32[6,128,256]{2,1,0:T(8,128)S(1)}, f32[6,128,256]{2,1,0:T(8,128)}, u32[]{:S(2)}, u32[]{:S(2)}) collective-permute-start(f32[6,128,256]{2,1,0:T(8,128)S(1)} %own_blocks.5.refs_6_.refs_5_), channel_id=1, source_target_pairs={{0,2},{1,3},{2,0},{3,1},{4,6},{5,7},{6,4},{7,5},{8,10},{9,11},{10,... | collective-permute-start | bytes 2359304 | tf_op jit(solution)/shard_map/ppermute | solution.py:139
  145.4 30.1 %collective-permute-start.30 = (f32[2,256,512]{2,1,0:T(8,128)}, f32[2,256,512]{2,1,0:T(8,128)}, u32[]{:S(2)}, u32[]{:S(2)}) collective-permute-start(f32[2,256,512]{2,1,0:T(8,128)} %side_payload.3.refs_7_), channel_id=1, source_target_pairs={{0,4},{4,0},{8,12},{12,8},{16,20},{20,16},{24,28},{28,24},{1,5},{5... | collective-permute-start | bytes 3145736 | tf_op jit(solution)/shard_map/ppermute | solution.py:139
  147.0 36.7 %collective-permute-start.16 = (f32[256,1024]{1,0:T(8,128)}, f32[256,1024]{1,0:T(8,128)}, u32[]{:S(2)}, u32[]{:S(2)}) collective-permute-start(f32[256,1024]{1,0:T(8,128)} %get-tuple-element.23), channel_id=1, source_target_pairs={{0,2},{1,3},{2,0},{3,1},{4,6},{5,7},{6,4},{7,5},{8,10},{9,11},{10,... | collective-permute-start | bytes 3145736 | tf_op jit(solution)/shard_map/ppermute | solution.py:139
  147.5 17.4 %collective-permute-start.24 = (f32[6,128,256]{2,1,0:T(8,128)S(1)}, f32[6,128,256]{2,1,0:T(8,128)}, u32[]{:S(2)}, u32[]{:S(2)}) collective-permute-start(f32[6,128,256]{2,1,0:T(8,128)S(1)} %own_blocks.5.refs_6_.refs_5_), channel_id=1, source_target_pairs={{0,1},{1,0},{2,3},{3,2},{4,5},{5,4},{6,7},{7,6},{8,9},{9,8},{10,11... | collective-permute-start | bytes 2359304 | tf_op jit(solution)/shard_map/ppermute | solution.py:139
  166.8 20.9 %collective-permute-start.31 = (f32[7,3,512]{2,1,0:T(4,128)S(1)}, f32[7,3,512]{2,1,0:T(4,128)S(1)}, u32[]{:S(2)}, u32[]{:S(2)}) collective-permute-start(f32[7,3,512]{2,1,0:T(4,128)S(1)} %get-tuple-element.29), channel_id=1, source_target_pairs={{0,16},{4,20},{8,24},{12,28},{16,0},{20,4},{24,8},{28,12},{1,17},{... | collective-permute-start | bytes 129032 | tf_op jit(solution)/shard_map/ppermute | solution.py:139
  (37 other events, 493.6 us)

commit v14 on v10

--- a/solution.py
+++ b/solution.py
@@ -148,19 +148,18 @@
     slab = BLOCK // 4
 
     def body(place, tokens, piece):
-        start = pl.multiple_of(place[2] * slab, slab)
-        for b in range(BLOCKS):
-            piece[b] = tokens[:, pl.ds(pl.multiple_of(BLOCK * b + start, slab), slab)].astype(
-                jnp.float32
-            ).T
-
-    return order.call(
-        body,
-        (place, tokens),
-        [SMEM, VMEM],
+        piece[...] = tokens[...].astype(jnp.float32).T
+
+    return order.call(
+        body,
+        (tokens,),
+        [pl.BlockSpec((rows, slab), lambda b, place: (0, 4 * b + place[2]))],
+        scalars=(place,),
         out_shape=jax.ShapeDtypeStruct((BLOCKS, slab, rows), jnp.float32),
-        out_specs=VMEM,
+        grid=(BLOCKS,),
+        out_specs=pl.BlockSpec((None, slab, rows), lambda b, place: (b, 0, 0)),
         name="turn_tokens",
+        vmem=62,
     )
 
 

time: 190 us -> 194 us (1.021)
  Pallas kernels: 75.2 us -> 78.6 us
  waiting for transfers between devices: 54.6 us -> 57 us
  local copies, waits for them, and re-layouts: 14.5 us -> 12.5 us
    pallas_call x26, Pallas kernels: 75.2 us -> 78.6 us  [call(): pl.pallas_call(short, out_shape=out_shape, grid_spec=pltpu.PrefetchScalar...]
    ppermute x21, waiting for transfers between devices: 31.7 us -> 34 us  [flipped(): lax.ppermute(array, axis, [(r, r ^ flip) for r in range(lax.axis_size(axi...]
    unnamed x60 -> x56, local copies, waits for them, and re-layouts: 14.5 us -> 12.5 us
  transfers between devices with their start and end apart: 32 -> 32, of which waited for: 12 -> 12; matrix products, arithmetic and copies ran while one was open for 0% -> 0% of each run, Pallas kernels for 39% -> 37%
where the time goes in v14:
time: 194 us; the launch traced here: 193 us
  Pallas kernels  78.6 us (41%)
  waiting for transfers between devices  57 us (29%)
  starting transfers between devices  42.7 us (22%)
  local copies, waits for them, and re-layouts  12.5 us (6%)
    pallas_call x26, Pallas kernels, call(): pl.pallas_call(short, out_shape=out_shape, grid_spec=pltpu.PrefetchScalar...  78.6 us
    ppermute x21, waiting for transfers between devices, flipped(): lax.ppermute(array, axis, [(r, r ^ flip) for r in range(lax.axis_size(axi...  34 us
    ppermute x11, waiting for transfers between devices, lines(): return lax.ppermute(array, 'rep', perm)  23 us
    ppermute x21, starting transfers between devices, flipped(): lax.ppermute(array, axis, [(r, r ^ flip) for r in range(lax.axis_size(axi...  22.1 us
    ppermute x11, starting transfers between devices, lines(): return lax.ppermute(array, 'rep', perm)  20.7 us
    unnamed x56, local copies, waits for them, and re-layouts  12.5 us
  transfers between devices with their start and end apart: 32, of which 12 were waited for; matrix products, arithmetic and copies ran while one was open for 0% of the time, Pallas kernels for 37%

profile of v14, /device:TPU:0, one launch (start us, length us, event | category | flops | bytes accessed | tf_op | source)
XLA Modules:
  0.0 192.6 jit_solution(9707823901926537059)
XLA Ops:
  1.3 6.0 %turn_tokens.1.refs_5_.refs_1_ = f32[8,128,256]{2,1,0:T(8,128)} custom-call(s32[3]{0:T(128)} %pad_add_fusion.1.refs_0_, bf16[256,4096]{1,0:T(8,128)(2,1)} %refs_1_.5), custom_call_target="tpu_custom_call" | custom-call | flops 128 | bytes 128 | tf_op jit(solution)/shard_map/turn_tokens/pallas_call | solution.py:111
  7.3 3.0 %collective-permute-start.1 = (f32[8,128,256]{2,1,0:T(8,128)}, f32[8,128,256]{2,1,0:T(8,128)}, u32[]{:S(2)}, u32[]{:S(2)}) collective-permute-start(f32[8,128,256]{2,1,0:T(8,128)} %turn_tokens.1.refs_5_.refs_1_), channel_id=1, source_target_pairs={{0,8},{4,12},{8,0},{12,4},{16,24},{20,28},{24,16},{28,20},{1,9},{5... | collective-permute-start | bytes 3145736 | tf_op jit(solution)/shard_map/ppermute | solution.py:135
  12.0 17.2 %gate.1 = (bf16[3,256,512]{2,1,0:T(8,128)(2,1)S(1)}, f32[7,3,512]{2,1,0:T(4,128)S(1)}, f32[1,256,512]{2,1,0:T(8,128)}, f32[2,256,512]{2,1,0:T(8,128)}, f32[2,256,512]{2,1,0:T(8,128)}) custom-call(s32[3]{0:T(128)S(1)} %copy-done.24, bf16[256,4096]{1,0:T(8,128)(2,1)} %refs_1_.5, bf16[3,4096,512]{2,1,0:T(8,128)(2,1)} %refs_2_.5, f32[7,3,512]{2,1,0:T(4,128)S(1)} %copy.7.refs_3_, ...), custom_call_target="tpu_custom_call" | custom-call | flops 128 | bytes 128 | tf_op jit(solution)/shard_map/gate/pallas_call | solution.py:111
  29.2 5.4 %collective-permute-start.2 = (f32[2,256,512]{2,1,0:T(8,128)}, f32[2,256,512]{2,1,0:T(8,128)S(1)}, u32[]{:S(2)}, u32[]{:S(2)}) collective-permute-start(f32[2,256,512]{2,1,0:T(8,128)} %get-tuple-element.18), channel_id=1, source_target_pairs={{0,8},{4,12},{24,16},{28,20},{1,9},{5,13},{25,17},{29,21},{2,10},{... | collective-permute-start | bytes 3145736 | tf_op jit(solution)/shard_map/ppermute | solution.py:135
  38.2 2.2 %other_blocks.3.refs_3_ = f32[6,128,256]{2,1,0:T(8,128)} custom-call(s32[3]{0:T(128)S(1)} %copy-done.24, f32[8,128,256]{2,1,0:T(8,128)S(1)} %copy-done.13, f32[8,128,256]{2,1,0:T(8,128)} %collective-permute-done.1.refs_2_.refs_1_, bf16[3,256,512]{2,1,0:T(8,128)(2,1)S(1)} %get-tuple-element.17.refs_3_.refs_1_.refs_2_), custom_call_target="tpu_custom_call" | custom-call | flops 128 | bytes 128 | tf_op jit(solution)/shard_map/other_blocks/pallas_call | solution.py:111
  40.4 7.9 %token_part.2.refs_2_ = f32[2,256,1024]{2,1,0:T(8,128)} custom-call(s32[2]{0:T(128)S(1)} %pad_add_fusion.2.refs_0_, bf16[3,256,512]{2,1,0:T(8,128)(2,1)S(1)} %get-tuple-element.17.refs_3_.refs_1_.refs_2_, bf16[3,4096,512]{2,1,0:T(8,128)(2,1)} %refs_2_.5, f32[6,128,256]{2,1,0:T(8,128)} %other_blocks.3.refs_3_), custom_call_target="tpu_custom_call" | custom-call | flops 128 | bytes 128 | tf_op jit(solution)/shard_map/token_part/pallas_call | solution.py:111
  48.3 2.2 %part_of.4.refs_3_ = f32[6,128,256]{2,1,0:T(8,128)} custom-call(s32[3]{0:T(128)S(1)} %copy-done.24, f32[8,128,256]{2,1,0:T(8,128)} %collective-permute-done.refs_1_, f32[2,256,1024]{2,1,0:T(8,128)} %token_part.2.refs_2_), custom_call_target="tpu_custom_call" | custom-call | flops 128 | bytes 128 | tf_op jit(solution)/shard_map/part_of/pallas_call | solution.py:111
  51.8 4.9 %collective-permute-done.2.refs_4_.refs_2_.refs_3_ = f32[2,256,512]{2,1,0:T(8,128)S(1)} collective-permute-done((f32[2,256,512]{2,1,0:T(8,128)}, f32[2,256,512]{2,1,0:T(8,128)S(1)}, u32[]{:S(2)}, u32[]{:S(2)}) %collective-permute-start.2) | collective-permute-done | bytes 1048608 | tf_op jit(solution)/shard_map/ppermute | solution.py:135
  59.1 2.4 %collective-permute-start.7 = (f32[1,256,512]{2,1,0:T(8,128)}, f32[1,256,512]{2,1,0:T(8,128)S(1)}, u32[]{:S(2)}, u32[]{:S(2)}) collective-permute-start(f32[1,256,512]{2,1,0:T(8,128)} %get-tuple-element.20), channel_id=1, source_target_pairs={{0,8},{4,12},{8,0},{12,4},{16,24},{20,28},{24,16},{28,20},{1,9},{5... | collective-permute-start | bytes 1572872 | tf_op jit(solution)/shard_map/ppermute | solution.py:135
  63.1 7.9 %token_part.3.refs_2_.refs_0_ = f32[2,256,1024]{2,1,0:T(8,128)} custom-call(s32[2]{0:T(128)S(1)} %pad_add_fusion.refs_0_, bf16[3,256,512]{2,1,0:T(8,128)(2,1)S(1)} %get-tuple-element.17.refs_3_.refs_1_.refs_2_, bf16[3,4096,512]{2,1,0:T(8,128)(2,1)} %refs_2_.5, f32[6,128,256]{2,1,0:T(8,128)} %part_of.4.refs_3_, ...), custom_call_target="tpu_custom_call" | custom-call | flops 128 | bytes 128 | tf_op jit(solution)/shard_map/token_part/pallas_call | solution.py:111
  77.2 6.9 %collective-permute-done.7.refs_1_.refs_4_ = f32[1,256,512]{2,1,0:T(8,128)S(1)} collective-permute-done((f32[1,256,512]{2,1,0:T(8,128)}, f32[1,256,512]{2,1,0:T(8,128)S(1)}, u32[]{:S(2)}, u32[]{:S(2)}) %collective-permute-start.7) | collective-permute-done | bytes 524320 | tf_op jit(solution)/shard_map/ppermute | solution.py:135
  91.6 4.6 %collective-permute-done.12.refs_3_ = f32[3,128,256]{2,1,0:T(8,128)S(1)} collective-permute-done((f32[3,128,256]{2,1,0:T(8,128)S(1)}, f32[3,128,256]{2,1,0:T(8,128)S(1)}, u32[]{:S(2)}, u32[]{:S(2)}) %collective-permute-start.12) | collective-permute-done | bytes 393248 | tf_op jit(solution)/shard_map/ppermute | solution.py:139
  97.7 2.9 %collective-permute-done.13.refs_2_ = f32[6,128,256]{2,1,0:T(8,128)S(1)} collective-permute-done((f32[6,128,256]{2,1,0:T(8,128)S(1)}, f32[6,128,256]{2,1,0:T(8,128)S(1)}, u32[]{:S(2)}, u32[]{:S(2)}) %collective-permute-start.13) | collective-permute-done | bytes 786464 | tf_op jit(solution)/shard_map/ppermute | solution.py:135
  106.1 12.2 %collective-permute-done.21.refs_1_ = f32[7,3,512]{2,1,0:T(4,128)S(1)} collective-permute-done((f32[7,3,512]{2,1,0:T(4,128)S(1)}, f32[7,3,512]{2,1,0:T(4,128)S(1)}, u32[]{:S(2)}, u32[]{:S(2)}) %collective-permute-start.21) | collective-permute-done | bytes 43040 | tf_op jit(solution)/shard_map/ppermute | solution.py:139
  124.2 8.2 %collective-permute-done.15.refs_4_.refs_2_.refs_6_ = f32[1,256,512]{2,1,0:T(8,128)S(1)} collective-permute-done((f32[1,256,512]{2,1,0:T(8,128)S(1)}, f32[1,256,512]{2,1,0:T(8,128)S(1)}, u32[]{:S(2)}, u32[]{:S(2)}) %collective-permute-start.15) | collective-permute-done | bytes 524320 | tf_op jit(solution)/shard_map/ppermute | solution.py:135
  134.3 2.8 %add.18 = (f32[256,1024]{1,0:T(8,128)S(1)}, f32[256,1024]{1,0:T(8,128)}) custom-call(f32[2,256,1024]{2,1,0:T(8,128)S(1)} %copy-done.4, f32[2,256,1024]{2,1,0:T(8,128)} %collective-permute-done.5.refs_5_.refs_1_, f32[2,256,512]{2,1,0:T(8,128)S(1)} %side_payload.2.refs_2_, f32[9,128,256]{2,1,0:T(8,128)S(1)} %collective-permute-done.14.refs_3_.refs_4_, ...), custom_call_target="tpu_custom_call" | custom-call | flops 128 | bytes 128 | tf_op jit(solution)/shard_map/add/pallas_call | solution.py:111
  137.1 2.6 %collective-permute-done.18.refs_6_.refs_3_ = f32[6,128,256]{2,1,0:T(8,128)} collective-permute-done((f32[6,128,256]{2,1,0:T(8,128)S(1)}, f32[6,128,256]{2,1,0:T(8,128)}, u32[]{:S(2)}, u32[]{:S(2)}) %collective-permute-start.18) | collective-permute-done | bytes 786464 | tf_op jit(solution)/shard_map/ppermute | solution.py:139
  141.9 2.7 %collective-permute-start.27 = (f32[7,3,512]{2,1,0:T(4,128)S(1)}, f32[7,3,512]{2,1,0:T(4,128)S(1)}, u32[]{:S(2)}, u32[]{:S(2)}) collective-permute-start(f32[7,3,512]{2,1,0:T(4,128)S(1)} %get-tuple-element.27), channel_id=1, source_target_pairs={{0,8},{4,12},{8,0},{12,4},{16,24},{20,28},{24,16},{28,20},{1,9},{5... | collective-permute-start | bytes 129032 | tf_op jit(solution)/shard_map/ppermute | solution.py:139
  149.6 8.8 %collective-permute-done.29.refs_5_.refs_4_ = f32[2,256,512]{2,1,0:T(8,128)S(1)} collective-permute-done((f32[2,256,512]{2,1,0:T(8,128)S(1)}, f32[2,256,512]{2,1,0:T(8,128)S(1)}, u32[]{:S(2)}, u32[]{:S(2)}) %collective-permute-start.29) | collective-permute-done | bytes 1048608 | tf_op jit(solution)/shard_map/ppermute | solution.py:139
  158.5 2.4 %collective-permute-done.25.refs_4_.refs_7_ = f32[6,128,256]{2,1,0:T(8,128)S(1)} collective-permute-done((f32[6,128,256]{2,1,0:T(8,128)S(1)}, f32[6,128,256]{2,1,0:T(8,128)S(1)}, u32[]{:S(2)}, u32[]{:S(2)}) %collective-permute-start.25) | collective-permute-done | bytes 786464 | tf_op jit(solution)/shard_map/ppermute | solution.py:139
  160.9 6.8 %weight_part.2.refs_2_.refs_8_ = f32[1536,512]{1,0:T(8,128)} custom-call(s32[3]{0:T(128)} %pad_add_fusion.1.refs_0_, bf16[3,512,1024]{2,1,0:T(8,128)(2,1)} %copy-done.1, bf16[3,256,512]{2,1,0:T(8,128)(2,1)} %copy-done.8, f32[2,256,512]{2,1,0:T(8,128)} %copy-done.11, f32[1,256,512]{2,1,0:T(8,128)} %copy-done.20, ...), custom_call_target="tpu_custom_call" | custom-call | flops 128 | bytes 128 | tf_op jit(solution)/shard_map/weight_part/pallas_call | solution.py:111
  169.7 2.6 %collective-permute-start.31 = (f32[7,3,512]{2,1,0:T(4,128)S(1)}, f32[7,3,512]{2,1,0:T(4,128)S(1)}, u32[]{:S(2)}, u32[]{:S(2)}) collective-permute-start(f32[7,3,512]{2,1,0:T(4,128)S(1)} %get-tuple-element.29), channel_id=1, source_target_pairs={{0,16},{4,20},{8,24},{12,28},{16,0},{20,4},{24,8},{28,12},{1,17},{... | collective-permute-start | bytes 129032 | tf_op jit(solution)/shard_map/ppermute | solution.py:139
  172.3 2.4 %arrange_tokens.3.refs_1_ = bf16[3,512,1024]{2,1,0:T(8,128)(2,1)S(1)} custom-call(s32[3]{0:T(128)S(1)} %copy-done.25, f32[6,128,256]{2,1,0:T(8,128)S(1)} %own_blocks.4.refs_2_.refs_1_, f32[6,128,256]{2,1,0:T(8,128)S(1)} %copy-done.19, f32[6,128,256]{2,1,0:T(8,128)} %collective-permute-done.18.refs_6_.refs_3_, ...), custom_call_target="tpu_custom_call" | custom-call | flops 128 | bytes 128 | tf_op jit(solution)/shard_map/arrange_tokens/pallas_call | solution.py:111
  178.2 8.1 %weight_part.3.refs_2_ = f32[1536,512]{1,0:T(8,128)} custom-call(s32[3]{0:T(128)} %pad_add_fusion.1.refs_0_, bf16[3,512,1024]{2,1,0:T(8,128)(2,1)} %copy-done.10, f32[2,256,512]{2,1,0:T(8,128)} %collective-permute-done.6.refs_1_.refs_2_, f32[1,256,512]{2,1,0:T(8,128)} %copy-done.21, f32[2,256,512]{2,1,0:T(8,128)} %copy-done.15, f32[2,256,512]{2,1,0:T(8,128)} %copy-done.12, ...), custom_call_target="tpu_custom_call" | custom-call | flops 128 | bytes 128 | tf_op jit(solution)/shard_map/weight_part/pallas_call | solution.py:111
  (125 shorter events, 58.4 us)
Async XLA Ops:
  7.3 28.9 %collective-permute-start.1 = (f32[8,128,256]{2,1,0:T(8,128)}, f32[8,128,256]{2,1,0:T(8,128)}, u32[]{:S(2)}, u32[]{:S(2)}) collective-permute-start(f32[8,128,256]{2,1,0:T(8,128)} %turn_tokens.1.refs_5_.refs_1_), channel_id=1, source_target_pairs={{0,8},{4,12},{8,0},{12,4},{16,24},{20,28},{24,16},{28,20},{1,9},{5... | collective-permute-start | bytes 3145736 | tf_op jit(solution)/shard_map/ppermute | solution.py:135
  10.3 38.0 %collective-permute-start = (f32[8,128,256]{2,1,0:T(8,128)}, f32[8,128,256]{2,1,0:T(8,128)}, u32[]{:S(2)}, u32[]{:S(2)}) collective-permute-start(f32[8,128,256]{2,1,0:T(8,128)} %turn_tokens.1.refs_5_.refs_1_), channel_id=1, source_target_pairs={{8,16},{12,20},{16,8},{20,12},{9,17},{13,21},{17,9},{21,13},{10,18... | collective-permute-start | bytes 3145736 | tf_op jit(solution)/shard_map/ppermute | solution.py:135
  29.2 27.5 %collective-permute-start.2 = (f32[2,256,512]{2,1,0:T(8,128)}, f32[2,256,512]{2,1,0:T(8,128)S(1)}, u32[]{:S(2)}, u32[]{:S(2)}) collective-permute-start(f32[2,256,512]{2,1,0:T(8,128)} %get-tuple-element.18), channel_id=1, source_target_pairs={{0,8},{4,12},{24,16},{28,20},{1,9},{5,13},{25,17},{29,21},{2,10},{... | collective-permute-start | bytes 3145736 | tf_op jit(solution)/shard_map/ppermute | solution.py:135
  34.6 24.4 %collective-permute-start.3 = (f32[2,256,512]{2,1,0:T(8,128)}, f32[2,256,512]{2,1,0:T(8,128)}, u32[]{:S(2)}, u32[]{:S(2)}) collective-permute-start(f32[2,256,512]{2,1,0:T(8,128)} %get-tuple-element.18), channel_id=1, source_target_pairs={{0,4},{4,0},{8,12},{12,8},{16,20},{20,16},{24,28},{28,24},{1,5},{5... | collective-permute-start | bytes 3145736 | tf_op jit(solution)/shard_map/ppermute | solution.py:139
  36.2 25.3 %collective-permute-start.4 = (f32[8,128,256]{2,1,0:T(8,128)}, f32[8,128,256]{2,1,0:T(8,128)S(1)}, u32[]{:S(2)}, u32[]{:S(2)}) collective-permute-start(f32[8,128,256]{2,1,0:T(8,128)} %collective-permute-done.1.refs_2_.refs_1_), channel_id=1, source_target_pairs={{8,16},{12,20},{16,8},{20,12},{9,17},{13,21},{17,9},{21,13},{10,18... | collective-permute-start | bytes 3145736 | tf_op jit(solution)/shard_map/ppermute | solution.py:135
  48.3 52.3 %collective-permute-start.5 = (f32[2,256,1024]{2,1,0:T(8,128)}, f32[2,256,1024]{2,1,0:T(8,128)}, u32[]{:S(2)}, u32[]{:S(2)}) collective-permute-start(f32[2,256,1024]{2,1,0:T(8,128)} %token_part.2.refs_2_), channel_id=1, source_target_pairs={{0,1},{1,0},{2,3},{3,2},{4,5},{5,4},{6,7},{7,6},{8,9},{9,8},{10,11... | collective-permute-start | bytes 6291464 | tf_op jit(solution)/shard_map/ppermute | solution.py:139
  50.5 23.9 %collective-permute-start.8 = (f32[6,128,256]{2,1,0:T(8,128)}, f32[6,128,256]{2,1,0:T(8,128)}, u32[]{:S(2)}, u32[]{:S(2)}) collective-permute-start(f32[6,128,256]{2,1,0:T(8,128)} %part_of.4.refs_3_), channel_id=1, source_target_pairs={{8,0},{12,4},{16,24},{20,28},{9,1},{13,5},{17,25},{21,29},{10,2},{... | collective-permute-start | bytes 2359304 | tf_op jit(solution)/shard_map/ppermute | solution.py:135
  56.7 30.2 %collective-permute-start.6 = (f32[2,256,512]{2,1,0:T(8,128)}, f32[2,256,512]{2,1,0:T(8,128)}, u32[]{:S(2)}, u32[]{:S(2)}) collective-permute-start(f32[2,256,512]{2,1,0:T(8,128)} %get-tuple-element.19), channel_id=1, source_target_pairs={{8,16},{12,20},{16,8},{20,12},{9,17},{13,21},{17,9},{21,13},{10,18... | collective-permute-start | bytes 3145736 | tf_op jit(solution)/shard_map/ppermute | solution.py:135
  59.1 25.1 %collective-permute-start.7 = (f32[1,256,512]{2,1,0:T(8,128)}, f32[1,256,512]{2,1,0:T(8,128)S(1)}, u32[]{:S(2)}, u32[]{:S(2)}) collective-permute-start(f32[1,256,512]{2,1,0:T(8,128)} %get-tuple-element.20), channel_id=1, source_target_pairs={{0,8},{4,12},{8,0},{12,4},{16,24},{20,28},{24,16},{28,20},{1,9},{5... | collective-permute-start | bytes 1572872 | tf_op jit(solution)/shard_map/ppermute | solution.py:135
  61.5 26.2 %collective-permute-start.9 = (f32[6,128,256]{2,1,0:T(8,128)}, f32[6,128,256]{2,1,0:T(8,128)}, u32[]{:S(2)}, u32[]{:S(2)}) collective-permute-start(f32[6,128,256]{2,1,0:T(8,128)} %other_blocks.3.refs_3_), channel_id=1, source_target_pairs={{0,4},{4,0},{8,12},{12,8},{16,20},{20,16},{24,28},{28,24},{1,5},{5... | collective-permute-start | bytes 2359304 | tf_op jit(solution)/shard_map/ppermute | solution.py:139
  74.4 26.2 %collective-permute-start.13 = (f32[6,128,256]{2,1,0:T(8,128)S(1)}, f32[6,128,256]{2,1,0:T(8,128)S(1)}, u32[]{:S(2)}, u32[]{:S(2)}) collective-permute-start(f32[6,128,256]{2,1,0:T(8,128)S(1)} %part_of.5.refs_3_), channel_id=1, source_target_pairs={{8,0},{12,4},{16,24},{20,28},{9,1},{13,5},{17,25},{21,29},{10,2},{... | collective-permute-start | bytes 2359304 | tf_op jit(solution)/shard_map/ppermute | solution.py:135
  87.7 31.9 %collective-permute-start.23 = (f32[2,256,512]{2,1,0:T(8,128)S(1)}, f32[2,256,512]{2,1,0:T(8,128)S(1)}, u32[]{:S(2)}, u32[]{:S(2)}) collective-permute-start(f32[2,256,512]{2,1,0:T(8,128)S(1)} %get-tuple-element.25), channel_id=1, source_target_pairs={{0,4},{4,0},{8,12},{12,8},{16,20},{20,16},{24,28},{28,24},{1,5},{5... | collective-permute-start | bytes 3145736 | tf_op jit(solution)/shard_map/ppermute | solution.py:139
  96.2 25.0 %collective-permute-start.14 = (f32[9,128,256]{2,1,0:T(8,128)S(1)}, f32[9,128,256]{2,1,0:T(8,128)S(1)}, u32[]{:S(2)}, u32[]{:S(2)}) collective-permute-start(f32[9,128,256]{2,1,0:T(8,128)S(1)} %own_blocks.3.refs_3_.refs_2_), channel_id=1, source_target_pairs={{0,2},{1,3},{2,0},{3,1},{4,6},{5,7},{6,4},{7,5},{8,10},{9,11},{10,... | collective-permute-start | bytes 3538952 | tf_op jit(solution)/shard_map/ppermute | solution.py:139
  100.6 20.7 %collective-permute-start.22 = (f32[9,128,256]{2,1,0:T(8,128)S(1)}, f32[9,128,256]{2,1,0:T(8,128)S(1)}, u32[]{:S(2)}, u32[]{:S(2)}) collective-permute-start(f32[9,128,256]{2,1,0:T(8,128)S(1)} %own_blocks.3.refs_3_.refs_2_), channel_id=1, source_target_pairs={{0,1},{1,0},{2,3},{3,2},{4,5},{5,4},{6,7},{7,6},{8,9},{9,8},{10,11... | collective-permute-start | bytes 3538952 | tf_op jit(solution)/shard_map/ppermute | solution.py:139
  100.7 18.9 %collective-permute-start.10 = (f32[1,256,512]{2,1,0:T(8,128)S(1)}, f32[1,256,512]{2,1,0:T(8,128)S(1)}, u32[]{:S(2)}, u32[]{:S(2)}) collective-permute-start(f32[1,256,512]{2,1,0:T(8,128)S(1)} %part_of.6.refs_3_), channel_id=1, source_target_pairs={{8,0},{12,4},{16,24},{20,28},{9,1},{13,5},{17,25},{21,29},{10,2},{... | collective-permute-start | bytes 1572872 | tf_op jit(solution)/shard_map/ppermute | solution.py:135
  119.5 17.5 %collective-permute-start.17 = (f32[6,128,256]{2,1,0:T(8,128)S(1)}, f32[6,128,256]{2,1,0:T(8,128)S(1)}, u32[]{:S(2)}, u32[]{:S(2)}) collective-permute-start(f32[6,128,256]{2,1,0:T(8,128)S(1)} %own_blocks.4.refs_2_.refs_1_), channel_id=1, source_target_pairs={{0,1},{1,0},{2,3},{3,2},{4,5},{5,4},{6,7},{7,6},{8,9},{9,8},{10,11... | collective-permute-start | bytes 2359304 | tf_op jit(solution)/shard_map/ppermute | solution.py:139
  119.6 20.0 %collective-permute-start.18 = (f32[6,128,256]{2,1,0:T(8,128)S(1)}, f32[6,128,256]{2,1,0:T(8,128)}, u32[]{:S(2)}, u32[]{:S(2)}) collective-permute-start(f32[6,128,256]{2,1,0:T(8,128)S(1)} %own_blocks.4.refs_2_.refs_1_), channel_id=1, source_target_pairs={{0,2},{1,3},{2,0},{3,1},{4,6},{5,7},{6,4},{7,5},{8,10},{9,11},{10,... | collective-permute-start | bytes 2359304 | tf_op jit(solution)/shard_map/ppermute | solution.py:139
  121.2 23.4 %collective-permute-start.28 = (f32[9,128,256]{2,1,0:T(8,128)S(1)}, f32[9,128,256]{2,1,0:T(8,128)S(1)}, u32[]{:S(2)}, u32[]{:S(2)}) collective-permute-start(f32[9,128,256]{2,1,0:T(8,128)S(1)} %collective-permute-done.14.refs_3_.refs_4_), channel_id=1, source_target_pairs={{0,1},{1,0},{2,3},{3,2},{4,5},{5,4},{6,7},{7,6},{8,9},{9,8},{10,11... | collective-permute-start | bytes 3538952 | tf_op jit(solution)/shard_map/ppermute | solution.py:139
  132.4 26.1 %collective-permute-start.29 = (f32[2,256,512]{2,1,0:T(8,128)S(1)}, f32[2,256,512]{2,1,0:T(8,128)S(1)}, u32[]{:S(2)}, u32[]{:S(2)}) collective-permute-start(f32[2,256,512]{2,1,0:T(8,128)S(1)} %side_payload.2.refs_2_), channel_id=1, source_target_pairs={{0,4},{4,0},{8,12},{12,8},{16,20},{20,16},{24,28},{28,24},{1,5},{5... | collective-permute-start | bytes 3145736 | tf_op jit(solution)/shard_map/ppermute | solution.py:139
  140.4 20.5 %collective-permute-start.25 = (f32[6,128,256]{2,1,0:T(8,128)S(1)}, f32[6,128,256]{2,1,0:T(8,128)S(1)}, u32[]{:S(2)}, u32[]{:S(2)}) collective-permute-start(f32[6,128,256]{2,1,0:T(8,128)S(1)} %own_blocks.5.refs_6_.refs_5_), channel_id=1, source_target_pairs={{0,2},{1,3},{2,0},{3,1},{4,6},{5,7},{6,4},{7,5},{8,10},{9,11},{10,... | collective-permute-start | bytes 2359304 | tf_op jit(solution)/shard_map/ppermute | solution.py:139
  147.6 30.6 %collective-permute-start.30 = (f32[2,256,512]{2,1,0:T(8,128)S(1)}, f32[2,256,512]{2,1,0:T(8,128)}, u32[]{:S(2)}, u32[]{:S(2)}) collective-permute-start(f32[2,256,512]{2,1,0:T(8,128)S(1)} %side_payload.3.refs_7_), channel_id=1, source_target_pairs={{0,4},{4,0},{8,12},{12,8},{16,20},{20,16},{24,28},{28,24},{1,5},{5... | collective-permute-start | bytes 3145736 | tf_op jit(solution)/shard_map/ppermute | solution.py:139
  149.1 37.2 %collective-permute-start.16 = (f32[256,1024]{1,0:T(8,128)}, f32[256,1024]{1,0:T(8,128)}, u32[]{:S(2)}, u32[]{:S(2)}) collective-permute-start(f32[256,1024]{1,0:T(8,128)} %get-tuple-element.23), channel_id=1, source_target_pairs={{0,2},{1,3},{2,0},{3,1},{4,6},{5,7},{6,4},{7,5},{8,10},{9,11},{10,... | collective-permute-start | bytes 3145736 | tf_op jit(solution)/shard_map/ppermute | solution.py:139
  149.6 18.1 %collective-permute-start.24 = (f32[6,128,256]{2,1,0:T(8,128)S(1)}, f32[6,128,256]{2,1,0:T(8,128)}, u32[]{:S(2)}, u32[]{:S(2)}) collective-permute-start(f32[6,128,256]{2,1,0:T(8,128)S(1)} %own_blocks.5.refs_6_.refs_5_), channel_id=1, source_target_pairs={{0,1},{1,0},{2,3},{3,2},{4,5},{5,4},{6,7},{7,6},{8,9},{9,8},{10,11... | collective-permute-start | bytes 2359304 | tf_op jit(solution)/shard_map/ppermute | solution.py:139
  169.7 20.6 %collective-permute-start.31 = (f32[7,3,512]{2,1,0:T(4,128)S(1)}, f32[7,3,512]{2,1,0:T(4,128)S(1)}, u32[]{:S(2)}, u32[]{:S(2)}) collective-permute-start(f32[7,3,512]{2,1,0:T(4,128)S(1)} %get-tuple-element.29), channel_id=1, source_target_pairs={{0,16},{4,20},{8,24},{12,28},{16,0},{20,4},{24,8},{28,12},{1,17},{... | collective-permute-start | bytes 129032 | tf_op jit(solution)/shard_map/ppermute | solution.py:139
  (35 other events, 356.2 us)
